TPU v7x, 32 devices: a whole 2x2x4 slice. The times are simulated.
32 devices in a mesh: dp: 16 (over z, x, core), tensor: 2 (over y).
Axes of the slice: x: 2, y: 2, z: 4, core: 2. Of those that a mesh axis runs over, the one named last changes fastest.
Arguments:
- activations: bfloat16 [10240, 1024], P('dp'), may hold values from -6 to 6
- cotangent: bfloat16 [10240, 1024], P('dp'), may hold values from -6 to 6
- parent_slot: int32 [80], replicated, may hold values from -1 to 79, as said below
- attention_gain: bfloat16 [1024], replicated, may hold values from 0.5 to 1.5
- attention_shift: bfloat16 [1024], replicated, may hold values from -1.75 to 1.75
- joined_weight: bfloat16 [1024, 3072], P(None, 'tensor'), may hold values from -0.25 to 0.25
- joined_bias: bfloat16 [2048], P('tensor'), may hold values from -3 to 3
- output_weight: bfloat16 [1024, 1024], P('tensor'), may hold values from -1.5 to 1.5
- output_bias: bfloat16 [1024], replicated, may hold values from -3 to 3
- feed_gain: bfloat16 [1024], replicated, may hold values from 0.5 to 1.5
- feed_shift: bfloat16 [1024], replicated, may hold values from -1.75 to 1.75
- expand_weight: bfloat16 [1024, 4096], P(None, 'tensor'), may hold values from -0.1875 to 0.1875
- expand_bias: bfloat16 [4096], P('tensor'), may hold values from -3 to 3
- contract_weight: bfloat16 [4096, 1024], P('tensor'), may hold values from -0.1875 to 0.1875
- contract_bias: bfloat16 [1024], replicated, may hold values from -3 to 3
Outputs:
- layer_output: bfloat16 [10240, 1024], P('dp')
- input_gradient: bfloat16 [10240, 1024], P('dp')
- attention_gain_gradient: float32 [1024], P('dp')
- attention_shift_gradient: float32 [1024], P('dp')
- joined_weight_gradient: float32 [1024, 3072], P('dp', 'tensor')
- joined_bias_gradient: float32 [1024, 2], P('dp', 'tensor')
- output_weight_gradient: float32 [1024, 1024], P('dp', 'tensor')
- output_bias_gradient: float32 [1024], P('dp')
- feed_gain_gradient: float32 [1024], P('dp')
- feed_shift_gradient: float32 [1024], P('dp')
- expand_weight_gradient: float32 [1024, 4096], P('dp', 'tensor')
- expand_bias_gradient: float32 [2048, 2], P('dp', 'tensor')
- contract_weight_gradient: float32 [1024, 4096], P('dp', 'tensor')
- contract_bias_gradient: float32 [1024], P('dp')
Inputs may be any that keep to these rules, and one draw needn't show every extreme that they name: parent_slot[s] is the slot of segment s's parent, -1 for a tree's root. Each tree has 8 trunk segments in a chain from the root, 4 branch segments whose parent is the last trunk segment, and 2 leaf segments under each branch; the 20 segments of a tree occupy 20 cyclically consecutive slots in any order.
All inputs are finite; a program needn't handle non-finite values.
Results may differ from a plain program's by a relative error of at most 0.017.
Values may be sent and summed in bfloat16 or wider, within the bound.
No kernel may reach another device: no remote copies, remote signals or barrier semaphores. Data moves between devices by JAX's collectives and lax.ppermute only.
A program may use at most 256 MiB of HBM per device.

v0:
```python
from functools import partial

import jax
import jax.numpy as jnp
from jax import lax
from jax.sharding import PartitionSpec as P

H = 16
HD = 64
SEG = 128
SEG_DEV = 5
ANC = 10
REACH = 4


EPSILON = 1e-05
NEGATIVE = -1e30


def for_sending(x):

    def short(part):
        return part.astype(jnp.bfloat16) if part.dtype == jnp.float32 else part

    return jax.tree.map(short, x)


def from_behind(value, axis, steps):
    count = lax.axis_size(axis)
    pairs = [(source, (source + steps) % count) for source in range(count)]
    return lax.ppermute(value, axis, pairs)


def norm_rows(rows, gain, shift):
    centered = rows - jnp.mean(rows, axis=-1, keepdims=True)
    variance = jnp.mean(centered * centered, axis=-1, keepdims=True)
    return centered * lax.rsqrt(variance + EPSILON) * gain + shift


def ancestry(parent_slot, first, count, depth_most):
    every = jnp.arange(parent_slot.shape[0], dtype=jnp.int32)
    current = first + jnp.arange(count, dtype=jnp.int32)
    chain = []
    for level in range(depth_most):
        chain.append(current)
        match = (current[:, None] == every[None, :]).astype(jnp.int32)
        upward = jnp.sum(match * parent_slot[None, :], axis=1)
        current = jnp.where(current >= 0, upward, -1)
    return jnp.stack(chain, axis=1)


def score_block(queries, keys, slope, valid_keys):
    seg_rows = queries.shape[1]
    span = keys.shape[1]
    raw = jnp.einsum("jqd,jkd->jqk", queries, keys, preferred_element_type=jnp.float32)
    query_pos = jnp.arange(seg_rows)[:, None]
    key_pos = jnp.arange(span)[None, :]
    level = key_pos // seg_rows
    distance = (level * seg_rows + query_pos - key_pos % seg_rows).astype(jnp.float32)
    allowed = ((level > 0) | (key_pos % seg_rows <= query_pos))[None] & valid_keys[:, None, :]
    return jnp.where(allowed, raw - slope * distance[None], NEGATIVE)


def fetch(pair, by):
    return jax.tree.map(
        lambda part, own: part.astype(own.dtype), from_behind(for_sending(pair), "dp", by), pair
    )


def send_back(pair, by):
    return (
        from_behind(pair[0].astype(jnp.bfloat16), "dp", by).astype(jnp.float32),
        from_behind(pair[1].astype(jnp.bfloat16), "dp", by).astype(jnp.float32),
    )


def assemble(pair, fetcher):
    pieces = []
    for offset in range(-REACH, REACH + 1):
        pieces.append(pair if offset == 0 else fetcher(pair, -offset))
    return (
        jnp.concatenate([piece[0] for piece in pieces], axis=0),
        jnp.concatenate([piece[1] for piece in pieces], axis=0),
    )


def shards(
    activations,
    cotangent,
    parent_slot,
    attention_gain,
    attention_shift,
    joined_weight,
    joined_bias,
    output_weight,
    output_bias,
    feed_gain,
    feed_shift,
    expand_weight,
    expand_bias,
    contract_weight,
    contract_bias,
):
    rows_here = activations.shape[0]
    heads_here = joined_weight.shape[1] // (3 * HD)
    width_here = heads_here * HD
    device_rank = lax.axis_index("dp")
    tensor_rank = lax.axis_index("tensor")
    scale = HD ** (-0.5)
    window_segs = (2 * REACH + 1) * SEG_DEV
    residual = activations.astype(jnp.float32)
    first_norm, first_back = jax.vjp(
        norm_rows, residual, attention_gain.astype(jnp.float32), attention_shift.astype(jnp.float32)
    )
    first_low = first_norm.astype(jnp.bfloat16)
    joined = jnp.dot(first_low, joined_weight, preferred_element_type=jnp.float32).reshape(
        rows_here, heads_here, 3, HD
    )
    bias_pair = joined_bias.astype(jnp.float32).reshape(heads_here, 2, HD)
    queries = ((joined[:, :, 0] + bias_pair[:, 0]) * scale).astype(jnp.bfloat16)
    keys_here = joined[:, :, 1].astype(jnp.bfloat16)
    values_here = (joined[:, :, 2] + bias_pair[:, 1]).astype(jnp.bfloat16)
    ancestors = ancestry(parent_slot, device_rank * SEG_DEV, SEG_DEV, ANC)
    valid = ancestors >= 0
    place = jnp.mod(ancestors - (device_rank - REACH) * SEG_DEV, parent_slot.shape[0])
    picker = (place[:, :, None] == jnp.arange(window_segs)[None, None, :]) & valid[:, :, None]
    picker_low = picker.astype(jnp.bfloat16)
    picker_wide = picker.astype(jnp.float32)
    valid_keys = jnp.repeat(valid, SEG, axis=1)

    def pick(window):
        shaped = window.reshape(window_segs, SEG, heads_here, HD)
        chosen = jnp.einsum("jaw,wshd->hjasd", picker_low, shaped)
        return chosen.reshape(heads_here, SEG_DEV, ANC * SEG, HD)

    key_window, value_window = assemble((keys_here, values_here), fetch)
    key_anc = pick(key_window)
    value_anc = pick(value_window)
    head_ids = tensor_rank * heads_here + jnp.arange(heads_here)
    slopes = jnp.exp2(-8.0 * (head_ids + 1).astype(jnp.float32) / H)
    query_heads = queries.reshape(SEG_DEV, SEG, heads_here, HD).transpose(2, 0, 1, 3)

    def forward_head(inputs):
        head_queries, head_keys, head_values, slope = inputs
        scores = score_block(head_queries, head_keys, slope, valid_keys)
        top = jnp.max(scores, axis=-1, keepdims=True)
        weights = jnp.exp(scores - top)
        total = jnp.sum(weights, axis=-1, keepdims=True)
        probs = (weights / total).astype(jnp.bfloat16)
        head_out = jnp.einsum(
            "jqk,jkd->jqd", probs, head_values, preferred_element_type=jnp.float32
        )
        return (head_out.astype(jnp.bfloat16), (top + jnp.log(total))[..., 0])

    out_heads, lse_heads = lax.map(forward_head, (query_heads, key_anc, value_anc, slopes))
    mixed = out_heads.transpose(1, 2, 0, 3).reshape(rows_here, width_here)
    attention_part = jnp.dot(mixed, output_weight, preferred_element_type=jnp.float32)
    attention_total = lax.psum(attention_part.astype(jnp.bfloat16), "tensor").astype(jnp.float32)
    middle = residual + attention_total + output_bias.astype(jnp.float32)
    second_norm, second_back = jax.vjp(
        norm_rows, middle, feed_gain.astype(jnp.float32), feed_shift.astype(jnp.float32)
    )
    second_low = second_norm.astype(jnp.bfloat16)
    hidden_pre = jnp.dot(
        second_low, expand_weight, preferred_element_type=jnp.float32
    ) + expand_bias.astype(jnp.float32)
    hidden_act, gelu_back = jax.vjp(partial(jax.nn.gelu, approximate=True), hidden_pre)
    hidden_low = hidden_act.astype(jnp.bfloat16)
    feed_part = jnp.dot(hidden_low, contract_weight, preferred_element_type=jnp.float32)
    feed_total = lax.psum(feed_part.astype(jnp.bfloat16), "tensor").astype(jnp.float32)
    layer_output = (middle + feed_total + contract_bias.astype(jnp.float32)).astype(jnp.bfloat16)
    out_grad = cotangent.astype(jnp.float32)
    contract_grad_t = jnp.einsum(
        "td,tf->df", cotangent, hidden_low, preferred_element_type=jnp.float32
    )
    contract_bias_grad = jnp.sum(out_grad, axis=0)
    hidden_grad = jnp.einsum(
        "td,fd->tf", cotangent, contract_weight, preferred_element_type=jnp.float32
    )
    pre_grad = gelu_back(hidden_grad)[0].astype(jnp.bfloat16)
    expand_grad = jnp.einsum("td,tf->df", second_low, pre_grad, preferred_element_type=jnp.float32)
    expand_bias_grad = jnp.sum(pre_grad.astype(jnp.float32), axis=0).reshape(-1, 1)
    second_part = jnp.einsum(
        "tf,df->td", pre_grad, expand_weight, preferred_element_type=jnp.float32
    )
    second_grad = lax.psum(second_part.astype(jnp.bfloat16), "tensor").astype(jnp.float32)
    middle_back, feed_gain_grad, feed_shift_grad = second_back(second_grad)
    middle_grad = middle_back + out_grad
    branch_low = middle_grad.astype(jnp.bfloat16)
    output_bias_grad = jnp.sum(middle_grad, axis=0)
    output_grad_t = jnp.einsum("td,tf->df", branch_low, mixed, preferred_element_type=jnp.float32)
    mixed_grad = jnp.einsum(
        "td,fd->tf", branch_low, output_weight, preferred_element_type=jnp.float32
    ).astype(jnp.bfloat16)
    grad_heads = mixed_grad.reshape(SEG_DEV, SEG, heads_here, HD).transpose(2, 0, 1, 3)

    def backward_head(inputs):
        head_queries, head_keys, head_values, slope, head_grad, head_lse = inputs
        scores = score_block(head_queries, head_keys, slope, valid_keys)
        probs = jnp.exp(scores - head_lse[..., None])
        prob_grad = jnp.einsum(
            "jqd,jkd->jqk", head_grad, head_values, preferred_element_type=jnp.float32
        )
        delta = jnp.sum(probs * prob_grad, axis=-1, keepdims=True)
        score_grad = (probs * (prob_grad - delta)).astype(jnp.bfloat16)
        query_grad = jnp.einsum(
            "jqk,jkd->jqd", score_grad, head_keys, preferred_element_type=jnp.float32
        )
        key_grad = jnp.einsum(
            "jqk,jqd->jkd", score_grad, head_queries, preferred_element_type=jnp.float32
        )
        value_grad = jnp.einsum(
            "jqk,jqd->jkd",
            probs.astype(jnp.bfloat16),
            head_grad,
            preferred_element_type=jnp.float32,
        )
        return (query_grad.astype(jnp.bfloat16), key_grad, value_grad)

    query_back, key_back, value_back = lax.map(
        backward_head, (query_heads, key_anc, value_anc, slopes, grad_heads, lse_heads)
    )
    key_spread = jnp.einsum(
        "jaw,hjasd->wshd", picker_wide, key_back.reshape(heads_here, SEG_DEV, ANC, SEG, HD)
    )
    value_spread = jnp.einsum(
        "jaw,hjasd->wshd", picker_wide, value_back.reshape(heads_here, SEG_DEV, ANC, SEG, HD)
    )
    key_spread = key_spread.reshape(2 * REACH + 1, rows_here, heads_here, HD)
    value_spread = value_spread.reshape(2 * REACH + 1, rows_here, heads_here, HD)
    key_total = key_spread[REACH]
    value_total = value_spread[REACH]
    for offset in range(-REACH, REACH + 1):
        if offset != 0:
            arrived = send_back((key_spread[offset + REACH], value_spread[offset + REACH]), offset)
            key_total = key_total + arrived[0]
            value_total = value_total + arrived[1]
    key_low = key_total.astype(jnp.bfloat16)
    value_low = value_total.astype(jnp.bfloat16)
    query_rows = query_back.transpose(1, 2, 0, 3).reshape(rows_here, heads_here, HD) * scale
    joined_grad = jnp.stack([query_rows, key_low, value_low], axis=2).reshape(
        rows_here, 3 * width_here
    )
    joined_weight_grad = jnp.einsum(
        "td,tf->df", first_low, joined_grad, preferred_element_type=jnp.float32
    )
    joined_bias_grad = jnp.stack(
        [
            jnp.sum(query_rows.astype(jnp.float32), axis=0),
            jnp.sum(value_low.astype(jnp.float32), axis=0),
        ],
        axis=1,
    ).reshape(-1, 1)
    first_part = jnp.einsum(
        "tf,df->td", joined_grad, joined_weight, preferred_element_type=jnp.float32
    )
    first_grad = lax.psum(first_part.astype(jnp.bfloat16), "tensor").astype(jnp.float32)
    residual_back, attention_gain_grad, attention_shift_grad = first_back(first_grad)
    input_gradient = (residual_back + middle_grad).astype(jnp.bfloat16)
    everything = (
        lax.psum_scatter(expand_grad, "dp", scatter_dimension=0, tiled=True),
        lax.psum_scatter(contract_grad_t, "dp", scatter_dimension=0, tiled=True),
        lax.psum_scatter(expand_bias_grad, "dp", scatter_dimension=0, tiled=True),
        lax.psum_scatter(feed_gain_grad, "dp", scatter_dimension=0, tiled=True),
        lax.psum_scatter(feed_shift_grad, "dp", scatter_dimension=0, tiled=True),
        lax.psum_scatter(contract_bias_grad, "dp", scatter_dimension=0, tiled=True),
        lax.psum_scatter(joined_weight_grad, "dp", scatter_dimension=0, tiled=True),
        lax.psum_scatter(output_grad_t, "dp", scatter_dimension=0, tiled=True),
        lax.psum_scatter(joined_bias_grad, "dp", scatter_dimension=0, tiled=True),
        lax.psum_scatter(attention_gain_grad, "dp", scatter_dimension=0, tiled=True),
        lax.psum_scatter(attention_shift_grad, "dp", scatter_dimension=0, tiled=True),
        lax.psum_scatter(output_bias_grad, "dp", scatter_dimension=0, tiled=True),
    )
    feed_done = everything[:6]
    attention_done = everything[6:]
    return (
        layer_output,
        input_gradient,
        attention_done[3],
        attention_done[4],
        attention_done[0],
        attention_done[2],
        attention_done[1],
        attention_done[5],
        feed_done[3],
        feed_done[4],
        feed_done[0],
        feed_done[2],
        feed_done[1],
        feed_done[5],
    )


def solution(mesh):
    in_specs = (
        P("dp", None),
        P("dp", None),
        P(),
        P(),
        P(),
        P(None, "tensor"),
        P("tensor"),
        P("tensor", None),
        P(),
        P(),
        P(),
        P(None, "tensor"),
        P("tensor"),
        P("tensor", None),
        P(),
    )
    out_specs = (
        P("dp", None),
        P("dp", None),
        P("dp"),
        P("dp"),
        P("dp", "tensor"),
        P("dp", "tensor"),
        P("dp", "tensor"),
        P("dp"),
        P("dp"),
        P("dp"),
        P("dp", "tensor"),
        P("dp", "tensor"),
        P("dp", "tensor"),
        P("dp"),
    )
    return jax.shard_map(shards, mesh=mesh, in_specs=in_specs, out_specs=out_specs, check_vma=False)
```

profile of v0, /device:TPU:0, one launch (start us, length us, event | category | flops | bytes accessed | tf_op | source)
XLA Modules:
  0.0 1323.4 jit_solution(12605186657035169986)
XLA Ops:
  38.7 15.0 %collective-permute-done.8 = bf16[640,8,64]{0,2,1:T(8,128)(2,1)} collective-permute-done((bf16[640,8,64]{0,2,1:T(8,128)(2,1)}, bf16[640,8,64]{0,2,1:T(8,128)(2,1)}, u32[]{:S(2)}, u32[]{:S(2)}) %collective-permute-start.8) | collective-permute-done | bytes 655392 | tf_op jit(solution)/shard_map/ppermute | solution.py:31
  64.5 28.4 %collective-permute-start.12 = (bf16[640,8,64]{0,2,1:T(8,128)(2,1)}, bf16[640,8,64]{0,2,1:T(8,128)(2,1)S(1)}, u32[]{:S(2)}, u32[]{:S(2)}) collective-permute-start(bf16[640,8,64]{0,2,1:T(8,128)(2,1)} %fusion.103), channel_id=1, source_target_pairs={{0,30},{2,0},{4,2},{6,4},{8,6},{10,8},{12,10},{14,12},{16,14},{18,... | collective-permute-start | bytes 1966088 | tf_op jit(solution)/shard_map/ppermute | solution.py:31
  110.1 15.1 %collective-permute-done.13 = bf16[640,8,64]{0,2,1:T(8,128)(2,1)S(1)} collective-permute-done((bf16[640,8,64]{0,2,1:T(8,128)(2,1)}, bf16[640,8,64]{0,2,1:T(8,128)(2,1)S(1)}, u32[]{:S(2)}, u32[]{:S(2)}) %collective-permute-start.13) | collective-permute-done | bytes 655392 | tf_op jit(solution)/shard_map/ppermute | solution.py:31
  131.1 10.2 reshape.1042
  151.0 17.6 %reshape.1048 = bf16[8,5,1280,64]{2,1,3,0:T(8,128)(2,1)} reshape(bf16[8,5,10,128,64]{3,2,1,4,0:T(8,128)(2,1)} %fusion.80) | data formatting | bytes 13107200 | tf_op jit(solution)/shard_map/reshape | solution.py:134
  240.7 17.6 %reshape.1046 = bf16[8,5,1280,64]{2,1,3,0:T(8,128)(2,1)} reshape(bf16[8,5,10,128,64]{3,2,1,4,0:T(8,128)(2,1)} %fusion.77) | data formatting | bytes 13107200 | tf_op jit(solution)/shard_map/reshape | solution.py:134
  267.8 57.5 %while.32 = (s32[]{:T(128)}, bf16[8,5,128,64]{2,3,1,0:T(8,128)(2,1)}, f32[8,5,128]{2,1,0:T(8,128)S(1)}, bf16[8,5,128,64]{2,3,1,0:T(8,128)(2,1)}, bf16[8,5,1280,6...) while((s32[]{:T(128)}, ...), condition=%wide.region_14.15_spmd.clone, body=%wide.region_11.14_spmd.clone.sunk | while | flops 218139520 | bytes 13352107 | solution.py:155
  331.8 49.6 %all-reduce.12.cloned.1.call-done = bf16[640,1024]{1,0:T(8,128)(2,1)} async-done(((bf16[640,1024]{1,0:T(8,128)(2,1)}), bf16[640,1024]{1,0:T(8,128)(2,1)}) %all-reduce.12.cloned.1.call-update) | async-done | bytes 1310736 | tf_op jit(solution)/shard_map/psum | solution.py:158
  401.5 45.8 %all-reduce.14.cloned.1.call-done = bf16[640,1024]{1,0:T(8,128)(2,1)} async-done(((bf16[640,1024]{1,0:T(8,128)(2,1)}), bf16[640,1024]{1,0:T(8,128)(2,1)}) %all-reduce.14.cloned.1.call-update) | async-done | bytes 1310736 | tf_op jit(solution)/shard_map/psum | solution.py:186
  467.3 107.3 %while.33 = (s32[]{:T(128)}, bf16[8,5,128,64]{2,3,1,0:T(8,128)(2,1)}, bf16[8,5,1280,64]{2,3,1,0:T(8,128)(2,1)}, bf16[8,5,1280,64]{2,3,1,0:T(8,128)(2,1)}, bf16[8...) while((s32[]{:T(128)}, ...), condition=%wide.region_24.25_spmd.clone, body=%wide.region_22.24_spmd.clone.sunk | while | flops 533531520 | bytes 32430276 | solution.py:220
  574.6 13.4 %reshape.1034 = bf16[8,5,10,128,64]{3,2,4,1,0:T(8,128)(2,1)} reshape(bf16[8,5,1280,64]{2,3,1,0:T(8,128)(2,1)} %get-tuple-element.265) | data formatting | bytes 13107200 | tf_op jit(solution)/shard_map/reshape | solution.py:227
  588.0 10.4 fusion.146
  625.8 13.5 %reshape.1033 = bf16[8,5,10,128,64]{3,2,4,1,0:T(8,128)(2,1)} reshape(bf16[8,5,1280,64]{2,3,1,0:T(8,128)(2,1)} %get-tuple-element.264) | data formatting | bytes 13107200 | tf_op jit(solution)/shard_map/reshape | solution.py:224
  641.3 12.3 fusion.147
  710.1 10.5 collective-permute-done.17
  722.1 12.5 collective-permute-done.18
  738.2 10.4 collective-permute-done.19
  806.0 10.4 convolution_bitcast_fusion.2
  839.1 27.2 %reduce-scatter.19.cloned.1.call-done = f32[64,1]{1,0:T(8,128)} async-done(((f32[1024,1]{1,0:T(8,128)}), f32[64,1]{1,0:T(8,128)}) %reduce-scatter.19.cloned.1.call-update) | async-done | bytes 272
  867.6 75.0 %all-reduce.16.cloned.1.call-done = (bf16[640,1024]{1,0:T(8,128)(2,1)}, bf16[640,1024]{1,0:T(8,128)(2,1)}) async-done(((bf16[640,1024]{1,0:T(8,128)(2,1)}, bf16[640,1024]{1,0:T(8,128)(2,1)}), (bf16[640,1024]{1,0:T(8,128)(2,1)}, bf16[640,1024]{1,0:T(8,128)(2,1)})) %all-reduce.16.cloned.1.call-update) | async-done | bytes 2621456 | tf_op jit(solution)/shard_map/psum | solution.py:170
  946.9 61.5 %all-reduce.6 = (f32[1024]{0:T(1024)S(1)}, f32[1024]{0:T(1024)S(1)}, f32[1024]{0:T(1024)S(1)}, f32[1024]{0:T(1024)S(1)}, f32[1024]{0:T(1024)S(1)}, /*index=5*/f32[1024]{0:T(1024)S(1)}) all-reduce(f32[1024]{0:T(1024)S(1)} %get-tuple-element.444, f32[1024]{0:T(1024)S(1)} %get-tuple-element.448, ...), channel_id=2, replica_groups=mesh['dp'=16,'tensor'=2] {'dp'}, use_global_device_ids=true, to_apply=%region_29.30.clone | all-reduce | flops 6144 | bytes 49152
  1017.0 80.8 %reduce-scatter.13.cloned.1.call-done = f32[64,1536]{1,0:T(8,128)} async-done(((f32[1024,1536]{1,0:T(8,128)}), f32[64,1536]{1,0:T(8,128)}) %reduce-scatter.13.cloned.1.call-update) | async-done | bytes 393232 | tf_op jit(solution)/shard_map/reduce_scatter | solution.py:267
  1097.8 109.0 %reduce-scatter.23.cloned.1.call-done = f32[64,2048]{1,0:T(8,128)} async-done(((f32[1024,2048]{1,0:T(8,128)}), f32[64,2048]{1,0:T(8,128)}) %reduce-scatter.23.cloned.1.call-update) | async-done | bytes 524304
  1206.8 109.7 %reduce-scatter.17.cloned.1.call-done = f32[64,2048]{1,0:T(8,128)} async-done(((f32[1024,2048]{1,0:T(8,128)}), f32[64,2048]{1,0:T(8,128)}) %reduce-scatter.17.cloned.1.call-update) | async-done | bytes 524304 | tf_op jit(solution)/shard_map/reduce_scatter | solution.py:261
  (510 shorter events, 551.5 us)
Async XLA Ops:
  7.2 374.1 %all-reduce.12.cloned.1.call-start = ((), (), s32[]{:S(2)}) async-start(), calls=%async_computation.6 | async-start | bytes 2621440 | tf_op jit(solution)/shard_map/psum | solution.py:158
  18.3 109.0 %collective-permute-start.15 = (bf16[640,8,64]{0,2,1:T(8,128)(2,1)}, bf16[640,8,64]{0,2,1:T(8,128)(2,1)}, u32[]{:S(2)}, u32[]{:S(2)}) collective-permute-start(bf16[640,8,64]{0,2,1:T(8,128)(2,1)} %fusion.103), channel_id=1, source_target_pairs={{0,24},{2,26},{4,28},{6,30},{8,0},{10,2},{12,4},{14,6},{16,8},{18,... | collective-permute-start | bytes 1966088 | tf_op jit(solution)/shard_map/ppermute | solution.py:31
  23.3 74.0 %collective-permute-start.11 = (bf16[640,8,64]{0,2,1:T(8,128)(2,1)}, bf16[640,8,64]{0,2,1:T(8,128)(2,1)}, u32[]{:S(2)}, u32[]{:S(2)}) collective-permute-start(bf16[640,8,64]{0,2,1:T(8,128)(2,1)} %fusion.103), channel_id=1, source_target_pairs={{0,2},{2,4},{4,6},{6,8},{8,10},{10,12},{12,14},{14,16},{16,18},{18... | collective-permute-start | bytes 1966088 | tf_op jit(solution)/shard_map/ppermute | solution.py:31
  23.3 71.5 %collective-permute-start.10 = (bf16[640,8,64]{0,2,1:T(8,128)(2,1)}, bf16[640,8,64]{0,2,1:T(8,128)(2,1)}, u32[]{:S(2)}, u32[]{:S(2)}) collective-permute-start(bf16[640,8,64]{0,2,1:T(8,128)(2,1)} %fusion.103), channel_id=1, source_target_pairs={{0,4},{2,6},{4,8},{6,10},{8,12},{10,14},{12,16},{14,18},{16,20},{1... | collective-permute-start | bytes 1966088 | tf_op jit(solution)/shard_map/ppermute | solution.py:31
  53.7 72.4 %collective-permute-start.14 = (bf16[640,8,64]{0,2,1:T(8,128)(2,1)}, bf16[640,8,64]{0,2,1:T(8,128)(2,1)S(1)}, u32[]{:S(2)}, u32[]{:S(2)}) collective-permute-start(bf16[640,8,64]{0,2,1:T(8,128)(2,1)} %fusion.103), channel_id=1, source_target_pairs={{0,26},{2,28},{4,30},{6,0},{8,2},{10,4},{12,6},{14,8},{16,10},{18,... | collective-permute-start | bytes 1966088 | tf_op jit(solution)/shard_map/ppermute | solution.py:31
  97.4 121.4 %collective-permute-start.7 = (bf16[640,8,64]{0,2,1:T(8,128)(2,1)}, bf16[640,8,64]{0,2,1:T(8,128)(2,1)}, u32[]{:S(2)}, u32[]{:S(2)}) collective-permute-start(bf16[640,8,64]{0,2,1:T(8,128)(2,1)} %fusion.106), channel_id=1, source_target_pairs={{0,24},{2,26},{4,28},{6,30},{8,0},{10,2},{12,4},{14,6},{16,8},{18,... | collective-permute-start | bytes 1966088 | tf_op jit(solution)/shard_map/ppermute | solution.py:31
  106.2 89.0 %collective-permute-start.3 = (bf16[640,8,64]{0,2,1:T(8,128)(2,1)}, bf16[640,8,64]{0,2,1:T(8,128)(2,1)}, u32[]{:S(2)}, u32[]{:S(2)}) collective-permute-start(bf16[640,8,64]{0,2,1:T(8,128)(2,1)} %fusion.106), channel_id=1, source_target_pairs={{0,2},{2,4},{4,6},{6,8},{8,10},{10,12},{12,14},{14,16},{16,18},{18... | collective-permute-start | bytes 1966088 | tf_op jit(solution)/shard_map/ppermute | solution.py:31
  125.2 67.7 %collective-permute-start.2 = (bf16[640,8,64]{0,2,1:T(8,128)(2,1)}, bf16[640,8,64]{0,2,1:T(8,128)(2,1)}, u32[]{:S(2)}, u32[]{:S(2)}) collective-permute-start(bf16[640,8,64]{0,2,1:T(8,128)(2,1)} %fusion.106), channel_id=1, source_target_pairs={{0,4},{2,6},{4,8},{6,10},{8,12},{10,14},{12,16},{14,18},{16,20},{1... | collective-permute-start | bytes 1966088 | tf_op jit(solution)/shard_map/ppermute | solution.py:31
  126.2 56.3 %collective-permute-start.1 = (bf16[640,8,64]{0,2,1:T(8,128)(2,1)}, bf16[640,8,64]{0,2,1:T(8,128)(2,1)}, u32[]{:S(2)}, u32[]{:S(2)}) collective-permute-start(bf16[640,8,64]{0,2,1:T(8,128)(2,1)} %fusion.106), channel_id=1, source_target_pairs={{0,6},{2,8},{4,10},{6,12},{8,14},{10,16},{12,18},{14,20},{16,22},{... | collective-permute-start | bytes 1966088 | tf_op jit(solution)/shard_map/ppermute | solution.py:31
  331.2 116.2 %all-reduce.14.cloned.1.call-start = ((), (), s32[]{:S(2)}) async-start(), calls=%async_computation.7 | async-start | bytes 2621440 | tf_op jit(solution)/shard_map/psum | solution.py:186
  401.5 436.2 %reduce-scatter.21.cloned.1.call-start = ((), (), s32[]{:S(2)}) async-start(), calls=%async_computation.12 | async-start | bytes 1114112
  609.0 257.3 %reduce-scatter.19.cloned.1.call-start = ((), (), s32[]{:S(2)}) async-start(), calls=%async_computation.11 | async-start | bytes 557056
  625.2 54.3 %collective-permute-start.28 = (bf16[640,8,64]{0,2,1:T(8,128)(2,1)}, bf16[640,8,64]{0,2,1:T(8,128)(2,1)}, u32[]{:S(2)}, u32[]{:S(2)}) collective-permute-start(bf16[640,8,64]{0,2,1:T(8,128)(2,1)} %convert_element_type.331), channel_id=1, source_target_pairs={{0,2},{2,4},{4,6},{6,8},{8,10},{10,12},{12,14},{14,16},{16,18},{18... | collective-permute-start | bytes 1966088 | tf_op jit(solution)/shard_map/ppermute | solution.py:31
  625.2 54.3 %collective-permute-start.29 = (bf16[640,8,64]{0,2,1:T(8,128)(2,1)}, bf16[640,8,64]{0,2,1:T(8,128)(2,1)}, u32[]{:S(2)}, u32[]{:S(2)}) collective-permute-start(bf16[640,8,64]{0,2,1:T(8,128)(2,1)} %convert_element_type.333), channel_id=1, source_target_pairs={{0,4},{2,6},{4,8},{6,10},{8,12},{10,14},{12,16},{14,18},{16,20},{1... | collective-permute-start | bytes 1966088 | tf_op jit(solution)/shard_map/ppermute | solution.py:31
  679.5 55.1 %collective-permute-start.18 = (bf16[640,8,64]{0,2,1:T(8,128)(2,1)}, bf16[640,8,64]{0,2,1:T(8,128)(2,1)}, u32[]{:S(2)}, u32[]{:S(2)}) collective-permute-start(bf16[640,8,64]{0,2,1:T(8,128)(2,1)} %convert_element_type.310), channel_id=1, source_target_pairs={{0,28},{2,30},{4,0},{6,2},{8,4},{10,6},{12,8},{14,10},{16,12},{18,... | collective-permute-start | bytes 1966088 | tf_op jit(solution)/shard_map/ppermute | solution.py:31
  682.3 66.3 %collective-permute-start.19 = (bf16[640,8,64]{0,2,1:T(8,128)(2,1)}, bf16[640,8,64]{0,2,1:T(8,128)(2,1)}, u32[]{:S(2)}, u32[]{:S(2)}) collective-permute-start(bf16[640,8,64]{0,2,1:T(8,128)(2,1)} %convert_element_type.312), channel_id=1, source_target_pairs={{0,30},{2,0},{4,2},{6,4},{8,6},{10,8},{12,10},{14,12},{16,14},{18,... | collective-permute-start | bytes 1966088 | tf_op jit(solution)/shard_map/ppermute | solution.py:31
  705.2 70.4 %collective-permute-start.20 = (bf16[640,8,64]{0,2,1:T(8,128)(2,1)}, bf16[640,8,64]{0,2,1:T(8,128)(2,1)}, u32[]{:S(2)}, u32[]{:S(2)}) collective-permute-start(bf16[640,8,64]{0,2,1:T(8,128)(2,1)} %convert_element_type.314), channel_id=1, source_target_pairs={{0,2},{2,4},{4,6},{6,8},{8,10},{10,12},{12,14},{14,16},{16,18},{18... | collective-permute-start | bytes 1966088 | tf_op jit(solution)/shard_map/ppermute | solution.py:31
  708.0 67.6 %collective-permute-start.21 = (bf16[640,8,64]{0,2,1:T(8,128)(2,1)}, bf16[640,8,64]{0,2,1:T(8,128)(2,1)}, u32[]{:S(2)}, u32[]{:S(2)}) collective-permute-start(bf16[640,8,64]{0,2,1:T(8,128)(2,1)} %convert_element_type.316), channel_id=1, source_target_pairs={{0,4},{2,6},{4,8},{6,10},{8,12},{10,14},{12,16},{14,18},{16,20},{1... | collective-permute-start | bytes 1966088 | tf_op jit(solution)/shard_map/ppermute | solution.py:31
  720.5 55.1 %collective-permute-start.22 = (bf16[640,8,64]{0,2,1:T(8,128)(2,1)}, bf16[640,8,64]{0,2,1:T(8,128)(2,1)}, u32[]{:S(2)}, u32[]{:S(2)}) collective-permute-start(bf16[640,8,64]{0,2,1:T(8,128)(2,1)} %convert_element_type.318), channel_id=1, source_target_pairs={{0,6},{2,8},{4,10},{6,12},{8,14},{10,16},{12,18},{14,20},{16,22},{... | collective-permute-start | bytes 1966088 | tf_op jit(solution)/shard_map/ppermute | solution.py:31
  788.6 154.0 %all-reduce.16.cloned.1.call-start = ((), (), s32[]{:S(2)}) async-start(), calls=%async_computation.14 | async-start | bytes 5242880 | tf_op jit(solution)/shard_map/psum | solution.py:170
  793.7 223.3 %reduce-scatter.15.cloned.1.call-start = ((), (), s32[]{:S(2)}) async-start(), calls=%async_computation.9 | async-start | bytes 2228224 | tf_op jit(solution)/shard_map/reduce_scatter | solution.py:268
  798.2 299.6 %reduce-scatter.13.cloned.1.call-start = ((), (), s32[]{:S(2)}) async-start(), calls=%async_computation.8 | async-start | bytes 6684672 | tf_op jit(solution)/shard_map/reduce_scatter | solution.py:267
  805.9 400.9 %reduce-scatter.23.cloned.1.call-start = ((), (), s32[]{:S(2)}) async-start(), calls=%async_computation.13 | async-start | bytes 8912896
  825.6 490.8 %reduce-scatter.17.cloned.1.call-start = ((), (), s32[]{:S(2)}) async-start(), calls=%async_computation.10 | async-start | bytes 8912896 | tf_op jit(solution)/shard_map/reduce_scatter | solution.py:261
  (61 other events, 981.5 us)
Sparse Core Ops, SparseCore 0:
  331.3 50.0 all-reduce.11
  401.6 45.7 all-reduce.13
  609.1 88.6 reduce-scatter.20
  788.7 77.5 reduce-scatter.18
  869.0 73.5 all-reduce.15
  947.2 61.6 reduce-scatter.14
  1013.5 84.2 reduce-scatter.12
  1103.0 103.7 reduce-scatter.22
  1212.0 104.4 reduce-scatter.16
where the time goes:
time: 1340 us; the launch traced here: 1320 us
  waiting for transfers between devices  587 us (44%)
  local copies, waits for them, and re-layouts  257 us (19%)
  matrix products  243 us (18%)
  starting transfers between devices  92.1 us (7%)
  other arithmetic  67.1 us (5%)
  blocking collectives  61.5 us (5%)
  between operations  15.7 us (1%)
    unnamed x12, waiting for transfers between devices  136 us
    reduce_scatter x1, waiting for transfers between devices, shards(): lax.psum_scatter(expand_grad, 'dp', scatter_dimension=0, tiled=True)  110 us
    ppermute x32, starting transfers between devices, from_behind(): return lax.ppermute(value, axis, pairs)  90.8 us
    ppermute x32, waiting for transfers between devices, from_behind(): return lax.ppermute(value, axis, pairs)  89.4 us
    reduce_scatter x1, waiting for transfers between devices, shards(): lax.psum_scatter(joined_weight_grad, 'dp', scatter_dimension=0, tiled=True)  80.8 us
    psum x1, waiting for transfers between devices, shards(): lax.psum(feed_part.astype(jnp.bfloat16), 'tensor').astype(jnp.float32)  75 us
    unnamed x1, blocking collectives  61.5 us
    reshape x4, local copies, waits for them, and re-layouts, pick(): return chosen.reshape(heads_here, SEG_DEV, ANC * SEG, HD)  52.2 us
  transfers between devices with their start and end apart: 41, of which 17 were waited for; matrix products, arithmetic and copies ran while one was open for 20% of the time, Pallas kernels for 0%

commit v1 on v0

v1 whole, which is shorter than its diff:
```python
from functools import partial

import jax
import jax.numpy as jnp
from jax import lax
from jax.experimental import pallas as pl
from jax.experimental.pallas import tpu as pltpu
from jax.sharding import PartitionSpec as P

H = 16
HD = 64
SEG = 128
SEG_DEV = 5
ANC = 10
TREE = 20
INNER = 12
MEMBERS = 4
PAIR = 2 * HD
POOL = TREE + 2 * INNER
EMPTY = POOL

EPSILON = 1e-05
NEGATIVE = -1e30

F32 = jnp.float32
BF16 = jnp.bfloat16

DEPTH_AT = TREE * ANC
UP_AT = DEPTH_AT + TREE
DOWN_AT = UP_AT + INNER
TABLE = 256

VM = pl.BlockSpec(memory_space=pltpu.VMEM)
SM = pl.BlockSpec(memory_space=pltpu.SMEM)
ANY = pl.BlockSpec(memory_space=pl.ANY)


def shaped(shape, kind):
    return jax.ShapeDtypeStruct(shape, kind)


def params(mib=48):
    return pltpu.CompilerParams(vmem_limit_bytes=mib * 2**20)


def dot(a, b, dims=((1,), (0,))):
    return lax.dot_general(a, b, (dims, ((), ())), preferred_element_type=F32)


def lanes(shape):
    return lax.broadcasted_iota(jnp.int32, shape, len(shape) - 1)


def rows_of(shape):
    return lax.broadcasted_iota(jnp.int32, shape, len(shape) - 2)


def table_kernel(count, meta, parent, out, inner, place):
    member, group = meta[0], meta[1]
    groups = count // TREE
    below = lax.rem(group + groups - 1, groups)
    above = lax.rem(group + 1, groups)

    def clear(i, _):
        inner[i] = 0
        place[i] = EMPTY
        return _

    lax.fori_loop(0, count, clear, 0)

    def mark(i, _):
        up = parent[i]

        @pl.when(up >= 0)
        def _mark():
            inner[up] = 1

        return _

    lax.fori_loop(0, count, mark, 0)

    def cover(i, mask):
        up = parent[i]
        ahead = lax.rem(up - i + count, count)
        forward = ahead < TREE
        low = jnp.where(forward, i, up)
        length = jnp.where(forward, ahead, count - ahead)
        length = jnp.where(up >= 0, length, 0)
        start = lax.rem(low + 1 + TREE, TREE)
        bits = lax.shift_left(1, length) - 1
        room = TREE - start
        first = lax.shift_left(bits & (lax.shift_left(1, room) - 1), start)
        second = lax.shift_right_logical(bits, room)
        return mask | first | second

    mask = lax.fori_loop(0, 2 * TREE - 1, cover, 0)

    def find(c, found):
        free = (lax.shift_right_logical(mask, c) & 1) == 0
        return jnp.where(free, c, found)

    offset = lax.fori_loop(0, TREE, find, 0)

    for i in range(2 * INNER):
        out[UP_AT + i] = -1

    def own(p, ranks):
        up_rank, down_rank = ranks
        spot = ((p // SEG_DEV) ^ member) * SEG_DEV + lax.rem(p, SEG_DEV)
        slot = group * TREE + p
        place[slot] = spot
        has = inner[slot] == 1
        goes_up = has & (p >= offset) & (offset > 0) & (up_rank < INNER)
        goes_down = has & (p < offset) & (down_rank < INNER)

        @pl.when(goes_up)
        def _up():
            out[UP_AT + up_rank] = spot

        @pl.when(goes_down)
        def _down():
            out[DOWN_AT + down_rank] = spot

        return up_rank + goes_up.astype(jnp.int32), down_rank + goes_down.astype(jnp.int32)

    lax.fori_loop(0, TREE, own, (0, 0))

    def others(p, ranks):
        low_rank, high_rank = ranks
        low_slot = below * TREE + p
        high_slot = above * TREE + p
        low = (inner[low_slot] == 1) & (p >= offset) & (offset > 0) & (low_rank < INNER)
        high = (inner[high_slot] == 1) & (p < offset) & (high_rank < INNER)

        @pl.when(low)
        def _low():
            place[low_slot] = TREE + low_rank

        @pl.when(high)
        def _high():
            place[high_slot] = TREE + INNER + high_rank

        return low_rank + low.astype(jnp.int32), high_rank + high.astype(jnp.int32)

    lax.fori_loop(0, TREE, others, (0, 0))

    def chain(q, _):
        slot = group * TREE + ((q // SEG_DEV) ^ member) * SEG_DEV + lax.rem(q, SEG_DEV)

        def step(a, state):
            at, depth = state
            good = at >= 0
            safe = jnp.maximum(at, 0)
            out[q * ANC + a] = jnp.where(good, place[safe], EMPTY)
            return jnp.where(good, parent[safe], -1), depth + good.astype(jnp.int32)

        _end, depth = lax.fori_loop(0, ANC, step, (slot, 0))
        out[DEPTH_AT + q] = depth
        return _

    lax.fori_loop(0, TREE, chain, 0)


def make_tables(meta, parent):
    count = parent.shape[0]
    return pl.pallas_call(
        partial(table_kernel, count),
        out_shape=shaped((TABLE,), jnp.int32),
        in_specs=[SM, SM],
        out_specs=SM,
        scratch_shapes=[pltpu.SMEM((count,), jnp.int32), pltpu.SMEM((count,), jnp.int32)],
        name="tables",
    )(meta, parent)


def normal(block):
    centered = block - jnp.mean(block, axis=-1, keepdims=True)
    variance = jnp.mean(centered * centered, axis=-1, keepdims=True)
    scale = lax.rsqrt(variance + EPSILON)
    return centered * scale, scale


def project_kernel(meta, x, gain, shift, weight, bias, normed, *outs):
    member = meta[0]
    rows = x.shape[0]
    step = 64

    def norm_step(i, _):
        at = pl.ds(pl.multiple_of(i * step, step), step)
        hat, _scale = normal(x[at, :].astype(F32))
        normed[at, :] = (hat * gain[...].astype(F32) + shift[...].astype(F32)).astype(BF16)
        return _

    lax.fori_loop(0, rows // step, norm_step, 0)
    low = lanes((1, PAIR)) < HD

    def one(d, _):
        pair = member ^ d
        block = weight[:, pl.ds(pl.multiple_of(pair * 3 * PAIR, PAIR), 3 * PAIR)]
        both = bias[:, pl.ds(pl.multiple_of(pair * 2 * PAIR, PAIR), 2 * PAIR)].astype(F32)
        first, second = both[:, :PAIR], both[:, PAIR:]
        query_bias = jnp.where(low, first, pltpu.roll(second, HD, 1))
        value_bias = jnp.where(low, pltpu.roll(first, HD, 1), second)
        joined = dot(normed[...], block)
        t0, t1, t2 = joined[:, :PAIR], joined[:, PAIR : 2 * PAIR], joined[:, 2 * PAIR :]
        queries = (jnp.where(low, t0, t1) + query_bias) * (HD ** (-0.5))
        keys = pltpu.roll(jnp.where(low, t2, t0), HD, 1)
        values = jnp.where(low, t1, t2) + value_bias
        for j in range(MEMBERS):

            @pl.when(d == j)
            def _store():
                outs[j][...] = queries.astype(BF16)
                outs[MEMBERS + j][:, :PAIR] = keys.astype(BF16)
                outs[MEMBERS + j][:, PAIR:] = values.astype(BF16)

        return _

    lax.fori_loop(0, MEMBERS, one, 0)


def project(meta, x, gain, shift, weight, bias):
    rows, width = x.shape
    outs = pl.pallas_call(
        project_kernel,
        out_shape=[shaped((rows, width), BF16)]
        + [shaped((rows, PAIR), BF16)] * MEMBERS
        + [shaped((rows, 2 * PAIR), BF16)] * MEMBERS,
        in_specs=[SM] + [VM] * 5,
        out_specs=[VM] * (1 + 2 * MEMBERS),
        compiler_params=params(),
        name="project",
    )(meta, x, gain, shift, weight, bias)
    return outs[0], outs[1 : 1 + MEMBERS], outs[1 + MEMBERS :]


def pack_kernel(table, kv0, kv1, kv2, kv3, up, down, sem):
    sources = (kv0, kv1, kv2, kv3)
    for side, at, target in ((0, UP_AT, up), (1, DOWN_AT, down)):
        for i in range(INNER):
            spot = jnp.maximum(table[at + i], 0)
            d, s = spot // SEG_DEV, lax.rem(spot, SEG_DEV)
            for j in range(MEMBERS):

                @pl.when(d == j)
                def _start():
                    pltpu.make_async_copy(
                        sources[j].at[pl.ds(pl.multiple_of(s * SEG, SEG), SEG)],
                        target.at[pl.ds(i * SEG, SEG)],
                        sem.at[side * INNER + i],
                    ).start()

    for side, target in ((0, up), (1, down)):
        for i in range(INNER):
            piece = target.at[pl.ds(i * SEG, SEG)]
            pltpu.make_async_copy(piece, piece, sem.at[side * INNER + i]).wait()


def pack(table, pairs):
    out = shaped((INNER * SEG, 2 * PAIR), BF16)
    return pl.pallas_call(
        pack_kernel,
        out_shape=[out, out],
        in_specs=[SM] + [ANY] * MEMBERS,
        out_specs=[ANY] * 2,
        scratch_shapes=[pltpu.SemaphoreType.DMA((2 * INNER,))],
        compiler_params=params(8),
        name="pack",
    )(table, *pairs)


LEVELS = (2, 4, 6, 8, 10)


def split_heads(tile):
    low = lanes((SEG, PAIR)) < HD
    wide = tile.astype(F32)
    zero = jnp.zeros_like(wide)
    return jnp.concatenate(
        [jnp.where(low, wide, zero), jnp.where(low, zero, wide)], axis=0
    ).astype(BF16)


def join_heads(turned):
    top = rows_of((PAIR, SEG)) < HD
    return jnp.where(top, turned[:, :SEG], turned[:, SEG:]).T


def slope_row(slopes, meta):
    first = meta[2]
    return jnp.where(lanes((1, 2 * SEG)) < SEG, slopes[first], slopes[first + 1])


def fill_bias(bias, slope):
    shape = (SEG, 2 * SEG)
    offset = lax.rem(lanes(shape), SEG)
    key = rows_of(shape)
    gap = slope * (key - offset).astype(F32)
    bias[0] = jnp.where(key <= offset, gap, NEGATIVE)
    bias[1] = gap


def load_pool(sources, table_unused, pool, sem):
    kvs, from_below, from_above = sources
    rows = SEG_DEV * SEG
    copies = []
    for j in range(MEMBERS):
        copies.append(
            pltpu.make_async_copy(kvs[j], pool.at[pl.ds(j * rows, rows)], sem.at[j])
        )
    for k, source in enumerate((from_below, from_above)):
        copies.append(
            pltpu.make_async_copy(
                source,
                pool.at[pl.ds((TREE + k * INNER) * SEG, INNER * SEG)],
                sem.at[MEMBERS + k],
            )
        )
    return copies


def segment(ref, at):
    return ref.at[pl.ds(pl.multiple_of(at * SEG, SEG), SEG)]


def attend_kernel(
    table, meta, slopes, q0, q1, q2, q3, kv0, kv1, kv2, kv3, below, above,
    o0, o1, o2, o3, lse, pool, turned, queries, result, bias, sem,
):
    rows = SEG_DEV * SEG
    copies = load_pool(((kv0, kv1, kv2, kv3), below, above), table, pool, sem)
    for j, source in enumerate((q0, q1, q2, q3)):
        copies.append(
            pltpu.make_async_copy(
                source, queries.at[pl.ds(j * rows, rows)], sem.at[MEMBERS + 2 + j]
            )
        )
    for copy in copies:
        copy.start()
    slope = slope_row(slopes, meta)
    fill_bias(bias, slope)
    pool[POOL * SEG :, :] = jnp.zeros((SEG, 2 * PAIR), BF16)
    for copy in copies:
        copy.wait()

    def turn(i, _):
        turned[i] = segment(pool, i)[:, PAIR:].astype(F32).T.astype(BF16)
        return _

    lax.fori_loop(0, POOL + 1, turn, 0)

    def one(s, _):
        depth = table[DEPTH_AT + s]
        for span in LEVELS:

            @pl.when((depth > span - 2) & (depth <= span))
            def _run():
                stacked = split_heads(segment(queries, s)[...])
                spots = [table[s * ANC + a] for a in range(span)]
                scores = []
                for a in range(span):
                    raw = dot(segment(pool, spots[a])[:, :PAIR], stacked, ((1,), (1,)))
                    level = slope * (-float(a * SEG))
                    if a == span - 1:
                        level = level + jnp.where(depth < span, NEGATIVE, 0.0)
                    scores.append(raw + bias[0 if a == 0 else 1] + level)
                top = scores[0]
                for part in scores[1:]:
                    top = jnp.maximum(top, part)
                top = jnp.max(top, axis=0, keepdims=True)
                total = jnp.zeros((1, 2 * SEG), F32)
                out = jnp.zeros((PAIR, 2 * SEG), F32)
                for a in range(span):
                    weights = jnp.exp(scores[a] - top)
                    total = total + jnp.sum(weights, axis=0, keepdims=True)
                    out = out + dot(turned[spots[a]], weights.astype(BF16))
                out = out * (1.0 / total)
                segment(result, s)[...] = join_heads(out).astype(BF16)
                lse[s] = top + jnp.log(total)

        return _

    lax.fori_loop(0, TREE, one, 0)
    copies = [
        pltpu.make_async_copy(result.at[pl.ds(j * rows, rows)], target, sem.at[j])
        for j, target in enumerate((o0, o1, o2, o3))
    ]
    for copy in copies:
        copy.start()
    for copy in copies:
        copy.wait()


def attend(table, meta, slopes, queries, pairs, below, above):
    rows = queries[0].shape[0]
    outs = pl.pallas_call(
        attend_kernel,
        out_shape=[shaped((rows, PAIR), BF16)] * MEMBERS + [shaped((TREE, 1, 2 * SEG), F32)],
        in_specs=[SM] * 3 + [ANY] * (2 * MEMBERS + 2),
        out_specs=[ANY] * MEMBERS + [VM],
        scratch_shapes=[
            pltpu.VMEM(((POOL + 1) * SEG, 2 * PAIR), BF16),
            pltpu.VMEM((POOL + 1, PAIR, SEG), BF16),
            pltpu.VMEM((TREE * SEG, PAIR), BF16),
            pltpu.VMEM((TREE * SEG, PAIR), BF16),
            pltpu.VMEM((2, SEG, 2 * SEG), F32),
            pltpu.SemaphoreType.DMA((2 * MEMBERS + 2,)),
        ],
        compiler_params=params(),
        name="attend",
    )(table, meta, slopes, *queries, *pairs, below, above)
    return outs[:MEMBERS], outs[MEMBERS]


def attend_back_kernel(
    table, meta, slopes, q0, q1, q2, q3, kv0, kv1, kv2, kv3, below, above,
    o0, o1, o2, o3, g0, g1, g2, g3, lse,
    dq0, dq1, dq2, dq3, own, to_below, to_above,
    pool, turned, queries, outs, grads, result, total, small, bias, sem,
):
    rows = SEG_DEV * SEG
    copies = load_pool(((kv0, kv1, kv2, kv3), below, above), table, pool, sem)
    base = MEMBERS + 2
    for k, (sources, target) in enumerate(
        (((q0, q1, q2, q3), queries), ((o0, o1, o2, o3), outs), ((g0, g1, g2, g3), grads))
    ):
        for j, source in enumerate(sources):
            copies.append(
                pltpu.make_async_copy(
                    source, target.at[pl.ds(j * rows, rows)], sem.at[base + k * MEMBERS + j]
                )
            )
    for copy in copies:
        copy.start()
    slope = slope_row(slopes, meta)
    fill_bias(bias, slope)
    pool[POOL * SEG :, :] = jnp.zeros((SEG, 2 * PAIR), BF16)

    def clear(i, _):
        segment(total, i)[...] = jnp.zeros((SEG, 2 * PAIR), F32)
        return _

    lax.fori_loop(0, POOL + 1, clear, 0)
    for copy in copies:
        copy.wait()

    def turn(i, _):
        turned[i] = segment(pool, i)[:, :PAIR].astype(F32).T.astype(BF16)
        return _

    lax.fori_loop(0, POOL + 1, turn, 0)

    def one(s, _):
        depth = table[DEPTH_AT + s]
        for span in LEVELS:

            @pl.when((depth > span - 2) & (depth <= span))
            def _run():
                stacked = split_heads(segment(queries, s)[...])
                grad = segment(grads, s)[...]
                stacked_grad = split_heads(grad)
                product = (grad.astype(F32) * segment(outs, s)[...].astype(F32)).T
                delta = jnp.concatenate(
                    [
                        jnp.sum(product[:HD], axis=0, keepdims=True),
                        jnp.sum(product[HD:], axis=0, keepdims=True),
                    ],
                    axis=1,
                )
                log_total = lse[s]
                spots = [table[s * ANC + a] for a in range(span)]
                query_grad = jnp.zeros((PAIR, 2 * SEG), F32)
                for a in range(span):
                    block = segment(pool, spots[a])
                    raw = dot(block[:, :PAIR], stacked, ((1,), (1,)))
                    level = slope * (-float(a * SEG)) - log_total
                    if a == span - 1:
                        level = level + jnp.where(depth < span, NEGATIVE, 0.0)
                    probs = jnp.exp(raw + bias[0 if a == 0 else 1] + level)
                    prob_grad = dot(block[:, PAIR:], stacked_grad, ((1,), (1,)))
                    score_grad = (probs * (prob_grad - delta)).astype(BF16)
                    into = segment(total, spots[a])
                    into[:, :PAIR] += dot(score_grad, stacked)
                    into[:, PAIR:] += dot(probs.astype(BF16), stacked_grad)
                    query_grad = query_grad + dot(turned[spots[a]], score_grad)
                segment(result, s)[...] = join_heads(query_grad).astype(BF16)

        return _

    lax.fori_loop(0, TREE, one, 0)
    copies = [
        pltpu.make_async_copy(result.at[pl.ds(j * rows, rows)], target, sem.at[j])
        for j, target in enumerate((dq0, dq1, dq2, dq3))
    ]
    copies.append(
        pltpu.make_async_copy(total.at[pl.ds(0, TREE * SEG)], own, sem.at[MEMBERS])
    )
    for copy in copies:
        copy.start()

    def shorten(i, _):
        segment(small, i)[...] = segment(total, TREE + i)[...].astype(BF16)
        return _

    lax.fori_loop(0, 2 * INNER, shorten, 0)
    for k, target in enumerate((to_below, to_above)):
        copy = pltpu.make_async_copy(
            small.at[pl.ds(k * INNER * SEG, INNER * SEG)], target, sem.at[MEMBERS + 1 + k]
        )
        copy.start()
        copies.append(copy)
    for copy in copies:
        copy.wait()


def attend_back(table, meta, slopes, queries, pairs, below, above, outs, grads, lse):
    rows = queries[0].shape[0]
    side = shaped((INNER * SEG, 2 * PAIR), BF16)
    result = pl.pallas_call(
        attend_back_kernel,
        out_shape=[shaped((rows, PAIR), BF16)] * MEMBERS
        + [shaped((TREE * SEG, 2 * PAIR), F32), side, side],
        in_specs=[SM] * 3 + [ANY] * (4 * MEMBERS + 2) + [VM],
        out_specs=[ANY] * (MEMBERS + 3),
        scratch_shapes=[
            pltpu.VMEM(((POOL + 1) * SEG, 2 * PAIR), BF16),
            pltpu.VMEM((POOL + 1, PAIR, SEG), BF16),
            pltpu.VMEM((TREE * SEG, PAIR), BF16),
            pltpu.VMEM((TREE * SEG, PAIR), BF16),
            pltpu.VMEM((TREE * SEG, PAIR), BF16),
            pltpu.VMEM((TREE * SEG, PAIR), BF16),
            pltpu.VMEM(((POOL + 1) * SEG, 2 * PAIR), F32),
            pltpu.VMEM((2 * INNER * SEG, 2 * PAIR), BF16),
            pltpu.VMEM((2, SEG, 2 * SEG), F32),
            pltpu.SemaphoreType.DMA((4 * MEMBERS + 2,)),
        ],
        compiler_params=params(),
        name="attend_back",
    )(table, meta, slopes, *queries, *pairs, below, above, *outs, *grads, lse)
    return result[:MEMBERS], result[MEMBERS], result[MEMBERS + 1], result[MEMBERS + 2]


def gather_back_kernel(table, own, from_above, from_below, k0, k1, k2, k3, total, sem):
    rows = SEG_DEV * SEG
    copy = pltpu.make_async_copy(own, total, sem)
    copy.start()
    copy.wait()
    for at, source in ((UP_AT, from_above), (DOWN_AT, from_below)):

        def add(i, _):
            spot = table[at + i]

            @pl.when(spot >= 0)
            def _add():
                segment(total, spot)[...] += segment(source, i)[...].astype(F32)

            return _

        lax.fori_loop(0, INNER, add, 0)
    for j, target in enumerate((k0, k1, k2, k3)):

        def short(i, _):
            segment(target, i)[...] = segment(total, j * SEG_DEV + i)[...].astype(BF16)
            return _

        lax.fori_loop(0, SEG_DEV, short, 0)


def gather_back(table, own, from_above, from_below):
    rows = SEG_DEV * SEG
    return pl.pallas_call(
        gather_back_kernel,
        out_shape=[shaped((rows, 2 * PAIR), BF16)] * MEMBERS,
        in_specs=[SM, ANY, VM, VM],
        out_specs=[VM] * MEMBERS,
        scratch_shapes=[
            pltpu.VMEM((TREE * SEG, 2 * PAIR), F32),
            pltpu.SemaphoreType.DMA(()),
        ],
        compiler_params=params(),
        name="gather_back",
    )(table, own, from_above, from_below)


def output_kernel(
    meta, x, bias, gain, shift, w_own, w_other, a0, a1, a2, a3, b0, b1, b2, b3,
    mixed_own, middle, normed, mixed, weight, sem,
):
    member, rank = meta[0], meta[3]
    rows, width = x.shape
    half = width // 2
    copies = []
    for k, source in enumerate((w_own, w_other)):
        at = pl.multiple_of((rank ^ k) * half, half)
        copies.append(pltpu.make_async_copy(source, weight.at[pl.ds(at, half)], sem.at[k]))
    for copy in copies:
        copy.start()
    for k, parts in enumerate(((a0, a1, a2, a3), (b0, b1, b2, b3))):
        for d in range(MEMBERS):
            inside = (member ^ d) * PAIR
            at = pl.multiple_of((rank ^ k) * half + inside, PAIR)
            mixed[:, pl.ds(at, PAIR)] = parts[d][...]
            if k == 0:
                mixed_own[:, pl.ds(pl.multiple_of(inside, PAIR), PAIR)] = parts[d][...]
    for copy in copies:
        copy.wait()
    tile = 256

    def column(t, _):
        at = pl.ds(pl.multiple_of(t * tile, tile), tile)
        middle[:, at] = (
            x[:, at].astype(F32) + (dot(mixed[...], weight[:, at]) + bias[:, at].astype(F32))
        )
        return _

    lax.fori_loop(0, width // tile, column, 0)
    step = 64

    def norm_step(i, _):
        at = pl.ds(pl.multiple_of(i * step, step), step)
        hat, _scale = normal(middle[at, :])
        normed[at, :] = (hat * gain[...].astype(F32) + shift[...].astype(F32)).astype(BF16)
        return _

    lax.fori_loop(0, rows // step, norm_step, 0)


def output_stage(meta, x, bias, gain, shift, w_own, w_other, parts_own, parts_other):
    rows, width = x.shape
    return pl.pallas_call(
        output_kernel,
        out_shape=[
            shaped((rows, width // 2), BF16),
            shaped((rows, width), F32),
            shaped((rows, width), BF16),
        ],
        in_specs=[SM] + [VM] * 4 + [ANY] * 2 + [VM] * (2 * MEMBERS),
        out_specs=[VM] * 3,
        scratch_shapes=[
            pltpu.VMEM((rows, width), BF16),
            pltpu.VMEM((width, width), BF16),
            pltpu.SemaphoreType.DMA((2,)),
        ],
        compiler_params=params(),
        name="output_stage",
    )(meta, x, bias, gain, shift, w_own, w_other, *parts_own, *parts_other)


def norm_back(hat, scale, up):
    mean_up = jnp.mean(up, axis=-1, keepdims=True)
    mean_both = jnp.mean(up * hat, axis=-1, keepdims=True)
    return scale * (up - mean_up - hat * mean_both)


def middle_back_kernel(
    meta, middle, part, other, grad, gain, weight,
    middle_grad, branch, vectors, g0, g1, g2, g3,
):
    member = meta[0]
    rows, width = middle.shape
    step = 64
    vectors[...] = jnp.zeros_like(vectors)

    def norm_step(i, _):
        at = pl.ds(pl.multiple_of(i * step, step), step)
        hat, scale = normal(middle[at, :])
        second = part[at, :].astype(F32) + other[at, :].astype(F32)
        back = grad[at, :].astype(F32) + norm_back(hat, scale, second * gain[...].astype(F32))
        middle_grad[at, :] = back
        branch[at, :] = back.astype(BF16)
        vectors[0:1, :] += jnp.sum(second * hat, axis=0, keepdims=True)
        vectors[1:2, :] += jnp.sum(second, axis=0, keepdims=True)
        vectors[2:3, :] += jnp.sum(back, axis=0, keepdims=True)
        vectors[3:4, :] += jnp.sum(grad[at, :].astype(F32), axis=0, keepdims=True)
        return _

    lax.fori_loop(0, rows // step, norm_step, 0)
    for d, target in enumerate((g0, g1, g2, g3)):
        at = pl.multiple_of((member ^ d) * PAIR, PAIR)
        target[...] = dot(branch[...], weight[pl.ds(at, PAIR), :], ((1,), (1,))).astype(BF16)


def middle_back(meta, middle, part, other, grad, gain, weight):
    rows, width = middle.shape
    outs = pl.pallas_call(
        middle_back_kernel,
        out_shape=[shaped((rows, width), F32), shaped((rows, width), BF16), shaped((8, width), F32)]
        + [shaped((rows, PAIR), BF16)] * MEMBERS,
        in_specs=[SM] + [VM] * 6,
        out_specs=[VM] * (3 + MEMBERS),
        compiler_params=params(),
        name="middle_back",
    )(meta, middle, part, other, grad, gain, weight)
    return outs[0], outs[1], outs[2], outs[3:]


def join_kernel(
    meta, x, gain_unused, weight, q0, q1, q2, q3, k0, k1, k2, k3, joined, part, vectors, sums
):
    member = meta[0]
    low = lanes((1, PAIR)) < HD
    for d, (query, both) in enumerate(((q0, k0), (q1, k1), (q2, k2), (q3, k3))):
        wide_q = query[...].astype(F32) * (HD ** (-0.5))
        wide_k = pltpu.roll(both[:, :PAIR].astype(F32), HD, 1)
        wide_v = both[:, PAIR:].astype(F32)
        at = (member ^ d) * 3 * PAIR
        for k, tile in enumerate(
            (
                jnp.where(low, wide_q, wide_k),
                jnp.where(low, wide_v, wide_q),
                jnp.where(low, wide_k, wide_v),
            )
        ):
            spot = pl.ds(pl.multiple_of(at + k * PAIR, PAIR), PAIR)
            joined[:, spot] = tile.astype(BF16)
            sums[0:1, spot] = jnp.sum(tile, axis=0, keepdims=True)
    rows, width = x.shape
    tile = 256

    def column(t, _):
        at = pl.ds(pl.multiple_of(t * tile, tile), tile)
        part[:, at] = dot(joined[...], weight[at, :], ((1,), (1,))).astype(BF16)
        return _

    lax.fori_loop(0, width // tile, column, 0)
    step = 64
    vectors[...] = jnp.zeros_like(vectors)

    def norm_step(i, _):
        at = pl.ds(pl.multiple_of(i * step, step), step)
        hat, _scale = normal(x[at, :].astype(F32))
        first = part[at, :].astype(F32)
        vectors[0:1, :] += jnp.sum(first * hat, axis=0, keepdims=True)
        vectors[1:2, :] += jnp.sum(first, axis=0, keepdims=True)
        return _

    lax.fori_loop(0, rows // step, norm_step, 0)


def join_stage(meta, x, gain, weight, query_grads, pair_grads):
    rows, width = x.shape
    across = weight.shape[1]
    return pl.pallas_call(
        join_kernel,
        out_shape=[
            shaped((rows, across), BF16),
            shaped((rows, width), BF16),
            shaped((8, width), F32),
            shaped((8, across), F32),
        ],
        in_specs=[SM] + [VM] * (3 + 2 * MEMBERS),
        out_specs=[VM] * 4,
        compiler_params=params(),
        name="join_stage",
    )(meta, x, gain, weight, *query_grads, *pair_grads)


def input_back_kernel(x, part, other, gain, middle_grad, out):
    rows = x.shape[0]
    step = 64

    def norm_step(i, _):
        at = pl.ds(pl.multiple_of(i * step, step), step)
        hat, scale = normal(x[at, :].astype(F32))
        first = part[at, :].astype(F32) + other[at, :].astype(F32)
        back = norm_back(hat, scale, first * gain[...].astype(F32))
        out[at, :] = (back + middle_grad[at, :]).astype(BF16)
        return _

    lax.fori_loop(0, rows // step, norm_step, 0)


def input_back(x, part, other, gain, middle_grad):
    return pl.pallas_call(
        input_back_kernel,
        out_shape=shaped(x.shape, BF16),
        in_specs=[VM] * 5,
        out_specs=VM,
        compiler_params=params(),
        name="input_back",
    )(x, part, other, gain, middle_grad)


def swap(value):
    return lax.ppermute(value, "tensor", [(0, 1), (1, 0)])


def to_member(value, d):
    count = lax.axis_size("dp")
    return lax.ppermute(value, "dp", [(i, i ^ d) for i in range(count)])


def to_member_across(value, d):
    count = lax.axis_size("dp")
    pairs = [(i * 2 + t, (i ^ d) * 2 + (1 - t)) for i in range(count) for t in range(2)]
    return lax.ppermute(value, ("dp", "tensor"), pairs)


def to_group(value, by):
    count = lax.axis_size("dp")
    step = by * MEMBERS
    return lax.ppermute(value, "dp", [(i, (i + step) % count) for i in range(count)])


def within(parts):
    return [parts[0]] + [to_member(parts[d], d) for d in range(1, MEMBERS)]


def reduce_rows(value):
    return lax.psum_scatter(value, "dp", scatter_dimension=0, tiled=True)


def reduce_low(value):
    return reduce_rows(value.astype(BF16)).astype(F32)


def shards(
    activations,
    cotangent,
    parent_slot,
    attention_gain,
    attention_shift,
    joined_weight,
    joined_bias,
    output_weight,
    output_bias,
    feed_gain,
    feed_shift,
    expand_weight,
    expand_bias,
    contract_weight,
    contract_bias,
):
    device = lax.axis_index("dp")
    rank = lax.axis_index("tensor")
    member = lax.rem(device, MEMBERS)
    heads_here = joined_weight.shape[1] // (3 * HD)
    meta = jnp.stack(
        [member, device // MEMBERS, rank * heads_here + 2 * member, rank]
    ).astype(jnp.int32)
    slopes = jnp.exp2(-8.0 * jnp.arange(1, H + 1, dtype=F32) / H)

    def row(v):
        return v.reshape(1, -1)

    gain_a, shift_a = row(attention_gain), row(attention_shift)
    gain_f, shift_f = row(feed_gain), row(feed_shift)

    table = make_tables(meta, parent_slot)
    first_low, queries, pairs = project(
        meta, activations, gain_a, shift_a, joined_weight, row(joined_bias)
    )
    other_output_weight = swap(output_weight)
    pairs = within(pairs)
    up, down = pack(table, pairs)
    below = to_group(up, 1)
    above = to_group(down, -1)
    queries = within(queries)
    outs, lse = attend(table, meta, slopes, queries, pairs, below, above)
    parts_own = within(outs)
    parts_other = [to_member_across(outs[d], d) for d in range(MEMBERS)]
    mixed, middle, second_low = output_stage(
        meta, activations, row(output_bias), gain_f, shift_f,
        output_weight, other_output_weight, parts_own, parts_other,
    )

    hidden_grad = jnp.einsum("td,fd->tf", cotangent, contract_weight, preferred_element_type=F32)
    hidden_pre = jnp.dot(second_low, expand_weight, preferred_element_type=F32) + expand_bias.astype(F32)
    hidden_act, gelu_back = jax.vjp(partial(jax.nn.gelu, approximate=True), hidden_pre)
    hidden_low = hidden_act.astype(BF16)
    pre_grad = gelu_back(hidden_grad)[0].astype(BF16)
    second_part = jnp.einsum("tf,df->td", pre_grad, expand_weight, preferred_element_type=F32).astype(BF16)
    second_other = swap(second_part)
    middle_grad, branch_low, feed_vectors, grad_parts = middle_back(
        meta, middle, second_part, second_other, cotangent, gain_f, output_weight
    )
    grad_parts = within(grad_parts)

    feed_part = jnp.dot(hidden_low, contract_weight, preferred_element_type=F32).astype(BF16)
    feed_other = swap(feed_part)
    layer_output = (
        middle + (feed_part.astype(F32) + feed_other.astype(F32)) + contract_bias.astype(F32)
    ).astype(BF16)
    contract_grad = jnp.einsum("td,tf->df", cotangent, hidden_low, preferred_element_type=F32)
    expand_grad = jnp.einsum("td,tf->df", second_low, pre_grad, preferred_element_type=F32)
    expand_bias_grad = jnp.sum(pre_grad.astype(F32), axis=0)
    output_grad = jnp.einsum("td,tf->df", branch_low, mixed, preferred_element_type=F32)

    query_grads, own, to_below, to_above = attend_back(
        table, meta, slopes, queries, pairs, below, above, outs, grad_parts, lse
    )
    from_above = to_group(to_below, -1)
    from_below = to_group(to_above, 1)
    query_grads = within(query_grads)
    pair_grads = within(gather_back(table, own, from_above, from_below))
    joined_grad, first_part, norm_vectors, joined_sums = join_stage(
        meta, activations, gain_a, joined_weight, query_grads, pair_grads
    )
    first_other = swap(first_part)
    input_gradient = input_back(activations, first_part, first_other, gain_a, middle_grad)
    joined_weight_grad = jnp.einsum("td,tf->df", first_low, joined_grad, preferred_element_type=F32)

    width = activations.shape[1]
    chosen = joined_sums[0].reshape(heads_here, 3, HD)
    joined_bias_grad = jnp.stack([chosen[:, 0], chosen[:, 2]], axis=1).reshape(width)
    small = jnp.concatenate(
        [
            feed_vectors[:4].T,
            norm_vectors[:2].T,
            joined_bias_grad.reshape(width, 1),
            expand_bias_grad.reshape(width, 2),
        ],
        axis=1,
    )
    high = small.astype(BF16)
    rest = (small - high.astype(F32)).astype(BF16)
    room = jnp.zeros((width, PAIR - 18), BF16)
    last = reduce_rows(
        jnp.concatenate([joined_weight_grad.astype(BF16), high, rest, room], axis=1)
    ).astype(F32)
    across = joined_weight.shape[1]
    smalls = last[:, across : across + 9] + last[:, across + 9 : across + 18]
    norms = smalls[:, 4:6].T
    norms = norms + swap(norms)

    return (
        layer_output,
        input_gradient,
        norms[0],
        norms[1],
        last[:, :across],
        smalls[:, 6:7],
        reduce_low(output_grad),
        smalls[:, 2],
        smalls[:, 0],
        smalls[:, 1],
        reduce_low(expand_grad),
        smalls[:, 7:9].reshape(-1, 1),
        reduce_low(contract_grad),
        smalls[:, 3],
    )


def solution(mesh):
    in_specs = (
        P("dp", None),
        P("dp", None),
        P(),
        P(),
        P(),
        P(None, "tensor"),
        P("tensor"),
        P("tensor", None),
        P(),
        P(),
        P(),
        P(None, "tensor"),
        P("tensor"),
        P("tensor", None),
        P(),
    )
    out_specs = (
        P("dp", None),
        P("dp", None),
        P("dp"),
        P("dp"),
        P("dp", "tensor"),
        P("dp", "tensor"),
        P("dp", "tensor"),
        P("dp"),
        P("dp"),
        P("dp"),
        P("dp", "tensor"),
        P("dp", "tensor"),
        P("dp", "tensor"),
        P("dp"),
    )
    return jax.shard_map(shards, mesh=mesh, in_specs=in_specs, out_specs=out_specs, check_vma=False)
```

time: 1340 us -> 529 us (0.39)
  waiting for transfers between devices: 587 us -> 237 us
  local copies, waits for them, and re-layouts: 257 us -> 55.3 us
  matrix products: 243 us -> 44.6 us
  Pallas kernels: 0 us -> 127 us
  blocking collectives: 61.5 us -> 0 us
  other arithmetic: 67.1 us -> 7.04 us
  starting transfers between devices: 92.1 us -> 34.6 us
    dot_general x71 -> x7, matrix products: 237 us -> 37.8 us  [the longest x1 9.51 us: shards(): jnp.einsum('td,tf->df', cotangent, hidden_low, preferred_element_type=F32)]
    psum x3 -> x0, waiting for transfers between devices: 170 us -> none  [the longest x1 75 us: shards(): lax.psum(feed_part.astype(jnp.bfloat16), 'tensor').astype(jnp.float32)]
    reduce_scatter x3, waiting for transfers between devices: 190 us -> 27.7 us  [reduce_rows(): return lax.psum_scatter(value, 'dp', scatter_dimension=0, tiled=True)]
    unnamed x12 -> x5, waiting for transfers between devices: 136 us -> 0.07 us
    pallas_call x0 -> x10, Pallas kernels: none -> 127 us  [the longest x1 46.7 us: attend_back(): pl.pallas_call(attend_back_kernel, out_shape=[shaped((rows, PAIR), BF16)]...]
    ppermute x32 -> x31, waiting for transfers between devices: 89.4 us -> 209 us  [the longest x5 82.9 us: swap(): return lax.ppermute(value, 'tensor', [(0, 1), (1, 0)])]
    reshape x11 -> x9, local copies, waits for them, and re-layouts: 103 us -> 7.27 us  [the longest x6 3.43 us: row(): return v.reshape(1, -1)]
    unnamed x1 -> x0, blocking collectives: 61.5 us -> none
  transfers between devices with their start and end apart: 41 -> 35, of which waited for: 17 -> 20; matrix products, arithmetic and copies ran while one was open for 20% -> 12% of each run, Pallas kernels for 0% -> 20%
where the time goes in v1:
time: 529 us; the launch traced here: 520 us
  waiting for transfers between devices  237 us (45%)
  Pallas kernels  127 us (24%)
  local copies, waits for them, and re-layouts  55.3 us (10%)
  matrix products  44.6 us (8%)
  starting transfers between devices  34.6 us (7%)
  between operations  14.8 us (3%)
  other arithmetic  7.04 us (1%)
    ppermute x5, waiting for transfers between devices, swap(): return lax.ppermute(value, 'tensor', [(0, 1), (1, 0)])  82.9 us
    ppermute x4, waiting for transfers between devices, to_group(): lax.ppermute(value, 'dp', [(i, (i + step) % count) for i in range(count)])  76.6 us
    pallas_call x1, Pallas kernels, attend_back(): pl.pallas_call(attend_back_kernel, out_shape=[shaped((rows, PAIR), BF16)]...  46.7 us
    ppermute x18, waiting for transfers between devices, to_member(): return lax.ppermute(value, 'dp', [(i, i ^ d) for i in range(count)])  42.8 us
    unnamed x152, local copies, waits for them, and re-layouts  37 us
    pallas_call x1, Pallas kernels, attend(): pl.pallas_call(attend_kernel, out_shape=[shaped((rows, PAIR), BF16)] * ME...  28.3 us
    reduce_scatter x3, waiting for transfers between devices, reduce_rows(): return lax.psum_scatter(value, 'dp', scatter_dimension=0, tiled=True)  27.7 us
    ppermute x18, starting transfers between devices, to_member(): return lax.ppermute(value, 'dp', [(i, i ^ d) for i in range(count)])  15.5 us
  transfers between devices with their start and end apart: 35, of which 20 were waited for; matrix products, arithmetic and copies ran while one was open for 12% of the time, Pallas kernels for 20%

profile of v1, /device:TPU:0, one launch (start us, length us, event | category | flops | bytes accessed | tf_op | source)
XLA Modules:
  0.0 520.0 jit_solution(15797684427835932441)
XLA Ops:
  10.7 8.1 %project.1 = (bf16[640,1024]{1,0:T(8,128)(2,1)S(1)}, bf16[640,128]{1,0:T(8,128)(2,1)S(1)}, bf16[640,128]{1,0:T(8,128)(2,1)S(1)}, bf16[640,128]{1,0:T(8,128)(2,1)...) custom-call(s32[4]{0:T(128)S(1)} %pad_add_fusion.meta, ...), custom_call_target="tpu_custom_call" | custom-call | tf_op jit(solution)/shard_map/project/pallas_call | solution.py:224
  32.3 6.7 %collective-permute-done.6.kv3 = bf16[640,256]{1,0:T(8,128)(2,1)S(1)} collective-permute-done((bf16[640,256]{1,0:T(8,128)(2,1)S(1)}, bf16[640,256]{1,0:T(8,128)(2,1)S(1)}, u32[]{:S(2)}, u32[]{:S(2)}) %collective-permute-start.6) | collective-permute-done | bytes 327712 | tf_op jit(solution)/shard_map/ppermute | solution.py:790
  57.0 8.6 %collective-permute-done.7.below = bf16[1536,256]{1,0:T(8,128)(2,1)S(1)} collective-permute-done((bf16[1536,256]{1,0:T(8,128)(2,1)S(1)}, bf16[1536,256]{1,0:T(8,128)(2,1)S(1)}, u32[]{:S(2)}, u32[]{:S(2)}) %collective-permute-start.7) | collective-permute-done | bytes 786464 | tf_op jit(solution)/shard_map/ppermute | solution.py:802
  65.6 16.2 %collective-permute-done.8.above = bf16[1536,256]{1,0:T(8,128)(2,1)S(1)} collective-permute-done((bf16[1536,256]{1,0:T(8,128)(2,1)S(1)}, bf16[1536,256]{1,0:T(8,128)(2,1)S(1)}, u32[]{:S(2)}, u32[]{:S(2)}) %collective-permute-start.8) | collective-permute-done | bytes 786464 | tf_op jit(solution)/shard_map/ppermute | solution.py:802
  86.1 28.3 %attend.1 = (bf16[640,128]{1,0:T(8,128)(2,1)S(1)}, bf16[640,128]{1,0:T(8,128)(2,1)S(1)}, bf16[640,128]{1,0:T(8,128)(2,1)S(1)}, bf16[640,128]{1,0:T(8,128)(2,1)S(1)}, f32[20,1,256]{2,1,0:T(1,128)S(1)}) custom-call(s32[256]{0:T(256)S(1)} %copy-done.43, s32[4]{0:T(128)S(1)} %copy-done.40, f32[16]{0:T(128)S(1)} %multiply_exponential_fusion.slopes, ...), custom_call_target="tpu_custom_call" | custom-call | tf_op jit(solution)/shard_map/attend/pallas_call | solution.py:396
  135.6 8.6 %output_stage.1 = (bf16[640,512]{1,0:T(8,128)(2,1)S(1)}, f32[640,1024]{1,0:T(8,128)}, bf16[640,1024]{1,0:T(8,128)(2,1)S(1)}) custom-call(s32[4]{0:T(128)S(1)} %copy-done.40, bf16[640,1024]{1,0:T(8,128)(2,1)} %x.7, bf16[1,1024]{1,0:T(2,128)(2,1)S(1)} %reshape.54.bias, bf16[1,1024]{1,0:T(2,128)(2,1)S(1)} %reshape.55.gain, bf16[1,1024]{1,0:T(2,128)(2,1)S(1)} %reshape.56.shift, ...), custom_call_target="tpu_custom_call" | custom-call | tf_op jit(solution)/shard_map/output_stage/pallas_call | solution.py:630
  147.3 6.8 %convert_reduce_fusion = (f32[2048]{0:T(1024)}, bf16[640,2048]{1,0:T(8,128)(2,1)S(1)}) fusion(f32[640,2048]{1,0:T(8,128)S(1)} %fusion.12, f32[2048]{0:T(1024)S(1)} %convert_element_type.66, bf16[640,1024]{1,0:T(8,128)(2,1)S(1)} %copy-done.64, bf16[2048,1024]{1,0:T(8,128)(2,1)S(1)} %copy-done.71), kind=kOutput, calls=%fused_computation.9 | convolution fusion | flops 2714499072 | bytes 13385728 | tf_op jit(solution)/shard_map/td,fd->tf/dot_general | solution.py:867
  158.6 29.1 %collective-permute-done.17.other = bf16[640,1024]{1,0:T(8,128)(2,1)S(1)} collective-permute-done((bf16[640,1024]{1,0:T(8,128)(2,1)S(1)}, bf16[640,1024]{1,0:T(8,128)(2,1)S(1)}, u32[]{:S(2)}, u32[]{:S(2)}) %collective-permute-start.17) | collective-permute-done | bytes 1310752 | tf_op jit(solution)/shard_map/ppermute | solution.py:785
  187.6 7.2 %middle_back.1 = (f32[640,1024]{1,0:T(8,128)}, bf16[640,1024]{1,0:T(8,128)(2,1)S(1)}, f32[8,1024]{1,0:T(8,128)S(1)}, bf16[640,128]{1,0:T(8,128)(2,1)S(1)}, bf16[...) custom-call(s32[4]{0:T(128)S(1)} %copy-done.40, ...), custom_call_target="tpu_custom_call" | custom-call | tf_op jit(solution)/shard_map/middle_back/pallas_call | solution.py:685
  200.2 9.5 %convert_bitcast_fusion = bf16[1024,2048]{0,1:T(8,128)(2,1)} fusion(bf16[640,1024]{1,0:T(8,128)(2,1)S(1)} %copy-done.65, f32[640,2048]{1,0:T(8,128)} %copy-done.72, f32[2048]{0:T(1024)S(1)} %convert_element_type.66), kind=kOutput, calls=%fused_computation.11 | convolution fusion | flops 2699558912 | bytes 10756096 | tf_op jit(solution)/shard_map/td,tf->df/dot_general | solution.py:884
  209.7 6.6 %copy.43 = bf16[1024,2048]{1,0:T(8,128)(2,1)} copy(bf16[1024,2048]{0,1:T(8,128)(2,1)} %convert_bitcast_fusion) | data formatting | bytes 8388608
  217.6 6.8 %convolution_convert_fusion.1 = bf16[1024,2048]{1,0:T(8,128)(2,1)} fusion(bf16[640,1024]{1,0:T(8,128)(2,1)S(1)} %copy-done.50, bf16[640,2048]{1,0:T(8,128)(2,1)} %copy-done.73), kind=kOutput, calls=%fused_computation.13 | convolution fusion | flops 2686451712 | bytes 8126464 | tf_op jit(solution)/shard_map/td,tf->df/dot_general | solution.py:885
  227.1 8.0 %collective-permute-done.19.g2 = bf16[640,128]{1,0:T(8,128)(2,1)S(1)} collective-permute-done((bf16[640,128]{1,0:T(8,128)(2,1)S(1)}, bf16[640,128]{1,0:T(8,128)(2,1)S(1)}, u32[]{:S(2)}, u32[]{:S(2)}) %collective-permute-start.19) | collective-permute-done | bytes 163872 | tf_op jit(solution)/shard_map/ppermute | solution.py:790
  241.5 46.7 %attend_back.1 = (bf16[640,128]{1,0:T(8,128)(2,1)S(1)}, bf16[640,128]{1,0:T(8,128)(2,1)}, bf16[640,128]{1,0:T(8,128)(2,1)S(1)}, bf16[640,128]{1,0:T(8,128)(2,1)S...) custom-call(s32[256]{0:T(256)S(1)} %copy-done.44, s32[4]{0:T(128)S(1)} %copy-done.41, ...), custom_call_target="tpu_custom_call" | custom-call | tf_op jit(solution)/shard_map/attend_back/pallas_call | solution.py:519
  294.3 42.0 %collective-permute-done.24.from_above = bf16[1536,256]{1,0:T(8,128)(2,1)S(1)} collective-permute-done((bf16[1536,256]{1,0:T(8,128)(2,1)S(1)}, bf16[1536,256]{1,0:T(8,128)(2,1)S(1)}, u32[]{:S(2)}, u32[]{:S(2)}) %collective-permute-start.24) | collective-permute-done | bytes 786464 | tf_op jit(solution)/shard_map/ppermute | solution.py:802
  336.4 9.8 %collective-permute-done.25.from_below = bf16[1536,256]{1,0:T(8,128)(2,1)S(1)} collective-permute-done((bf16[1536,256]{1,0:T(8,128)(2,1)S(1)}, bf16[1536,256]{1,0:T(8,128)(2,1)S(1)}, u32[]{:S(2)}, u32[]{:S(2)}) %collective-permute-start.25) | collective-permute-done | bytes 786464 | tf_op jit(solution)/shard_map/ppermute | solution.py:802
  358.7 13.1 %collective-permute-done.22.q2 = bf16[640,128]{1,0:T(8,128)(2,1)S(1)} collective-permute-done((bf16[640,128]{1,0:T(8,128)(2,1)}, bf16[640,128]{1,0:T(8,128)(2,1)S(1)}, u32[]{:S(2)}, u32[]{:S(2)}) %collective-permute-start.22) | collective-permute-done | bytes 163872 | tf_op jit(solution)/shard_map/ppermute | solution.py:790
  378.8 9.0 %join_stage.1 = (bf16[640,1536]{1,0:T(8,128)(2,1)}, bf16[640,1024]{1,0:T(8,128)(2,1)S(1)}, f32[8,1024]{1,0:T(8,128)S(1)}, f32[8,1536]{1,0:T(8,128)S(1)}) custom-call(s32[4]{0:T(128)S(1)} %copy-done.41, bf16[640,1024]{1,0:T(8,128)(2,1)S(1)} %copy-done.1, bf16[1,1024]{1,0:T(2,128)(2,1)S(1)} %reshape.57.gain.gain_unused, bf16[1024,1536]{1,0:T(8,128)(2,1)} %weight.5, ...), custom_call_target="tpu_custom_call" | custom-call | tf_op jit(solution)/shard_map/join_stage/pallas_call | solution.py:743
  394.7 6.5 %concatenate.7 = bf16[1024,1664]{1,0:T(8,128)(2,1)} concatenate(bf16[1024,1536]{1,0:T(8,128)(2,1)} %convolution_convert_fusion, bf16[1024,9]{1,0:T(8,128)(2,1)S(1)} %copy.39, bf16[1024,9]{1,0:T(8,128)(2,1)S(1)} %copy.40, bf16[1024,110]{1,0:T(8,128)(2,1)S(1)} %broadcast_in_dim.2), dimensions={1} | concatenate | bytes 6815744 | tf_op jit(solution)/shard_map/concatenate | solution.py:919
  401.2 7.4 %convolution_convert_fusion.3 = bf16[640,1024]{1,0:T(8,128)(2,1)S(1)} fusion(bf16[2048,1024]{1,0:T(8,128)(2,1)} %param.28, f32[640,2048]{1,0:T(8,128)} %copy-done.72, f32[2048]{0:T(1024)S(1)} %copy-done.67), kind=kOutput, calls=%fused_computation.16 | convolution fusion | flops 2698117120 | bytes 10756096 | tf_op jit(solution)/shard_map/dot_general | solution.py:879
  410.7 29.6 %collective-permute-done.16 = bf16[640,1024]{1,0:T(8,128)(2,1)S(1)} collective-permute-done((bf16[640,1024]{1,0:T(8,128)(2,1)S(1)}, bf16[640,1024]{1,0:T(8,128)(2,1)S(1)}, u32[]{:S(2)}, u32[]{:S(2)}) %collective-permute-start.16) | collective-permute-done | bytes 1310752 | tf_op jit(solution)/shard_map/ppermute | solution.py:785
  443.6 24.3 %collective-permute-done.29.other = bf16[640,1024]{1,0:T(8,128)(2,1)} collective-permute-done((bf16[640,1024]{1,0:T(8,128)(2,1)S(1)}, bf16[640,1024]{1,0:T(8,128)(2,1)}, u32[]{:S(2)}, u32[]{:S(2)}) %collective-permute-start.29) | collective-permute-done | bytes 1310752 | tf_op jit(solution)/shard_map/ppermute | solution.py:785
  467.9 6.3 %input_back.1 = bf16[640,1024]{1,0:T(8,128)(2,1)} custom-call(bf16[640,1024]{1,0:T(8,128)(2,1)S(1)} %copy-done.1, bf16[640,1024]{1,0:T(8,128)(2,1)S(1)} %get-tuple-element.87.part, bf16[640,1024]{1,0:T(8,128)(2,1)} %collective-permute-done.29.other, bf16[1,1024]{1,0:T(2,128)(2,1)S(1)} %reshape.57.gain.gain_unused, f32[640,1024]{1,0:T(8,128)} %get-tuple-element.88.middle_grad), custom_call_target="tpu_custom_call" | custom-call | tf_op jit(solution)/shard_map/input_back/pallas_call | solution.py:774
  478.2 27.7 %reduce-scatter.7.cloned.1.call-done = bf16[64,1664]{1,0:T(8,128)(2,1)} async-done(((bf16[1024,1664]{1,0:T(8,128)(2,1)}), bf16[64,1664]{1,0:T(8,128)(2,1)}) %reduce-scatter.7.cloned.1.call-update) | async-done | bytes 213008 | tf_op jit(solution)/shard_map/reduce_scatter | solution.py:810
  (256 shorter events, 132.5 us)
Async XLA Ops:
  7.2 434.9 %reduce-scatter.9.cloned.1.call-start = ((), (), s32[]{:S(2)}) async-start(), calls=%async_computation.5 | async-start | bytes 1114112 | tf_op jit(solution)/shard_map/reduce_scatter | solution.py:810
  20.8 11.2 %collective-permute-start.4 = (bf16[640,256]{1,0:T(8,128)(2,1)S(1)}, bf16[640,256]{1,0:T(8,128)(2,1)S(1)}, u32[]{:S(2)}, u32[]{:S(2)}) collective-permute-start(bf16[640,256]{1,0:T(8,128)(2,1)S(1)} %get-tuple-element.60), channel_id=1, source_target_pairs={{0,2},{2,0},{4,6},{6,4},{8,10},{10,8},{12,14},{14,12},{16,18},{18,... | collective-permute-start | bytes 983048 | tf_op jit(solution)/shard_map/ppermute | solution.py:790
  23.8 15.2 %collective-permute-start.6 = (bf16[640,256]{1,0:T(8,128)(2,1)S(1)}, bf16[640,256]{1,0:T(8,128)(2,1)S(1)}, u32[]{:S(2)}, u32[]{:S(2)}) collective-permute-start(bf16[640,256]{1,0:T(8,128)(2,1)S(1)} %get-tuple-element.62), channel_id=1, source_target_pairs={{0,6},{2,4},{4,2},{6,0},{8,14},{10,12},{12,10},{14,8},{16,22},{18,... | collective-permute-start | bytes 983048 | tf_op jit(solution)/shard_map/ppermute | solution.py:790
  24.3 95.4 %collective-permute-start = (bf16[512,1024]{1,0:T(8,128)(2,1)S(1)}, bf16[512,1024]{1,0:T(8,128)(2,1)}, u32[]{:S(2)}, u32[]{:S(2)}) collective-permute-start(bf16[512,1024]{1,0:T(8,128)(2,1)S(1)} %copy-done.2), channel_id=1, source_target_pairs={{0,1},{1,0},{2,3},{3,2},{4,5},{5,4},{6,7},{7,6},{8,9},{9,8},{10,11... | collective-permute-start | bytes 3145736 | tf_op jit(solution)/shard_map/ppermute | solution.py:785
  43.3 22.3 %collective-permute-start.7 = (bf16[1536,256]{1,0:T(8,128)(2,1)S(1)}, bf16[1536,256]{1,0:T(8,128)(2,1)S(1)}, u32[]{:S(2)}, u32[]{:S(2)}) collective-permute-start(bf16[1536,256]{1,0:T(8,128)(2,1)S(1)} %get-tuple-element.63), channel_id=1, source_target_pairs={{0,8},{2,10},{4,12},{6,14},{8,16},{10,18},{12,20},{14,22},{16,24},... | collective-permute-start | bytes 2359304 | tf_op jit(solution)/shard_map/ppermute | solution.py:802
  44.9 36.8 %collective-permute-start.8 = (bf16[1536,256]{1,0:T(8,128)(2,1)S(1)}, bf16[1536,256]{1,0:T(8,128)(2,1)S(1)}, u32[]{:S(2)}, u32[]{:S(2)}) collective-permute-start(bf16[1536,256]{1,0:T(8,128)(2,1)S(1)} %get-tuple-element.64), channel_id=1, source_target_pairs={{0,24},{2,26},{4,28},{6,30},{8,0},{10,2},{12,4},{14,6},{16,8},{18,... | collective-permute-start | bytes 2359304 | tf_op jit(solution)/shard_map/ppermute | solution.py:802
  116.6 15.2 %collective-permute-start.9 = (bf16[640,128]{1,0:T(8,128)(2,1)S(1)}, bf16[640,128]{1,0:T(8,128)(2,1)S(1)}, u32[]{:S(2)}, u32[]{:S(2)}) collective-permute-start(bf16[640,128]{1,0:T(8,128)(2,1)S(1)} %get-tuple-element.66.o1), channel_id=1, source_target_pairs={{0,2},{2,0},{4,6},{6,4},{8,10},{10,8},{12,14},{14,12},{16,18},{18,... | collective-permute-start | bytes 491528 | tf_op jit(solution)/shard_map/ppermute | solution.py:790
  117.2 14.6 %collective-permute-start.14 = (bf16[640,128]{1,0:T(8,128)(2,1)S(1)}, bf16[640,128]{1,0:T(8,128)(2,1)S(1)}, u32[]{:S(2)}, u32[]{:S(2)}) collective-permute-start(bf16[640,128]{1,0:T(8,128)(2,1)S(1)} %get-tuple-element.67.o2), channel_id=1, source_target_pairs={{0,5},{1,4},{2,7},{3,6},{4,1},{5,0},{6,3},{7,2},{8,13},{9,12},{10,... | collective-permute-start | bytes 491528 | tf_op jit(solution)/shard_map/ppermute | solution.py:796
  119.6 12.1 %collective-permute-start.10 = (bf16[640,128]{1,0:T(8,128)(2,1)S(1)}, bf16[640,128]{1,0:T(8,128)(2,1)S(1)}, u32[]{:S(2)}, u32[]{:S(2)}) collective-permute-start(bf16[640,128]{1,0:T(8,128)(2,1)S(1)} %get-tuple-element.67.o2), channel_id=1, source_target_pairs={{0,4},{2,6},{4,0},{6,2},{8,12},{10,14},{12,8},{14,10},{16,20},{18,... | collective-permute-start | bytes 491528 | tf_op jit(solution)/shard_map/ppermute | solution.py:790
  157.2 30.4 %collective-permute-start.17 = (bf16[640,1024]{1,0:T(8,128)(2,1)S(1)}, bf16[640,1024]{1,0:T(8,128)(2,1)S(1)}, u32[]{:S(2)}, u32[]{:S(2)}) collective-permute-start(bf16[640,1024]{1,0:T(8,128)(2,1)S(1)} %convolution_convert_fusion.2.part), channel_id=1, source_target_pairs={{0,1},{1,0},{2,3},{3,2},{4,5},{5,4},{6,7},{7,6},{8,9},{9,8},{10,11... | collective-permute-start | bytes 3932168 | tf_op jit(solution)/shard_map/ppermute | solution.py:785
  200.1 274.1 %reduce-scatter.13.cloned.1.call-start = ((), (), s32[]{:S(2)}) async-start(), calls=%async_computation.7 | async-start | bytes 4456448
  216.3 260.1 %reduce-scatter.11.cloned.1.call-start = ((), (), s32[]{:S(2)}) async-start(), calls=%async_computation.6 | async-start | bytes 4456448 | tf_op jit(solution)/shard_map/reduce_scatter | solution.py:810
  224.5 281.4 %reduce-scatter.7.cloned.1.call-start = ((), (), s32[]{:S(2)}) async-start(), calls=%async_computation.4 | async-start | bytes 3620864 | tf_op jit(solution)/shard_map/reduce_scatter | solution.py:810
  226.4 11.4 %collective-permute-start.20 = (bf16[640,128]{1,0:T(8,128)(2,1)S(1)}, bf16[640,128]{1,0:T(8,128)(2,1)S(1)}, u32[]{:S(2)}, u32[]{:S(2)}) collective-permute-start(bf16[640,128]{1,0:T(8,128)(2,1)S(1)} %copy-done.56), channel_id=1, source_target_pairs={{0,6},{2,4},{4,2},{6,0},{8,14},{10,12},{12,10},{14,8},{16,22},{18,... | collective-permute-start | bytes 491528 | tf_op jit(solution)/shard_map/ppermute | solution.py:790
  289.5 46.8 %collective-permute-start.24 = (bf16[1536,256]{1,0:T(8,128)(2,1)S(1)}, bf16[1536,256]{1,0:T(8,128)(2,1)S(1)}, u32[]{:S(2)}, u32[]{:S(2)}) collective-permute-start(bf16[1536,256]{1,0:T(8,128)(2,1)S(1)} %get-tuple-element.81), channel_id=1, source_target_pairs={{0,24},{2,26},{4,28},{6,30},{8,0},{10,2},{12,4},{14,6},{16,8},{18,... | collective-permute-start | bytes 2359304 | tf_op jit(solution)/shard_map/ppermute | solution.py:802
  293.9 52.2 %collective-permute-start.25 = (bf16[1536,256]{1,0:T(8,128)(2,1)S(1)}, bf16[1536,256]{1,0:T(8,128)(2,1)S(1)}, u32[]{:S(2)}, u32[]{:S(2)}) collective-permute-start(bf16[1536,256]{1,0:T(8,128)(2,1)S(1)} %get-tuple-element.82), channel_id=1, source_target_pairs={{0,8},{2,10},{4,12},{6,14},{8,16},{10,18},{12,20},{14,22},{16,24},... | collective-permute-start | bytes 2359304 | tf_op jit(solution)/shard_map/ppermute | solution.py:802
  293.9 62.5 %collective-permute-start.21 = (bf16[640,128]{1,0:T(8,128)(2,1)}, bf16[640,128]{1,0:T(8,128)(2,1)S(1)}, u32[]{:S(2)}, u32[]{:S(2)}) collective-permute-start(bf16[640,128]{1,0:T(8,128)(2,1)} %get-tuple-element.77), channel_id=1, source_target_pairs={{0,2},{2,0},{4,6},{6,4},{8,10},{10,8},{12,14},{14,12},{16,18},{18,... | collective-permute-start | bytes 491528 | tf_op jit(solution)/shard_map/ppermute | solution.py:790
  350.4 24.0 %collective-permute-start.26 = (bf16[640,256]{1,0:T(8,128)(2,1)}, bf16[640,256]{1,0:T(8,128)(2,1)S(1)}, u32[]{:S(2)}, u32[]{:S(2)}) collective-permute-start(bf16[640,256]{1,0:T(8,128)(2,1)} %get-tuple-element.84), channel_id=1, source_target_pairs={{0,2},{2,0},{4,6},{6,4},{8,10},{10,8},{12,14},{14,12},{16,18},{18,... | collective-permute-start | bytes 983048 | tf_op jit(solution)/shard_map/ppermute | solution.py:790
  350.5 23.9 %collective-permute-start.27 = (bf16[640,256]{1,0:T(8,128)(2,1)}, bf16[640,256]{1,0:T(8,128)(2,1)S(1)}, u32[]{:S(2)}, u32[]{:S(2)}) collective-permute-start(bf16[640,256]{1,0:T(8,128)(2,1)} %get-tuple-element.85), channel_id=1, source_target_pairs={{0,4},{2,6},{4,0},{6,2},{8,12},{10,14},{12,8},{14,10},{16,20},{18,... | collective-permute-start | bytes 983048 | tf_op jit(solution)/shard_map/ppermute | solution.py:790
  351.5 23.7 %collective-permute-start.28 = (bf16[640,256]{1,0:T(8,128)(2,1)S(1)}, bf16[640,256]{1,0:T(8,128)(2,1)S(1)}, u32[]{:S(2)}, u32[]{:S(2)}) collective-permute-start(bf16[640,256]{1,0:T(8,128)(2,1)S(1)} %get-tuple-element.86), channel_id=1, source_target_pairs={{0,6},{2,4},{4,2},{6,0},{8,14},{10,12},{12,10},{14,8},{16,22},{18,... | collective-permute-start | bytes 983048 | tf_op jit(solution)/shard_map/ppermute | solution.py:790
  355.5 16.3 %collective-permute-start.22 = (bf16[640,128]{1,0:T(8,128)(2,1)}, bf16[640,128]{1,0:T(8,128)(2,1)S(1)}, u32[]{:S(2)}, u32[]{:S(2)}) collective-permute-start(bf16[640,128]{1,0:T(8,128)(2,1)} %copy-done.53), channel_id=1, source_target_pairs={{0,4},{2,6},{4,0},{6,2},{8,12},{10,14},{12,8},{14,10},{16,20},{18,... | collective-permute-start | bytes 491528 | tf_op jit(solution)/shard_map/ppermute | solution.py:790
  357.2 17.2 %collective-permute-start.23 = (bf16[640,128]{1,0:T(8,128)(2,1)S(1)}, bf16[640,128]{1,0:T(8,128)(2,1)S(1)}, u32[]{:S(2)}, u32[]{:S(2)}) collective-permute-start(bf16[640,128]{1,0:T(8,128)(2,1)S(1)} %copy-done.52), channel_id=1, source_target_pairs={{0,6},{2,4},{4,2},{6,0},{8,14},{10,12},{12,10},{14,8},{16,22},{18,... | collective-permute-start | bytes 491528 | tf_op jit(solution)/shard_map/ppermute | solution.py:790
  408.6 31.7 %collective-permute-start.16 = (bf16[640,1024]{1,0:T(8,128)(2,1)S(1)}, bf16[640,1024]{1,0:T(8,128)(2,1)S(1)}, u32[]{:S(2)}, u32[]{:S(2)}) collective-permute-start(bf16[640,1024]{1,0:T(8,128)(2,1)S(1)} %convolution_convert_fusion.3), channel_id=1, source_target_pairs={{0,1},{1,0},{2,3},{3,2},{4,5},{5,4},{6,7},{7,6},{8,9},{9,8},{10,11... | collective-permute-start | bytes 3932168 | tf_op jit(solution)/shard_map/ppermute | solution.py:785
  410.5 57.4 %collective-permute-start.29 = (bf16[640,1024]{1,0:T(8,128)(2,1)S(1)}, bf16[640,1024]{1,0:T(8,128)(2,1)}, u32[]{:S(2)}, u32[]{:S(2)}) collective-permute-start(bf16[640,1024]{1,0:T(8,128)(2,1)S(1)} %get-tuple-element.87.part), channel_id=1, source_target_pairs={{0,1},{1,0},{2,3},{3,2},{4,5},{5,4},{6,7},{7,6},{8,9},{9,8},{10,11... | collective-permute-start | bytes 3932168 | tf_op jit(solution)/shard_map/ppermute | solution.py:785
  (85 other events, 1310.7 us)
Sparse Core Ops, SparseCore 0:
  200.2 59.8 reduce-scatter.8
  264.5 95.4 reduce-scatter.12
  363.8 71.3 reduce-scatter.10
  439.5 66.3 reduce-scatter.6

commit v2 on v1

v2 whole, which is shorter than its diff:
```python
from functools import partial

import jax
import jax.numpy as jnp
from jax import lax
from jax.experimental import pallas as pl
from jax.experimental.pallas import tpu as pltpu
from jax.sharding import PartitionSpec as P

H = 16
HD = 64
SEG = 128
SEG_DEV = 5
ANC = 10
TREE = 20
INNER = 12
MEMBERS = 4
PAIR = 2 * HD
POOL = TREE + 2 * INNER
EMPTY = POOL

EPSILON = 1e-05
NEGATIVE = -1e30

F32 = jnp.float32
BF16 = jnp.bfloat16

LISTS = TREE * ANC
SLOT_AT = (0, 2 * LISTS)
LEVEL_AT = (LISTS, 3 * LISTS)
COUNT_AT = (4 * LISTS, 4 * LISTS + TREE)
UP_AT = 4 * LISTS + 2 * TREE
DOWN_AT = UP_AT + INNER
TABLE = 896

VM = pl.BlockSpec(memory_space=pltpu.VMEM)
SM = pl.BlockSpec(memory_space=pltpu.SMEM)
ANY = pl.BlockSpec(memory_space=pl.ANY)


def shaped(shape, kind):
    return jax.ShapeDtypeStruct(shape, kind)


def params(mib=60):
    return pltpu.CompilerParams(vmem_limit_bytes=mib * 2**20)


def dot(a, b, dims=((1,), (0,))):
    return lax.dot_general(a, b, (dims, ((), ())), preferred_element_type=F32)


def lanes(shape):
    return lax.broadcasted_iota(jnp.int32, shape, len(shape) - 1)


def rows_of(shape):
    return lax.broadcasted_iota(jnp.int32, shape, len(shape) - 2)


def table_kernel(count, meta, parent, out, inner, place):
    member, group = meta[0], meta[1]
    groups = count // TREE
    below = lax.rem(group + groups - 1, groups)
    above = lax.rem(group + 1, groups)

    def clear(i, _):
        inner[i] = 0
        place[i] = EMPTY
        return _

    lax.fori_loop(0, count, clear, 0)

    def mark(i, _):
        up = parent[i]

        @pl.when(up >= 0)
        def _mark():
            inner[up] = 1

        return _

    lax.fori_loop(0, count, mark, 0)

    def cover(i, mask):
        up = parent[i]
        ahead = lax.rem(up - i + count, count)
        forward = ahead < TREE
        low = jnp.where(forward, i, up)
        length = jnp.where(forward, ahead, count - ahead)
        length = jnp.where(up >= 0, length, 0)
        start = lax.rem(low + 1 + TREE, TREE)
        bits = lax.shift_left(1, length) - 1
        room = TREE - start
        first = lax.shift_left(bits & (lax.shift_left(1, room) - 1), start)
        second = lax.shift_right_logical(bits, room)
        return mask | first | second

    mask = lax.fori_loop(0, 2 * TREE - 1, cover, 0)

    def find(c, found):
        free = (lax.shift_right_logical(mask, c) & 1) == 0
        return jnp.where(free, c, found)

    offset = lax.fori_loop(0, TREE, find, 0)

    for i in range(2 * INNER):
        out[UP_AT + i] = -1

    def own(p, ranks):
        up_rank, down_rank = ranks
        spot = ((p // SEG_DEV) ^ member) * SEG_DEV + lax.rem(p, SEG_DEV)
        slot = group * TREE + p
        place[slot] = spot
        has = inner[slot] == 1
        goes_up = has & (p >= offset) & (offset > 0) & (up_rank < INNER)
        goes_down = has & (p < offset) & (down_rank < INNER)

        @pl.when(goes_up)
        def _up():
            out[UP_AT + up_rank] = spot

        @pl.when(goes_down)
        def _down():
            out[DOWN_AT + down_rank] = spot

        return up_rank + goes_up.astype(jnp.int32), down_rank + goes_down.astype(jnp.int32)

    lax.fori_loop(0, TREE, own, (0, 0))

    def others(p, ranks):
        low_rank, high_rank = ranks
        low_slot = below * TREE + p
        high_slot = above * TREE + p
        low = (inner[low_slot] == 1) & (p >= offset) & (offset > 0) & (low_rank < INNER)
        high = (inner[high_slot] == 1) & (p < offset) & (high_rank < INNER)

        @pl.when(low)
        def _low():
            place[low_slot] = TREE + low_rank

        @pl.when(high)
        def _high():
            place[high_slot] = TREE + INNER + high_rank

        return low_rank + low.astype(jnp.int32), high_rank + high.astype(jnp.int32)

    lax.fori_loop(0, TREE, others, (0, 0))

    def chain(q, _):
        slot = group * TREE + ((q // SEG_DEV) ^ member) * SEG_DEV + lax.rem(q, SEG_DEV)
        for i in range(ANC):
            out[SLOT_AT[0] + q * ANC + i] = TREE
            out[SLOT_AT[1] + q * ANC + i] = 2 * INNER
            out[LEVEL_AT[0] + q * ANC + i] = 0
            out[LEVEL_AT[1] + q * ANC + i] = 0

        def step(a, state):
            at, near, far = state
            good = at >= 0
            safe = jnp.maximum(at, 0)
            spot = place[safe]
            is_near = good & (spot < TREE)
            is_far = good & (spot >= TREE)

            @pl.when(is_near)
            def _near():
                out[SLOT_AT[0] + q * ANC + near] = spot
                out[LEVEL_AT[0] + q * ANC + near] = a

            @pl.when(is_far)
            def _far():
                out[SLOT_AT[1] + q * ANC + far] = spot - TREE
                out[LEVEL_AT[1] + q * ANC + far] = a

            return (
                jnp.where(good, parent[safe], -1),
                near + is_near.astype(jnp.int32),
                far + is_far.astype(jnp.int32),
            )

        _end, near, far = lax.fori_loop(0, ANC, step, (slot, 0, 0))
        out[COUNT_AT[0] + q] = near
        out[COUNT_AT[1] + q] = far
        return _

    lax.fori_loop(0, TREE, chain, 0)


def make_tables(meta, parent):
    count = parent.shape[0]
    return pl.pallas_call(
        partial(table_kernel, count),
        out_shape=shaped((TABLE,), jnp.int32),
        in_specs=[SM, SM],
        out_specs=SM,
        scratch_shapes=[pltpu.SMEM((count,), jnp.int32), pltpu.SMEM((count,), jnp.int32)],
        name="tables",
    )(meta, parent)


def normal(block):
    centered = block - jnp.mean(block, axis=-1, keepdims=True)
    variance = jnp.mean(centered * centered, axis=-1, keepdims=True)
    scale = lax.rsqrt(variance + EPSILON)
    return centered * scale, scale


def project_kernel(meta, x, gain, shift, weight, bias, normed, *outs):
    member = meta[0]
    rows = x.shape[0]
    step = 64

    def norm_step(i, _):
        at = pl.ds(pl.multiple_of(i * step, step), step)
        hat, _scale = normal(x[at, :].astype(F32))
        normed[at, :] = (hat * gain[...].astype(F32) + shift[...].astype(F32)).astype(BF16)
        return _

    lax.fori_loop(0, rows // step, norm_step, 0)
    low = lanes((1, PAIR)) < HD

    def one(d, _):
        pair = member ^ d
        block = weight[:, pl.ds(pl.multiple_of(pair * 3 * PAIR, PAIR), 3 * PAIR)]
        both = bias[:, pl.ds(pl.multiple_of(pair * 2 * PAIR, PAIR), 2 * PAIR)].astype(F32)
        first, second = both[:, :PAIR], both[:, PAIR:]
        query_bias = jnp.where(low, first, pltpu.roll(second, HD, 1))
        value_bias = jnp.where(low, pltpu.roll(first, HD, 1), second)
        joined = dot(normed[...], block)
        t0, t1, t2 = joined[:, :PAIR], joined[:, PAIR : 2 * PAIR], joined[:, 2 * PAIR :]
        queries = (jnp.where(low, t0, t1) + query_bias) * (HD ** (-0.5))
        keys = pltpu.roll(jnp.where(low, t2, t0), HD, 1)
        values = jnp.where(low, t1, t2) + value_bias
        for j in range(MEMBERS):

            @pl.when(d == j)
            def _store():
                outs[j][...] = queries.astype(BF16)
                outs[MEMBERS + j][:, :PAIR] = keys.astype(BF16)
                outs[MEMBERS + j][:, PAIR:] = values.astype(BF16)

        return _

    lax.fori_loop(0, MEMBERS, one, 0)


def project(meta, x, gain, shift, weight, bias):
    rows, width = x.shape
    outs = pl.pallas_call(
        project_kernel,
        out_shape=[shaped((rows, width), BF16)]
        + [shaped((rows, PAIR), BF16)] * MEMBERS
        + [shaped((rows, 2 * PAIR), BF16)] * MEMBERS,
        in_specs=[SM] + [VM] * 5,
        out_specs=[VM] * (1 + 2 * MEMBERS),
        compiler_params=params(),
        name="project",
    )(meta, x, gain, shift, weight, bias)
    return outs[0], outs[1 : 1 + MEMBERS], outs[1 + MEMBERS :]


def pack_kernel(table, kv0, kv1, kv2, kv3, up, down, sem):
    sources = (kv0, kv1, kv2, kv3)
    for side, at, target in ((0, UP_AT, up), (1, DOWN_AT, down)):
        for i in range(INNER):
            spot = jnp.maximum(table[at + i], 0)
            d, s = spot // SEG_DEV, lax.rem(spot, SEG_DEV)
            for j in range(MEMBERS):

                @pl.when(d == j)
                def _start():
                    pltpu.make_async_copy(
                        sources[j].at[pl.ds(pl.multiple_of(s * SEG, SEG), SEG)],
                        target.at[pl.ds(i * SEG, SEG)],
                        sem.at[side * INNER + i],
                    ).start()

    for side, target in ((0, up), (1, down)):
        for i in range(INNER):
            piece = target.at[pl.ds(i * SEG, SEG)]
            pltpu.make_async_copy(piece, piece, sem.at[side * INNER + i]).wait()


def pack(table, pairs):
    out = shaped((INNER * SEG, 2 * PAIR), BF16)
    return pl.pallas_call(
        pack_kernel,
        out_shape=[out, out],
        in_specs=[SM] + [ANY] * MEMBERS,
        out_specs=[ANY] * 2,
        scratch_shapes=[pltpu.SemaphoreType.DMA((2 * INNER,))],
        compiler_params=params(8),
        name="pack",
    )(table, *pairs)


LEVELS = (2, 4, 6, 8, 10)


def split_heads(tile):
    low = lanes((SEG, PAIR)) < HD
    wide = tile.astype(F32)
    zero = jnp.zeros_like(wide)
    return jnp.concatenate(
        [jnp.where(low, wide, zero), jnp.where(low, zero, wide)], axis=0
    ).astype(BF16)


def join_heads(turned):
    top = rows_of((PAIR, SEG)) < HD
    return jnp.where(top, turned[:, :SEG], turned[:, SEG:]).T


def slope_row(slopes, meta):
    first = meta[2]
    return jnp.where(lanes((1, 2 * SEG)) < SEG, slopes[first], slopes[first + 1])


def fill_bias(bias, slope):
    shape = (SEG, 2 * SEG)
    offset = lax.rem(lanes(shape), SEG)
    key = rows_of(shape)
    gap = slope * (key - offset).astype(F32)
    bias[0] = jnp.where(key <= offset, gap, NEGATIVE)
    bias[1] = gap


def start_all(copies):
    for copy in copies:
        copy.start()


def wait_all(copies):
    for copy in copies:
        copy.wait()


def loads(sources, target, sem, first):
    copies, at = [], 0
    for k, source in enumerate(sources):
        rows = source.shape[0]
        copies.append(
            pltpu.make_async_copy(source, target.at[pl.ds(at, rows)], sem.at[first + k])
        )
        at += rows
    return copies


def segment(ref, at):
    return ref.at[pl.ds(pl.multiple_of(at * SEG, SEG), SEG)]


def turn_all(pool, turned, count, first):
    def turn(i, _):
        turned[i] = segment(pool, i)[:, first : first + PAIR].astype(F32).T.astype(BF16)
        return _

    lax.fori_loop(0, count, turn, 0)


def entries(table, side, s, span):
    at = s * ANC
    spots = [table[SLOT_AT[side] + at + i] for i in range(span)]
    levels = [table[LEVEL_AT[side] + at + i] for i in range(span)]
    return spots, levels


def level_row(slope, levels, i, count, span):
    row = slope * (levels[i] * (-SEG)).astype(F32)
    if i == span - 1:
        row = row + jnp.where(count < span, NEGATIVE, 0.0)
    return row


def chosen_heads(wide):
    top = rows_of((PAIR, SEG)) < HD
    return jnp.where(top, wide[:, :SEG], wide[:, SEG:])


def weigh(side, span, table, s, slope, bias, pool, turned, stacked):
    count = table[COUNT_AT[side] + s]
    spots, levels = entries(table, side, s, span)
    scores = []
    for i in range(span):
        raw = dot(segment(pool, spots[i])[:, :PAIR], stacked, ((1,), (1,)))
        own = side == 0 and i == 0
        scores.append(raw + bias[0 if own else 1] + level_row(slope, levels, i, count, span))
    top = scores[0]
    for part in scores[1:]:
        top = jnp.maximum(top, part)
    top = jnp.max(top, axis=0, keepdims=True)
    sums, out = None, None
    for i in range(span):
        weights = jnp.exp(scores[i] - top)
        part = dot(turned[spots[i]], weights.astype(BF16))
        sums = weights if sums is None else sums + weights
        out = part if out is None else out + part
    return top, jnp.sum(sums, axis=0, keepdims=True), chosen_heads(out)


def attend_near_kernel(
    table, meta, slopes, q0, q1, q2, q3, kv0, kv1, kv2, kv3,
    kept, stats, pool, turned, queries, bias, sem,
):
    copies = loads((kv0, kv1, kv2, kv3), pool, sem, 0)
    copies += loads((q0, q1, q2, q3), queries, sem, MEMBERS)
    start_all(copies)
    slope = slope_row(slopes, meta)
    fill_bias(bias, slope)
    pool[TREE * SEG :, :] = jnp.zeros((SEG, 2 * PAIR), BF16)
    wait_all(copies)
    turn_all(pool, turned, TREE + 1, PAIR)

    def one(s, _):
        count = table[COUNT_AT[0] + s]
        stacked = split_heads(segment(queries, s)[...])
        for span in LEVELS:

            @pl.when((count > span - 2) & (count <= span))
            def _run():
                top, total, out = weigh(
                    0, span, table, s, slope, bias, pool, turned, stacked
                )
                stats[s, 0:1, :] = top
                stats[s, 1:2, :] = total
                kept[s] = out

        return _

    lax.fori_loop(0, TREE, one, 0)


def attend_near(table, meta, slopes, queries, pairs):
    return pl.pallas_call(
        attend_near_kernel,
        out_shape=[shaped((TREE, PAIR, SEG), F32), shaped((TREE, 8, 2 * SEG), F32)],
        in_specs=[SM] * 3 + [ANY] * (2 * MEMBERS),
        out_specs=[VM, VM],
        scratch_shapes=[
            pltpu.VMEM(((TREE + 1) * SEG, 2 * PAIR), BF16),
            pltpu.VMEM((TREE + 1, PAIR, SEG), BF16),
            pltpu.VMEM((TREE * SEG, PAIR), BF16),
            pltpu.VMEM((2, SEG, 2 * SEG), F32),
            pltpu.SemaphoreType.DMA((2 * MEMBERS,)),
        ],
        compiler_params=params(),
        name="attend_near",
    )(table, meta, slopes, *queries, *pairs)


def attend_far_kernel(
    table, meta, slopes, q0, q1, q2, q3, below, above, kept, stats,
    o0, o1, o2, o3, lse, pool, turned, queries, result, bias, sem,
):
    rows = SEG_DEV * SEG
    copies = loads((below, above), pool, sem, 0)
    copies += loads((q0, q1, q2, q3), queries, sem, 2)
    start_all(copies)
    slope = slope_row(slopes, meta)
    fill_bias(bias, slope)
    pool[2 * INNER * SEG :, :] = jnp.zeros((SEG, 2 * PAIR), BF16)
    wait_all(copies)
    turn_all(pool, turned, 2 * INNER + 1, PAIR)

    def finish(s, top, total, out):
        wide = 1.0 / total
        segment(result, s)[...] = (out * chosen_heads(jnp.broadcast_to(wide, (PAIR, 2 * SEG)))).T.astype(BF16)
        lse[s] = top + jnp.log(total)

    def one(s, _):
        count = table[COUNT_AT[1] + s]

        @pl.when(count == 0)
        def _none():
            finish(s, stats[s, 0:1, :], stats[s, 1:2, :], kept[s])

        for span in LEVELS:

            @pl.when((count > span - 2) & (count <= span) & (count > 0))
            def _run():
                stacked = split_heads(segment(queries, s)[...])
                top, total, out = weigh(
                    1, span, table, s, slope, bias, pool, turned, stacked
                )
                near = stats[s, 0:1, :]
                both = jnp.maximum(near, top)
                near_scale = jnp.exp(near - both)
                far_scale = jnp.exp(top - both)
                total = stats[s, 1:2, :] * near_scale + total * far_scale
                shape = (PAIR, 2 * SEG)
                out = kept[s] * chosen_heads(jnp.broadcast_to(near_scale, shape)) + out * (
                    chosen_heads(jnp.broadcast_to(far_scale, shape))
                )
                finish(s, both, total, out)

        return _

    lax.fori_loop(0, TREE, one, 0)
    copies = [
        pltpu.make_async_copy(result.at[pl.ds(j * rows, rows)], target, sem.at[j])
        for j, target in enumerate((o0, o1, o2, o3))
    ]
    start_all(copies)
    wait_all(copies)


def attend_far(table, meta, slopes, queries, below, above, kept, stats):
    rows = queries[0].shape[0]
    outs = pl.pallas_call(
        attend_far_kernel,
        out_shape=[shaped((rows, PAIR), BF16)] * MEMBERS + [shaped((TREE, 1, 2 * SEG), F32)],
        in_specs=[SM] * 3 + [ANY] * (MEMBERS + 2) + [VM] * 2,
        out_specs=[ANY] * MEMBERS + [VM],
        scratch_shapes=[
            pltpu.VMEM(((2 * INNER + 1) * SEG, 2 * PAIR), BF16),
            pltpu.VMEM((2 * INNER + 1, PAIR, SEG), BF16),
            pltpu.VMEM((TREE * SEG, PAIR), BF16),
            pltpu.VMEM((TREE * SEG, PAIR), BF16),
            pltpu.VMEM((2, SEG, 2 * SEG), F32),
            pltpu.SemaphoreType.DMA((MEMBERS + 2,)),
        ],
        compiler_params=params(),
        name="attend_far",
    )(table, meta, slopes, *queries, below, above, kept, stats)
    return outs[:MEMBERS], outs[MEMBERS]


def spread(side, span, table, s, slope, bias, pool, turned, total, queries, outs, grads, lse):
    count = table[COUNT_AT[side] + s]
    stacked = split_heads(segment(queries, s)[...])
    grad = segment(grads, s)[...]
    stacked_grad = split_heads(grad)
    product = (grad.astype(F32) * segment(outs, s)[...].astype(F32)).T
    delta = jnp.concatenate(
        [
            jnp.sum(product[:HD], axis=0, keepdims=True),
            jnp.sum(product[HD:], axis=0, keepdims=True),
        ],
        axis=1,
    )
    log_total = lse[s]
    spots, levels = entries(table, side, s, span)
    query_grad = None
    for i in range(span):
        block = segment(pool, spots[i])
        raw = dot(block[:, :PAIR], stacked, ((1,), (1,)))
        row = level_row(slope, levels, i, count, span) - log_total
        own = side == 0 and i == 0
        probs = jnp.exp(raw + bias[0 if own else 1] + row)
        prob_grad = dot(block[:, PAIR:], stacked_grad, ((1,), (1,)))
        score_grad = (probs * (prob_grad - delta)).astype(BF16)
        into = segment(total, spots[i])
        into[:, :PAIR] += dot(score_grad, stacked)
        into[:, PAIR:] += dot(probs.astype(BF16), stacked_grad)
        part = dot(turned[spots[i]], score_grad)
        query_grad = part if query_grad is None else query_grad + part
    return chosen_heads(query_grad)


def clear_all(total, count):
    def clear(i, _):
        segment(total, i)[...] = jnp.zeros((SEG, 2 * PAIR), F32)
        return _

    lax.fori_loop(0, count, clear, 0)


def back_far_kernel(
    table, meta, slopes, q0, q1, q2, q3, below, above, o0, o1, o2, o3, g0, g1, g2, g3, lse,
    to_below, to_above, kept,
    pool, turned, queries, outs, grads, total, small, bias, sem,
):
    copies = loads((below, above), pool, sem, 0)
    copies += loads((q0, q1, q2, q3), queries, sem, 2)
    copies += loads((o0, o1, o2, o3), outs, sem, 2 + MEMBERS)
    copies += loads((g0, g1, g2, g3), grads, sem, 2 + 2 * MEMBERS)
    start_all(copies)
    slope = slope_row(slopes, meta)
    fill_bias(bias, slope)
    pool[2 * INNER * SEG :, :] = jnp.zeros((SEG, 2 * PAIR), BF16)
    clear_all(total, 2 * INNER + 1)
    wait_all(copies)
    turn_all(pool, turned, 2 * INNER + 1, 0)

    def one(s, _):
        count = table[COUNT_AT[1] + s]

        @pl.when(count == 0)
        def _none():
            kept[s] = jnp.zeros((PAIR, SEG), F32)

        for span in LEVELS:

            @pl.when((count > span - 2) & (count <= span) & (count > 0))
            def _run():
                kept[s] = spread(
                    1, span, table, s, slope, bias, pool, turned, total, queries, outs, grads, lse
                )

        return _

    lax.fori_loop(0, TREE, one, 0)

    def shorten(i, _):
        segment(small, i)[...] = segment(total, i)[...].astype(BF16)
        return _

    lax.fori_loop(0, 2 * INNER, shorten, 0)
    copies = [
        pltpu.make_async_copy(
            small.at[pl.ds(k * INNER * SEG, INNER * SEG)], target, sem.at[k]
        )
        for k, target in enumerate((to_below, to_above))
    ]
    start_all(copies)
    wait_all(copies)


def back_far(table, meta, slopes, queries, below, above, outs, grads, lse):
    side = shaped((INNER * SEG, 2 * PAIR), BF16)
    return pl.pallas_call(
        back_far_kernel,
        out_shape=[side, side, shaped((TREE, PAIR, SEG), F32)],
        in_specs=[SM] * 3 + [ANY] * (3 * MEMBERS + 2) + [VM],
        out_specs=[ANY] * 2 + [VM],
        scratch_shapes=[
            pltpu.VMEM(((2 * INNER + 1) * SEG, 2 * PAIR), BF16),
            pltpu.VMEM((2 * INNER + 1, PAIR, SEG), BF16),
            pltpu.VMEM((TREE * SEG, PAIR), BF16),
            pltpu.VMEM((TREE * SEG, PAIR), BF16),
            pltpu.VMEM((TREE * SEG, PAIR), BF16),
            pltpu.VMEM(((2 * INNER + 1) * SEG, 2 * PAIR), F32),
            pltpu.VMEM((2 * INNER * SEG, 2 * PAIR), BF16),
            pltpu.VMEM((2, SEG, 2 * SEG), F32),
            pltpu.SemaphoreType.DMA((3 * MEMBERS + 2,)),
        ],
        compiler_params=params(),
        name="back_far",
    )(table, meta, slopes, *queries, below, above, *outs, *grads, lse)


def back_near_kernel(
    table, meta, slopes, q0, q1, q2, q3, kv0, kv1, kv2, kv3, o0, o1, o2, o3, g0, g1, g2, g3,
    lse, kept, dq0, dq1, dq2, dq3, own,
    pool, turned, queries, outs, grads, result, total, bias, sem,
):
    rows = SEG_DEV * SEG
    copies = loads((kv0, kv1, kv2, kv3), pool, sem, 0)
    copies += loads((q0, q1, q2, q3), queries, sem, MEMBERS)
    copies += loads((o0, o1, o2, o3), outs, sem, 2 * MEMBERS)
    copies += loads((g0, g1, g2, g3), grads, sem, 3 * MEMBERS)
    start_all(copies)
    slope = slope_row(slopes, meta)
    fill_bias(bias, slope)
    pool[TREE * SEG :, :] = jnp.zeros((SEG, 2 * PAIR), BF16)
    clear_all(total, TREE + 1)
    wait_all(copies)
    turn_all(pool, turned, TREE + 1, 0)

    def one(s, _):
        count = table[COUNT_AT[0] + s]
        for span in LEVELS:

            @pl.when((count > span - 2) & (count <= span))
            def _run():
                part = spread(
                    0, span, table, s, slope, bias, pool, turned, total, queries, outs, grads, lse
                )
                segment(result, s)[...] = (kept[s] + part).T.astype(BF16)

        return _

    lax.fori_loop(0, TREE, one, 0)
    copies = [
        pltpu.make_async_copy(result.at[pl.ds(j * rows, rows)], target, sem.at[j])
        for j, target in enumerate((dq0, dq1, dq2, dq3))
    ]
    copies.append(
        pltpu.make_async_copy(total.at[pl.ds(0, TREE * SEG)], own, sem.at[MEMBERS])
    )
    start_all(copies)
    wait_all(copies)


def back_near(table, meta, slopes, queries, pairs, outs, grads, lse, kept):
    rows = queries[0].shape[0]
    result = pl.pallas_call(
        back_near_kernel,
        out_shape=[shaped((rows, PAIR), BF16)] * MEMBERS + [shaped((TREE * SEG, 2 * PAIR), F32)],
        in_specs=[SM] * 3 + [ANY] * (4 * MEMBERS) + [VM] * 2,
        out_specs=[ANY] * (MEMBERS + 1),
        scratch_shapes=[
            pltpu.VMEM(((TREE + 1) * SEG, 2 * PAIR), BF16),
            pltpu.VMEM((TREE + 1, PAIR, SEG), BF16),
            pltpu.VMEM((TREE * SEG, PAIR), BF16),
            pltpu.VMEM((TREE * SEG, PAIR), BF16),
            pltpu.VMEM((TREE * SEG, PAIR), BF16),
            pltpu.VMEM((TREE * SEG, PAIR), BF16),
            pltpu.VMEM(((TREE + 1) * SEG, 2 * PAIR), F32),
            pltpu.VMEM((2, SEG, 2 * SEG), F32),
            pltpu.SemaphoreType.DMA((4 * MEMBERS,)),
        ],
        compiler_params=params(),
        name="back_near",
    )(table, meta, slopes, *queries, *pairs, *outs, *grads, lse, kept)
    return result[:MEMBERS], result[MEMBERS]


def gather_back_kernel(table, own, from_above, from_below, k0, k1, k2, k3, total, sem):
    rows = SEG_DEV * SEG
    copy = pltpu.make_async_copy(own, total, sem)
    copy.start()
    copy.wait()
    for at, source in ((UP_AT, from_above), (DOWN_AT, from_below)):

        def add(i, _):
            spot = table[at + i]

            @pl.when(spot >= 0)
            def _add():
                segment(total, spot)[...] += segment(source, i)[...].astype(F32)

            return _

        lax.fori_loop(0, INNER, add, 0)
    for j, target in enumerate((k0, k1, k2, k3)):

        def short(i, _):
            segment(target, i)[...] = segment(total, j * SEG_DEV + i)[...].astype(BF16)
            return _

        lax.fori_loop(0, SEG_DEV, short, 0)


def gather_back(table, own, from_above, from_below):
    rows = SEG_DEV * SEG
    return pl.pallas_call(
        gather_back_kernel,
        out_shape=[shaped((rows, 2 * PAIR), BF16)] * MEMBERS,
        in_specs=[SM, ANY, VM, VM],
        out_specs=[VM] * MEMBERS,
        scratch_shapes=[
            pltpu.VMEM((TREE * SEG, 2 * PAIR), F32),
            pltpu.SemaphoreType.DMA(()),
        ],
        compiler_params=params(),
        name="gather_back",
    )(table, own, from_above, from_below)


TILE = 256
NORM_ROWS = 32


def norm_loop(rows, body):
    def step(i, _):
        body(pl.ds(pl.multiple_of(i * NORM_ROWS, NORM_ROWS), NORM_ROWS))
        return _

    lax.fori_loop(0, rows // NORM_ROWS, step, 0)


def feed_kernel(
    meta, x, out_bias, gain, shift, up_bias, a0, a1, a2, a3, b0, b1, b2, b3,
    w_own, w_other, w_up, hidden_grad,
    mixed_out, middle_out, normed_out, act_out, pre_out, part, sums,
    mixed_own, middle, normed, act, pre_grad, mixed, weight, up, hidden, sem, out_sem,
):
    member, rank = meta[0], meta[3]
    rows, width = x.shape
    half = width // 2
    inner = w_up.shape[1]
    copies = []
    for k, source in enumerate((w_own, w_other)):
        at = pl.multiple_of((rank ^ k) * half, half)
        copies.append(pltpu.make_async_copy(source, weight.at[pl.ds(at, half)], sem.at[k]))
    late = [
        pltpu.make_async_copy(w_up, up, sem.at[2]),
        pltpu.make_async_copy(hidden_grad, hidden, sem.at[3]),
    ]
    start_all(copies + late)
    for k, parts in enumerate(((a0, a1, a2, a3), (b0, b1, b2, b3))):
        for d in range(MEMBERS):
            inside = (member ^ d) * PAIR
            at = pl.multiple_of((rank ^ k) * half + inside, PAIR)
            mixed[:, pl.ds(at, PAIR)] = parts[d][...]
            if k == 0:
                mixed_own[:, pl.ds(pl.multiple_of(inside, PAIR), PAIR)] = parts[d][...]
    stores = [pltpu.make_async_copy(mixed_own, mixed_out, out_sem.at[0])]
    stores[0].start()
    wait_all(copies)

    def column(t, _):
        at = pl.ds(pl.multiple_of(t * TILE, TILE), TILE)
        middle[:, at] = (
            x[:, at].astype(F32) + (dot(mixed[...], weight[:, at]) + out_bias[:, at].astype(F32))
        )
        return _

    lax.fori_loop(0, width // TILE, column, 0)
    stores.append(pltpu.make_async_copy(middle, middle_out, out_sem.at[1]))
    stores[1].start()

    def norm_step(at):
        hat, _scale = normal(middle[at, :])
        normed[at, :] = (hat * gain[...].astype(F32) + shift[...].astype(F32)).astype(BF16)

    norm_loop(rows, norm_step)
    stores.append(pltpu.make_async_copy(normed, normed_out, out_sem.at[2]))
    stores[2].start()
    wait_all(late)

    def hidden_step(t, _):
        at = pl.ds(pl.multiple_of(t * TILE, TILE), TILE)
        pre = dot(normed[...], up[:, at]) + up_bias[:, at].astype(F32)
        square = pre * pre
        c = 0.7978845608028654
        t_ = jnp.tanh(pre * (c + (c * 0.044715) * square))
        low = 0.5 * (1.0 + t_)
        act[:, at] = (pre * low).astype(BF16)
        slope = low + (0.5 * pre) * (1.0 - t_ * t_) * (c + (3.0 * c * 0.044715) * square)
        grad = (hidden[:, at] * slope).astype(BF16)
        pre_grad[:, at] = grad
        sums[0:1, at] = jnp.sum(grad.astype(F32), axis=0, keepdims=True)
        return _

    lax.fori_loop(0, inner // TILE, hidden_step, 0)
    stores.append(pltpu.make_async_copy(act, act_out, out_sem.at[3]))
    stores.append(pltpu.make_async_copy(pre_grad, pre_out, out_sem.at[4]))
    start_all(stores[3:])

    def back(t, _):
        at = pl.ds(pl.multiple_of(t * TILE, TILE), TILE)
        part[:, at] = dot(pre_grad[...], up[at, :], ((1,), (1,))).astype(BF16)
        return _

    lax.fori_loop(0, width // TILE, back, 0)
    wait_all(stores)


def feed(meta, x, out_bias, gain, shift, up_bias, parts_own, parts_other, w_own, w_other, w_up, hidden_grad):
    rows, width = x.shape
    inner = w_up.shape[1]
    half = width // 2
    return pl.pallas_call(
        feed_kernel,
        out_shape=[
            shaped((rows, half), BF16),
            shaped((rows, width), F32),
            shaped((rows, width), BF16),
            shaped((rows, inner), BF16),
            shaped((rows, inner), BF16),
            shaped((rows, width), BF16),
            shaped((8, inner), F32),
        ],
        in_specs=[SM] + [VM] * (5 + 2 * MEMBERS) + [ANY] * 4,
        out_specs=[ANY] * 5 + [VM] * 2,
        scratch_shapes=[
            pltpu.VMEM((rows, half), BF16),
            pltpu.VMEM((rows, width), F32),
            pltpu.VMEM((rows, width), BF16),
            pltpu.VMEM((rows, inner), BF16),
            pltpu.VMEM((rows, inner), BF16),
            pltpu.VMEM((rows, width), BF16),
            pltpu.VMEM((width, width), BF16),
            pltpu.VMEM((width, inner), BF16),
            pltpu.VMEM((rows, inner), F32),
            pltpu.SemaphoreType.DMA((4,)),
            pltpu.SemaphoreType.DMA((5,)),
        ],
        compiler_params=params(),
        name="feed",
    )(meta, x, out_bias, gain, shift, up_bias, *parts_own, *parts_other, w_own, w_other, w_up, hidden_grad)


def turn_rows(source, target):
    def step(i, _):
        at = pl.ds(pl.multiple_of(i * SEG, SEG), SEG)
        target[at, :] = source[:, at].astype(F32).T.astype(BF16)
        return _

    lax.fori_loop(0, source.shape[1] // SEG, step, 0)


def feed_grads_kernel(grad, act, normed, pre_grad, out, turned):
    t = pl.program_id(0)
    tiles = pl.num_programs(0) // 2

    @pl.when(t == 0)
    def _first():
        turn_rows(grad, turned)

    @pl.when(t == tiles)
    def _second():
        turn_rows(normed, turned)

    @pl.when(t < tiles)
    def _contract():
        out[...] = dot(turned[...], act[...]).astype(BF16)

    @pl.when(t >= tiles)
    def _expand():
        out[...] = dot(turned[...], pre_grad[...]).astype(BF16)


def feed_grads(grad, act, normed, pre_grad, across):
    rows, width = grad.shape
    tiles = act.shape[1] // TILE
    whole = pl.BlockSpec((rows, width), lambda t: (0, 0))
    return pl.pallas_call(
        feed_grads_kernel,
        grid=(2 * tiles,),
        out_shape=shaped((width, across), BF16),
        in_specs=[
            whole,
            pl.BlockSpec((rows, TILE), lambda t: (0, jnp.minimum(t, tiles - 1))),
            whole,
            pl.BlockSpec((rows, TILE), lambda t: (0, jnp.maximum(t - tiles, 0))),
        ],
        out_specs=pl.BlockSpec((width, TILE), lambda t: (0, t)),
        scratch_shapes=[pltpu.VMEM((width, rows), BF16)],
        compiler_params=params(),
        name="feed_grads",
    )(grad, act, normed, pre_grad)


def in_two(rows8):
    high = rows8.astype(BF16).astype(F32)
    low = rows8 - high
    return jnp.concatenate([high, low, jnp.zeros((SEG - 16, rows8.shape[1]), F32)], axis=0)


def output_grads_kernel(branch, mixed, vectors, extra, held, out, turned, result, small, sem):
    width, half = branch.shape[1], mixed.shape[1]
    turn_rows(branch, turned)

    def column(t, _):
        at = pl.ds(pl.multiple_of(t * TILE, TILE), TILE)
        result[:, at] = dot(turned[...], mixed[:, at]).astype(BF16)
        return _

    lax.fori_loop(0, half // TILE, column, 0)
    for i in range(width // SEG):
        at = slice(i * SEG, (i + 1) * SEG)
        rows8 = jnp.concatenate([vectors[0:4, at], extra[0:2, at], jnp.zeros((2, SEG), F32)], axis=0)
        small[at, :] = in_two(rows8).T.astype(BF16)
    first = out.shape[1] - half - SEG
    copies = [
        pltpu.make_async_copy(result, out.at[:, pl.ds(first, half)], sem.at[0]),
        pltpu.make_async_copy(small, out.at[:, pl.ds(first + half, SEG)], sem.at[1]),
    ]
    start_all(copies)
    wait_all(copies)


def output_grads(branch, mixed, vectors, extra, held):
    rows, width = branch.shape
    half = mixed.shape[1]
    return pl.pallas_call(
        output_grads_kernel,
        out_shape=shaped(held.shape, held.dtype),
        in_specs=[VM] * 4 + [ANY],
        out_specs=ANY,
        input_output_aliases={4: 0},
        scratch_shapes=[
            pltpu.VMEM((width, rows), BF16),
            pltpu.VMEM((width, half), BF16),
            pltpu.VMEM((width, SEG), BF16),
            pltpu.SemaphoreType.DMA((2,)),
        ],
        compiler_params=params(),
        name="output_grads",
    )(branch, mixed, vectors, extra, held)


def feed_finish_kernel(inner, got, contract, expand, output, v0, v1, v2, v3, bias):
    rows = got.shape[0]
    half = output.shape[1]
    contract[...] = got[:, :inner].astype(F32)
    expand[...] = got[:, inner : 2 * inner].astype(F32)
    output[...] = got[:, 2 * inner : 2 * inner + half].astype(F32)
    small = got[:, 2 * inner + half :].astype(F32).T
    whole = small[0:8] + small[8:16]
    for k, target in enumerate((v0, v1, v2, v3)):
        target[...] = whole[k : k + 1]
    bias[...] = whole[4:6]


def feed_finish(got, inner, half):
    rows = got.shape[0]
    return pl.pallas_call(
        partial(feed_finish_kernel, inner),
        out_shape=[shaped((rows, inner), F32)] * 2
        + [shaped((rows, half), F32)]
        + [shaped((1, rows), F32)] * 4
        + [shaped((2, rows), F32)],
        in_specs=[VM],
        out_specs=[VM] * 8,
        compiler_params=params(),
        name="feed_finish",
    )(got)


def norm_back(hat, scale, up):
    mean_up = jnp.mean(up, axis=-1, keepdims=True)
    mean_both = jnp.mean(up * hat, axis=-1, keepdims=True)
    return scale * (up - mean_up - hat * mean_both)


def middle_back_kernel(
    meta, middle, part, other, grad, gain, weight,
    middle_grad, branch, vectors, g0, g1, g2, g3,
):
    member = meta[0]
    rows, width = middle.shape
    step = 64
    vectors[...] = jnp.zeros_like(vectors)

    def norm_step(i, _):
        at = pl.ds(pl.multiple_of(i * step, step), step)
        hat, scale = normal(middle[at, :])
        second = part[at, :].astype(F32) + other[at, :].astype(F32)
        back = grad[at, :].astype(F32) + norm_back(hat, scale, second * gain[...].astype(F32))
        middle_grad[at, :] = back
        branch[at, :] = back.astype(BF16)
        vectors[0:1, :] += jnp.sum(second * hat, axis=0, keepdims=True)
        vectors[1:2, :] += jnp.sum(second, axis=0, keepdims=True)
        vectors[2:3, :] += jnp.sum(back, axis=0, keepdims=True)
        vectors[3:4, :] += jnp.sum(grad[at, :].astype(F32), axis=0, keepdims=True)
        return _

    lax.fori_loop(0, rows // step, norm_step, 0)
    for d, target in enumerate((g0, g1, g2, g3)):
        at = pl.multiple_of((member ^ d) * PAIR, PAIR)
        target[...] = dot(branch[...], weight[pl.ds(at, PAIR), :], ((1,), (1,))).astype(BF16)


def middle_back(meta, middle, part, other, grad, gain, weight):
    rows, width = middle.shape
    outs = pl.pallas_call(
        middle_back_kernel,
        out_shape=[shaped((rows, width), F32), shaped((rows, width), BF16), shaped((8, width), F32)]
        + [shaped((rows, PAIR), BF16)] * MEMBERS,
        in_specs=[SM] + [VM] * 6,
        out_specs=[VM] * (3 + MEMBERS),
        compiler_params=params(),
        name="middle_back",
    )(meta, middle, part, other, grad, gain, weight)
    return outs[0], outs[1], outs[2], outs[3:]


def join_kernel(meta, weight, q0, q1, q2, q3, k0, k1, k2, k3, joined, part, sums):
    member = meta[0]
    low = lanes((1, PAIR)) < HD
    for d, (query, both) in enumerate(((q0, k0), (q1, k1), (q2, k2), (q3, k3))):
        wide_q = query[...].astype(F32) * (HD ** (-0.5))
        wide_k = pltpu.roll(both[:, :PAIR].astype(F32), HD, 1)
        wide_v = both[:, PAIR:].astype(F32)
        at = (member ^ d) * 3 * PAIR
        for k, tile in enumerate(
            (
                jnp.where(low, wide_q, wide_k),
                jnp.where(low, wide_v, wide_q),
                jnp.where(low, wide_k, wide_v),
            )
        ):
            joined[:, pl.ds(pl.multiple_of(at + k * PAIR, PAIR), PAIR)] = tile.astype(BF16)
        sum_q = jnp.sum(wide_q, axis=0, keepdims=True)
        sum_v = jnp.sum(wide_v, axis=0, keepdims=True)
        spot = pl.multiple_of((member ^ d) * 2 * PAIR, PAIR)
        sums[0:1, pl.ds(spot, PAIR)] = jnp.where(low, sum_q, pltpu.roll(sum_v, HD, 1))
        sums[0:1, pl.ds(pl.multiple_of(spot + PAIR, PAIR), PAIR)] = jnp.where(
            low, pltpu.roll(sum_q, HD, 1), sum_v
        )
    width = weight.shape[0]

    def column(t, _):
        at = pl.ds(pl.multiple_of(t * TILE, TILE), TILE)
        part[:, at] = dot(joined[...], weight[at, :], ((1,), (1,))).astype(BF16)
        return _

    lax.fori_loop(0, width // TILE, column, 0)


def join_stage(meta, weight, query_grads, pair_grads):
    rows = query_grads[0].shape[0]
    width, across = weight.shape
    return pl.pallas_call(
        join_kernel,
        out_shape=[
            shaped((rows, across), BF16),
            shaped((rows, width), BF16),
            shaped((8, 2 * MEMBERS * PAIR), F32),
        ],
        in_specs=[SM] + [VM] * (1 + 2 * MEMBERS),
        out_specs=[VM] * 3,
        compiler_params=params(),
        name="join_stage",
    )(meta, weight, *query_grads, *pair_grads)


ORDERS = ((0, 1, 2, 3), (0, 2, 3, 1))
FIRST_PART = 1024


def block_place(relative, order):
    place = 0
    for bit in order:
        place = place * 2 + (lax.shift_right_logical(relative, bit) & 1)
    return place


def turn_ordered(tile, target, i, device, order, share):
    for k in range(SEG // share):
        block = i * (SEG // share) + k
        at = block_place(block ^ device, order) * share
        target[pl.ds(pl.multiple_of(at, share), share), :] = tile[k * share : (k + 1) * share]


def turn_source(source, target, device, order, share):
    def step(i, _):
        at = pl.ds(pl.multiple_of(i * SEG, SEG), SEG)
        tile = source[:, at].astype(F32).T.astype(BF16)
        turn_ordered(tile, target, i, device, order, share)
        return _

    lax.fori_loop(0, source.shape[1] // SEG, step, 0)


def joined_first_kernel(meta, x, part, normed, joined, keep, send, vectors, turned):
    rows, width = x.shape
    device = meta[4]
    turn_source(normed, turned, device, ORDERS[0], width // 16)
    half = width // 2
    tile = TILE

    def column(t, _):
        at = pl.ds(pl.multiple_of(t * tile, tile), tile)
        keep[:, at] = dot(turned[:half], joined[:, at])
        send[:, at] = dot(turned[half:], joined[:, at]).astype(BF16)
        return _

    lax.fori_loop(0, keep.shape[1] // tile, column, 0)
    vectors[...] = jnp.zeros_like(vectors)

    def norm_step(at):
        hat, _scale = normal(x[at, :].astype(F32))
        first = part[at, :].astype(F32)
        vectors[0:1, :] += jnp.sum(first * hat, axis=0, keepdims=True)
        vectors[1:2, :] += jnp.sum(first, axis=0, keepdims=True)

    norm_loop(rows, norm_step)


def joined_first(meta, x, part, normed, joined):
    rows, width = x.shape
    half = width // 2
    return pl.pallas_call(
        joined_first_kernel,
        out_shape=[
            shaped((half, FIRST_PART), F32),
            shaped((half, FIRST_PART), BF16),
            shaped((8, width), F32),
        ],
        in_specs=[SM] + [VM] * 4,
        out_specs=[VM] * 3,
        scratch_shapes=[pltpu.VMEM((width, rows), BF16)],
        compiler_params=params(),
        name="joined_first",
    )(meta, x, part, normed, joined)


def joined_second_kernel(meta, normed, joined, vectors, other, sums, keep, send, turned, small):
    width = normed.shape[1]
    device = meta[4]
    share = width // 16
    turn_source(normed, turned, device, ORDERS[1], share)
    half = width // 2
    across = joined.shape[1] - FIRST_PART
    tile = TILE

    def column(t, _):
        at = pl.ds(pl.multiple_of(t * tile, tile), tile)
        source = pl.ds(pl.multiple_of(FIRST_PART + t * tile, tile), tile)
        keep[:, at] = dot(turned[:half], joined[:, source])
        send[:, at] = dot(turned[half:], joined[:, source]).astype(BF16)
        return _

    lax.fori_loop(0, across // tile, column, 0)
    for i in range(width // SEG):
        at = slice(i * SEG, (i + 1) * SEG)
        rows8 = jnp.concatenate(
            [vectors[0:2, at] + other[0:2, at], sums[0:1, at], jnp.zeros((5, SEG), F32)], axis=0
        )
        turn_ordered(in_two(rows8).T, small, i, device, ORDERS[1], share)
    keep[:, across:] = small[:half]
    send[:, across:] = small[half:].astype(BF16)


def joined_second(meta, normed, joined, vectors, other, sums):
    rows, width = normed.shape
    half = width // 2
    across = joined.shape[1] - FIRST_PART + SEG
    return pl.pallas_call(
        joined_second_kernel,
        out_shape=[shaped((half, across), F32), shaped((half, across), BF16)],
        in_specs=[SM] + [VM] * 5,
        out_specs=[VM] * 2,
        scratch_shapes=[pltpu.VMEM((width, rows), BF16), pltpu.VMEM((width, SEG), F32)],
        compiler_params=params(),
        name="joined_second",
    )(meta, normed, joined, vectors, other, sums)


def joined_finish_kernel(a, got_a, b, got_b, weight, v0, v1, v2):
    total = b[...] + got_b[...].astype(F32)
    cut = a.shape[1]
    rest = b.shape[1] - SEG
    weight[:, :cut] = a[...] + got_a[...].astype(F32)
    weight[:, cut:] = total[:, :rest]
    small = total[:, rest:].T
    whole = small[0:8] + small[8:16]
    for k, target in enumerate((v0, v1, v2)):
        target[...] = whole[k : k + 1]


def joined_finish(a, got_a, b, got_b):
    rows = a.shape[0]
    across = a.shape[1] + b.shape[1] - SEG
    return pl.pallas_call(
        joined_finish_kernel,
        out_shape=[shaped((rows, across), F32)] + [shaped((1, rows), F32)] * 3,
        in_specs=[VM] * 4,
        out_specs=[VM] * 4,
        compiler_params=params(),
        name="joined_finish",
    )(a, got_a, b, got_b)


def input_back_kernel(x, part, other, gain, middle_grad, out):
    rows = x.shape[0]
    step = 64

    def norm_step(i, _):
        at = pl.ds(pl.multiple_of(i * step, step), step)
        hat, scale = normal(x[at, :].astype(F32))
        first = part[at, :].astype(F32) + other[at, :].astype(F32)
        back = norm_back(hat, scale, first * gain[...].astype(F32))
        out[at, :] = (back + middle_grad[at, :]).astype(BF16)
        return _

    lax.fori_loop(0, rows // step, norm_step, 0)


def input_back(x, part, other, gain, middle_grad):
    return pl.pallas_call(
        input_back_kernel,
        out_shape=shaped(x.shape, BF16),
        in_specs=[VM] * 5,
        out_specs=VM,
        compiler_params=params(),
        name="input_back",
    )(x, part, other, gain, middle_grad)


def swap(value):
    return lax.ppermute(value, "tensor", [(0, 1), (1, 0)])


def to_member(value, d):
    count = lax.axis_size("dp")
    return lax.ppermute(value, "dp", [(i, i ^ d) for i in range(count)])


def to_member_across(value, d):
    count = lax.axis_size("dp")
    pairs = [(i * 2 + t, (i ^ d) * 2 + (1 - t)) for i in range(count) for t in range(2)]
    return lax.ppermute(value, ("dp", "tensor"), pairs)


def to_group(value, by):
    count = lax.axis_size("dp")
    step = by * MEMBERS
    return lax.ppermute(value, "dp", [(i, (i + step) % count) for i in range(count)])


def within(parts):
    return [parts[0]] + [to_member(parts[d], d) for d in range(1, MEMBERS)]


def reduce_rows(value):
    return lax.psum_scatter(value, "dp", scatter_dimension=0, tiled=True)


def after(value, *others):
    return lax.optimization_barrier((value, *others))[0]


def halve(keep, send, bits):
    for bit in bits[:-1]:
        total = keep + to_member(send, 1 << bit).astype(F32)
        half = total.shape[0] // 2
        keep, send = total[:half], total[half:].astype(BF16)
    return keep, to_member(send, 1 << bits[-1])


def joined_sums(meta, x, part, first_low, joined_grad, sums):
    count = lax.axis_size("dp")
    width, across = x.shape[1], joined_grad.shape[1]
    if count == 16:
        keep_a, send_a, vectors = joined_first(meta, x, part, first_low, joined_grad)
        other = swap(vectors)
        keep_b, send_b = joined_second(meta, first_low, joined_grad, vectors, other, sums)
        last_a = halve(keep_a, send_a, ORDERS[0])
        last_b = halve(keep_b, send_b, ORDERS[1])
        return joined_finish(*last_a, *last_b)
    hat, _scale = normal(x.astype(F32))
    wide = part.astype(F32)
    vectors = jnp.stack([jnp.sum(wide * hat, axis=0), jnp.sum(wide, axis=0)], axis=1)
    vectors = jnp.concatenate([vectors + swap(vectors), sums[:1].T], axis=1)
    grad = jnp.einsum("td,tf->df", first_low, joined_grad, preferred_element_type=F32)
    high = vectors.astype(BF16)
    rest = (vectors - high.astype(F32)).astype(BF16)
    room = jnp.zeros((width, PAIR - 6), BF16)
    got = reduce_rows(jnp.concatenate([grad.astype(BF16), high, rest, room], axis=1)).astype(F32)
    small = got[:, across : across + 3] + got[:, across + 3 : across + 6]
    return got[:, :across], small[:, 0], small[:, 1], small[:, 2]


def shards(
    activations,
    cotangent,
    parent_slot,
    attention_gain,
    attention_shift,
    joined_weight,
    joined_bias,
    output_weight,
    output_bias,
    feed_gain,
    feed_shift,
    expand_weight,
    expand_bias,
    contract_weight,
    contract_bias,
):
    device = lax.axis_index("dp")
    count = lax.axis_size("dp")
    rank = lax.axis_index("tensor")
    member = lax.rem(device, MEMBERS)
    heads_here = joined_weight.shape[1] // (3 * HD)
    width = activations.shape[1]
    inner = expand_weight.shape[1]
    half = output_weight.shape[0]
    meta = jnp.stack(
        [member, device // MEMBERS, rank * heads_here + 2 * member, rank, device]
    ).astype(jnp.int32)
    slopes = jnp.exp2(-8.0 * jnp.arange(1, H + 1, dtype=F32) / H)

    def row(v):
        return v.reshape(1, -1)

    gain_a, shift_a = row(attention_gain), row(attention_shift)
    gain_f, shift_f = row(feed_gain), row(feed_shift)

    first_low, queries, pairs = project(
        meta, activations, gain_a, shift_a, joined_weight, row(joined_bias)
    )
    table = make_tables(meta, parent_slot)
    pairs = within(pairs)
    queries = within(queries)
    hidden_grad = jnp.einsum("td,fd->tf", cotangent, contract_weight, preferred_element_type=F32)
    table = after(table, hidden_grad)
    up, down = pack(table, pairs)
    below = to_group(up, 1)
    above = to_group(down, -1)
    other_output_weight = swap(after(output_weight, up))
    kept, stats = attend_near(table, meta, slopes, queries, pairs)
    outs, lse = attend_far(table, meta, slopes, queries, below, above, kept, stats)
    parts_other = [to_member_across(outs[d], d) for d in range(MEMBERS)]
    parts_own = within(outs)
    mixed, middle, second_low, hidden_low, pre_grad, second_part, bias_sums = feed(
        meta, activations, row(output_bias), gain_f, shift_f, row(expand_bias),
        parts_own, parts_other, output_weight, other_output_weight, expand_weight, hidden_grad,
    )
    second_other = swap(second_part)
    held = feed_grads(cotangent, hidden_low, second_low, pre_grad, 2 * inner + half + SEG)
    feed_part = jnp.dot(hidden_low, contract_weight, preferred_element_type=F32).astype(BF16)
    second_other = after(second_other, held, feed_part)
    middle_grad, branch_low, feed_vectors, grad_parts = middle_back(
        meta, middle, second_part, second_other, cotangent, gain_f, output_weight
    )
    grad_parts = within(grad_parts)
    feed_part = after(feed_part, branch_low)
    feed_other = swap(feed_part)
    extra = bias_sums[0].reshape(count, 2, width // count).transpose(1, 0, 2).reshape(2, width)
    held = output_grads(branch_low, mixed, feed_vectors, extra, held)
    grad_parts[1] = after(grad_parts[1], held)
    feed_sums = reduce_rows(held)

    to_below, to_above, kept_grad = back_far(
        table, meta, slopes, queries, below, above, outs, grad_parts, lse
    )
    from_above = to_group(to_below, -1)
    from_below = to_group(to_above, 1)
    kept_grad = after(kept_grad, feed_other)
    query_grads, own = back_near(
        table, meta, slopes, queries, pairs, outs, grad_parts, lse, kept_grad
    )
    query_grads = within(query_grads)
    layer_output = (
        middle + (feed_part.astype(F32) + feed_other.astype(F32)) + contract_bias.astype(F32)
    ).astype(BF16)
    from_above = after(from_above, layer_output)
    pair_grads = within(gather_back(table, own, from_above, from_below))
    joined_grad, first_part, joined_bias_sums = join_stage(
        meta, joined_weight, query_grads, pair_grads
    )
    first_other = swap(first_part)
    joined_done, gain_grad, shift_grad, joined_bias_grad = joined_sums(
        meta, activations, first_part, first_low, joined_grad, joined_bias_sums
    )
    input_gradient = input_back(activations, first_part, first_other, gain_a, middle_grad)
    (
        contract_done, expand_done, output_done,
        feed_gain_grad, feed_shift_grad, output_bias_grad, contract_bias_grad, expand_bias_grad,
    ) = feed_finish(feed_sums, inner, half)

    return (
        layer_output,
        input_gradient,
        gain_grad.reshape(-1),
        shift_grad.reshape(-1),
        joined_done,
        joined_bias_grad.reshape(-1, 1),
        output_done,
        output_bias_grad.reshape(-1),
        feed_gain_grad.reshape(-1),
        feed_shift_grad.reshape(-1),
        expand_done,
        expand_bias_grad.reshape(-1, 1),
        contract_done,
        contract_bias_grad.reshape(-1),
    )


def solution(mesh):
    in_specs = (
        P("dp", None),
        P("dp", None),
        P(),
        P(),
        P(),
        P(None, "tensor"),
        P("tensor"),
        P("tensor", None),
        P(),
        P(),
        P(),
        P(None, "tensor"),
        P("tensor"),
        P("tensor", None),
        P(),
    )
    out_specs = (
        P("dp", None),
        P("dp", None),
        P("dp"),
        P("dp"),
        P("dp", "tensor"),
        P("dp", "tensor"),
        P("dp", "tensor"),
        P("dp"),
        P("dp"),
        P("dp"),
        P("dp", "tensor"),
        P("dp", "tensor"),
        P("dp", "tensor"),
        P("dp"),
    )
    return jax.shard_map(shards, mesh=mesh, in_specs=in_specs, out_specs=out_specs, check_vma=False)
```

time: 529 us -> 424 us (0.80); the launches traced: 520 us -> 424 us
  waiting for transfers between devices: 237 us -> 110 us
  Pallas kernels: 127 us -> 211 us
  local copies, waits for them, and re-layouts: 55.3 us -> 20.4 us
  matrix products: 44.6 us -> 13 us
  starting transfers between devices: 34.6 us -> 51.3 us
    pallas_call x3 -> x11, Pallas kernels: 83.6 us -> 161 us  [the longest x1 31.8 us: back_near(): pl.pallas_call(back_near_kernel, out_shape=[shaped((rows, PAIR), BF16)] *...]
    ppermute x5, waiting for transfers between devices: 82.9 us -> 9.45 us  [swap(): return lax.ppermute(value, 'tensor', [(0, 1), (1, 0)])]
    ppermute x4, waiting for transfers between devices: 76.6 us -> 29.7 us  [to_group(): lax.ppermute(value, 'dp', [(i, (i + step) % count) for i in range(count)])]
    dot_general x6 -> x0, matrix products: 30.4 us -> none  [the longest x1 9.51 us: shards(): jnp.einsum('td,tf->df', cotangent, hidden_low, preferred_element_type=F32)]
    unnamed x152 -> x94, local copies, waits for them, and re-layouts: 37 us -> 9.16 us
    reduce_scatter x3 -> x1, waiting for transfers between devices: 27.7 us -> 0.01 us  [reduce_rows(): return lax.psum_scatter(value, 'dp', scatter_dimension=0, tiled=True)]
    ppermute x18 -> x26, waiting for transfers between devices: 42.8 us -> 67 us  [to_member(): return lax.ppermute(value, 'dp', [(i, i ^ d) for i in range(count)])]
    ppermute x4, starting transfers between devices: 8.43 us -> 17.7 us  [to_group(): lax.ppermute(value, 'dp', [(i, (i + step) % count) for i in range(count)])]
  transfers between devices with their start and end apart: 35 -> 40, of which waited for: 20 -> 19; matrix products, arithmetic and copies ran while one was open for 12% -> 5% of each run, Pallas kernels for 20% -> 38%
where the time goes in v2:
time: 424 us
  Pallas kernels  211 us (50%)
  waiting for transfers between devices  110 us (26%)
  starting transfers between devices  51.3 us (12%)
  local copies, waits for them, and re-layouts  20.4 us (5%)
  between operations  14.6 us (3%)
  matrix products  13 us (3%)
  other arithmetic  4.29 us (1%)
    ppermute x26, waiting for transfers between devices, to_member(): return lax.ppermute(value, 'dp', [(i, i ^ d) for i in range(count)])  67 us
    pallas_call x1, Pallas kernels, back_near(): pl.pallas_call(back_near_kernel, out_shape=[shaped((rows, PAIR), BF16)] *...  31.8 us
    ppermute x4, waiting for transfers between devices, to_group(): lax.ppermute(value, 'dp', [(i, (i + step) % count) for i in range(count)])  29.7 us
    pallas_call x1, Pallas kernels, back_far(): pl.pallas_call(back_far_kernel, out_shape=[side, side, shaped((TREE, PAIR...  23.7 us
    pallas_call x1, Pallas kernels, feed(): pl.pallas_call(feed_kernel, out_shape=[shaped((rows, half), BF16), shaped...  21.4 us
    pallas_call x1, Pallas kernels, attend_near(): pl.pallas_call(attend_near_kernel, out_shape=[shaped((TREE, PAIR, SEG), F...  20 us
    pallas_call x1, Pallas kernels, attend_far(): pl.pallas_call(attend_far_kernel, out_shape=[shaped((rows, PAIR), BF16)]...  18.7 us
    ppermute x26, starting transfers between devices, to_member(): return lax.ppermute(value, 'dp', [(i, i ^ d) for i in range(count)])  18.6 us
  transfers between devices with their start and end apart: 40, of which 19 were waited for; matrix products, arithmetic and copies ran while one was open for 5% of the time, Pallas kernels for 38%

profile of v2, /device:TPU:0, one launch (start us, length us, event | category | flops | bytes accessed | tf_op | source)
XLA Modules:
  0.0 424.1 jit_solution(3652200103699322468)
XLA Ops:
  11.7 10.2 %project.1 = (bf16[640,1024]{1,0:T(8,128)(2,1)}, bf16[640,128]{1,0:T(8,128)(2,1)}, bf16[640,128]{1,0:T(8,128)(2,1)}, bf16[640,128]{1,0:T(8,128)(2,1)}, bf16[640,...) custom-call(s32[5]{0:T(128)} %stack.23.meta, ...), custom_call_target="tpu_custom_call" | custom-call | tf_op jit(solution)/shard_map/project/pallas_call | solution.py:250
  25.0 6.9 %fusion.hidden_grad = f32[640,2048]{1,0:T(8,128)} fusion(bf16[640,1024]{1,0:T(8,128)(2,1)S(1)} %copy-done.6, bf16[2048,1024]{1,0:T(8,128)(2,1)} %param.28), kind=kOutput, calls=%fused_computation.17 | convolution fusion | flops 2684354560 | bytes 10747904 | tf_op jit(solution)/shard_map/td,fd->tf/dot_general | solution.py:1373
  31.8 7.8 %tables.1.table = s32[896]{0:T(1024)} custom-call(s32[5]{0:T(128)} %stack.23.meta, s32[80]{0:T(128)} %parent.1), custom_call_target="tpu_custom_call" | custom-call | tf_op jit(solution)/shard_map/tables/pallas_call | solution.py:192
  60.6 20.0 %attend_near.1 = (f32[20,128,128]{2,1,0:T(8,128)}, f32[20,8,256]{2,1,0:T(8,128)}) custom-call(s32[896]{0:T(1024)} %tables.1.table, s32[5]{0:T(128)} %stack.23.meta, f32[16]{0:T(128)} %multiply_exponential_fusion.slopes, bf16[640,128]{1,0:T(8,128)(2,1)} %get-tuple-element.86.q0, bf16[640,128]{1,0:T(8,128)(2,1)} %copy-done.9, bf16[640,128]{1,0:T(8,128)(2,1)} %copy-done.10, ...), custom_call_target="tpu_custom_call" | custom-call | tf_op jit(solution)/shard_map/attend_near/pallas_call | solution.py:435
  82.6 18.7 %attend_far.1 = (bf16[640,128]{1,0:T(8,128)(2,1)}, bf16[640,128]{1,0:T(8,128)(2,1)}, bf16[640,128]{1,0:T(8,128)(2,1)}, bf16[640,128]{1,0:T(8,128)(2,1)}, f32[20,1,256]{2,1,0:T(1,128)}) custom-call(s32[896]{0:T(1024)} %tables.1.table, s32[5]{0:T(128)} %stack.23.meta, f32[16]{0:T(128)} %multiply_exponential_fusion.slopes, ...), custom_call_target="tpu_custom_call" | custom-call | tf_op jit(solution)/shard_map/attend_far/pallas_call | solution.py:510
  121.3 21.4 %feed.1 = (bf16[640,512]{1,0:T(8,128)(2,1)}, f32[640,1024]{1,0:T(8,128)}, bf16[640,1024]{1,0:T(8,128)(2,1)}, bf16[640,2048]{1,0:T(8,128)(2,1)}, bf16[640,2048]{1...) custom-call(s32[5]{0:T(128)} %stack.23.meta, bf16[640,1024]{1,0:T(8,128)(2,1)} %x.7, ...), custom_call_target="tpu_custom_call" | custom-call | tf_op jit(solution)/shard_map/feed/pallas_call | solution.py:846
  145.9 18.4 %feed_grads.1.held = bf16[1024,4736]{1,0:T(8,128)(2,1)} custom-call(bf16[640,1024]{1,0:T(8,128)(2,1)} %grad.3, bf16[640,2048]{1,0:T(8,128)(2,1)} %get-tuple-element.104.act, bf16[640,1024]{1,0:T(8,128)(2,1)} %get-tuple-element.106.normed, bf16[640,2048]{1,0:T(8,128)(2,1)} %get-tuple-element.107.pre_grad), custom_call_target="tpu_custom_call" | custom-call | tf_op jit(solution)/shard_map/feed_grads/pallas_call | solution.py:911
  164.3 6.1 %convolution_convert_fusion = bf16[640,1024]{1,0:T(8,128)(2,1)} fusion(bf16[640,2048]{1,0:T(8,128)(2,1)S(1)} %copy-done.12, bf16[2048,1024]{1,0:T(8,128)(2,1)} %param.28), kind=kOutput, calls=%fused_computation.2 | convolution fusion | flops 2685009920 | bytes 8126464 | tf_op jit(solution)/shard_map/dot_general | solution.py:1389
  174.4 8.9 %middle_back.1 = (f32[640,1024]{1,0:T(8,128)}, bf16[640,1024]{1,0:T(8,128)(2,1)}, f32[8,1024]{1,0:T(8,128)}, bf16[640,128]{1,0:T(8,128)(2,1)}, bf16[640,128]{1,0...) custom-call(s32[5]{0:T(128)} %stack.23.meta, f32[640,1024]{1,0:T(8,128)} %get-tuple-element.103.middle, ...), custom_call_target="tpu_custom_call" | custom-call | tf_op jit(solution)/shard_map/middle_back/pallas_call | solution.py:1041
  183.3 4.9 %output_grads.1 = bf16[1024,4736]{1,0:T(8,128)(2,1)} custom-call(bf16[640,1024]{1,0:T(8,128)(2,1)} %get-tuple-element.109.branch, bf16[640,512]{1,0:T(8,128)(2,1)} %get-tuple-element.113.mixed, f32[8,1024]{1,0:T(8,128)} %get-tuple-element.114.vectors, f32[2,1024]{1,0:T(2,128)} %reshape.84.extra, ...), custom_call_target="tpu_custom_call", output_to_operand_aliasing={{}: (4, {})} | custom-call | tf_op jit(solution)/shard_map/output_grads/pallas_call | solution.py:960
  192.9 5.2 %collective-permute-done.19.g2 = bf16[640,128]{1,0:T(8,128)(2,1)S(1)} collective-permute-done((bf16[640,128]{1,0:T(8,128)(2,1)S(1)}, bf16[640,128]{1,0:T(8,128)(2,1)S(1)}, u32[]{:S(2)}, u32[]{:S(2)}) %collective-permute-start.19) | collective-permute-done | bytes 163872 | tf_op jit(solution)/shard_map/ppermute | solution.py:1273
  201.4 23.7 %back_far.1 = (bf16[1536,256]{1,0:T(8,128)(2,1)}, bf16[1536,256]{1,0:T(8,128)(2,1)}, f32[20,128,128]{2,1,0:T(8,128)}) custom-call(s32[896]{0:T(1024)} %tables.1.table, s32[5]{0:T(128)} %stack.23.meta, f32[16]{0:T(128)} %multiply_exponential_fusion.slopes, bf16[640,128]{1,0:T(8,128)(2,1)} %get-tuple-element.86.q0, bf16[640,128]{1,0:T(8,128)(2,1)} %copy-done.9, ...), custom_call_target="tpu_custom_call" | custom-call | tf_op jit(solution)/shard_map/back_far/pallas_call | solution.py:622
  225.1 13.7 %collective-permute-start.24 = (bf16[1536,256]{1,0:T(8,128)(2,1)}, bf16[1536,256]{1,0:T(8,128)(2,1)}, u32[]{:S(2)}, u32[]{:S(2)}) collective-permute-start(bf16[1536,256]{1,0:T(8,128)(2,1)} %get-tuple-element.127), channel_id=1, source_target_pairs={{0,24},{2,26},{4,28},{6,30},{8,0},{10,2},{12,4},{14,6},{16,8},{18,... | collective-permute-start | bytes 2359304 | tf_op jit(solution)/shard_map/ppermute | solution.py:1285
  238.9 31.8 %back_near.1 = (bf16[640,128]{1,0:T(8,128)(2,1)}, bf16[640,128]{1,0:T(8,128)(2,1)}, bf16[640,128]{1,0:T(8,128)(2,1)}, bf16[640,128]{1,0:T(8,128)(2,1)}, f32[2560,256]{1,0:T(8,128)}) custom-call(s32[896]{0:T(1024)} %tables.1.table, s32[5]{0:T(128)} %stack.23.meta, f32[16]{0:T(128)} %multiply_exponential_fusion.slopes, bf16[640,128]{1,0:T(8,128)(2,1)} %get-tuple-element.86.q0, ...), custom_call_target="tpu_custom_call" | custom-call | tf_op jit(solution)/shard_map/back_near/pallas_call | solution.py:688
  274.2 17.5 %collective-permute-done.24.from_above = bf16[1536,256]{1,0:T(8,128)(2,1)} collective-permute-done((bf16[1536,256]{1,0:T(8,128)(2,1)}, bf16[1536,256]{1,0:T(8,128)(2,1)}, u32[]{:S(2)}, u32[]{:S(2)}) %collective-permute-start.24) | collective-permute-done | bytes 786464 | tf_op jit(solution)/shard_map/ppermute | solution.py:1285
  291.7 10.3 %collective-permute-done.25.from_below = bf16[1536,256]{1,0:T(8,128)(2,1)} collective-permute-done((bf16[1536,256]{1,0:T(8,128)(2,1)}, bf16[1536,256]{1,0:T(8,128)(2,1)}, u32[]{:S(2)}, u32[]{:S(2)}) %collective-permute-start.25) | collective-permute-done | bytes 786464 | tf_op jit(solution)/shard_map/ppermute | solution.py:1285
  302.0 4.9 %gather_back.1 = (bf16[640,256]{1,0:T(8,128)(2,1)}, bf16[640,256]{1,0:T(8,128)(2,1)}, bf16[640,256]{1,0:T(8,128)(2,1)}, bf16[640,256]{1,0:T(8,128)(2,1)}) custom-call(s32[896]{0:T(1024)} %tables.1.table, f32[2560,256]{1,0:T(8,128)} %get-tuple-element.126.own, bf16[1536,256]{1,0:T(8,128)(2,1)} %collective-permute-done.24.from_above, ...), custom_call_target="tpu_custom_call" | custom-call | tf_op jit(solution)/shard_map/gather_back/pallas_call | solution.py:738
  310.7 24.2 %collective-permute-done.22.q2 = bf16[640,128]{1,0:T(8,128)(2,1)S(1)} collective-permute-done((bf16[640,128]{1,0:T(8,128)(2,1)S(1)}, bf16[640,128]{1,0:T(8,128)(2,1)S(1)}, u32[]{:S(2)}, u32[]{:S(2)}) %collective-permute-start.22) | collective-permute-done | bytes 163872 | tf_op jit(solution)/shard_map/ppermute | solution.py:1273
  338.4 7.3 %join_stage.1 = (bf16[640,1536]{1,0:T(8,128)(2,1)}, bf16[640,1024]{1,0:T(8,128)(2,1)}, f32[8,1024]{1,0:T(8,128)}) custom-call(s32[5]{0:T(128)} %stack.23.meta, bf16[1024,1536]{1,0:T(8,128)(2,1)} %weight.5, bf16[640,128]{1,0:T(8,128)(2,1)} %get-tuple-element.122.q0, bf16[640,128]{1,0:T(8,128)(2,1)} %copy-done.24, bf16[640,128]{1,0:T(8,128)(2,1)} %copy-done.25, ...), custom_call_target="tpu_custom_call" | custom-call | tf_op jit(solution)/shard_map/join_stage/pallas_call | solution.py:1089
  345.7 12.1 %joined_first.1 = (f32[512,1024]{1,0:T(8,128)}, bf16[512,1024]{1,0:T(8,128)(2,1)}, f32[8,1024]{1,0:T(8,128)}) custom-call(s32[5]{0:T(128)} %stack.23.meta, bf16[640,1024]{1,0:T(8,128)(2,1)} %x.7, bf16[640,1024]{1,0:T(8,128)(2,1)} %get-tuple-element.134.part, bf16[640,1024]{1,0:T(8,128)(2,1)} %get-tuple-element.136.normed, ...), custom_call_target="tpu_custom_call" | custom-call | tf_op jit(solution)/shard_map/joined_first/pallas_call | solution.py:1159
  363.3 5.7 %joined_second.1 = (f32[512,640]{1,0:T(8,128)}, bf16[512,640]{1,0:T(8,128)(2,1)}) custom-call(s32[5]{0:T(128)} %stack.23.meta, bf16[640,1024]{1,0:T(8,128)(2,1)} %get-tuple-element.136.normed, bf16[640,1536]{1,0:T(8,128)(2,1)} %get-tuple-element.137.joined, f32[8,1024]{1,0:T(8,128)} %get-tuple-element.140.vectors, f32[8,1024]{1,0:T(8,128)} %copy-done.36, ...), custom_call_target="tpu_custom_call" | custom-call | tf_op jit(solution)/shard_map/joined_second/pallas_call | solution.py:1205
  372.5 11.2 %collective-permute-done.31 = bf16[256,1024]{1,0:T(8,128)(2,1)S(1)} collective-permute-done((bf16[256,1024]{1,0:T(8,128)(2,1)S(1)}, bf16[256,1024]{1,0:T(8,128)(2,1)S(1)}, u32[]{:S(2)}, u32[]{:S(2)}) %collective-permute-start.31) | collective-permute-done | bytes 524320 | tf_op jit(solution)/shard_map/ppermute | solution.py:1273
  385.1 10.4 %collective-permute-done.32 = bf16[128,1024]{1,0:T(8,128)(2,1)S(1)} collective-permute-done((bf16[128,1024]{1,0:T(8,128)(2,1)S(1)}, bf16[128,1024]{1,0:T(8,128)(2,1)S(1)}, u32[]{:S(2)}, u32[]{:S(2)}) %collective-permute-start.32) | collective-permute-done | bytes 262176 | tf_op jit(solution)/shard_map/ppermute | solution.py:1273
  402.8 7.2 %input_back.1 = bf16[640,1024]{1,0:T(8,128)(2,1)} custom-call(bf16[640,1024]{1,0:T(8,128)(2,1)} %x.7, bf16[640,1024]{1,0:T(8,128)(2,1)} %get-tuple-element.134.part, bf16[640,1024]{1,0:T(8,128)(2,1)} %copy-done.14, bf16[1,1024]{1,0:T(2,128)(2,1)} %reshape.81.gain, f32[640,1024]{1,0:T(8,128)} %get-tuple-element.135.middle_grad), custom_call_target="tpu_custom_call" | custom-call | tf_op jit(solution)/shard_map/input_back/pallas_call | solution.py:1257
  (201 shorter events, 101.0 us)
Async XLA Ops:
  7.2 406.8 %reduce-scatter.2.cloned.1.call-start = ((), (), s32[]{:S(2)}) async-start(), calls=%async_computation.1 | async-start | bytes 10305536 | tf_op jit(solution)/shard_map/reduce_scatter | solution.py:1293
  21.9 17.8 %collective-permute-start.3 = (bf16[640,256]{1,0:T(8,128)(2,1)}, bf16[640,256]{1,0:T(8,128)(2,1)S(1)}, u32[]{:S(2)}, u32[]{:S(2)}) collective-permute-start(bf16[640,256]{1,0:T(8,128)(2,1)} %get-tuple-element.91), channel_id=1, source_target_pairs={{0,2},{2,0},{4,6},{6,4},{8,10},{10,8},{12,14},{14,12},{16,18},{18,... | collective-permute-start | bytes 983048 | tf_op jit(solution)/shard_map/ppermute | solution.py:1273
  22.3 17.3 %collective-permute-start.4 = (bf16[640,256]{1,0:T(8,128)(2,1)}, bf16[640,256]{1,0:T(8,128)(2,1)S(1)}, u32[]{:S(2)}, u32[]{:S(2)}) collective-permute-start(bf16[640,256]{1,0:T(8,128)(2,1)} %get-tuple-element.92), channel_id=1, source_target_pairs={{0,4},{2,6},{4,0},{6,2},{8,12},{10,14},{12,8},{14,10},{16,20},{18,... | collective-permute-start | bytes 983048 | tf_op jit(solution)/shard_map/ppermute | solution.py:1273
  24.8 15.4 %collective-permute-start.5 = (bf16[640,256]{1,0:T(8,128)(2,1)}, bf16[640,256]{1,0:T(8,128)(2,1)S(1)}, u32[]{:S(2)}, u32[]{:S(2)}) collective-permute-start(bf16[640,256]{1,0:T(8,128)(2,1)} %get-tuple-element.93), channel_id=1, source_target_pairs={{0,6},{2,4},{4,2},{6,0},{8,14},{10,12},{12,10},{14,8},{16,22},{18,... | collective-permute-start | bytes 983048 | tf_op jit(solution)/shard_map/ppermute | solution.py:1273
  44.5 36.1 %collective-permute-start.6 = (bf16[1536,256]{1,0:T(8,128)(2,1)S(1)}, bf16[1536,256]{1,0:T(8,128)(2,1)S(1)}, u32[]{:S(2)}, u32[]{:S(2)}) collective-permute-start(bf16[1536,256]{1,0:T(8,128)(2,1)S(1)} %get-tuple-element.94), channel_id=1, source_target_pairs={{0,8},{2,10},{4,12},{6,14},{8,16},{10,18},{12,20},{14,22},{16,24},... | collective-permute-start | bytes 2359304 | tf_op jit(solution)/shard_map/ppermute | solution.py:1285
  46.2 36.4 %collective-permute-start.7 = (bf16[1536,256]{1,0:T(8,128)(2,1)S(1)}, bf16[1536,256]{1,0:T(8,128)(2,1)}, u32[]{:S(2)}, u32[]{:S(2)}) collective-permute-start(bf16[1536,256]{1,0:T(8,128)(2,1)S(1)} %get-tuple-element.95), channel_id=1, source_target_pairs={{0,24},{2,26},{4,28},{6,30},{8,0},{10,2},{12,4},{14,6},{16,8},{18,... | collective-permute-start | bytes 2359304 | tf_op jit(solution)/shard_map/ppermute | solution.py:1285
  48.5 72.0 %collective-permute-start.15 = (bf16[512,1024]{1,0:T(8,128)(2,1)}, bf16[512,1024]{1,0:T(8,128)(2,1)}, u32[]{:S(2)}, u32[]{:S(2)}) collective-permute-start(bf16[512,1024]{1,0:T(8,128)(2,1)} %weight.4), channel_id=1, source_target_pairs={{0,1},{1,0},{2,3},{3,2},{4,5},{5,4},{6,7},{7,6},{8,9},{9,8},{10,11... | collective-permute-start | bytes 3145736 | tf_op jit(solution)/shard_map/ppermute | solution.py:1268
  103.2 17.2 %collective-permute-start.12 = (bf16[640,128]{1,0:T(8,128)(2,1)}, bf16[640,128]{1,0:T(8,128)(2,1)S(1)}, u32[]{:S(2)}, u32[]{:S(2)}) collective-permute-start(bf16[640,128]{1,0:T(8,128)(2,1)} %get-tuple-element.99.o1), channel_id=1, source_target_pairs={{0,3},{1,2},{2,1},{3,0},{4,7},{5,6},{6,5},{7,4},{8,11},{9,10},{10,... | collective-permute-start | bytes 491528 | tf_op jit(solution)/shard_map/ppermute | solution.py:1279
  104.7 15.8 %collective-permute-start.11 = (bf16[640,128]{1,0:T(8,128)(2,1)}, bf16[640,128]{1,0:T(8,128)(2,1)S(1)}, u32[]{:S(2)}, u32[]{:S(2)}) collective-permute-start(bf16[640,128]{1,0:T(8,128)(2,1)} %get-tuple-element.98.a0.o0), channel_id=1, source_target_pairs={{0,1},{1,0},{2,3},{3,2},{4,5},{5,4},{6,7},{7,6},{8,9},{9,8},{10,11... | collective-permute-start | bytes 491528 | tf_op jit(solution)/shard_map/ppermute | solution.py:1279
  108.6 11.8 %collective-permute-start.13 = (bf16[640,128]{1,0:T(8,128)(2,1)}, bf16[640,128]{1,0:T(8,128)(2,1)S(1)}, u32[]{:S(2)}, u32[]{:S(2)}) collective-permute-start(bf16[640,128]{1,0:T(8,128)(2,1)} %get-tuple-element.100.o2), channel_id=1, source_target_pairs={{0,5},{1,4},{2,7},{3,6},{4,1},{5,0},{6,3},{7,2},{8,13},{9,12},{10,... | collective-permute-start | bytes 491528 | tf_op jit(solution)/shard_map/ppermute | solution.py:1279
  142.7 30.6 %collective-permute-start.16 = (bf16[640,1024]{1,0:T(8,128)(2,1)}, bf16[640,1024]{1,0:T(8,128)(2,1)S(1)}, u32[]{:S(2)}, u32[]{:S(2)}) collective-permute-start(bf16[640,1024]{1,0:T(8,128)(2,1)} %get-tuple-element.105.part), channel_id=1, source_target_pairs={{0,1},{1,0},{2,3},{3,2},{4,5},{5,4},{6,7},{7,6},{8,9},{9,8},{10,11... | collective-permute-start | bytes 3932168 | tf_op jit(solution)/shard_map/ppermute | solution.py:1268
  189.5 49.3 %collective-permute-start.17 = (bf16[640,1024]{1,0:T(8,128)(2,1)S(1)}, bf16[640,1024]{1,0:T(8,128)(2,1)}, u32[]{:S(2)}, u32[]{:S(2)}) collective-permute-start(bf16[640,1024]{1,0:T(8,128)(2,1)S(1)} %copy-done.17), channel_id=1, source_target_pairs={{0,1},{1,0},{2,3},{3,2},{4,5},{5,4},{6,7},{7,6},{8,9},{9,8},{10,11... | collective-permute-start | bytes 3932168 | tf_op jit(solution)/shard_map/ppermute | solution.py:1268
  225.1 66.5 %collective-permute-start.24 = (bf16[1536,256]{1,0:T(8,128)(2,1)}, bf16[1536,256]{1,0:T(8,128)(2,1)}, u32[]{:S(2)}, u32[]{:S(2)}) collective-permute-start(bf16[1536,256]{1,0:T(8,128)(2,1)} %get-tuple-element.127), channel_id=1, source_target_pairs={{0,24},{2,26},{4,28},{6,30},{8,0},{10,2},{12,4},{14,6},{16,8},{18,... | collective-permute-start | bytes 2359304 | tf_op jit(solution)/shard_map/ppermute | solution.py:1285
  238.8 63.2 %collective-permute-start.25 = (bf16[1536,256]{1,0:T(8,128)(2,1)}, bf16[1536,256]{1,0:T(8,128)(2,1)}, u32[]{:S(2)}, u32[]{:S(2)}) collective-permute-start(bf16[1536,256]{1,0:T(8,128)(2,1)} %get-tuple-element.129), channel_id=1, source_target_pairs={{0,8},{2,10},{4,12},{6,14},{8,16},{10,18},{12,20},{14,22},{16,24},... | collective-permute-start | bytes 2359304 | tf_op jit(solution)/shard_map/ppermute | solution.py:1285
  270.7 39.7 %collective-permute-start.21 = (bf16[640,128]{1,0:T(8,128)(2,1)}, bf16[640,128]{1,0:T(8,128)(2,1)S(1)}, u32[]{:S(2)}, u32[]{:S(2)}) collective-permute-start(bf16[640,128]{1,0:T(8,128)(2,1)} %get-tuple-element.123), channel_id=1, source_target_pairs={{0,2},{2,0},{4,6},{6,4},{8,10},{10,8},{12,14},{14,12},{16,18},{18,... | collective-permute-start | bytes 491528 | tf_op jit(solution)/shard_map/ppermute | solution.py:1273
  306.9 30.5 %collective-permute-start.26 = (bf16[640,256]{1,0:T(8,128)(2,1)}, bf16[640,256]{1,0:T(8,128)(2,1)S(1)}, u32[]{:S(2)}, u32[]{:S(2)}) collective-permute-start(bf16[640,256]{1,0:T(8,128)(2,1)} %get-tuple-element.131), channel_id=1, source_target_pairs={{0,2},{2,0},{4,6},{6,4},{8,10},{10,8},{12,14},{14,12},{16,18},{18,... | collective-permute-start | bytes 983048 | tf_op jit(solution)/shard_map/ppermute | solution.py:1273
  307.1 30.3 %collective-permute-start.27 = (bf16[640,256]{1,0:T(8,128)(2,1)}, bf16[640,256]{1,0:T(8,128)(2,1)S(1)}, u32[]{:S(2)}, u32[]{:S(2)}) collective-permute-start(bf16[640,256]{1,0:T(8,128)(2,1)} %get-tuple-element.132), channel_id=1, source_target_pairs={{0,4},{2,6},{4,0},{6,2},{8,12},{10,14},{12,8},{14,10},{16,20},{18,... | collective-permute-start | bytes 983048 | tf_op jit(solution)/shard_map/ppermute | solution.py:1273
  308.6 28.9 %collective-permute-start.28 = (bf16[640,256]{1,0:T(8,128)(2,1)}, bf16[640,256]{1,0:T(8,128)(2,1)S(1)}, u32[]{:S(2)}, u32[]{:S(2)}) collective-permute-start(bf16[640,256]{1,0:T(8,128)(2,1)} %get-tuple-element.133), channel_id=1, source_target_pairs={{0,6},{2,4},{4,2},{6,0},{8,14},{10,12},{12,10},{14,8},{16,22},{18,... | collective-permute-start | bytes 983048 | tf_op jit(solution)/shard_map/ppermute | solution.py:1273
  308.9 26.0 %collective-permute-start.22 = (bf16[640,128]{1,0:T(8,128)(2,1)S(1)}, bf16[640,128]{1,0:T(8,128)(2,1)S(1)}, u32[]{:S(2)}, u32[]{:S(2)}) collective-permute-start(bf16[640,128]{1,0:T(8,128)(2,1)S(1)} %copy-done.43), channel_id=1, source_target_pairs={{0,4},{2,6},{4,0},{6,2},{8,12},{10,14},{12,8},{14,10},{16,20},{18,... | collective-permute-start | bytes 491528 | tf_op jit(solution)/shard_map/ppermute | solution.py:1273
  310.4 27.0 %collective-permute-start.23 = (bf16[640,128]{1,0:T(8,128)(2,1)S(1)}, bf16[640,128]{1,0:T(8,128)(2,1)S(1)}, u32[]{:S(2)}, u32[]{:S(2)}) collective-permute-start(bf16[640,128]{1,0:T(8,128)(2,1)S(1)} %copy-done.42), channel_id=1, source_target_pairs={{0,6},{2,4},{4,2},{6,0},{8,14},{10,12},{12,10},{14,8},{16,22},{18,... | collective-permute-start | bytes 491528 | tf_op jit(solution)/shard_map/ppermute | solution.py:1273
  369.4 14.4 %collective-permute-start.31 = (bf16[256,1024]{1,0:T(8,128)(2,1)S(1)}, bf16[256,1024]{1,0:T(8,128)(2,1)S(1)}, u32[]{:S(2)}, u32[]{:S(2)}) collective-permute-start(bf16[256,1024]{1,0:T(8,128)(2,1)S(1)} %slice.81), channel_id=1, source_target_pairs={{0,4},{2,6},{4,0},{6,2},{8,12},{10,14},{12,8},{14,10},{16,20},{18,... | collective-permute-start | bytes 1572872 | tf_op jit(solution)/shard_map/ppermute | solution.py:1273
  370.9 30.9 %collective-permute-start.29 = (bf16[640,1024]{1,0:T(8,128)(2,1)S(1)}, bf16[640,1024]{1,0:T(8,128)(2,1)S(1)}, u32[]{:S(2)}, u32[]{:S(2)}) collective-permute-start(bf16[640,1024]{1,0:T(8,128)(2,1)S(1)} %copy-done.7), channel_id=1, source_target_pairs={{0,1},{1,0},{2,3},{3,2},{4,5},{5,4},{6,7},{7,6},{8,9},{9,8},{10,11... | collective-permute-start | bytes 3932168 | tf_op jit(solution)/shard_map/ppermute | solution.py:1268
  395.5 15.2 %collective-permute-start.33 = (bf16[64,1024]{1,0:T(8,128)(2,1)S(1)}, bf16[64,1024]{1,0:T(8,128)(2,1)S(1)}, u32[]{:S(2)}, u32[]{:S(2)}) collective-permute-start(bf16[64,1024]{1,0:T(8,128)(2,1)S(1)} %slice.85), channel_id=1, source_target_pairs={{0,16},{2,18},{4,20},{6,22},{8,24},{10,26},{12,28},{14,30},{16,0},... | collective-permute-start | bytes 393224 | tf_op jit(solution)/shard_map/ppermute | solution.py:1273
  395.7 15.1 %collective-permute-start.38 = (bf16[64,640]{1,0:T(8,128)(2,1)S(1)}, bf16[64,640]{1,0:T(8,128)(2,1)S(1)}, u32[]{:S(2)}, u32[]{:S(2)}) collective-permute-start(bf16[64,640]{1,0:T(8,128)(2,1)S(1)} %slice.86), channel_id=1, source_target_pairs={{0,4},{2,6},{4,0},{6,2},{8,12},{10,14},{12,8},{14,10},{16,20},{18,... | collective-permute-start | bytes 245768 | tf_op jit(solution)/shard_map/ppermute | solution.py:1273
  (63 other events, 588.3 us)
Sparse Core Ops, SparseCore 0:
  188.4 152.5 reduce-scatter.1

commit v3 on v2

--- a/solution.py
+++ b/solution.py
@@ -31,7 +31,11 @@
 COUNT_AT = (4 * LISTS, 4 * LISTS + TREE)
 UP_AT = 4 * LISTS + 2 * TREE
 DOWN_AT = UP_AT + INNER
-TABLE = 896
+ORDER_AT = (DOWN_AT + INNER, DOWN_AT + INNER + TREE)
+TABLE = 1024
+GROUP = 4
+
+GAIN_A, SHIFT_A, GAIN_F, SHIFT_F, OUT_BIAS, CONTRACT_BIAS, JOINED_BIAS, UP_BIAS = range(8)
 
 VM = pl.BlockSpec(memory_space=pltpu.VMEM)
 SM = pl.BlockSpec(memory_space=pltpu.SMEM)
@@ -46,6 +50,28 @@
     return pltpu.CompilerParams(vmem_limit_bytes=mib * 2**20)
 
 
+LASTS = {
+    "project": 9, "tables": 9, "pack": 4, "attend_near": 14, "hidden_grad": 5, "attend_far": 15,
+    "feed": 18, "feed_grads": 20, "middle_back": 8, "output_grads": 9, "back_far": 14,
+    "back_near": 15, "second_step": 5, "gather_back": 5, "third_step": 3, "join_stage": 7,
+    "joined_first": 9, "joined_second": 6, "fourth_step": 3, "fifth_step": 4,
+    "sixth_step": 2, "seventh_step": 2, "add": 1,
+    "input_back": 6, "finish": 2, "feed_part": 4, "after_all": 0,
+}
+FLOPS_PER_US = 500_000_000
+
+
+def lasting(name):
+    return pl.CostEstimate(flops=LASTS[name] * FLOPS_PER_US, bytes_accessed=0, transcendentals=0)
+
+
+def skipping(kernel, used, skipped):
+    def run(*refs):
+        kernel(*refs[:used], *refs[used + skipped :])
+
+    return run
+
+
 def dot(a, b, dims=((1,), (0,))):
     return lax.dot_general(a, b, (dims, ((), ())), preferred_element_type=F32)
 
@@ -58,7 +84,7 @@
     return lax.broadcasted_iota(jnp.int32, shape, len(shape) - 2)
 
 
-def table_kernel(count, meta, parent, out, inner, place):
+def table_kernel(count, meta, parent, out, inner, place, starts):
     member, group = meta[0], meta[1]
     groups = count // TREE
     below = lax.rem(group + groups - 1, groups)
@@ -186,6 +212,32 @@
 
     lax.fori_loop(0, TREE, chain, 0)
 
+    for side in range(2):
+        for i in range(ANC + 1):
+            starts[i] = 0
+
+        def tally(q, _):
+            starts[out[COUNT_AT[side] + q]] += 1
+            return _
+
+        lax.fori_loop(0, TREE, tally, 0)
+
+        def running(i, n):
+            number = starts[ANC - i]
+            starts[ANC - i] = n
+            return n + number
+
+        lax.fori_loop(0, ANC + 1, running, 0)
+
+        def put(q, _):
+            number = out[COUNT_AT[side] + q]
+            at = starts[number]
+            out[ORDER_AT[side] + at] = q
+            starts[number] = at + 1
+            return _
+
+        lax.fori_loop(0, TREE, put, 0)
+
 
 def make_tables(meta, parent):
     count = parent.shape[0]
@@ -194,7 +246,7 @@
         out_shape=shaped((TABLE,), jnp.int32),
         in_specs=[SM, SM],
         out_specs=SM,
-        scratch_shapes=[pltpu.SMEM((count,), jnp.int32), pltpu.SMEM((count,), jnp.int32)],
+        scratch_shapes=[pltpu.SMEM((size,), jnp.int32) for size in (count, count, 16)],
         name="tables",
     )(meta, parent)
 
@@ -206,24 +258,34 @@
     return centered * scale, scale
 
 
-def project_kernel(meta, x, gain, shift, weight, bias, normed, *outs):
+NORM_ROWS = 128
+
+
+def norm_loop(rows, body):
+    def step(i, _):
+        body(pl.ds(pl.multiple_of(i * NORM_ROWS, NORM_ROWS), NORM_ROWS))
+        return _
+
+    lax.fori_loop(0, rows // NORM_ROWS, step, 0)
+
+
+def project_kernel(meta, x, vectors, weight, normed, *outs):
     member = meta[0]
     rows = x.shape[0]
-    step = 64
-
-    def norm_step(i, _):
-        at = pl.ds(pl.multiple_of(i * step, step), step)
+
+    def norm_step(at):
         hat, _scale = normal(x[at, :].astype(F32))
-        normed[at, :] = (hat * gain[...].astype(F32) + shift[...].astype(F32)).astype(BF16)
-        return _
-
-    lax.fori_loop(0, rows // step, norm_step, 0)
+        normed[at, :] = (
+            hat * vectors[GAIN_A : GAIN_A + 1] + vectors[SHIFT_A : SHIFT_A + 1]
+        ).astype(BF16)
+
+    norm_loop(rows, norm_step)
     low = lanes((1, PAIR)) < HD
 
     def one(d, _):
         pair = member ^ d
         block = weight[:, pl.ds(pl.multiple_of(pair * 3 * PAIR, PAIR), 3 * PAIR)]
-        both = bias[:, pl.ds(pl.multiple_of(pair * 2 * PAIR, PAIR), 2 * PAIR)].astype(F32)
+        both = vectors[JOINED_BIAS : JOINED_BIAS + 1, pl.ds(pl.multiple_of(pair * 2 * PAIR, PAIR), 2 * PAIR)]
         first, second = both[:, :PAIR], both[:, PAIR:]
         query_bias = jnp.where(low, first, pltpu.roll(second, HD, 1))
         value_bias = jnp.where(low, pltpu.roll(first, HD, 1), second)
@@ -245,18 +307,19 @@
     lax.fori_loop(0, MEMBERS, one, 0)
 
 
-def project(meta, x, gain, shift, weight, bias):
+def project(meta, x, vectors, weight):
     rows, width = x.shape
     outs = pl.pallas_call(
         project_kernel,
         out_shape=[shaped((rows, width), BF16)]
         + [shaped((rows, PAIR), BF16)] * MEMBERS
         + [shaped((rows, 2 * PAIR), BF16)] * MEMBERS,
-        in_specs=[SM] + [VM] * 5,
+        in_specs=[SM] + [VM] * 3,
         out_specs=[VM] * (1 + 2 * MEMBERS),
         compiler_params=params(),
+        cost_estimate=lasting("project"),
         name="project",
-    )(meta, x, gain, shift, weight, bias)
+    )(meta, x, vectors, weight)
     return outs[0], outs[1 : 1 + MEMBERS], outs[1 + MEMBERS :]
 
 
@@ -291,11 +354,12 @@
         out_specs=[ANY] * 2,
         scratch_shapes=[pltpu.SemaphoreType.DMA((2 * INNER,))],
         compiler_params=params(8),
+        cost_estimate=lasting("pack"),
         name="pack",
     )(table, *pairs)
 
 
-LEVELS = (2, 4, 6, 8, 10)
+LEVELS = (1, 2, 3, 4, 5, 6, 8, 10)
 
 
 def split_heads(tile):
@@ -324,6 +388,15 @@
     gap = slope * (key - offset).astype(F32)
     bias[0] = jnp.where(key <= offset, gap, NEGATIVE)
     bias[1] = gap
+
+
+def split_turned(tile):
+    top = rows_of((PAIR, SEG)) < HD
+    wide = tile.astype(F32).T
+    zero = jnp.zeros_like(wide)
+    return jnp.concatenate(
+        [jnp.where(top, wide, zero), jnp.where(top, zero, wide)], axis=1
+    ).astype(BF16)
 
 
 def start_all(copies):
@@ -356,7 +429,8 @@
         turned[i] = segment(pool, i)[:, first : first + PAIR].astype(F32).T.astype(BF16)
         return _
 
-    lax.fori_loop(0, count, turn, 0)
+    lax.fori_loop(0, count, turn, 0, unroll=4)
+    turned[count] = jnp.zeros((PAIR, SEG), BF16)
 
 
 def entries(table, side, s, span):
@@ -366,11 +440,30 @@
     return spots, levels
 
 
-def level_row(slope, levels, i, count, span):
+def level_row(slope, levels, i, count):
     row = slope * (levels[i] * (-SEG)).astype(F32)
-    if i == span - 1:
-        row = row + jnp.where(count < span, NEGATIVE, 0.0)
-    return row
+    return row + jnp.where(count <= i, NEGATIVE, 0.0)
+
+
+def by_groups(table, side, body, empty=None):
+    def step(g, _):
+        group = [table[ORDER_AT[side] + g * GROUP + k] for k in range(GROUP)]
+        most = table[COUNT_AT[side] + group[0]]
+        if empty is not None:
+
+            @pl.when(most == 0)
+            def _none():
+                empty(group)
+
+        for below, span in zip((0,) + LEVELS[:-1], LEVELS):
+
+            @pl.when((most > below) & (most <= span))
+            def _run():
+                body(group, span)
+
+        return _
+
+    lax.fori_loop(0, TREE // GROUP, step, 0)
 
 
 def chosen_heads(wide):
@@ -381,21 +474,24 @@
 def weigh(side, span, table, s, slope, bias, pool, turned, stacked):
     count = table[COUNT_AT[side] + s]
     spots, levels = entries(table, side, s, span)
+    keys = jnp.concatenate([segment(pool, spot)[:, :PAIR] for spot in spots], axis=0)
+    whole = dot(keys, stacked)
     scores = []
     for i in range(span):
-        raw = dot(segment(pool, spots[i])[:, :PAIR], stacked, ((1,), (1,)))
+        raw = whole[i * SEG : (i + 1) * SEG]
         own = side == 0 and i == 0
-        scores.append(raw + bias[0 if own else 1] + level_row(slope, levels, i, count, span))
+        scores.append(raw + bias[0 if own else 1] + level_row(slope, levels, i, count))
     top = scores[0]
     for part in scores[1:]:
         top = jnp.maximum(top, part)
     top = jnp.max(top, axis=0, keepdims=True)
-    sums, out = None, None
+    sums, short = None, []
     for i in range(span):
         weights = jnp.exp(scores[i] - top)
-        part = dot(turned[spots[i]], weights.astype(BF16))
+        short.append(weights.astype(BF16))
         sums = weights if sums is None else sums + weights
-        out = part if out is None else out + part
+    values = jnp.concatenate([turned[spot] for spot in spots], axis=1)
+    out = dot(values, jnp.concatenate(short, axis=0))
     return top, jnp.sum(sums, axis=0, keepdims=True), chosen_heads(out)
 
 
@@ -410,25 +506,17 @@
     fill_bias(bias, slope)
     pool[TREE * SEG :, :] = jnp.zeros((SEG, 2 * PAIR), BF16)
     wait_all(copies)
-    turn_all(pool, turned, TREE + 1, PAIR)
-
-    def one(s, _):
-        count = table[COUNT_AT[0] + s]
-        stacked = split_heads(segment(queries, s)[...])
-        for span in LEVELS:
-
-            @pl.when((count > span - 2) & (count <= span))
-            def _run():
-                top, total, out = weigh(
-                    0, span, table, s, slope, bias, pool, turned, stacked
-                )
-                stats[s, 0:1, :] = top
-                stats[s, 1:2, :] = total
-                kept[s] = out
-
-        return _
-
-    lax.fori_loop(0, TREE, one, 0)
+    turn_all(pool, turned, TREE, PAIR)
+
+    def body(group, span):
+        for s in group:
+            stacked = split_turned(segment(queries, s)[...])
+            top, total, out = weigh(0, span, table, s, slope, bias, pool, turned, stacked)
+            stats[s, 0:1, :] = top
+            stats[s, 1:2, :] = total
+            kept[s] = out
+
+    by_groups(table, 0, body)
 
 
 def attend_near(table, meta, slopes, queries, pairs):
@@ -445,6 +533,7 @@
             pltpu.SemaphoreType.DMA((2 * MEMBERS,)),
         ],
         compiler_params=params(),
+        cost_estimate=lasting("attend_near"),
         name="attend_near",
     )(table, meta, slopes, *queries, *pairs)
 
@@ -461,42 +550,33 @@
     fill_bias(bias, slope)
     pool[2 * INNER * SEG :, :] = jnp.zeros((SEG, 2 * PAIR), BF16)
     wait_all(copies)
-    turn_all(pool, turned, 2 * INNER + 1, PAIR)
+    turn_all(pool, turned, 2 * INNER, PAIR)
 
     def finish(s, top, total, out):
         wide = 1.0 / total
         segment(result, s)[...] = (out * chosen_heads(jnp.broadcast_to(wide, (PAIR, 2 * SEG)))).T.astype(BF16)
         lse[s] = top + jnp.log(total)
 
-    def one(s, _):
-        count = table[COUNT_AT[1] + s]
-
-        @pl.when(count == 0)
-        def _none():
+    def alone(group):
+        for s in group:
             finish(s, stats[s, 0:1, :], stats[s, 1:2, :], kept[s])
 
-        for span in LEVELS:
-
-            @pl.when((count > span - 2) & (count <= span) & (count > 0))
-            def _run():
-                stacked = split_heads(segment(queries, s)[...])
-                top, total, out = weigh(
-                    1, span, table, s, slope, bias, pool, turned, stacked
-                )
-                near = stats[s, 0:1, :]
-                both = jnp.maximum(near, top)
-                near_scale = jnp.exp(near - both)
-                far_scale = jnp.exp(top - both)
-                total = stats[s, 1:2, :] * near_scale + total * far_scale
-                shape = (PAIR, 2 * SEG)
-                out = kept[s] * chosen_heads(jnp.broadcast_to(near_scale, shape)) + out * (
-                    chosen_heads(jnp.broadcast_to(far_scale, shape))
-                )
-                finish(s, both, total, out)
-
-        return _
-
-    lax.fori_loop(0, TREE, one, 0)
+    def body(group, span):
+        shape = (PAIR, 2 * SEG)
+        for s in group:
+            stacked = split_turned(segment(queries, s)[...])
+            top, total, out = weigh(1, span, table, s, slope, bias, pool, turned, stacked)
+            near = stats[s, 0:1, :]
+            both = jnp.maximum(near, top)
+            near_scale = jnp.exp(near - both)
+            far_scale = jnp.exp(top - both)
+            total = stats[s, 1:2, :] * near_scale + total * far_scale
+            out = kept[s] * chosen_heads(jnp.broadcast_to(near_scale, shape)) + out * (
+                chosen_heads(jnp.broadcast_to(far_scale, shape))
+            )
+            finish(s, both, total, out)
+
+    by_groups(table, 1, body, alone)
     copies = [
         pltpu.make_async_copy(result.at[pl.ds(j * rows, rows)], target, sem.at[j])
         for j, target in enumerate((o0, o1, o2, o3))
@@ -505,12 +585,14 @@
     wait_all(copies)
 
 
-def attend_far(table, meta, slopes, queries, below, above, kept, stats):
+def attend_far(table, meta, slopes, queries, below, above, kept, stats, deps=()):
     rows = queries[0].shape[0]
+    specs = [SM] * 3 + [ANY] * (MEMBERS + 2) + [VM] * 2
+    used = len(specs)
     outs = pl.pallas_call(
-        attend_far_kernel,
+        skipping(attend_far_kernel, used, len(deps)),
         out_shape=[shaped((rows, PAIR), BF16)] * MEMBERS + [shaped((TREE, 1, 2 * SEG), F32)],
-        in_specs=[SM] * 3 + [ANY] * (MEMBERS + 2) + [VM] * 2,
+        in_specs=specs + [ANY] * len(deps),
         out_specs=[ANY] * MEMBERS + [VM],
         scratch_shapes=[
             pltpu.VMEM(((2 * INNER + 1) * SEG, 2 * PAIR), BF16),
@@ -521,14 +603,16 @@
             pltpu.SemaphoreType.DMA((MEMBERS + 2,)),
         ],
         compiler_params=params(),
+        cost_estimate=lasting("attend_far"),
         name="attend_far",
-    )(table, meta, slopes, *queries, below, above, kept, stats)
+    )(table, meta, slopes, *queries, below, above, kept, stats, *deps)
     return outs[:MEMBERS], outs[MEMBERS]
 
 
 def spread(side, span, table, s, slope, bias, pool, turned, total, queries, outs, grads, lse):
     count = table[COUNT_AT[side] + s]
-    stacked = split_heads(segment(queries, s)[...])
+    query = segment(queries, s)[...]
+    stacked = split_heads(query)
     grad = segment(grads, s)[...]
     stacked_grad = split_heads(grad)
     product = (grad.astype(F32) * segment(outs, s)[...].astype(F32)).T
@@ -541,21 +625,28 @@
     )
     log_total = lse[s]
     spots, levels = entries(table, side, s, span)
-    query_grad = None
+    keys = jnp.concatenate([segment(pool, spot)[:, :PAIR] for spot in spots], axis=0)
+    values = jnp.concatenate([segment(pool, spot)[:, PAIR:] for spot in spots], axis=0)
+    raw = dot(keys, split_turned(query))
+    prob_grad = dot(values, split_turned(grad))
+    probs, score_grads = [], []
     for i in range(span):
-        block = segment(pool, spots[i])
-        raw = dot(block[:, :PAIR], stacked, ((1,), (1,)))
-        row = level_row(slope, levels, i, count, span) - log_total
+        at = slice(i * SEG, (i + 1) * SEG)
+        row = level_row(slope, levels, i, count) - log_total
         own = side == 0 and i == 0
-        probs = jnp.exp(raw + bias[0 if own else 1] + row)
-        prob_grad = dot(block[:, PAIR:], stacked_grad, ((1,), (1,)))
-        score_grad = (probs * (prob_grad - delta)).astype(BF16)
+        prob = jnp.exp(raw[at] + bias[0 if own else 1] + row)
+        score_grads.append((prob * (prob_grad[at] - delta)).astype(BF16))
+        probs.append(prob.astype(BF16))
+    score_grad = jnp.concatenate(score_grads, axis=0)
+    key_grad = dot(score_grad, stacked)
+    value_grad = dot(jnp.concatenate(probs, axis=0), stacked_grad)
+    for i in range(span):
+        at = slice(i * SEG, (i + 1) * SEG)
         into = segment(total, spots[i])
-        into[:, :PAIR] += dot(score_grad, stacked)
-        into[:, PAIR:] += dot(probs.astype(BF16), stacked_grad)
-        part = dot(turned[spots[i]], score_grad)
-        query_grad = part if query_grad is None else query_grad + part
-    return chosen_heads(query_grad)
+        into[:, :PAIR] += key_grad[at]
+        into[:, PAIR:] += value_grad[at]
+    across = jnp.concatenate([turned[spot] for spot in spots], axis=1)
+    return chosen_heads(dot(across, score_grad))
 
 
 def clear_all(total, count):
@@ -563,7 +654,7 @@
         segment(total, i)[...] = jnp.zeros((SEG, 2 * PAIR), F32)
         return _
 
-    lax.fori_loop(0, count, clear, 0)
+    lax.fori_loop(0, count, clear, 0, unroll=True)
 
 
 def back_far_kernel(
@@ -581,26 +672,19 @@
     pool[2 * INNER * SEG :, :] = jnp.zeros((SEG, 2 * PAIR), BF16)
     clear_all(total, 2 * INNER + 1)
     wait_all(copies)
-    turn_all(pool, turned, 2 * INNER + 1, 0)
-
-    def one(s, _):
-        count = table[COUNT_AT[1] + s]
-
-        @pl.when(count == 0)
-        def _none():
+    turn_all(pool, turned, 2 * INNER, 0)
+
+    def alone(group):
+        for s in group:
             kept[s] = jnp.zeros((PAIR, SEG), F32)
 
-        for span in LEVELS:
-
-            @pl.when((count > span - 2) & (count <= span) & (count > 0))
-            def _run():
-                kept[s] = spread(
-                    1, span, table, s, slope, bias, pool, turned, total, queries, outs, grads, lse
-                )
-
-        return _
-
-    lax.fori_loop(0, TREE, one, 0)
+    def body(group, span):
+        for s in group:
+            kept[s] = spread(
+                1, span, table, s, slope, bias, pool, turned, total, queries, outs, grads, lse
+            )
+
+    by_groups(table, 1, body, alone)
 
     def shorten(i, _):
         segment(small, i)[...] = segment(total, i)[...].astype(BF16)
@@ -617,12 +701,14 @@
     wait_all(copies)
 
 
-def back_far(table, meta, slopes, queries, below, above, outs, grads, lse):
+def back_far(table, meta, slopes, queries, below, above, outs, grads, lse, deps=()):
     side = shaped((INNER * SEG, 2 * PAIR), BF16)
+    specs = [SM] * 3 + [ANY] * (3 * MEMBERS + 2) + [VM]
+    used = len(specs)
     return pl.pallas_call(
-        back_far_kernel,
+        skipping(back_far_kernel, used, len(deps)),
         out_shape=[side, side, shaped((TREE, PAIR, SEG), F32)],
-        in_specs=[SM] * 3 + [ANY] * (3 * MEMBERS + 2) + [VM],
+        in_specs=specs + [ANY] * len(deps),
         out_specs=[ANY] * 2 + [VM],
         scratch_shapes=[
             pltpu.VMEM(((2 * INNER + 1) * SEG, 2 * PAIR), BF16),
@@ -636,8 +722,9 @@
             pltpu.SemaphoreType.DMA((3 * MEMBERS + 2,)),
         ],
         compiler_params=params(),
+        cost_estimate=lasting("back_far"),
         name="back_far",
-    )(table, meta, slopes, *queries, below, above, *outs, *grads, lse)
+    )(table, meta, slopes, *queries, below, above, *outs, *grads, lse, *deps)
 
 
 def back_near_kernel(
@@ -656,22 +743,16 @@
     pool[TREE * SEG :, :] = jnp.zeros((SEG, 2 * PAIR), BF16)
     clear_all(total, TREE + 1)
     wait_all(copies)
-    turn_all(pool, turned, TREE + 1, 0)
-
-    def one(s, _):
-        count = table[COUNT_AT[0] + s]
-        for span in LEVELS:
-
-            @pl.when((count > span - 2) & (count <= span))
-            def _run():
-                part = spread(
-                    0, span, table, s, slope, bias, pool, turned, total, queries, outs, grads, lse
-                )
-                segment(result, s)[...] = (kept[s] + part).T.astype(BF16)
-
-        return _
-
-    lax.fori_loop(0, TREE, one, 0)
+    turn_all(pool, turned, TREE, 0)
+
+    def body(group, span):
+        for s in group:
+            part = spread(
+                0, span, table, s, slope, bias, pool, turned, total, queries, outs, grads, lse
+            )
+            segment(result, s)[...] = (kept[s] + part).T.astype(BF16)
+
+    by_groups(table, 0, body)
     copies = [
         pltpu.make_async_copy(result.at[pl.ds(j * rows, rows)], target, sem.at[j])
         for j, target in enumerate((dq0, dq1, dq2, dq3))
@@ -683,12 +764,14 @@
     wait_all(copies)
 
 
-def back_near(table, meta, slopes, queries, pairs, outs, grads, lse, kept):
+def back_near(table, meta, slopes, queries, pairs, outs, grads, lse, kept, deps=()):
     rows = queries[0].shape[0]
+    specs = [SM] * 3 + [ANY] * (4 * MEMBERS) + [VM] * 2
+    used = len(specs)
     result = pl.pallas_call(
-        back_near_kernel,
+        skipping(back_near_kernel, used, len(deps)),
         out_shape=[shaped((rows, PAIR), BF16)] * MEMBERS + [shaped((TREE * SEG, 2 * PAIR), F32)],
-        in_specs=[SM] * 3 + [ANY] * (4 * MEMBERS) + [VM] * 2,
+        in_specs=specs + [ANY] * len(deps),
         out_specs=[ANY] * (MEMBERS + 1),
         scratch_shapes=[
             pltpu.VMEM(((TREE + 1) * SEG, 2 * PAIR), BF16),
@@ -702,8 +785,9 @@
             pltpu.SemaphoreType.DMA((4 * MEMBERS,)),
         ],
         compiler_params=params(),
+        cost_estimate=lasting("back_near"),
         name="back_near",
-    )(table, meta, slopes, *queries, *pairs, *outs, *grads, lse, kept)
+    )(table, meta, slopes, *queries, *pairs, *outs, *grads, lse, kept, *deps)
     return result[:MEMBERS], result[MEMBERS]
 
 
@@ -733,36 +817,28 @@
         lax.fori_loop(0, SEG_DEV, short, 0)
 
 
-def gather_back(table, own, from_above, from_below):
+def gather_back(table, own, from_above, from_below, deps=()):
     rows = SEG_DEV * SEG
+    specs = [SM, ANY, VM, VM]
+    used = len(specs)
     return pl.pallas_call(
-        gather_back_kernel,
+        skipping(gather_back_kernel, used, len(deps)),
         out_shape=[shaped((rows, 2 * PAIR), BF16)] * MEMBERS,
-        in_specs=[SM, ANY, VM, VM],
+        in_specs=specs + [ANY] * len(deps),
         out_specs=[VM] * MEMBERS,
         scratch_shapes=[
             pltpu.VMEM((TREE * SEG, 2 * PAIR), F32),
             pltpu.SemaphoreType.DMA(()),
         ],
         compiler_params=params(),
+        cost_estimate=lasting("gather_back"),
         name="gather_back",
-    )(table, own, from_above, from_below)
+    )(table, own, from_above, from_below, *deps)
 
 
 TILE = 256
-NORM_ROWS = 32
-
-
-def norm_loop(rows, body):
-    def step(i, _):
-        body(pl.ds(pl.multiple_of(i * NORM_ROWS, NORM_ROWS), NORM_ROWS))
-        return _
-
-    lax.fori_loop(0, rows // NORM_ROWS, step, 0)
-
-
 def feed_kernel(
-    meta, x, out_bias, gain, shift, up_bias, a0, a1, a2, a3, b0, b1, b2, b3,
+    meta, x, vectors, a0, a1, a2, a3, b0, b1, b2, b3,
     w_own, w_other, w_up, hidden_grad,
     mixed_out, middle_out, normed_out, act_out, pre_out, part, sums,
     mixed_own, middle, normed, act, pre_grad, mixed, weight, up, hidden, sem, out_sem,
@@ -794,7 +870,7 @@
     def column(t, _):
         at = pl.ds(pl.multiple_of(t * TILE, TILE), TILE)
         middle[:, at] = (
-            x[:, at].astype(F32) + (dot(mixed[...], weight[:, at]) + out_bias[:, at].astype(F32))
+            x[:, at].astype(F32) + (dot(mixed[...], weight[:, at]) + vectors[OUT_BIAS : OUT_BIAS + 1, at])
         )
         return _
 
@@ -804,7 +880,7 @@
 
     def norm_step(at):
         hat, _scale = normal(middle[at, :])
-        normed[at, :] = (hat * gain[...].astype(F32) + shift[...].astype(F32)).astype(BF16)
+        normed[at, :] = (hat * vectors[GAIN_F : GAIN_F + 1] + vectors[SHIFT_F : SHIFT_F + 1]).astype(BF16)
 
     norm_loop(rows, norm_step)
     stores.append(pltpu.make_async_copy(normed, normed_out, out_sem.at[2]))
@@ -813,7 +889,9 @@
 
     def hidden_step(t, _):
         at = pl.ds(pl.multiple_of(t * TILE, TILE), TILE)
-        pre = dot(normed[...], up[:, at]) + up_bias[:, at].astype(F32)
+        per = width // TILE
+        bias = vectors[pl.ds(UP_BIAS + t // per, 1), pl.ds(pl.multiple_of(lax.rem(t, per) * TILE, TILE), TILE)]
+        pre = dot(normed[...], up[:, at]) + bias
         square = pre * pre
         c = 0.7978845608028654
         t_ = jnp.tanh(pre * (c + (c * 0.044715) * square))
@@ -839,7 +917,7 @@
     wait_all(stores)
 
 
-def feed(meta, x, out_bias, gain, shift, up_bias, parts_own, parts_other, w_own, w_other, w_up, hidden_grad):
+def feed(meta, x, vectors, parts_own, parts_other, w_own, w_other, w_up, hidden_grad):
     rows, width = x.shape
     inner = w_up.shape[1]
     half = width // 2
@@ -854,7 +932,7 @@
             shaped((rows, width), BF16),
             shaped((8, inner), F32),
         ],
-        in_specs=[SM] + [VM] * (5 + 2 * MEMBERS) + [ANY] * 4,
+        in_specs=[SM] + [VM] * (2 + 2 * MEMBERS) + [ANY] * 4,
         out_specs=[ANY] * 5 + [VM] * 2,
         scratch_shapes=[
             pltpu.VMEM((rows, half), BF16),
@@ -870,8 +948,33 @@
             pltpu.SemaphoreType.DMA((5,)),
         ],
         compiler_params=params(),
+        cost_estimate=lasting("feed"),
         name="feed",
-    )(meta, x, out_bias, gain, shift, up_bias, *parts_own, *parts_other, w_own, w_other, w_up, hidden_grad)
+    )(meta, x, vectors, *parts_own, *parts_other, w_own, w_other, w_up, hidden_grad)
+
+
+def product_kernel(dims, left, right, out):
+    out[...] = dot(left[...], right[...], dims).astype(out.dtype)
+
+
+def product(name, left, right, turned, kind, deps=()):
+    rows, depth = left.shape
+    across = right.shape[0] if turned else right.shape[1]
+    block = (TILE, depth) if turned else (depth, TILE)
+    return pl.pallas_call(
+        skipping(partial(product_kernel, ((1,), (1,) if turned else (0,))), 2, len(deps)),
+        grid=(across // TILE,),
+        out_shape=shaped((rows, across), kind),
+        in_specs=[
+            pl.BlockSpec((rows, depth), lambda t: (0, 0)),
+            pl.BlockSpec(block, (lambda t: (t, 0)) if turned else (lambda t: (0, t))),
+        ]
+        + [ANY] * len(deps),
+        out_specs=pl.BlockSpec((rows, TILE), lambda t: (0, t)),
+        compiler_params=params(),
+        cost_estimate=lasting(name),
+        name=name,
+    )(left, right, *deps)
 
 
 def turn_rows(source, target):
@@ -883,46 +986,116 @@
     lax.fori_loop(0, source.shape[1] // SEG, step, 0)
 
 
-def feed_grads_kernel(grad, act, normed, pre_grad, out, turned):
+X_FIRST = (0, 1, 2, 3)
+Z_FIRST = (0, 2, 3, 1)
+MIXED = (0, 2, 1, 3)
+DEVICES = 16
+
+
+def block_place(relative, order):
+    place = 0
+    for bit in order:
+        place = place * 2 + (lax.shift_right_logical(relative, bit) & 1)
+    return place
+
+
+def turn_ordered(tile, target, i, device, order, share):
+    for k in range(SEG // share):
+        block = i * (SEG // share) + k
+        at = block_place(block ^ device, order) * share
+        target[pl.ds(pl.multiple_of(at, share), share), :] = tile[k * share : (k + 1) * share]
+
+
+def turn_source(source, target, device, order, share):
+    def step(i, _):
+        at = pl.ds(pl.multiple_of(i * SEG, SEG), SEG)
+        tile = source[:, at].astype(F32).T.astype(BF16)
+        turn_ordered(tile, target, i, device, order, share)
+        return _
+
+    lax.fori_loop(0, source.shape[1] // SEG, step, 0)
+
+
+def feed_grads_kernel(
+    meta, grad, act, normed, pre_grad, weight,
+    keep_c, send_c0, send_c1, keep_e, send_e0, send_e1, part, turned,
+):
     t = pl.program_id(0)
     tiles = pl.num_programs(0) // 2
+    width = grad.shape[1]
+    half = width // 2
+    tile = pre_grad.shape[1]
 
     @pl.when(t == 0)
     def _first():
-        turn_rows(grad, turned)
+        turn_source(grad, turned, meta[4], MIXED, width // DEVICES)
 
     @pl.when(t == tiles)
     def _second():
-        turn_rows(normed, turned)
+        turn_source(normed, turned, meta[4], X_FIRST, width // DEVICES)
 
     @pl.when(t < tiles)
     def _contract():
-        out[...] = dot(turned[...], act[...]).astype(BF16)
+        right = act[:, pl.ds(pl.multiple_of(t * tile, tile), tile)]
+        keep_c[...] = dot(turned[:half], right).astype(BF16)
+        leave = dot(turned[half:], right).astype(BF16)
+
+        @pl.when(t < tiles // 2)
+        def _low():
+            send_c0[...] = leave
+
+        @pl.when(t >= tiles // 2)
+        def _high():
+            send_c1[...] = leave
 
     @pl.when(t >= tiles)
     def _expand():
-        out[...] = dot(turned[...], pre_grad[...]).astype(BF16)
-
-
-def feed_grads(grad, act, normed, pre_grad, across):
+        keep_e[...] = dot(turned[:half], pre_grad[...]).astype(BF16)
+        leave = dot(turned[half:], pre_grad[...]).astype(BF16)
+
+        @pl.when(t < tiles + tiles // 2)
+        def _low():
+            send_e0[...] = leave
+
+        @pl.when(t >= tiles + tiles // 2)
+        def _high():
+            send_e1[...] = leave
+
+    part[...] = dot(act[...], weight[...]).astype(BF16)
+
+
+def feed_grads(meta, grad, act, normed, pre_grad, weight):
     rows, width = grad.shape
-    tiles = act.shape[1] // TILE
+    inner = act.shape[1]
+    tile = 2 * TILE
+    tiles = inner // tile
+    piece = width // (2 * tiles)
+
+    def steps(start, number):
+        return pl.BlockSpec((width // 2, tile), lambda t: (0, jnp.clip(t - start, 0, number - 1)))
+
+    both = [steps(0, tiles), steps(0, tiles // 2), steps(tiles // 2, tiles // 2)]
+    both += [steps(tiles, tiles), steps(tiles, tiles // 2), steps(tiles + tiles // 2, tiles // 2)]
+    kept, sent = shaped((width // 2, inner), BF16), shaped((width // 2, inner // 2), BF16)
     whole = pl.BlockSpec((rows, width), lambda t: (0, 0))
     return pl.pallas_call(
         feed_grads_kernel,
         grid=(2 * tiles,),
-        out_shape=shaped((width, across), BF16),
+        out_shape=[kept, sent, sent, kept, sent, sent, shaped((rows, width), BF16)],
         in_specs=[
+            SM,
             whole,
-            pl.BlockSpec((rows, TILE), lambda t: (0, jnp.minimum(t, tiles - 1))),
+            pl.BlockSpec((rows, inner), lambda t: (0, 0)),
             whole,
-            pl.BlockSpec((rows, TILE), lambda t: (0, jnp.maximum(t - tiles, 0))),
+            pl.BlockSpec((rows, tile), lambda t: (0, jnp.maximum(t - tiles, 0))),
+            pl.BlockSpec((inner, piece), lambda t: (0, t)),
         ],
-        out_specs=pl.BlockSpec((width, TILE), lambda t: (0, t)),
+        out_specs=both + [pl.BlockSpec((rows, piece), lambda t: (0, t))],
         scratch_shapes=[pltpu.VMEM((width, rows), BF16)],
         compiler_params=params(),
+        cost_estimate=lasting("feed_grads"),
         name="feed_grads",
-    )(grad, act, normed, pre_grad)
+    )(meta, grad, act, normed, pre_grad, weight)
 
 
 def in_two(rows8):
@@ -931,75 +1104,197 @@
     return jnp.concatenate([high, low, jnp.zeros((SEG - 16, rows8.shape[1]), F32)], axis=0)
 
 
-def output_grads_kernel(branch, mixed, vectors, extra, held, out, turned, result, small, sem):
-    width, half = branch.shape[1], mixed.shape[1]
-    turn_rows(branch, turned)
-
-    def column(t, _):
-        at = pl.ds(pl.multiple_of(t * TILE, TILE), TILE)
-        result[:, at] = dot(turned[...], mixed[:, at]).astype(BF16)
-        return _
-
-    lax.fori_loop(0, half // TILE, column, 0)
-    for i in range(width // SEG):
-        at = slice(i * SEG, (i + 1) * SEG)
-        rows8 = jnp.concatenate([vectors[0:4, at], extra[0:2, at], jnp.zeros((2, SEG), F32)], axis=0)
-        small[at, :] = in_two(rows8).T.astype(BF16)
-    first = out.shape[1] - half - SEG
-    copies = [
-        pltpu.make_async_copy(result, out.at[:, pl.ds(first, half)], sem.at[0]),
-        pltpu.make_async_copy(small, out.at[:, pl.ds(first + half, SEG)], sem.at[1]),
-    ]
-    start_all(copies)
-    wait_all(copies)
-
-
-def output_grads(branch, mixed, vectors, extra, held):
+def add_half(keep, got, stay, leave):
+    half = stay.shape[0]
+    stay[...] = keep[:half].astype(F32) + got[:half].astype(F32)
+    leave[...] = (keep[half:].astype(F32) + got[half:].astype(F32)).astype(BF16)
+
+
+TAKE_STEPS = 4
+
+
+def take_specs(shape):
+    rows, across = shape
+    if across % (TAKE_STEPS * PAIR) == 0:
+        tile, at = across // TAKE_STEPS, lambda t: (0, t)
+    else:
+        tile, at = across, lambda t: (0, 0)
+    return pl.BlockSpec((rows, tile), at), pl.BlockSpec((rows // 2, tile), at)
+
+
+def add_halves(flags, ins, outs):
+    for k, split in enumerate(flags):
+        step = partial(add_half, ins[2 * k], ins[2 * k + 1], outs[2 * k], outs[2 * k + 1])
+        if split:
+            step()
+        else:
+            pl.when(pl.program_id(0) == 0)(step)
+
+
+def halves_of(pairs):
+    specs, outs, shapes, flags, args = [], [], [], [], []
+    for keep, got in pairs:
+        whole, part = take_specs(keep.shape)
+        half = (keep.shape[0] // 2, keep.shape[1])
+        specs += [whole, whole]
+        outs += [part, part]
+        shapes += [shaped(half, F32), shaped(half, BF16)]
+        flags.append(whole.block_shape[1] != keep.shape[1])
+        args += [keep, got]
+    return specs, outs, shapes, flags, args
+
+
+def takes_kernel(flags, count, *refs):
+    ins, outs = refs[: 2 * len(flags)], refs[2 * len(flags) + count :]
+    add_halves(flags, ins, outs)
+
+
+def takes(name, pairs, deps=()):
+    specs, outs, shapes, flags, args = halves_of(pairs)
+    got = pl.pallas_call(
+        partial(takes_kernel, flags, len(deps)),
+        grid=(TAKE_STEPS,),
+        out_shape=shapes,
+        in_specs=specs + [ANY] * len(deps),
+        out_specs=outs,
+        compiler_params=params(),
+        cost_estimate=lasting(name),
+        name=name,
+    )(*args, *deps)
+    return [tuple(got[2 * k : 2 * k + 2]) for k in range(len(pairs))]
+
+
+def output_grads_kernel(count, meta, branch, mixed, vectors, extra, *refs):
+    ins = refs[: 3 * count]
+    keep, send = refs[3 * count : 3 * count + 2]
+    outs = refs[3 * count + 2 : -2]
+    turned, small = refs[-2:]
+    t = pl.program_id(0)
+    width, across = branch.shape[1], mixed.shape[1]
+    share = width // DEVICES
+    half = width // 2
+
+    @pl.when(t == 0)
+    def _first():
+        turn_source(branch, turned, meta[4], X_FIRST, share)
+        for i in range(width // SEG):
+            at = slice(i * SEG, (i + 1) * SEG)
+            rows8 = jnp.concatenate(
+                [vectors[0:4, at], extra[0:2, at], jnp.zeros((2, SEG), F32)], axis=0
+            )
+            turn_ordered(in_two(rows8).T, small, i, meta[4], X_FIRST, share)
+        keep[:, across:] = small[:half].astype(BF16)
+        send[:, across:] = small[half:].astype(BF16)
+
+    tile = across // TAKE_STEPS
+    at = pl.ds(pl.multiple_of(t * tile, tile), tile)
+    keep[:, at] = dot(turned[:half], mixed[:, at]).astype(BF16)
+    send[:, at] = dot(turned[half:], mixed[:, at]).astype(BF16)
+    for k in range(count):
+        kept, low, high = ins[3 * k : 3 * k + 3]
+
+        @pl.when(t < TAKE_STEPS // 2)
+        def _low():
+            add_half(kept, low, outs[2 * k], outs[2 * k + 1])
+
+        @pl.when(t >= TAKE_STEPS // 2)
+        def _high():
+            add_half(kept, high, outs[2 * k], outs[2 * k + 1])
+
+
+def output_grads(meta, branch, mixed, vectors, extra, pairs):
     rows, width = branch.shape
-    half = mixed.shape[1]
+    across = mixed.shape[1]
+    half_steps = TAKE_STEPS // 2
+    specs, outs, shapes, args = [], [], [], []
+    for kept, low, high in pairs:
+        high_rows, cols = kept.shape
+        tile = cols // TAKE_STEPS
+        specs += [
+            pl.BlockSpec((high_rows, tile), lambda t: (0, t)),
+            pl.BlockSpec((high_rows, tile), lambda t: (0, jnp.minimum(t, half_steps - 1))),
+            pl.BlockSpec((high_rows, tile), lambda t: (0, jnp.maximum(t - half_steps, 0))),
+        ]
+        outs += [pl.BlockSpec((high_rows // 2, tile), lambda t: (0, t))] * 2
+        shapes += [shaped((high_rows // 2, cols), F32), shaped((high_rows // 2, cols), BF16)]
+        args += [kept, low, high]
+
+    def whole(shape):
+        return pl.BlockSpec(shape, lambda t: (0, 0))
+
+    own = whole((width // 2, across + SEG))
+    got = pl.pallas_call(
+        partial(output_grads_kernel, len(pairs)),
+        grid=(TAKE_STEPS,),
+        out_shape=[shaped((width // 2, across + SEG), BF16)] * 2 + shapes,
+        in_specs=[SM, whole(branch.shape), whole(mixed.shape), whole(vectors.shape), whole(extra.shape)]
+        + specs,
+        out_specs=[own, own] + outs,
+        scratch_shapes=[pltpu.VMEM((width, rows), BF16), pltpu.VMEM((width, SEG), F32)],
+        compiler_params=params(),
+        cost_estimate=lasting("output_grads"),
+        name="output_grads",
+    )(meta, branch, mixed, vectors, extra, *args)
+    return (got[0], got[1]), [tuple(got[2 + 2 * k : 4 + 2 * k]) for k in range(len(pairs))]
+
+
+def add_kernel(keep, got, out):
+    out[...] = keep[...] + got[...].astype(F32)
+
+
+def add(keep, got):
     return pl.pallas_call(
-        output_grads_kernel,
-        out_shape=shaped(held.shape, held.dtype),
-        in_specs=[VM] * 4 + [ANY],
-        out_specs=ANY,
-        input_output_aliases={4: 0},
-        scratch_shapes=[
-            pltpu.VMEM((width, rows), BF16),
-            pltpu.VMEM((width, half), BF16),
-            pltpu.VMEM((width, SEG), BF16),
-            pltpu.SemaphoreType.DMA((2,)),
-        ],
+        add_kernel,
+        out_shape=shaped(keep.shape, F32),
+        in_specs=[VM] * 2,
+        out_specs=VM,
         compiler_params=params(),
-        name="output_grads",
-    )(branch, mixed, vectors, extra, held)
-
-
-def feed_finish_kernel(inner, got, contract, expand, output, v0, v1, v2, v3, bias):
-    rows = got.shape[0]
-    half = output.shape[1]
-    contract[...] = got[:, :inner].astype(F32)
-    expand[...] = got[:, inner : 2 * inner].astype(F32)
-    output[...] = got[:, 2 * inner : 2 * inner + half].astype(F32)
-    small = got[:, 2 * inner + half :].astype(F32).T
+        cost_estimate=lasting("add"),
+        name="add",
+    )(keep, got)
+
+
+def finish_kernel(
+    o, got_o, a, got_a, b, got_b,
+    output, weight, v0, v1, v2, v3, bias, w0, w1, w2,
+):
+    total = o[...] + got_o[...].astype(F32)
+    across = output.shape[1]
+    output[...] = total[:, :across]
+    small = total[:, across:].T
     whole = small[0:8] + small[8:16]
     for k, target in enumerate((v0, v1, v2, v3)):
         target[...] = whole[k : k + 1]
-    bias[...] = whole[4:6]
-
-
-def feed_finish(got, inner, half):
-    rows = got.shape[0]
+    bias[...] = jnp.concatenate([whole[4:5], whole[5:6]], axis=1)
+    total = b[...] + got_b[...].astype(F32)
+    cut = a.shape[1]
+    rest = b.shape[1] - SEG
+    weight[:, :cut] = a[...] + got_a[...].astype(F32)
+    weight[:, cut:] = total[:, :rest]
+    small = total[:, rest:].T
+    whole = small[0:8] + small[8:16]
+    for k, target in enumerate((w0, w1, w2)):
+        target[...] = whole[k : k + 1]
+
+
+def finish(o, a, b):
+    rows = o[0].shape[0]
+    vector = shaped((1, rows), F32)
     return pl.pallas_call(
-        partial(feed_finish_kernel, inner),
-        out_shape=[shaped((rows, inner), F32)] * 2
-        + [shaped((rows, half), F32)]
-        + [shaped((1, rows), F32)] * 4
-        + [shaped((2, rows), F32)],
-        in_specs=[VM],
-        out_specs=[VM] * 8,
+        finish_kernel,
+        out_shape=[
+            shaped((rows, o[0].shape[1] - SEG), F32),
+            shaped((rows, a[0].shape[1] + b[0].shape[1] - SEG), F32),
+        ]
+        + [vector] * 4
+        + [shaped((1, 2 * rows), F32)]
+        + [vector] * 3,
+        in_specs=[VM] * 6,
+        out_specs=[VM] * 10,
         compiler_params=params(),
-        name="feed_finish",
-    )(got)
+        cost_estimate=lasting("finish"),
+        name="finish",
+    )(*o, *a, *b)
 
 
 def norm_back(hat, scale, up):
@@ -1009,45 +1304,45 @@
 
 
 def middle_back_kernel(
-    meta, middle, part, other, grad, gain, weight,
-    middle_grad, branch, vectors, g0, g1, g2, g3,
+    meta, middle, part, other, grad, gains, weight,
+    branch, vectors, g0, g1, g2, g3,
 ):
     member = meta[0]
     rows, width = middle.shape
-    step = 64
     vectors[...] = jnp.zeros_like(vectors)
 
-    def norm_step(i, _):
-        at = pl.ds(pl.multiple_of(i * step, step), step)
+    def norm_step(at):
         hat, scale = normal(middle[at, :])
         second = part[at, :].astype(F32) + other[at, :].astype(F32)
-        back = grad[at, :].astype(F32) + norm_back(hat, scale, second * gain[...].astype(F32))
-        middle_grad[at, :] = back
+        given = grad[at, :].astype(F32)
+        back = given + norm_back(hat, scale, second * gains[GAIN_F : GAIN_F + 1])
         branch[at, :] = back.astype(BF16)
         vectors[0:1, :] += jnp.sum(second * hat, axis=0, keepdims=True)
         vectors[1:2, :] += jnp.sum(second, axis=0, keepdims=True)
         vectors[2:3, :] += jnp.sum(back, axis=0, keepdims=True)
-        vectors[3:4, :] += jnp.sum(grad[at, :].astype(F32), axis=0, keepdims=True)
-        return _
-
-    lax.fori_loop(0, rows // step, norm_step, 0)
+        vectors[3:4, :] += jnp.sum(given, axis=0, keepdims=True)
+
+    norm_loop(rows, norm_step)
     for d, target in enumerate((g0, g1, g2, g3)):
         at = pl.multiple_of((member ^ d) * PAIR, PAIR)
         target[...] = dot(branch[...], weight[pl.ds(at, PAIR), :], ((1,), (1,))).astype(BF16)
 
 
-def middle_back(meta, middle, part, other, grad, gain, weight):
+def middle_back(meta, middle, part, other, grad, gains, weight, deps=()):
     rows, width = middle.shape
+    specs = [SM] + [VM] * 6
+    used = len(specs)
     outs = pl.pallas_call(
-        middle_back_kernel,
-        out_shape=[shaped((rows, width), F32), shaped((rows, width), BF16), shaped((8, width), F32)]
+        skipping(middle_back_kernel, used, len(deps)),
+        out_shape=[shaped((rows, width), BF16), shaped((8, width), F32)]
         + [shaped((rows, PAIR), BF16)] * MEMBERS,
-        in_specs=[SM] + [VM] * 6,
-        out_specs=[VM] * (3 + MEMBERS),
+        in_specs=specs + [ANY] * len(deps),
+        out_specs=[VM] * (2 + MEMBERS),
         compiler_params=params(),
+        cost_estimate=lasting("middle_back"),
         name="middle_back",
-    )(meta, middle, part, other, grad, gain, weight)
-    return outs[0], outs[1], outs[2], outs[3:]
+    )(meta, middle, part, other, grad, gains, weight, *deps)
+    return outs[0], outs[1], outs[2:]
 
 
 def join_kernel(meta, weight, q0, q1, q2, q3, k0, k1, k2, k3, joined, part, sums):
@@ -1083,55 +1378,33 @@
     lax.fori_loop(0, width // TILE, column, 0)
 
 
-def join_stage(meta, weight, query_grads, pair_grads):
+def join_stage(meta, weight, query_grads, pair_grads, deps=()):
     rows = query_grads[0].shape[0]
     width, across = weight.shape
+    specs = [SM] + [VM] * (1 + 2 * MEMBERS)
+    used = len(specs)
     return pl.pallas_call(
-        join_kernel,
+        skipping(join_kernel, used, len(deps)),
         out_shape=[
             shaped((rows, across), BF16),
             shaped((rows, width), BF16),
             shaped((8, 2 * MEMBERS * PAIR), F32),
         ],
-        in_specs=[SM] + [VM] * (1 + 2 * MEMBERS),
+        in_specs=specs + [ANY] * len(deps),
         out_specs=[VM] * 3,
         compiler_params=params(),
+        cost_estimate=lasting("join_stage"),
         name="join_stage",
-    )(meta, weight, *query_grads, *pair_grads)
-
-
-ORDERS = ((0, 1, 2, 3), (0, 2, 3, 1))
+    )(meta, weight, *query_grads, *pair_grads, *deps)
+
+
 FIRST_PART = 1024
-
-
-def block_place(relative, order):
-    place = 0
-    for bit in order:
-        place = place * 2 + (lax.shift_right_logical(relative, bit) & 1)
-    return place
-
-
-def turn_ordered(tile, target, i, device, order, share):
-    for k in range(SEG // share):
-        block = i * (SEG // share) + k
-        at = block_place(block ^ device, order) * share
-        target[pl.ds(pl.multiple_of(at, share), share), :] = tile[k * share : (k + 1) * share]
-
-
-def turn_source(source, target, device, order, share):
-    def step(i, _):
-        at = pl.ds(pl.multiple_of(i * SEG, SEG), SEG)
-        tile = source[:, at].astype(F32).T.astype(BF16)
-        turn_ordered(tile, target, i, device, order, share)
-        return _
-
-    lax.fori_loop(0, source.shape[1] // SEG, step, 0)
 
 
 def joined_first_kernel(meta, x, part, normed, joined, keep, send, vectors, turned):
     rows, width = x.shape
     device = meta[4]
-    turn_source(normed, turned, device, ORDERS[0], width // 16)
+    turn_source(normed, turned, device, X_FIRST, width // DEVICES)
     half = width // 2
     tile = TILE
 
@@ -1153,29 +1426,30 @@
     norm_loop(rows, norm_step)
 
 
-def joined_first(meta, x, part, normed, joined):
+def joined_first(meta, x, part, normed, joined, deps=()):
     rows, width = x.shape
     half = width // 2
     return pl.pallas_call(
-        joined_first_kernel,
+        skipping(joined_first_kernel, 5, len(deps)),
         out_shape=[
             shaped((half, FIRST_PART), F32),
             shaped((half, FIRST_PART), BF16),
             shaped((8, width), F32),
         ],
-        in_specs=[SM] + [VM] * 4,
+        in_specs=[SM] + [VM] * 4 + [ANY] * len(deps),
         out_specs=[VM] * 3,
         scratch_shapes=[pltpu.VMEM((width, rows), BF16)],
         compiler_params=params(),
+        cost_estimate=lasting("joined_first"),
         name="joined_first",
-    )(meta, x, part, normed, joined)
+    )(meta, x, part, normed, joined, *deps)
 
 
 def joined_second_kernel(meta, normed, joined, vectors, other, sums, keep, send, turned, small):
     width = normed.shape[1]
     device = meta[4]
-    share = width // 16
-    turn_source(normed, turned, device, ORDERS[1], share)
+    share = width // DEVICES
+    turn_source(normed, turned, device, Z_FIRST, share)
     half = width // 2
     across = joined.shape[1] - FIRST_PART
     tile = TILE
@@ -1193,75 +1467,67 @@
         rows8 = jnp.concatenate(
             [vectors[0:2, at] + other[0:2, at], sums[0:1, at], jnp.zeros((5, SEG), F32)], axis=0
         )
-        turn_ordered(in_two(rows8).T, small, i, device, ORDERS[1], share)
+        turn_ordered(in_two(rows8).T, small, i, device, Z_FIRST, share)
     keep[:, across:] = small[:half]
     send[:, across:] = small[half:].astype(BF16)
 
 
-def joined_second(meta, normed, joined, vectors, other, sums):
+def joined_second(meta, normed, joined, vectors, other, sums, deps=()):
     rows, width = normed.shape
     half = width // 2
     across = joined.shape[1] - FIRST_PART + SEG
     return pl.pallas_call(
-        joined_second_kernel,
+        skipping(joined_second_kernel, 6, len(deps)),
         out_shape=[shaped((half, across), F32), shaped((half, across), BF16)],
-        in_specs=[SM] + [VM] * 5,
+        in_specs=[SM] + [VM] * 5 + [ANY] * len(deps),
         out_specs=[VM] * 2,
         scratch_shapes=[pltpu.VMEM((width, rows), BF16), pltpu.VMEM((width, SEG), F32)],
         compiler_params=params(),
+        cost_estimate=lasting("joined_second"),
         name="joined_second",
-    )(meta, normed, joined, vectors, other, sums)
-
-
-def joined_finish_kernel(a, got_a, b, got_b, weight, v0, v1, v2):
-    total = b[...] + got_b[...].astype(F32)
-    cut = a.shape[1]
-    rest = b.shape[1] - SEG
-    weight[:, :cut] = a[...] + got_a[...].astype(F32)
-    weight[:, cut:] = total[:, :rest]
-    small = total[:, rest:].T
-    whole = small[0:8] + small[8:16]
-    for k, target in enumerate((v0, v1, v2)):
-        target[...] = whole[k : k + 1]
-
-
-def joined_finish(a, got_a, b, got_b):
-    rows = a.shape[0]
-    across = a.shape[1] + b.shape[1] - SEG
-    return pl.pallas_call(
-        joined_finish_kernel,
-        out_shape=[shaped((rows, across), F32)] + [shaped((1, rows), F32)] * 3,
-        in_specs=[VM] * 4,
-        out_specs=[VM] * 4,
-        compiler_params=params(),
-        name="joined_finish",
-    )(a, got_a, b, got_b)
-
-
-def input_back_kernel(x, part, other, gain, middle_grad, out):
-    rows = x.shape[0]
-    step = 64
-
-    def norm_step(i, _):
-        at = pl.ds(pl.multiple_of(i * step, step), step)
+    )(meta, normed, joined, vectors, other, sums, *deps)
+
+
+def input_back_kernel(x, part, other, gains, middle_grad, out):
+    def norm_step(at):
         hat, scale = normal(x[at, :].astype(F32))
         first = part[at, :].astype(F32) + other[at, :].astype(F32)
-        back = norm_back(hat, scale, first * gain[...].astype(F32))
-        out[at, :] = (back + middle_grad[at, :]).astype(BF16)
-        return _
-
-    lax.fori_loop(0, rows // step, norm_step, 0)
-
-
-def input_back(x, part, other, gain, middle_grad):
+        back = norm_back(hat, scale, first * gains[GAIN_A : GAIN_A + 1])
+        out[at, :] = (back + middle_grad[at, :].astype(F32)).astype(BF16)
+
+    norm_loop(x.shape[0], norm_step)
+
+
+def input_back(x, part, other, gains, middle_grad):
     return pl.pallas_call(
         input_back_kernel,
         out_shape=shaped(x.shape, BF16),
         in_specs=[VM] * 5,
         out_specs=VM,
         compiler_params=params(),
+        cost_estimate=lasting("input_back"),
         name="input_back",
-    )(x, part, other, gain, middle_grad)
+    )(x, part, other, gains, middle_grad)
+
+
+def stack_kernel(*refs):
+    out, at = refs[-1], 0
+    for ref in refs[:-1]:
+        rows = ref.shape[0] // out.shape[1]
+        out[at : at + rows, :] = ref[...].astype(F32).reshape(rows, out.shape[1])
+        at += rows
+
+
+def stack_vectors(*vectors):
+    width = vectors[0].shape[0]
+    rows = sum(vector.shape[0] for vector in vectors) // width
+    return pl.pallas_call(
+        stack_kernel,
+        out_shape=shaped((rows, width), F32),
+        in_specs=[VM] * len(vectors),
+        out_specs=VM,
+        name="stack_vectors",
+    )(*vectors)
 
 
 def swap(value):
@@ -1289,43 +1555,43 @@
     return [parts[0]] + [to_member(parts[d], d) for d in range(1, MEMBERS)]
 
 
+def same_kernel(*refs):
+    pass
+
+
+def after_all(value, *others):
+    return pl.pallas_call(
+        same_kernel,
+        out_shape=shaped(value.shape, value.dtype),
+        in_specs=[ANY] * (1 + len(others)),
+        out_specs=ANY,
+        input_output_aliases={0: 0},
+        cost_estimate=lasting("after_all"),
+        name="after_all",
+    )(value, *others)
+
+
 def reduce_rows(value):
     return lax.psum_scatter(value, "dp", scatter_dimension=0, tiled=True)
 
 
-def after(value, *others):
-    return lax.optimization_barrier((value, *others))[0]
-
-
-def halve(keep, send, bits):
-    for bit in bits[:-1]:
-        total = keep + to_member(send, 1 << bit).astype(F32)
-        half = total.shape[0] // 2
-        keep, send = total[:half], total[half:].astype(BF16)
-    return keep, to_member(send, 1 << bits[-1])
-
-
-def joined_sums(meta, x, part, first_low, joined_grad, sums):
-    count = lax.axis_size("dp")
-    width, across = x.shape[1], joined_grad.shape[1]
-    if count == 16:
-        keep_a, send_a, vectors = joined_first(meta, x, part, first_low, joined_grad)
-        other = swap(vectors)
-        keep_b, send_b = joined_second(meta, first_low, joined_grad, vectors, other, sums)
-        last_a = halve(keep_a, send_a, ORDERS[0])
-        last_b = halve(keep_b, send_b, ORDERS[1])
-        return joined_finish(*last_a, *last_b)
+def plain_sum(left, right):
+    grad = jnp.einsum("td,tf->df", left, right, preferred_element_type=F32)
+    return reduce_rows(grad.astype(BF16)).astype(F32)
+
+
+def plain_sums(x, part, first_low, joined_grad, sums, cotangent, hidden_low, second_low, pre_grad, branch_low, mixed, feed_vectors, extra):
     hat, _scale = normal(x.astype(F32))
     wide = part.astype(F32)
-    vectors = jnp.stack([jnp.sum(wide * hat, axis=0), jnp.sum(wide, axis=0)], axis=1)
-    vectors = jnp.concatenate([vectors + swap(vectors), sums[:1].T], axis=1)
-    grad = jnp.einsum("td,tf->df", first_low, joined_grad, preferred_element_type=F32)
-    high = vectors.astype(BF16)
-    rest = (vectors - high.astype(F32)).astype(BF16)
-    room = jnp.zeros((width, PAIR - 6), BF16)
-    got = reduce_rows(jnp.concatenate([grad.astype(BF16), high, rest, room], axis=1)).astype(F32)
-    small = got[:, across : across + 3] + got[:, across + 3 : across + 6]
-    return got[:, :across], small[:, 0], small[:, 1], small[:, 2]
+    vectors = jnp.stack([jnp.sum(wide * hat, axis=0), jnp.sum(wide, axis=0)], axis=0)
+    vectors = vectors + swap(vectors)
+    small = reduce_rows(jnp.concatenate([feed_vectors[:4], extra, vectors, sums[:1]], axis=0).T)
+    return (
+        plain_sum(cotangent, hidden_low), plain_sum(second_low, pre_grad),
+        plain_sum(branch_low, mixed), plain_sum(first_low, joined_grad),
+        small[:, 0], small[:, 1], small[:, 2], small[:, 3], small[:, 4:6].T,
+        small[:, 6], small[:, 7], small[:, 8],
+    )
 
 
 def shards(
@@ -1358,74 +1624,131 @@
     ).astype(jnp.int32)
     slopes = jnp.exp2(-8.0 * jnp.arange(1, H + 1, dtype=F32) / H)
 
-    def row(v):
-        return v.reshape(1, -1)
-
-    gain_a, shift_a = row(attention_gain), row(attention_shift)
-    gain_f, shift_f = row(feed_gain), row(feed_shift)
-
-    first_low, queries, pairs = project(
-        meta, activations, gain_a, shift_a, joined_weight, row(joined_bias)
+    vectors = stack_vectors(
+        attention_gain, attention_shift, feed_gain, feed_shift, output_bias, contract_bias,
+        joined_bias, expand_bias,
     )
+    first_low, queries, pairs = project(meta, activations, vectors, joined_weight)
     table = make_tables(meta, parent_slot)
     pairs = within(pairs)
     queries = within(queries)
-    hidden_grad = jnp.einsum("td,fd->tf", cotangent, contract_weight, preferred_element_type=F32)
-    table = after(table, hidden_grad)
     up, down = pack(table, pairs)
     below = to_group(up, 1)
     above = to_group(down, -1)
-    other_output_weight = swap(after(output_weight, up))
+    hidden_grad = product("hidden_grad", cotangent, contract_weight, True, F32, deps=(up,))
+    other_output_weight = swap(output_weight)
     kept, stats = attend_near(table, meta, slopes, queries, pairs)
-    outs, lse = attend_far(table, meta, slopes, queries, below, above, kept, stats)
+    outs, lse = attend_far(
+        table, meta, slopes, queries, below, above, kept, stats,
+        deps=(hidden_grad, other_output_weight),
+    )
     parts_other = [to_member_across(outs[d], d) for d in range(MEMBERS)]
     parts_own = within(outs)
     mixed, middle, second_low, hidden_low, pre_grad, second_part, bias_sums = feed(
-        meta, activations, row(output_bias), gain_f, shift_f, row(expand_bias),
+        meta, activations, vectors,
         parts_own, parts_other, output_weight, other_output_weight, expand_weight, hidden_grad,
     )
     second_other = swap(second_part)
-    held = feed_grads(cotangent, hidden_low, second_low, pre_grad, 2 * inner + half + SEG)
-    feed_part = jnp.dot(hidden_low, contract_weight, preferred_element_type=F32).astype(BF16)
-    second_other = after(second_other, held, feed_part)
-    middle_grad, branch_low, feed_vectors, grad_parts = middle_back(
-        meta, middle, second_part, second_other, cotangent, gain_f, output_weight
+    extra = bias_sums[0].reshape(count, 2, width // count).transpose(1, 0, 2).reshape(2, width)
+    by_halves = count == DEVICES
+    if by_halves:
+        keep_c, c0, c1, keep_e, e0, e1, feed_part = feed_grads(
+            meta, cotangent, hidden_low, second_low, pre_grad, contract_weight
+        )
+        c0, c1, e0, e1 = (to_member(part, 1) for part in (c0, c1, e0, e1))
+    else:
+        feed_part = product("feed_part", hidden_low, contract_weight, False, BF16)
+    branch_low, feed_vectors, grad_parts = middle_back(
+        meta, middle, second_part, second_other, cotangent, vectors, output_weight,
+        deps=(feed_part,),
     )
     grad_parts = within(grad_parts)
-    feed_part = after(feed_part, branch_low)
-    feed_other = swap(feed_part)
-    extra = bias_sums[0].reshape(count, 2, width // count).transpose(1, 0, 2).reshape(2, width)
-    held = output_grads(branch_low, mixed, feed_vectors, extra, held)
-    grad_parts[1] = after(grad_parts[1], held)
-    feed_sums = reduce_rows(held)
-
+    feed_other = swap(after_all(feed_part, branch_low))
+    fill = ()
+    if by_halves:
+        (keep_o, send_o), ((keep_c, send_c), (keep_e, send_e)) = output_grads(
+            meta, branch_low, mixed, feed_vectors, extra, [(keep_c, c0, c1), (keep_e, e0, e1)]
+        )
+        got_o, got_c, got_e = to_member(send_o, 1), to_member(send_c, 4), to_member(send_e, 2)
+        fill = (keep_o,)
     to_below, to_above, kept_grad = back_far(
-        table, meta, slopes, queries, below, above, outs, grad_parts, lse
+        table, meta, slopes, queries, below, above, outs, grad_parts, lse, deps=fill
     )
     from_above = to_group(to_below, -1)
     from_below = to_group(to_above, 1)
-    kept_grad = after(kept_grad, feed_other)
     query_grads, own = back_near(
-        table, meta, slopes, queries, pairs, outs, grad_parts, lse, kept_grad
+        table, meta, slopes, queries, pairs, outs, grad_parts, lse, kept_grad, deps=(feed_other,)
     )
     query_grads = within(query_grads)
     layer_output = (
-        middle + (feed_part.astype(F32) + feed_other.astype(F32)) + contract_bias.astype(F32)
+        middle + (feed_part.astype(F32) + feed_other.astype(F32)) + vectors[CONTRACT_BIAS]
     ).astype(BF16)
-    from_above = after(from_above, layer_output)
-    pair_grads = within(gather_back(table, own, from_above, from_below))
+    fill = ()
+    if by_halves:
+        (keep_c, send_c), (keep_e, send_e), (keep_o, send_o) = takes(
+            "second_step", [(keep_c, got_c), (keep_e, got_e), (keep_o, got_o)], deps=(own,)
+        )
+        got_c, got_o = to_member(send_c, 2), to_member(send_o, 2)
+        fill = (keep_o,)
+    own_pairs = gather_back(
+        table, own, from_above, from_below, deps=tuple(query_grads) + (layer_output,) + fill
+    )
+    pair_grads = within(own_pairs)
+    fill = ()
+    if by_halves:
+        got_e = to_member(after_all(send_e, own_pairs[0]), 4)
+        (keep_c, send_c), (keep_o, send_o) = takes(
+            "third_step", [(keep_c, got_c), (keep_o, got_o)], deps=(own_pairs[0],)
+        )
+        got_c, got_o = to_member(send_c, 8), to_member(send_o, 4)
+        fill = (keep_o,)
     joined_grad, first_part, joined_bias_sums = join_stage(
-        meta, joined_weight, query_grads, pair_grads
+        meta, joined_weight, query_grads, pair_grads, deps=fill
     )
     first_other = swap(first_part)
-    joined_done, gain_grad, shift_grad, joined_bias_grad = joined_sums(
-        meta, activations, first_part, first_low, joined_grad, joined_bias_sums
-    )
-    input_gradient = input_back(activations, first_part, first_other, gain_a, middle_grad)
+    input_gradient = input_back(activations, first_part, first_other, vectors, branch_low)
+    if by_halves:
+        (keep_e, send_e), (keep_o, send_o) = takes(
+            "fourth_step", [(keep_e, got_e), (keep_o, got_o)], deps=(first_part,)
+        )
+        got_e, got_o = to_member(send_e, 8), to_member(send_o, 8)
+        keep_a, send_a, norm_vectors = joined_first(
+            meta, activations, first_part, first_low, joined_grad, deps=(keep_o,)
+        )
+        got_a = to_member(send_a, 1)
+        contract_done = add(keep_c, got_c)
+        norm_other = swap(norm_vectors)
+        keep_b, send_b = joined_second(
+            meta, first_low, joined_grad, norm_vectors, norm_other, joined_bias_sums,
+            deps=(contract_done,),
+        )
+        got_b = to_member(send_b, 1)
+        (keep_a, send_a), (keep_b, send_b) = takes(
+            "fifth_step", [(keep_a, got_a), (keep_b, got_b)]
+        )
+        got_a, got_b = to_member(send_a, 2), to_member(send_b, 4)
+        (keep_a, send_a), (keep_b, send_b) = takes(
+            "sixth_step", [(keep_a, got_a), (keep_b, got_b)]
+        )
+        got_a, got_b = to_member(send_a, 4), to_member(send_b, 8)
+        expand_done = add(keep_e, got_e)
+        (keep_a, send_a), (keep_b, send_b) = takes(
+            "seventh_step", [(keep_a, got_a), (keep_b, got_b)], deps=(input_gradient, expand_done)
+        )
+        got_a, got_b = to_member(send_a, 8), to_member(send_b, 2)
+        done = (contract_done, expand_done) + tuple(
+            finish((keep_o, got_o), (keep_a, got_a), (keep_b, got_b))
+        )
+    else:
+        done = plain_sums(
+            activations, first_part, first_low, joined_grad, joined_bias_sums, cotangent,
+            hidden_low, second_low, pre_grad, branch_low, mixed, feed_vectors, extra,
+        )
     (
-        contract_done, expand_done, output_done,
+        contract_done, expand_done, output_done, joined_done,
         feed_gain_grad, feed_shift_grad, output_bias_grad, contract_bias_grad, expand_bias_grad,
-    ) = feed_finish(feed_sums, inner, half)
+        gain_grad, shift_grad, joined_bias_grad,
+    ) = done
 
     return (
         layer_output,

time: 424 us -> 378 us (0.89)
  waiting for transfers between devices: 110 us -> 58.7 us
  Pallas kernels: 211 us -> 230 us
  between operations: 14.6 us -> 1.29 us
  matrix products: 13 us -> 0 us
  starting transfers between devices: 51.3 us -> 59.9 us
    ppermute x26 -> x40, waiting for transfers between devices: 67 us -> 28.7 us  [to_member(): return lax.ppermute(value, 'dp', [(i, i ^ d) for i in range(count)])]
    pallas_call x12 -> x23, Pallas kernels: 140 us -> 165 us  [the longest x6 26.5 us: takes(): pl.pallas_call(partial(takes_kernel, flags, len(deps)), grid=(TAKE_STEPS,...]
    ppermute x26 -> x40, starting transfers between devices: 18.6 us -> 42.4 us  [to_member(): return lax.ppermute(value, 'dp', [(i, i ^ d) for i in range(count)])]
    dot_general x2 -> x0, matrix products: 13 us -> none  [the longest x1 6.86 us: shards(): jnp.einsum('td,fd->tf', cotangent, contract_weight, preferred_element_typ...]
    ppermute x4, waiting for transfers between devices: 29.7 us -> 16.8 us  [to_group(): lax.ppermute(value, 'dp', [(i, (i + step) % count) for i in range(count)])]
    ppermute x4, starting transfers between devices: 17.7 us -> 5.96 us  [to_group(): lax.ppermute(value, 'dp', [(i, (i + step) % count) for i in range(count)])]
    unnamed x94 -> x99, local copies, waits for them, and re-layouts: 9.16 us -> 19.3 us
    reshape x8 -> x0, local copies, waits for them, and re-layouts: 7.45 us -> none  [the longest x7 6.2 us: row(): return v.reshape(1, -1)]
  transfers between devices with their start and end apart: 40 -> 53, of which waited for: 19 -> 16; matrix products, arithmetic and copies ran while one was open for 5% -> 2% of each run, Pallas kernels for 38% -> 46%
where the time goes in v3:
time: 378 us; the launch traced here: 376 us
  Pallas kernels  230 us (61%)
  starting transfers between devices  59.9 us (16%)
  waiting for transfers between devices  58.7 us (16%)
  local copies, waits for them, and re-layouts  22.2 us (6%)
    ppermute x40, starting transfers between devices, to_member(): return lax.ppermute(value, 'dp', [(i, i ^ d) for i in range(count)])  42.4 us
    ppermute x40, waiting for transfers between devices, to_member(): return lax.ppermute(value, 'dp', [(i, i ^ d) for i in range(count)])  28.7 us
    pallas_call x6, Pallas kernels, takes(): pl.pallas_call(partial(takes_kernel, flags, len(deps)), grid=(TAKE_STEPS,...  26.5 us
    pallas_call x1, Pallas kernels, feed_grads(): pl.pallas_call(feed_grads_kernel, grid=(2 * tiles,), out_shape=[kept, sen...  22.3 us
    pallas_call x1, Pallas kernels, attend_far(): pl.pallas_call(skipping(attend_far_kernel, used, len(deps)), out_shape=[s...  21.9 us
    unnamed x99, local copies, waits for them, and re-layouts  19.3 us
    pallas_call x1, Pallas kernels, back_near(): pl.pallas_call(skipping(back_near_kernel, used, len(deps)), out_shape=[sh...  19.1 us
    pallas_call x1, Pallas kernels, feed(): pl.pallas_call(feed_kernel, out_shape=[shaped((rows, half), BF16), shaped...  18.7 us
  transfers between devices with their start and end apart: 53, of which 16 were waited for; matrix products, arithmetic and copies ran while one was open for 2% of the time, Pallas kernels for 46%

profile of v3, /device:TPU:0, one launch (start us, length us, event | category | flops | bytes accessed | tf_op | source)
XLA Modules:
  0.0 375.7 jit_solution(14500299224687698029)
XLA Ops:
  2.7 9.3 %project.1 = (bf16[640,1024]{1,0:T(8,128)(2,1)}, bf16[640,128]{1,0:T(8,128)(2,1)}, bf16[640,128]{1,0:T(8,128)(2,1)}, bf16[640,128]{1,0:T(8,128)(2,1)}, bf16[640,...) custom-call(s32[5]{0:T(128)} %stack.23.meta.refs_1_.refs_0_, ...), custom_call_target="tpu_custom_call" | custom-call | flops 4499999744 | tf_op jit(solution)/shard_map/project/pallas_call | solution.py:312
  17.1 8.8 %tables.1.table.refs_0_ = s32[1024]{0:T(1024)} custom-call(s32[5]{0:T(128)} %stack.23.meta.refs_1_.refs_0_, s32[80]{0:T(128)} %parent.1), custom_call_target="tpu_custom_call" | custom-call | tf_op jit(solution)/shard_map/tables/pallas_call | solution.py:244
  39.6 9.2 %hidden_grad.1.refs_11_ = f32[640,2048]{1,0:T(8,128)} custom-call(bf16[640,1024]{1,0:T(8,128)(2,1)} %refs_4_.3, bf16[2048,1024]{1,0:T(8,128)(2,1)} %weight.3, bf16[1536,256]{1,0:T(8,128)(2,1)} %copy-done), custom_call_target="tpu_custom_call" | custom-call | flops 2500000000 | tf_op jit(solution)/shard_map/hidden_grad/pallas_call | solution.py:964
  48.8 18.3 %attend_near.1 = (f32[20,128,128]{2,1,0:T(8,128)}, f32[20,8,256]{2,1,0:T(8,128)}) custom-call(s32[1024]{0:T(1024)} %tables.1.table.refs_0_, s32[5]{0:T(128)} %stack.23.meta.refs_1_.refs_0_, f32[16]{0:T(128)} %multiply_exponential_fusion.slopes.refs_2_, bf16[640,128]{1,0:T(8,128)(2,1)} %get-tuple-element.114.q0.refs_3_, bf16[640,128]{1,0:T(8,128)(2,1)} %copy-done.30, ...), custom_call_target="tpu_custom_call" | custom-call | flops 7000000000 | tf_op jit(solution)/shard_map/attend_near/pallas_call | solution.py:523
  67.2 7.3 %collective-permute-done.7.refs_8_ = bf16[1536,256]{1,0:T(8,128)(2,1)S(1)} collective-permute-done((bf16[1536,256]{1,0:T(8,128)(2,1)S(1)}, bf16[1536,256]{1,0:T(8,128)(2,1)S(1)}, u32[]{:S(2)}, u32[]{:S(2)}) %collective-permute-start.7) | collective-permute-done | bytes 786464 | tf_op jit(solution)/shard_map/ppermute | solution.py:1551
  75.4 21.9 %attend_far.1 = (bf16[640,128]{1,0:T(8,128)(2,1)}, bf16[640,128]{1,0:T(8,128)(2,1)}, bf16[640,128]{1,0:T(8,128)(2,1)}, bf16[640,128]{1,0:T(8,128)(2,1)}, f32[20,1,256]{2,1,0:T(1,128)}) custom-call(s32[1024]{0:T(1024)} %tables.1.table.refs_0_, s32[5]{0:T(128)} %stack.23.meta.refs_1_.refs_0_, f32[16]{0:T(128)} %multiply_exponential_fusion.slopes.refs_2_, ...), custom_call_target="tpu_custom_call" | custom-call | flops 7500000256 | tf_op jit(solution)/shard_map/attend_far/pallas_call | solution.py:592
  107.3 8.9 %collective-permute-done.12.b0 = bf16[640,128]{1,0:T(8,128)(2,1)S(1)} collective-permute-done((bf16[640,128]{1,0:T(8,128)(2,1)}, bf16[640,128]{1,0:T(8,128)(2,1)S(1)}, u32[]{:S(2)}, u32[]{:S(2)}) %collective-permute-start.12) | collective-permute-done | bytes 163872 | tf_op jit(solution)/shard_map/ppermute | solution.py:1545
  117.7 18.7 %feed.1 = (bf16[640,512]{1,0:T(8,128)(2,1)}, f32[640,1024]{1,0:T(8,128)}, bf16[640,1024]{1,0:T(8,128)(2,1)}, bf16[640,2048]{1,0:T(8,128)(2,1)}, bf16[640,2048]{1...) custom-call(s32[5]{0:T(128)} %stack.23.meta.refs_1_.refs_0_, bf16[640,1024]{1,0:T(8,128)(2,1)} %refs_1_.7, ...), custom_call_target="tpu_custom_call" | custom-call | flops 8999999488 | tf_op jit(solution)/shard_map/feed/pallas_call | solution.py:924
  138.0 22.3 %feed_grads.1 = (bf16[512,2048]{1,0:T(8,128)(2,1)}, bf16[512,1024]{1,0:T(8,128)(2,1)}, bf16[512,1024]{1,0:T(8,128)(2,1)}, bf16[512,2048]{1,0:T(8,128)(2,1)}, bf1...) custom-call(s32[5]{0:T(128)} %stack.23.meta.refs_1_.refs_0_, ...), custom_call_target="tpu_custom_call" | custom-call | flops 10000000000 | tf_op jit(solution)/shard_map/feed_grads/pallas_call | solution.py:1081
  168.2 8.1 %middle_back.1 = (bf16[640,1024]{1,0:T(8,128)(2,1)}, f32[8,1024]{1,0:T(8,128)}, bf16[640,128]{1,0:T(8,128)(2,1)}, bf16[640,128]{1,0:T(8,128)(2,1)}, bf16[640,128]{1,0:T(8,128)(2,1)}, /*index=5*/bf16[640,128]{1,0:T(8,128)(2,1)}) custom-call(s32[5]{0:T(128)} %stack.23.meta.refs_1_.refs_0_, f32[640,1024]{1,0:T(8,128)} %get-tuple-element.130.refs_1_, ...), custom_call_target="tpu_custom_call" | custom-call | flops 4000000000 | tf_op jit(solution)/shard_map/middle_back/pallas_call | solution.py:1335
  182.3 10.4 %output_grads.1 = (bf16[512,640]{1,0:T(8,128)(2,1)}, bf16[512,640]{1,0:T(8,128)(2,1)}, f32[256,2048]{1,0:T(8,128)}, bf16[256,2048]{1,0:T(8,128)(2,1)}, f32[256,2048]{1,0:T(8,128)}, /*index=5*/bf16[256,2048]{1,0:T(8,128)(2,1)}) custom-call(s32[5]{0:T(128)} %stack.23.meta.refs_1_.refs_0_, bf16[640,1024]{1,0:T(8,128)(2,1)} %get-tuple-element.136.refs_1_.branch.middle_grad, ...), custom_call_target="tpu_custom_call" | custom-call | flops 4499999744 | tf_op jit(solution)/shard_map/output_grads/pallas_call | solution.py:1226
  196.6 13.5 %back_far.1 = (bf16[1536,256]{1,0:T(8,128)(2,1)}, bf16[1536,256]{1,0:T(8,128)(2,1)}, f32[20,128,128]{2,1,0:T(8,128)}) custom-call(s32[1024]{0:T(1024)} %tables.1.table.refs_0_, s32[5]{0:T(128)} %stack.23.meta.refs_1_.refs_0_, f32[16]{0:T(128)} %multiply_exponential_fusion.slopes.refs_2_, bf16[640,128]{1,0:T(8,128)(2,1)} %get-tuple-element.114.q0.refs_3_, ...), custom_call_target="tpu_custom_call" | custom-call | flops 7000000000 | tf_op jit(solution)/shard_map/back_far/pallas_call | solution.py:708
  213.2 19.1 %back_near.1 = (bf16[640,128]{1,0:T(8,128)(2,1)}, bf16[640,128]{1,0:T(8,128)(2,1)}, bf16[640,128]{1,0:T(8,128)(2,1)}, bf16[640,128]{1,0:T(8,128)(2,1)}, f32[2560,256]{1,0:T(8,128)}) custom-call(s32[1024]{0:T(1024)} %tables.1.table.refs_0_, s32[5]{0:T(128)} %stack.23.meta.refs_1_.refs_0_, f32[16]{0:T(128)} %multiply_exponential_fusion.slopes.refs_2_, ...), custom_call_target="tpu_custom_call" | custom-call | flops 7500000256 | tf_op jit(solution)/shard_map/back_near/pallas_call | solution.py:771
  234.9 6.2 %second_step.1 = (f32[128,2048]{1,0:T(8,128)}, bf16[128,2048]{1,0:T(8,128)(2,1)}, f32[128,2048]{1,0:T(8,128)}, bf16[128,2048]{1,0:T(8,128)(2,1)}, f32[256,640]{1,0:T(8,128)}, /*index=5*/bf16[256,640]{1,0:T(8,128)(2,1)}) custom-call(f32[256,2048]{1,0:T(8,128)} %get-tuple-element.160.refs_0_, bf16[256,2048]{1,0:T(8,128)(2,1)} %copy-done.9, ...), custom_call_target="tpu_custom_call" | custom-call | flops 2500000000 | tf_op jit(solution)/shard_map/second_step/pallas_call | solution.py:1154
  245.0 9.5 %collective-permute-done.29.refs_3_ = bf16[1536,256]{1,0:T(8,128)(2,1)} collective-permute-done((bf16[1536,256]{1,0:T(8,128)(2,1)}, bf16[1536,256]{1,0:T(8,128)(2,1)}, u32[]{:S(2)}, u32[]{:S(2)}) %collective-permute-start.29) | collective-permute-done | bytes 786464 | tf_op jit(solution)/shard_map/ppermute | solution.py:1551
  278.3 7.3 %join_stage.1 = (bf16[640,1536]{1,0:T(8,128)(2,1)}, bf16[640,1024]{1,0:T(8,128)(2,1)}, f32[8,1024]{1,0:T(8,128)}) custom-call(s32[5]{0:T(128)} %stack.23.meta.refs_1_.refs_0_, bf16[1024,1536]{1,0:T(8,128)(2,1)} %refs_1_.6, bf16[640,128]{1,0:T(8,128)(2,1)} %get-tuple-element.153.refs_4_.refs_2_, bf16[640,128]{1,0:T(8,128)(2,1)} %collective-permute-done.25.refs_5_.refs_3_, ...), custom_call_target="tpu_custom_call" | custom-call | flops 3500000000 | tf_op jit(solution)/shard_map/join_stage/pallas_call | solution.py:1386
  290.6 9.0 %joined_first.1 = (f32[512,1024]{1,0:T(8,128)}, bf16[512,1024]{1,0:T(8,128)(2,1)}, f32[8,1024]{1,0:T(8,128)}) custom-call(s32[5]{0:T(128)} %stack.23.meta.refs_1_.refs_0_, bf16[640,1024]{1,0:T(8,128)(2,1)} %refs_1_.7, bf16[640,1024]{1,0:T(8,128)(2,1)} %get-tuple-element.174.part.refs_4_.refs_2_, bf16[640,1024]{1,0:T(8,128)(2,1)} %get-tuple-element.180.refs_3_.refs_1_, ...), custom_call_target="tpu_custom_call" | custom-call | flops 4499999744 | tf_op jit(solution)/shard_map/joined_first/pallas_call | solution.py:1432
  304.6 5.8 %joined_second.1 = (f32[512,640]{1,0:T(8,128)}, bf16[512,640]{1,0:T(8,128)(2,1)}) custom-call(s32[5]{0:T(128)} %stack.23.meta.refs_1_.refs_0_, bf16[640,1024]{1,0:T(8,128)(2,1)} %get-tuple-element.180.refs_3_.refs_1_, bf16[640,1536]{1,0:T(8,128)(2,1)} %get-tuple-element.181.refs_4_.refs_2_, f32[8,1024]{1,0:T(8,128)} %get-tuple-element.184.refs_3_, ...), custom_call_target="tpu_custom_call" | custom-call | flops 3000000000 | tf_op jit(solution)/shard_map/joined_second/pallas_call | solution.py:1479
  314.6 5.0 %fifth_step.1 = (f32[256,1024]{1,0:T(8,128)}, bf16[256,1024]{1,0:T(8,128)(2,1)}, f32[256,640]{1,0:T(8,128)}, bf16[256,640]{1,0:T(8,128)(2,1)}) custom-call(f32[512,1024]{1,0:T(8,128)} %get-tuple-element.182.refs_0_, bf16[512,1024]{1,0:T(8,128)(2,1)} %copy-done.15, f32[512,640]{1,0:T(8,128)} %get-tuple-element.188.refs_2_, bf16[512,640]{1,0:T(8,128)(2,1)} %copy-done.18), custom_call_target="tpu_custom_call" | custom-call | flops 2000000000 | tf_op jit(solution)/shard_map/fifth_step/pallas_call | solution.py:1154
  320.7 5.2 %collective-permute-start.50 = (bf16[64,2048]{1,0:T(8,128)(2,1)S(1)}, bf16[64,2048]{1,0:T(8,128)(2,1)S(1)}, u32[]{:S(2)}, u32[]{:S(2)}) collective-permute-start(bf16[64,2048]{1,0:T(8,128)(2,1)S(1)} %copy-done.26), channel_id=1, source_target_pairs={{0,16},{2,18},{4,20},{6,22},{8,24},{10,26},{12,28},{14,30},{16,0},... | collective-permute-start | bytes 786440 | tf_op jit(solution)/shard_map/ppermute | solution.py:1539
  325.9 7.6 %collective-permute-done.50.got = bf16[64,2048]{1,0:T(8,128)(2,1)S(1)} collective-permute-done((bf16[64,2048]{1,0:T(8,128)(2,1)S(1)}, bf16[64,2048]{1,0:T(8,128)(2,1)S(1)}, u32[]{:S(2)}, u32[]{:S(2)}) %collective-permute-start.50) | collective-permute-done | bytes 262176 | tf_op jit(solution)/shard_map/ppermute | solution.py:1539
  341.1 6.1 %collective-permute-start.48 = (bf16[128,1024]{1,0:T(8,128)(2,1)}, bf16[128,1024]{1,0:T(8,128)(2,1)S(1)}, u32[]{:S(2)}, u32[]{:S(2)}) collective-permute-start(bf16[128,1024]{1,0:T(8,128)(2,1)} %get-tuple-element.195), channel_id=1, source_target_pairs={{0,8},{2,10},{4,12},{6,14},{8,0},{10,2},{12,4},{14,6},{16,24},{18,... | collective-permute-start | bytes 786440 | tf_op jit(solution)/shard_map/ppermute | solution.py:1539
  349.6 5.8 %input_back.1.refs_4_ = bf16[640,1024]{1,0:T(8,128)(2,1)} custom-call(bf16[640,1024]{1,0:T(8,128)(2,1)} %refs_1_.7, bf16[640,1024]{1,0:T(8,128)(2,1)} %get-tuple-element.174.part.refs_4_.refs_2_, bf16[640,1024]{1,0:T(8,128)(2,1)} %copy-done.12, f32[9,1024]{1,0:T(8,128)} %stack_vectors.1.vectors.refs_5_.gains, ...), custom_call_target="tpu_custom_call" | custom-call | flops 3000000000 | tf_op jit(solution)/shard_map/input_back/pallas_call | solution.py:1502
  365.5 7.1 %collective-permute-done.41.got_o = bf16[64,640]{1,0:T(8,128)(2,1)S(1)} collective-permute-done((bf16[64,640]{1,0:T(8,128)(2,1)S(1)}, bf16[64,640]{1,0:T(8,128)(2,1)S(1)}, u32[]{:S(2)}, u32[]{:S(2)}) %collective-permute-start.41) | collective-permute-done | bytes 81952 | tf_op jit(solution)/shard_map/ppermute | solution.py:1539
  (218 shorter events, 123.8 us)
Async XLA Ops:
  15.1 22.3 %collective-permute-start = (bf16[640,128]{1,0:T(8,128)(2,1)}, bf16[640,128]{1,0:T(8,128)(2,1)S(1)}, u32[]{:S(2)}, u32[]{:S(2)}) collective-permute-start(bf16[640,128]{1,0:T(8,128)(2,1)} %get-tuple-element.115), channel_id=1, source_target_pairs={{0,2},{2,0},{4,6},{6,4},{8,10},{10,8},{12,14},{14,12},{16,18},{18,... | collective-permute-start | bytes 491528 | tf_op jit(solution)/shard_map/ppermute | solution.py:1539
  15.2 33.6 %collective-permute-start.1 = (bf16[640,128]{1,0:T(8,128)(2,1)}, bf16[640,128]{1,0:T(8,128)(2,1)}, u32[]{:S(2)}, u32[]{:S(2)}) collective-permute-start(bf16[640,128]{1,0:T(8,128)(2,1)} %get-tuple-element.116), channel_id=1, source_target_pairs={{0,4},{2,6},{4,0},{6,2},{8,12},{10,14},{12,8},{14,10},{16,20},{18,... | collective-permute-start | bytes 491528 | tf_op jit(solution)/shard_map/ppermute | solution.py:1539
  26.5 22.3 %collective-permute-start.2 = (bf16[640,128]{1,0:T(8,128)(2,1)}, bf16[640,128]{1,0:T(8,128)(2,1)}, u32[]{:S(2)}, u32[]{:S(2)}) collective-permute-start(bf16[640,128]{1,0:T(8,128)(2,1)} %get-tuple-element.117), channel_id=1, source_target_pairs={{0,6},{2,4},{4,2},{6,0},{8,14},{10,12},{12,10},{14,8},{16,22},{18,... | collective-permute-start | bytes 491528 | tf_op jit(solution)/shard_map/ppermute | solution.py:1539
  26.5 40.6 %collective-permute-start.8 = (bf16[512,1024]{1,0:T(8,128)(2,1)}, bf16[512,1024]{1,0:T(8,128)(2,1)}, u32[]{:S(2)}, u32[]{:S(2)}) collective-permute-start(bf16[512,1024]{1,0:T(8,128)(2,1)} %refs_6_.3), channel_id=1, source_target_pairs={{0,1},{1,0},{2,3},{3,2},{4,5},{5,4},{6,7},{7,6},{8,9},{9,8},{10,11... | collective-permute-start | bytes 3145736 | tf_op jit(solution)/shard_map/ppermute | solution.py:1534
  35.7 31.4 %collective-permute-start.6 = (bf16[1536,256]{1,0:T(8,128)(2,1)S(1)}, bf16[1536,256]{1,0:T(8,128)(2,1)S(1)}, u32[]{:S(2)}, u32[]{:S(2)}) collective-permute-start(bf16[1536,256]{1,0:T(8,128)(2,1)S(1)} %get-tuple-element.122.refs_2_), channel_id=1, source_target_pairs={{0,8},{2,10},{4,12},{6,14},{8,16},{10,18},{12,20},{14,22},{16,24},... | collective-permute-start | bytes 2359304 | tf_op jit(solution)/shard_map/ppermute | solution.py:1551
  37.4 37.0 %collective-permute-start.7 = (bf16[1536,256]{1,0:T(8,128)(2,1)S(1)}, bf16[1536,256]{1,0:T(8,128)(2,1)S(1)}, u32[]{:S(2)}, u32[]{:S(2)}) collective-permute-start(bf16[1536,256]{1,0:T(8,128)(2,1)S(1)} %get-tuple-element.123), channel_id=1, source_target_pairs={{0,24},{2,26},{4,28},{6,30},{8,0},{10,2},{12,4},{14,6},{16,8},{18,... | collective-permute-start | bytes 2359304 | tf_op jit(solution)/shard_map/ppermute | solution.py:1551
  136.4 30.8 %collective-permute-start.16 = (bf16[640,1024]{1,0:T(8,128)(2,1)}, bf16[640,1024]{1,0:T(8,128)(2,1)S(1)}, u32[]{:S(2)}, u32[]{:S(2)}) collective-permute-start(bf16[640,1024]{1,0:T(8,128)(2,1)} %get-tuple-element.135.refs_2_), channel_id=1, source_target_pairs={{0,1},{1,0},{2,3},{3,2},{4,5},{5,4},{6,7},{7,6},{8,9},{9,8},{10,11... | collective-permute-start | bytes 3932168 | tf_op jit(solution)/shard_map/ppermute | solution.py:1534
  160.2 20.1 %collective-permute-start.21 = (bf16[512,1024]{1,0:T(8,128)(2,1)}, bf16[512,1024]{1,0:T(8,128)(2,1)S(1)}, u32[]{:S(2)}, u32[]{:S(2)}) collective-permute-start(bf16[512,1024]{1,0:T(8,128)(2,1)} %get-tuple-element.146), channel_id=1, source_target_pairs={{0,2},{2,0},{4,6},{6,4},{8,10},{10,8},{12,14},{14,12},{16,18},{18,... | collective-permute-start | bytes 3145736 | tf_op jit(solution)/shard_map/ppermute | solution.py:1539
  160.3 20.1 %collective-permute-start.22 = (bf16[512,1024]{1,0:T(8,128)(2,1)}, bf16[512,1024]{1,0:T(8,128)(2,1)}, u32[]{:S(2)}, u32[]{:S(2)}) collective-permute-start(bf16[512,1024]{1,0:T(8,128)(2,1)} %get-tuple-element.147), channel_id=1, source_target_pairs={{0,2},{2,0},{4,6},{6,4},{8,10},{10,8},{12,14},{14,12},{16,18},{18,... | collective-permute-start | bytes 3145736 | tf_op jit(solution)/shard_map/ppermute | solution.py:1539
  160.8 20.2 %collective-permute-start.23 = (bf16[512,1024]{1,0:T(8,128)(2,1)}, bf16[512,1024]{1,0:T(8,128)(2,1)}, u32[]{:S(2)}, u32[]{:S(2)}) collective-permute-start(bf16[512,1024]{1,0:T(8,128)(2,1)} %get-tuple-element.149), channel_id=1, source_target_pairs={{0,2},{2,0},{4,6},{6,4},{8,10},{10,8},{12,14},{14,12},{16,18},{18,... | collective-permute-start | bytes 3145736 | tf_op jit(solution)/shard_map/ppermute | solution.py:1539
  160.9 21.4 %collective-permute-start.24 = (bf16[512,1024]{1,0:T(8,128)(2,1)}, bf16[512,1024]{1,0:T(8,128)(2,1)}, u32[]{:S(2)}, u32[]{:S(2)}) collective-permute-start(bf16[512,1024]{1,0:T(8,128)(2,1)} %get-tuple-element.150), channel_id=1, source_target_pairs={{0,2},{2,0},{4,6},{6,4},{8,10},{10,8},{12,14},{14,12},{16,18},{18,... | collective-permute-start | bytes 3145736 | tf_op jit(solution)/shard_map/ppermute | solution.py:1539
  176.4 35.7 %collective-permute-start.17 = (bf16[640,1024]{1,0:T(8,128)(2,1)}, bf16[640,1024]{1,0:T(8,128)(2,1)S(1)}, u32[]{:S(2)}, u32[]{:S(2)}) collective-permute-start(bf16[640,1024]{1,0:T(8,128)(2,1)} %after_all.2), channel_id=1, source_target_pairs={{0,1},{1,0},{2,3},{3,2},{4,5},{5,4},{6,7},{7,6},{8,9},{9,8},{10,11... | collective-permute-start | bytes 3932168 | tf_op jit(solution)/shard_map/ppermute | solution.py:1534
  192.7 39.8 %collective-permute-start.30 = (bf16[256,2048]{1,0:T(8,128)(2,1)}, bf16[256,2048]{1,0:T(8,128)(2,1)S(1)}, u32[]{:S(2)}, u32[]{:S(2)}) collective-permute-start(bf16[256,2048]{1,0:T(8,128)(2,1)} %get-tuple-element.161), channel_id=1, source_target_pairs={{0,8},{2,10},{4,12},{6,14},{8,0},{10,2},{12,4},{14,6},{16,24},{18,... | collective-permute-start | bytes 3145736 | tf_op jit(solution)/shard_map/ppermute | solution.py:1539
  195.4 38.6 %collective-permute-start.31 = (bf16[256,2048]{1,0:T(8,128)(2,1)}, bf16[256,2048]{1,0:T(8,128)(2,1)S(1)}, u32[]{:S(2)}, u32[]{:S(2)}) collective-permute-start(bf16[256,2048]{1,0:T(8,128)(2,1)} %get-tuple-element.163), channel_id=1, source_target_pairs={{0,4},{2,6},{4,0},{6,2},{8,12},{10,14},{12,8},{14,10},{16,20},{18,... | collective-permute-start | bytes 3145736 | tf_op jit(solution)/shard_map/ppermute | solution.py:1539
  195.9 36.4 %collective-permute-start.32 = (bf16[512,640]{1,0:T(8,128)(2,1)}, bf16[512,640]{1,0:T(8,128)(2,1)}, u32[]{:S(2)}, u32[]{:S(2)}) collective-permute-start(bf16[512,640]{1,0:T(8,128)(2,1)} %get-tuple-element.164), channel_id=1, source_target_pairs={{0,2},{2,0},{4,6},{6,4},{8,10},{10,8},{12,14},{14,12},{16,18},{18,... | collective-permute-start | bytes 1966088 | tf_op jit(solution)/shard_map/ppermute | solution.py:1539
  210.1 31.0 %collective-permute-start.28 = (bf16[1536,256]{1,0:T(8,128)(2,1)}, bf16[1536,256]{1,0:T(8,128)(2,1)}, u32[]{:S(2)}, u32[]{:S(2)}) collective-permute-start(bf16[1536,256]{1,0:T(8,128)(2,1)} %get-tuple-element.158), channel_id=1, source_target_pairs={{0,24},{2,26},{4,28},{6,30},{8,0},{10,2},{12,4},{14,6},{16,8},{18,... | collective-permute-start | bytes 2359304 | tf_op jit(solution)/shard_map/ppermute | solution.py:1551
  212.1 42.4 %collective-permute-start.29 = (bf16[1536,256]{1,0:T(8,128)(2,1)}, bf16[1536,256]{1,0:T(8,128)(2,1)}, u32[]{:S(2)}, u32[]{:S(2)}) collective-permute-start(bf16[1536,256]{1,0:T(8,128)(2,1)} %get-tuple-element.159), channel_id=1, source_target_pairs={{0,8},{2,10},{4,12},{6,14},{8,16},{10,18},{12,20},{14,22},{16,24},... | collective-permute-start | bytes 2359304 | tf_op jit(solution)/shard_map/ppermute | solution.py:1551
  232.3 22.9 %collective-permute-start.25 = (bf16[640,128]{1,0:T(8,128)(2,1)}, bf16[640,128]{1,0:T(8,128)(2,1)}, u32[]{:S(2)}, u32[]{:S(2)}) collective-permute-start(bf16[640,128]{1,0:T(8,128)(2,1)} %get-tuple-element.154), channel_id=1, source_target_pairs={{0,2},{2,0},{4,6},{6,4},{8,10},{10,8},{12,14},{14,12},{16,18},{18,... | collective-permute-start | bytes 491528 | tf_op jit(solution)/shard_map/ppermute | solution.py:1539
  232.5 22.6 %collective-permute-start.26 = (bf16[640,128]{1,0:T(8,128)(2,1)}, bf16[640,128]{1,0:T(8,128)(2,1)}, u32[]{:S(2)}, u32[]{:S(2)}) collective-permute-start(bf16[640,128]{1,0:T(8,128)(2,1)} %get-tuple-element.155), channel_id=1, source_target_pairs={{0,4},{2,6},{4,0},{6,2},{8,12},{10,14},{12,8},{14,10},{16,20},{18,... | collective-permute-start | bytes 491528 | tf_op jit(solution)/shard_map/ppermute | solution.py:1539
  233.9 21.2 %collective-permute-start.27 = (bf16[640,128]{1,0:T(8,128)(2,1)}, bf16[640,128]{1,0:T(8,128)(2,1)}, u32[]{:S(2)}, u32[]{:S(2)}) collective-permute-start(bf16[640,128]{1,0:T(8,128)(2,1)} %get-tuple-element.156), channel_id=1, source_target_pairs={{0,6},{2,4},{4,2},{6,0},{8,14},{10,12},{12,10},{14,8},{16,22},{18,... | collective-permute-start | bytes 491528 | tf_op jit(solution)/shard_map/ppermute | solution.py:1539
  241.1 23.6 %collective-permute-start.36 = (bf16[128,2048]{1,0:T(8,128)(2,1)}, bf16[128,2048]{1,0:T(8,128)(2,1)}, u32[]{:S(2)}, u32[]{:S(2)}) collective-permute-start(bf16[128,2048]{1,0:T(8,128)(2,1)} %get-tuple-element.171), channel_id=1, source_target_pairs={{0,4},{2,6},{4,0},{6,2},{8,12},{10,14},{12,8},{14,10},{16,20},{18,... | collective-permute-start | bytes 1572872 | tf_op jit(solution)/shard_map/ppermute | solution.py:1539
  264.8 20.8 %collective-permute-start.39 = (bf16[128,2048]{1,0:T(8,128)(2,1)}, bf16[128,2048]{1,0:T(8,128)(2,1)S(1)}, u32[]{:S(2)}, u32[]{:S(2)}) collective-permute-start(bf16[128,2048]{1,0:T(8,128)(2,1)} %after_all.3), channel_id=1, source_target_pairs={{0,8},{2,10},{4,12},{6,14},{8,0},{10,2},{12,4},{14,6},{16,24},{18,... | collective-permute-start | bytes 1572872 | tf_op jit(solution)/shard_map/ppermute | solution.py:1539
  270.9 29.7 %collective-permute-start.44 = (bf16[64,2048]{1,0:T(8,128)(2,1)}, bf16[64,2048]{1,0:T(8,128)(2,1)S(1)}, u32[]{:S(2)}, u32[]{:S(2)}) collective-permute-start(bf16[64,2048]{1,0:T(8,128)(2,1)} %get-tuple-element.187), channel_id=1, source_target_pairs={{0,16},{2,18},{4,20},{6,22},{8,24},{10,26},{12,28},{14,30},{16,0},... | collective-permute-start | bytes 786440 | tf_op jit(solution)/shard_map/ppermute | solution.py:1539
  310.5 38.0 %collective-permute-start.38 = (bf16[640,1024]{1,0:T(8,128)(2,1)S(1)}, bf16[640,1024]{1,0:T(8,128)(2,1)S(1)}, u32[]{:S(2)}, u32[]{:S(2)}) collective-permute-start(bf16[640,1024]{1,0:T(8,128)(2,1)S(1)} %copy-done.11), channel_id=1, source_target_pairs={{0,1},{1,0},{2,3},{3,2},{4,5},{5,4},{6,7},{7,6},{8,9},{9,8},{10,11... | collective-permute-start | bytes 3932168 | tf_op jit(solution)/shard_map/ppermute | solution.py:1534
  (78 other events, 510.6 us)

commit v4 on v3

--- a/solution.py
+++ b/solution.py
@@ -54,8 +54,7 @@
     "project": 9, "tables": 9, "pack": 4, "attend_near": 14, "hidden_grad": 5, "attend_far": 15,
     "feed": 18, "feed_grads": 20, "middle_back": 8, "output_grads": 9, "back_far": 14,
     "back_near": 15, "second_step": 5, "gather_back": 5, "third_step": 3, "join_stage": 7,
-    "joined_first": 9, "joined_second": 6, "fourth_step": 3, "fifth_step": 4,
-    "sixth_step": 2, "seventh_step": 2, "add": 1,
+    "joined_first": 9, "joined_second": 60, "first_sums": 1, "second_sums": 1,
     "input_back": 6, "finish": 2, "feed_part": 4, "after_all": 0,
 }
 FLOPS_PER_US = 500_000_000
@@ -989,6 +988,7 @@
 X_FIRST = (0, 1, 2, 3)
 Z_FIRST = (0, 2, 3, 1)
 MIXED = (0, 2, 1, 3)
+Z_BLOCKS = (8, 4, 12)
 DEVICES = 16
 
 
@@ -1238,30 +1238,68 @@
     return (got[0], got[1]), [tuple(got[2 + 2 * k : 4 + 2 * k]) for k in range(len(pairs))]
 
 
-def add_kernel(keep, got, out):
-    out[...] = keep[...] + got[...].astype(F32)
-
-
-def add(keep, got):
+def first_sums_kernel(
+    a, got_a, b, got_b, last_b, stay_a, leave_a, stay_b, b1, b2, b3
+):
+    add_half(a, got_a, stay_a, leave_a)
+    rows = stay_b.shape[0]
+    cut = got_b.shape[1]
+    for cols, got in ((slice(0, cut), got_b), (slice(cut, b.shape[1]), last_b)):
+        stay_b[:, cols] = b[:rows, cols].astype(F32) + got[:rows].astype(F32)
+        for k, target in enumerate((b1, b2, b3)):
+            at = slice((k + 1) * rows, (k + 2) * rows)
+            target[:, cols] = (b[at, cols].astype(F32) + got[at].astype(F32)).astype(BF16)
+
+
+def first_sums(a, b):
+    half, across_a = a[0].shape
+    across_b = b[0].shape[1]
+    part_a, part_b = (half // 2, across_a), (half // 4, across_b)
     return pl.pallas_call(
-        add_kernel,
-        out_shape=shaped(keep.shape, F32),
-        in_specs=[VM] * 2,
-        out_specs=VM,
+        first_sums_kernel,
+        out_shape=[shaped(part_a, F32), shaped(part_a, BF16), shaped(part_b, F32)]
+        + [shaped(part_b, BF16)] * 3,
+        in_specs=[VM] * 5,
+        out_specs=[VM] * 6,
         compiler_params=params(),
-        cost_estimate=lasting("add"),
-        name="add",
-    )(keep, got)
-
-
-def finish_kernel(
-    o, got_o, a, got_a, b, got_b,
-    output, weight, v0, v1, v2, v3, bias, w0, w1, w2,
-):
-    total = o[...] + got_o[...].astype(F32)
+        cost_estimate=lasting("first_sums"),
+        name="first_sums",
+    )(*a, *b)
+
+
+def second_sums_kernel(a, got_a, b, g1, g2, g3, stay_a, a1, a2, a3, stay_b, leave_b):
+    rows = stay_a.shape[0]
+    stay_a[...] = a[:rows] + got_a[:rows].astype(F32)
+    for k, target in enumerate((a1, a2, a3)):
+        at = slice((k + 1) * rows, (k + 2) * rows)
+        target[...] = (a[at] + got_a[at].astype(F32)).astype(BF16)
+    total = b[...] + g1[...].astype(F32) + g2[...].astype(F32) + g3[...].astype(F32)
+    half = stay_b.shape[0]
+    stay_b[...] = total[:half]
+    leave_b[...] = total[half:].astype(BF16)
+
+
+def second_sums(a, b, got_b, deps=()):
+    rows, across_a = a[0].shape
+    half, across_b = b.shape
+    part_a, part_b = (rows // 4, across_a), (half // 2, across_b)
+    return pl.pallas_call(
+        skipping(second_sums_kernel, 6, len(deps)),
+        out_shape=[shaped(part_a, F32)]
+        + [shaped(part_a, BF16)] * 3
+        + [shaped(part_b, F32), shaped(part_b, BF16)],
+        in_specs=[VM] * 6 + [ANY] * len(deps),
+        out_specs=[VM] * 6,
+        compiler_params=params(),
+        cost_estimate=lasting("second_sums"),
+        name="second_sums",
+    )(*a, b, *got_b, *deps)
+
+
+def finish_kernel(o, a, g1, g2, g3, b, got_b, output, weight, v0, v1, v2, v3, bias, w0, w1, w2):
     across = output.shape[1]
-    output[...] = total[:, :across]
-    small = total[:, across:].T
+    output[...] = o[:, :across]
+    small = o[:, across:].T
     whole = small[0:8] + small[8:16]
     for k, target in enumerate((v0, v1, v2, v3)):
         target[...] = whole[k : k + 1]
@@ -1269,7 +1307,7 @@
     total = b[...] + got_b[...].astype(F32)
     cut = a.shape[1]
     rest = b.shape[1] - SEG
-    weight[:, :cut] = a[...] + got_a[...].astype(F32)
+    weight[:, :cut] = a[...] + g1[...].astype(F32) + g2[...].astype(F32) + g3[...].astype(F32)
     weight[:, cut:] = total[:, :rest]
     small = total[:, rest:].T
     whole = small[0:8] + small[8:16]
@@ -1277,24 +1315,24 @@
         target[...] = whole[k : k + 1]
 
 
-def finish(o, a, b):
-    rows = o[0].shape[0]
+def finish(o, a, got_a, b, got_b):
+    rows = o.shape[0]
     vector = shaped((1, rows), F32)
     return pl.pallas_call(
         finish_kernel,
         out_shape=[
-            shaped((rows, o[0].shape[1] - SEG), F32),
-            shaped((rows, a[0].shape[1] + b[0].shape[1] - SEG), F32),
+            shaped((rows, o.shape[1] - SEG), F32),
+            shaped((rows, a.shape[1] + b.shape[1] - SEG), F32),
         ]
         + [vector] * 4
         + [shaped((1, 2 * rows), F32)]
         + [vector] * 3,
-        in_specs=[VM] * 6,
+        in_specs=[VM] * 7,
         out_specs=[VM] * 10,
         compiler_params=params(),
         cost_estimate=lasting("finish"),
         name="finish",
-    )(*o, *a, *b)
+    )(o, a, *got_a, b, got_b)
 
 
 def norm_back(hat, scale, up):
@@ -1345,7 +1383,14 @@
     return outs[0], outs[1], outs[2:]
 
 
-def join_kernel(meta, weight, q0, q1, q2, q3, k0, k1, k2, k3, joined, part, sums):
+def join_kernel(riders, meta, weight, q0, q1, q2, q3, k0, k1, k2, k3, *refs):
+    joined, part, sums = refs[2 * riders : 2 * riders + 3]
+    at = 0
+    for k in range(riders):
+        keep, got, stay = refs[2 * k], refs[2 * k + 1], refs[2 * riders + 3 + k]
+        leave = refs[-1].at[:, at : at + keep.shape[1]]
+        add_half(keep, got, stay, leave)
+        at += keep.shape[1]
     member = meta[0]
     low = lanes((1, PAIR)) < HD
     for d, (query, both) in enumerate(((q0, k0), (q1, k1), (q2, k2), (q3, k3))):
@@ -1378,24 +1423,27 @@
     lax.fori_loop(0, width // TILE, column, 0)
 
 
-def join_stage(meta, weight, query_grads, pair_grads, deps=()):
+def join_stage(meta, weight, query_grads, pair_grads, riders=()):
     rows = query_grads[0].shape[0]
     width, across = weight.shape
-    specs = [SM] + [VM] * (1 + 2 * MEMBERS)
-    used = len(specs)
+    outs = [
+        shaped((rows, across), BF16),
+        shaped((rows, width), BF16),
+        shaped((8, 2 * MEMBERS * PAIR), F32),
+    ]
+    if riders:
+        half = riders[0][0].shape[0] // 2
+        outs += [shaped((half, keep.shape[1]), F32) for keep, _got in riders]
+        outs.append(shaped((half, sum(keep.shape[1] for keep, _got in riders)), BF16))
     return pl.pallas_call(
-        skipping(join_kernel, used, len(deps)),
-        out_shape=[
-            shaped((rows, across), BF16),
-            shaped((rows, width), BF16),
-            shaped((8, 2 * MEMBERS * PAIR), F32),
-        ],
-        in_specs=specs + [ANY] * len(deps),
-        out_specs=[VM] * 3,
+        partial(join_kernel, len(riders)),
+        out_shape=outs,
+        in_specs=[SM] + [VM] * (1 + 2 * MEMBERS + 2 * len(riders)),
+        out_specs=[VM] * len(outs),
         compiler_params=params(),
         cost_estimate=lasting("join_stage"),
         name="join_stage",
-    )(meta, weight, *query_grads, *pair_grads, *deps)
+    )(meta, weight, *query_grads, *pair_grads, *[part for pair in riders for part in pair])
 
 
 FIRST_PART = 1024
@@ -1410,7 +1458,7 @@
 
     def column(t, _):
         at = pl.ds(pl.multiple_of(t * tile, tile), tile)
-        keep[:, at] = dot(turned[:half], joined[:, at])
+        keep[:, at] = dot(turned[:half], joined[:, at]).astype(BF16)
         send[:, at] = dot(turned[half:], joined[:, at]).astype(BF16)
         return _
 
@@ -1432,7 +1480,7 @@
     return pl.pallas_call(
         skipping(joined_first_kernel, 5, len(deps)),
         out_shape=[
-            shaped((half, FIRST_PART), F32),
+            shaped((half, FIRST_PART), BF16),
             shaped((half, FIRST_PART), BF16),
             shaped((8, width), F32),
         ],
@@ -1445,7 +1493,14 @@
     )(meta, x, part, normed, joined, *deps)
 
 
-def joined_second_kernel(meta, normed, joined, vectors, other, sums, keep, send, turned, small):
+def joined_second_kernel(
+    meta, normed, joined, vectors, other, sums, c, got_c, e, o, got_eo,
+    keep, send, last, contract, expand, output, turned, small,
+):
+    contract[...] = c[...] + got_c[...].astype(F32)
+    inner = e.shape[1]
+    expand[...] = e[...] + got_eo[:, :inner].astype(F32)
+    output[...] = o[...] + got_eo[:, inner:].astype(F32)
     width = normed.shape[1]
     device = meta[4]
     share = width // DEVICES
@@ -1457,8 +1512,16 @@
     def column(t, _):
         at = pl.ds(pl.multiple_of(t * tile, tile), tile)
         source = pl.ds(pl.multiple_of(FIRST_PART + t * tile, tile), tile)
-        keep[:, at] = dot(turned[:half], joined[:, source])
-        send[:, at] = dot(turned[half:], joined[:, source]).astype(BF16)
+        keep[:, at] = dot(turned[:half], joined[:, source]).astype(BF16)
+        leave = dot(turned[half:], joined[:, source]).astype(BF16)
+
+        @pl.when(t == 0)
+        def _first():
+            send[...] = leave
+
+        @pl.when(t == 1)
+        def _last():
+            last[:, :tile] = leave
         return _
 
     lax.fori_loop(0, across // tile, column, 0)
@@ -1468,24 +1531,31 @@
             [vectors[0:2, at] + other[0:2, at], sums[0:1, at], jnp.zeros((5, SEG), F32)], axis=0
         )
         turn_ordered(in_two(rows8).T, small, i, device, Z_FIRST, share)
-    keep[:, across:] = small[:half]
-    send[:, across:] = small[half:].astype(BF16)
-
-
-def joined_second(meta, normed, joined, vectors, other, sums, deps=()):
+    keep[:, across:] = small[:half].astype(BF16)
+    last[:, tile:] = small[half:].astype(BF16)
+
+
+def joined_second(meta, normed, joined, vectors, other, sums, c, got_c, e, o, got_eo):
     rows, width = normed.shape
     half = width // 2
     across = joined.shape[1] - FIRST_PART + SEG
     return pl.pallas_call(
-        skipping(joined_second_kernel, 6, len(deps)),
-        out_shape=[shaped((half, across), F32), shaped((half, across), BF16)],
-        in_specs=[SM] + [VM] * 5 + [ANY] * len(deps),
-        out_specs=[VM] * 2,
+        joined_second_kernel,
+        out_shape=[
+            shaped((half, across), BF16),
+            shaped((half, TILE), BF16),
+            shaped((half, across - TILE), BF16),
+            shaped(c.shape, F32),
+            shaped(e.shape, F32),
+            shaped(o.shape, F32),
+        ],
+        in_specs=[SM] + [VM] * 10,
+        out_specs=[VM] * 6,
         scratch_shapes=[pltpu.VMEM((width, rows), BF16), pltpu.VMEM((width, SEG), F32)],
         compiler_params=params(),
         cost_estimate=lasting("joined_second"),
         name="joined_second",
-    )(meta, normed, joined, vectors, other, sums, *deps)
+    )(meta, normed, joined, vectors, other, sums, c, got_c, e, o, got_eo)
 
 
 def input_back_kernel(x, part, other, gains, middle_grad, out):
@@ -1694,56 +1764,47 @@
         table, own, from_above, from_below, deps=tuple(query_grads) + (layer_output,) + fill
     )
     pair_grads = within(own_pairs)
-    fill = ()
+    riders = ()
     if by_halves:
         got_e = to_member(after_all(send_e, own_pairs[0]), 4)
         (keep_c, send_c), (keep_o, send_o) = takes(
             "third_step", [(keep_c, got_c), (keep_o, got_o)], deps=(own_pairs[0],)
         )
         got_c, got_o = to_member(send_c, 8), to_member(send_o, 4)
-        fill = (keep_o,)
-    joined_grad, first_part, joined_bias_sums = join_stage(
-        meta, joined_weight, query_grads, pair_grads, deps=fill
+        riders = ((keep_e, got_e), (keep_o, got_o))
+    joined_grad, first_part, joined_bias_sums, *ridden = join_stage(
+        meta, joined_weight, query_grads, pair_grads, riders
     )
-    first_other = swap(first_part)
-    input_gradient = input_back(activations, first_part, first_other, vectors, branch_low)
     if by_halves:
-        (keep_e, send_e), (keep_o, send_o) = takes(
-            "fourth_step", [(keep_e, got_e), (keep_o, got_o)], deps=(first_part,)
-        )
-        got_e, got_o = to_member(send_e, 8), to_member(send_o, 8)
+        keep_e, keep_o, send_eo = ridden
+        got_eo = to_member(send_eo, 8)
         keep_a, send_a, norm_vectors = joined_first(
-            meta, activations, first_part, first_low, joined_grad, deps=(keep_o,)
+            meta, activations, first_part, first_low, joined_grad
         )
         got_a = to_member(send_a, 1)
-        contract_done = add(keep_c, got_c)
         norm_other = swap(norm_vectors)
-        keep_b, send_b = joined_second(
+        first_other = swap(after_all(first_part, norm_other))
+        keep_b, send_b, last_b, contract_done, expand_done, output_sum = joined_second(
             meta, first_low, joined_grad, norm_vectors, norm_other, joined_bias_sums,
-            deps=(contract_done,),
+            keep_c, got_c, keep_e, keep_o, got_eo,
         )
-        got_b = to_member(send_b, 1)
-        (keep_a, send_a), (keep_b, send_b) = takes(
-            "fifth_step", [(keep_a, got_a), (keep_b, got_b)]
-        )
-        got_a, got_b = to_member(send_a, 2), to_member(send_b, 4)
-        (keep_a, send_a), (keep_b, send_b) = takes(
-            "sixth_step", [(keep_a, got_a), (keep_b, got_b)]
-        )
-        got_a, got_b = to_member(send_a, 4), to_member(send_b, 8)
-        expand_done = add(keep_e, got_e)
-        (keep_a, send_a), (keep_b, send_b) = takes(
-            "seventh_step", [(keep_a, got_a), (keep_b, got_b)], deps=(input_gradient, expand_done)
-        )
-        got_a, got_b = to_member(send_a, 8), to_member(send_b, 2)
+        got_b, last_b = to_member(send_b, 1), to_member(last_b, 1)
+        keep_a, send_a, keep_b, b1, b2, b3 = first_sums((keep_a, got_a), (keep_b, got_b, last_b))
+        got_a = to_member(send_a, 2)
+        got_b = [to_member(part, d) for part, d in zip((b1, b2, b3), Z_BLOCKS)]
+        keep_a, a1, a2, a3, keep_b, send_b = second_sums((keep_a, got_a), keep_b, got_b)
+        got_a = [to_member(part, d) for part, d in zip((a1, a2, a3), Z_BLOCKS)]
+        got_b = to_member(send_b, 2)
         done = (contract_done, expand_done) + tuple(
-            finish((keep_o, got_o), (keep_a, got_a), (keep_b, got_b))
+            finish(output_sum, keep_a, got_a, keep_b, got_b)
         )
     else:
+        first_other = swap(first_part)
         done = plain_sums(
             activations, first_part, first_low, joined_grad, joined_bias_sums, cotangent,
             hidden_low, second_low, pre_grad, branch_low, mixed, feed_vectors, extra,
         )
+    input_gradient = input_back(activations, first_part, first_other, vectors, branch_low)
     (
         contract_done, expand_done, output_done, joined_done,
         feed_gain_grad, feed_shift_grad, output_bias_grad, contract_bias_grad, expand_bias_grad,

time: 378 us -> 361 us (0.955)
  Pallas kernels: 230 us -> 219 us
  starting transfers between devices: 59.9 us -> 51.6 us
    pallas_call x6 -> x2, Pallas kernels: 26.5 us -> 10.2 us  [takes(): pl.pallas_call(partial(takes_kernel, flags, len(deps)), grid=(TAKE_STEPS,...]
    ppermute x40 -> x42, starting transfers between devices: 42.4 us -> 34.8 us  [to_member(): return lax.ppermute(value, 'dp', [(i, i ^ d) for i in range(count)])]
    pallas_call x5, Pallas kernels: 19.1 us -> 22.9 us  [the longest x1 8.27 us: join_stage(): pl.pallas_call(partial(join_kernel, len(riders)), out_shape=outs, in_spec...]
    ppermute x40 -> x42, waiting for transfers between devices: 28.7 us -> 27.8 us  [to_member(): return lax.ppermute(value, 'dp', [(i, i ^ d) for i in range(count)])]
    unnamed x99 -> x106, local copies, waits for them, and re-layouts: 19.3 us -> 18.6 us
  transfers between devices with their start and end apart: 53 -> 55, of which waited for: 16 -> 17; matrix products, arithmetic and copies ran while one was open for 2% -> 3% of each run, Pallas kernels for 46% -> 46%
where the time goes in v4:
time: 361 us; the launch traced here: 357 us
  Pallas kernels  219 us (61%)
  waiting for transfers between devices  60.1 us (17%)
  starting transfers between devices  51.6 us (14%)
  local copies, waits for them, and re-layouts  21.6 us (6%)
    ppermute x42, starting transfers between devices, to_member(): return lax.ppermute(value, 'dp', [(i, i ^ d) for i in range(count)])  34.8 us
    ppermute x42, waiting for transfers between devices, to_member(): return lax.ppermute(value, 'dp', [(i, i ^ d) for i in range(count)])  27.8 us
    pallas_call x1, Pallas kernels, feed_grads(): pl.pallas_call(feed_grads_kernel, grid=(2 * tiles,), out_shape=[kept, sen...  22.2 us
    pallas_call x1, Pallas kernels, attend_far(): pl.pallas_call(skipping(attend_far_kernel, used, len(deps)), out_shape=[s...  21.9 us
    pallas_call x1, Pallas kernels, back_near(): pl.pallas_call(skipping(back_near_kernel, used, len(deps)), out_shape=[sh...  19.4 us
    pallas_call x1, Pallas kernels, feed(): pl.pallas_call(feed_kernel, out_shape=[shaped((rows, half), BF16), shaped...  18.7 us
    unnamed x106, local copies, waits for them, and re-layouts  18.6 us
    pallas_call x1, Pallas kernels, attend_near(): pl.pallas_call(attend_near_kernel, out_shape=[shaped((TREE, PAIR, SEG), F...  18.5 us
  transfers between devices with their start and end apart: 55, of which 17 were waited for; matrix products, arithmetic and copies ran while one was open for 3% of the time, Pallas kernels for 46%

profile of v4, /device:TPU:0, one launch (start us, length us, event | category | flops | bytes accessed | tf_op | source)
XLA Modules:
  0.0 356.9 jit_solution(6331340981365916890)
XLA Ops:
  2.7 9.3 %project.1 = (bf16[640,1024]{1,0:T(8,128)(2,1)}, bf16[640,128]{1,0:T(8,128)(2,1)}, bf16[640,128]{1,0:T(8,128)(2,1)}, bf16[640,128]{1,0:T(8,128)(2,1)}, bf16[640,...) custom-call(s32[5]{0:T(128)} %stack.23.meta.refs_1_.refs_0_, ...), custom_call_target="tpu_custom_call" | custom-call | flops 4499999744 | tf_op jit(solution)/shard_map/project/pallas_call | solution.py:311
  17.1 8.8 %tables.1.table.refs_0_ = s32[1024]{0:T(1024)} custom-call(s32[5]{0:T(128)} %stack.23.meta.refs_1_.refs_0_, s32[80]{0:T(128)} %parent.1), custom_call_target="tpu_custom_call" | custom-call | tf_op jit(solution)/shard_map/tables/pallas_call | solution.py:243
  39.6 9.3 %hidden_grad.1.refs_11_ = f32[640,2048]{1,0:T(8,128)} custom-call(bf16[640,1024]{1,0:T(8,128)(2,1)} %refs_4_.3, bf16[2048,1024]{1,0:T(8,128)(2,1)} %weight.4, bf16[1536,256]{1,0:T(8,128)(2,1)} %copy-done), custom_call_target="tpu_custom_call" | custom-call | flops 2500000000 | tf_op jit(solution)/shard_map/hidden_grad/pallas_call | solution.py:963
  48.9 18.5 %attend_near.1 = (f32[20,128,128]{2,1,0:T(8,128)}, f32[20,8,256]{2,1,0:T(8,128)}) custom-call(s32[1024]{0:T(1024)} %tables.1.table.refs_0_, s32[5]{0:T(128)} %stack.23.meta.refs_1_.refs_0_, f32[16]{0:T(128)} %multiply_exponential_fusion.slopes.refs_2_, bf16[640,128]{1,0:T(8,128)(2,1)} %get-tuple-element.117.q0.refs_3_, bf16[640,128]{1,0:T(8,128)(2,1)} %copy-done.35, ...), custom_call_target="tpu_custom_call" | custom-call | flops 7000000000 | tf_op jit(solution)/shard_map/attend_near/pallas_call | solution.py:522
  67.4 7.0 %collective-permute-done.7.refs_8_ = bf16[1536,256]{1,0:T(8,128)(2,1)S(1)} collective-permute-done((bf16[1536,256]{1,0:T(8,128)(2,1)S(1)}, bf16[1536,256]{1,0:T(8,128)(2,1)S(1)}, u32[]{:S(2)}, u32[]{:S(2)}) %collective-permute-start.7) | collective-permute-done | bytes 786464 | tf_op jit(solution)/shard_map/ppermute | solution.py:1621
  75.3 21.9 %attend_far.1 = (bf16[640,128]{1,0:T(8,128)(2,1)}, bf16[640,128]{1,0:T(8,128)(2,1)}, bf16[640,128]{1,0:T(8,128)(2,1)}, bf16[640,128]{1,0:T(8,128)(2,1)}, f32[20,1,256]{2,1,0:T(1,128)}) custom-call(s32[1024]{0:T(1024)} %tables.1.table.refs_0_, s32[5]{0:T(128)} %stack.23.meta.refs_1_.refs_0_, f32[16]{0:T(128)} %multiply_exponential_fusion.slopes.refs_2_, ...), custom_call_target="tpu_custom_call" | custom-call | flops 7500000256 | tf_op jit(solution)/shard_map/attend_far/pallas_call | solution.py:591
  107.2 8.9 %collective-permute-done.12.b0 = bf16[640,128]{1,0:T(8,128)(2,1)S(1)} collective-permute-done((bf16[640,128]{1,0:T(8,128)(2,1)}, bf16[640,128]{1,0:T(8,128)(2,1)S(1)}, u32[]{:S(2)}, u32[]{:S(2)}) %collective-permute-start.12) | collective-permute-done | bytes 163872 | tf_op jit(solution)/shard_map/ppermute | solution.py:1615
  117.6 18.7 %feed.1 = (bf16[640,512]{1,0:T(8,128)(2,1)}, f32[640,1024]{1,0:T(8,128)}, bf16[640,1024]{1,0:T(8,128)(2,1)}, bf16[640,2048]{1,0:T(8,128)(2,1)}, bf16[640,2048]{1...) custom-call(s32[5]{0:T(128)} %stack.23.meta.refs_1_.refs_0_, bf16[640,1024]{1,0:T(8,128)(2,1)} %x.5, ...), custom_call_target="tpu_custom_call" | custom-call | flops 8999999488 | tf_op jit(solution)/shard_map/feed/pallas_call | solution.py:923
  137.9 22.2 %feed_grads.1 = (bf16[512,2048]{1,0:T(8,128)(2,1)}, bf16[512,1024]{1,0:T(8,128)(2,1)}, bf16[512,1024]{1,0:T(8,128)(2,1)}, bf16[512,2048]{1,0:T(8,128)(2,1)}, bf1...) custom-call(s32[5]{0:T(128)} %stack.23.meta.refs_1_.refs_0_, ...), custom_call_target="tpu_custom_call" | custom-call | flops 10000000000 | tf_op jit(solution)/shard_map/feed_grads/pallas_call | solution.py:1081
  168.2 8.2 %middle_back.1 = (bf16[640,1024]{1,0:T(8,128)(2,1)}, f32[8,1024]{1,0:T(8,128)}, bf16[640,128]{1,0:T(8,128)(2,1)}, bf16[640,128]{1,0:T(8,128)(2,1)}, bf16[640,128]{1,0:T(8,128)(2,1)}, /*index=5*/bf16[640,128]{1,0:T(8,128)(2,1)}) custom-call(s32[5]{0:T(128)} %stack.23.meta.refs_1_.refs_0_, f32[640,1024]{1,0:T(8,128)} %get-tuple-element.133.refs_1_, ...), custom_call_target="tpu_custom_call" | custom-call | flops 4000000000 | tf_op jit(solution)/shard_map/middle_back/pallas_call | solution.py:1373
  182.2 10.4 %output_grads.1 = (bf16[512,640]{1,0:T(8,128)(2,1)}, bf16[512,640]{1,0:T(8,128)(2,1)}, f32[256,2048]{1,0:T(8,128)}, bf16[256,2048]{1,0:T(8,128)(2,1)}, f32[256,2048]{1,0:T(8,128)}, /*index=5*/bf16[256,2048]{1,0:T(8,128)(2,1)}) custom-call(s32[5]{0:T(128)} %stack.23.meta.refs_1_.refs_0_, bf16[640,1024]{1,0:T(8,128)(2,1)} %get-tuple-element.139.refs_1_.branch.middle_grad, ...), custom_call_target="tpu_custom_call" | custom-call | flops 4499999744 | tf_op jit(solution)/shard_map/output_grads/pallas_call | solution.py:1226
  194.9 14.2 %back_far.1 = (bf16[1536,256]{1,0:T(8,128)(2,1)}, bf16[1536,256]{1,0:T(8,128)(2,1)}, f32[20,128,128]{2,1,0:T(8,128)}) custom-call(s32[1024]{0:T(1024)} %tables.1.table.refs_0_, s32[5]{0:T(128)} %stack.23.meta.refs_1_.refs_0_, f32[16]{0:T(128)} %multiply_exponential_fusion.slopes.refs_2_, bf16[640,128]{1,0:T(8,128)(2,1)} %get-tuple-element.117.q0.refs_3_, ...), custom_call_target="tpu_custom_call" | custom-call | flops 7000000000 | tf_op jit(solution)/shard_map/back_far/pallas_call | solution.py:707
  212.2 19.4 %back_near.1 = (bf16[640,128]{1,0:T(8,128)(2,1)}, bf16[640,128]{1,0:T(8,128)(2,1)}, bf16[640,128]{1,0:T(8,128)(2,1)}, bf16[640,128]{1,0:T(8,128)(2,1)}, f32[2560,256]{1,0:T(8,128)}) custom-call(s32[1024]{0:T(1024)} %tables.1.table.refs_0_, s32[5]{0:T(128)} %stack.23.meta.refs_1_.refs_0_, f32[16]{0:T(128)} %multiply_exponential_fusion.slopes.refs_2_, ...), custom_call_target="tpu_custom_call" | custom-call | flops 7500000256 | tf_op jit(solution)/shard_map/back_near/pallas_call | solution.py:770
  234.4 6.2 %second_step.1 = (f32[128,2048]{1,0:T(8,128)}, bf16[128,2048]{1,0:T(8,128)(2,1)}, f32[128,2048]{1,0:T(8,128)}, bf16[128,2048]{1,0:T(8,128)(2,1)}, f32[256,640]{1,0:T(8,128)}, /*index=5*/bf16[256,640]{1,0:T(8,128)(2,1)}) custom-call(f32[256,2048]{1,0:T(8,128)} %get-tuple-element.163.refs_0_, bf16[256,2048]{1,0:T(8,128)(2,1)} %copy-done.10, ...), custom_call_target="tpu_custom_call" | custom-call | flops 2500000000 | tf_op jit(solution)/shard_map/second_step/pallas_call | solution.py:1154
  244.4 10.2 %collective-permute-done.29.refs_3_ = bf16[1536,256]{1,0:T(8,128)(2,1)} collective-permute-done((bf16[1536,256]{1,0:T(8,128)(2,1)}, bf16[1536,256]{1,0:T(8,128)(2,1)}, u32[]{:S(2)}, u32[]{:S(2)}) %collective-permute-start.29) | collective-permute-done | bytes 786464 | tf_op jit(solution)/shard_map/ppermute | solution.py:1621
  255.2 4.9 %gather_back.1 = (bf16[640,256]{1,0:T(8,128)(2,1)}, bf16[640,256]{1,0:T(8,128)(2,1)}, bf16[640,256]{1,0:T(8,128)(2,1)}, bf16[640,256]{1,0:T(8,128)(2,1)}) custom-call(s32[1024]{0:T(1024)} %tables.1.table.refs_0_, f32[2560,256]{1,0:T(8,128)} %get-tuple-element.160.refs_6_.refs_1_, bf16[1536,256]{1,0:T(8,128)(2,1)} %collective-permute-done.28.refs_2_, ...), custom_call_target="tpu_custom_call" | custom-call | flops 2500000000 | tf_op jit(solution)/shard_map/gather_back/pallas_call | solution.py:823
  268.9 4.3 %collective-permute-start.42 = (bf16[64,2048]{1,0:T(8,128)(2,1)}, bf16[64,2048]{1,0:T(8,128)(2,1)S(1)}, u32[]{:S(2)}, u32[]{:S(2)}) collective-permute-start(bf16[64,2048]{1,0:T(8,128)(2,1)} %get-tuple-element.186), channel_id=1, source_target_pairs={{0,16},{2,18},{4,20},{6,22},{8,24},{10,26},{12,28},{14,30},{16,0},... | collective-permute-start | bytes 786440 | tf_op jit(solution)/shard_map/ppermute | solution.py:1609
  273.2 4.7 %collective-permute-done.35.k3 = bf16[640,256]{1,0:T(8,128)(2,1)S(1)} collective-permute-done((bf16[640,256]{1,0:T(8,128)(2,1)S(1)}, bf16[640,256]{1,0:T(8,128)(2,1)S(1)}, u32[]{:S(2)}, u32[]{:S(2)}) %collective-permute-start.35) | collective-permute-done | bytes 327712 | tf_op jit(solution)/shard_map/ppermute | solution.py:1609
  280.8 8.3 %join_stage.1 = (bf16[640,1536]{1,0:T(8,128)(2,1)}, bf16[640,1024]{1,0:T(8,128)(2,1)}, f32[8,1024]{1,0:T(8,128)}, f32[64,2048]{1,0:T(8,128)}, f32[64,640]{1,0:T(8,128)}, /*index=5*/bf16[64,2688]{1,0:T(8,128)(2,1)}) custom-call(s32[5]{0:T(128)} %stack.23.meta.refs_1_.refs_0_, bf16[1024,1536]{1,0:T(8,128)(2,1)} %weight.5, ...), custom_call_target="tpu_custom_call" | custom-call | flops 3500000000 | tf_op jit(solution)/shard_map/join_stage/pallas_call | solution.py:1438
  289.1 8.8 %joined_first.1 = (bf16[512,1024]{1,0:T(8,128)(2,1)}, bf16[512,1024]{1,0:T(8,128)(2,1)}, f32[8,1024]{1,0:T(8,128)}) custom-call(s32[5]{0:T(128)} %stack.23.meta.refs_1_.refs_0_, bf16[640,1024]{1,0:T(8,128)(2,1)} %x.5, bf16[640,1024]{1,0:T(8,128)(2,1)} %get-tuple-element.180.refs_2_.part, bf16[640,1024]{1,0:T(8,128)(2,1)} %get-tuple-element.181.refs_3_.normed, ...), custom_call_target="tpu_custom_call" | custom-call | flops 4499999744 | tf_op jit(solution)/shard_map/joined_first/pallas_call | solution.py:1480
  306.8 6.4 %joined_second.1 = (bf16[512,640]{1,0:T(8,128)(2,1)}, bf16[512,256]{1,0:T(8,128)(2,1)}, bf16[512,384]{1,0:T(8,128)(2,1)}, f32[64,2048]{1,0:T(8,128)}, f32[64,2048]{1,0:T(8,128)}, /*index=5*/f32[64,640]{1,0:T(8,128)}) custom-call(s32[5]{0:T(128)} %stack.23.meta.refs_1_.refs_0_, bf16[640,1024]{1,0:T(8,128)(2,1)} %get-tuple-element.181.refs_3_.normed, ...), custom_call_target="tpu_custom_call" | custom-call | flops 30000001024 | tf_op jit(solution)/shard_map/joined_second/pallas_call | solution.py:1542
  326.2 8.6 %collective-permute-done.48.refs_3_ = bf16[128,640]{1,0:T(8,128)(2,1)S(1)} collective-permute-done((bf16[128,640]{1,0:T(8,128)(2,1)}, bf16[128,640]{1,0:T(8,128)(2,1)S(1)}, u32[]{:S(2)}, u32[]{:S(2)}) %collective-permute-start.48) | collective-permute-done | bytes 163872 | tf_op jit(solution)/shard_map/ppermute | solution.py:1609
  338.4 4.7 %collective-permute-start.51 = (bf16[64,1024]{1,0:T(8,128)(2,1)}, bf16[64,1024]{1,0:T(8,128)(2,1)S(1)}, u32[]{:S(2)}, u32[]{:S(2)}) collective-permute-start(bf16[64,1024]{1,0:T(8,128)(2,1)} %get-tuple-element.203), channel_id=1, source_target_pairs={{0,16},{2,18},{4,20},{6,22},{8,24},{10,26},{12,28},{14,30},{16,0},... | collective-permute-start | bytes 393224 | tf_op jit(solution)/shard_map/ppermute | solution.py:1609
  347.0 5.8 %input_back.1 = bf16[640,1024]{1,0:T(8,128)(2,1)} custom-call(bf16[640,1024]{1,0:T(8,128)(2,1)} %x.5, bf16[640,1024]{1,0:T(8,128)(2,1)} %get-tuple-element.180.refs_2_.part, bf16[640,1024]{1,0:T(8,128)(2,1)} %copy-done.20, f32[9,1024]{1,0:T(8,128)} %stack_vectors.1.vectors.refs_5_.gains, bf16[640,1024]{1,0:T(8,128)(2,1)} %get-tuple-element.139.refs_1_.branch.middle_grad), custom_call_target="tpu_custom_call" | custom-call | flops 3000000000 | tf_op jit(solution)/shard_map/input_back/pallas_call | solution.py:1572
  (226 shorter events, 105.9 us)
Async XLA Ops:
  15.1 22.3 %collective-permute-start = (bf16[640,128]{1,0:T(8,128)(2,1)}, bf16[640,128]{1,0:T(8,128)(2,1)S(1)}, u32[]{:S(2)}, u32[]{:S(2)}) collective-permute-start(bf16[640,128]{1,0:T(8,128)(2,1)} %get-tuple-element.118), channel_id=1, source_target_pairs={{0,2},{2,0},{4,6},{6,4},{8,10},{10,8},{12,14},{14,12},{16,18},{18,... | collective-permute-start | bytes 491528 | tf_op jit(solution)/shard_map/ppermute | solution.py:1609
  15.2 33.6 %collective-permute-start.1 = (bf16[640,128]{1,0:T(8,128)(2,1)}, bf16[640,128]{1,0:T(8,128)(2,1)}, u32[]{:S(2)}, u32[]{:S(2)}) collective-permute-start(bf16[640,128]{1,0:T(8,128)(2,1)} %get-tuple-element.119), channel_id=1, source_target_pairs={{0,4},{2,6},{4,0},{6,2},{8,12},{10,14},{12,8},{14,10},{16,20},{18,... | collective-permute-start | bytes 491528 | tf_op jit(solution)/shard_map/ppermute | solution.py:1609
  26.5 22.4 %collective-permute-start.2 = (bf16[640,128]{1,0:T(8,128)(2,1)}, bf16[640,128]{1,0:T(8,128)(2,1)}, u32[]{:S(2)}, u32[]{:S(2)}) collective-permute-start(bf16[640,128]{1,0:T(8,128)(2,1)} %get-tuple-element.120), channel_id=1, source_target_pairs={{0,6},{2,4},{4,2},{6,0},{8,14},{10,12},{12,10},{14,8},{16,22},{18,... | collective-permute-start | bytes 491528 | tf_op jit(solution)/shard_map/ppermute | solution.py:1609
  26.5 40.9 %collective-permute-start.8 = (bf16[512,1024]{1,0:T(8,128)(2,1)}, bf16[512,1024]{1,0:T(8,128)(2,1)}, u32[]{:S(2)}, u32[]{:S(2)}) collective-permute-start(bf16[512,1024]{1,0:T(8,128)(2,1)} %refs_6_.3), channel_id=1, source_target_pairs={{0,1},{1,0},{2,3},{3,2},{4,5},{5,4},{6,7},{7,6},{8,9},{9,8},{10,11... | collective-permute-start | bytes 3145736 | tf_op jit(solution)/shard_map/ppermute | solution.py:1604
  35.7 31.7 %collective-permute-start.6 = (bf16[1536,256]{1,0:T(8,128)(2,1)S(1)}, bf16[1536,256]{1,0:T(8,128)(2,1)S(1)}, u32[]{:S(2)}, u32[]{:S(2)}) collective-permute-start(bf16[1536,256]{1,0:T(8,128)(2,1)S(1)} %get-tuple-element.125.refs_2_), channel_id=1, source_target_pairs={{0,8},{2,10},{4,12},{6,14},{8,16},{10,18},{12,20},{14,22},{16,24},... | collective-permute-start | bytes 2359304 | tf_op jit(solution)/shard_map/ppermute | solution.py:1621
  37.4 37.0 %collective-permute-start.7 = (bf16[1536,256]{1,0:T(8,128)(2,1)S(1)}, bf16[1536,256]{1,0:T(8,128)(2,1)S(1)}, u32[]{:S(2)}, u32[]{:S(2)}) collective-permute-start(bf16[1536,256]{1,0:T(8,128)(2,1)S(1)} %get-tuple-element.126), channel_id=1, source_target_pairs={{0,24},{2,26},{4,28},{6,30},{8,0},{10,2},{12,4},{14,6},{16,8},{18,... | collective-permute-start | bytes 2359304 | tf_op jit(solution)/shard_map/ppermute | solution.py:1621
  136.3 30.8 %collective-permute-start.16 = (bf16[640,1024]{1,0:T(8,128)(2,1)}, bf16[640,1024]{1,0:T(8,128)(2,1)S(1)}, u32[]{:S(2)}, u32[]{:S(2)}) collective-permute-start(bf16[640,1024]{1,0:T(8,128)(2,1)} %get-tuple-element.138.refs_2_), channel_id=1, source_target_pairs={{0,1},{1,0},{2,3},{3,2},{4,5},{5,4},{6,7},{7,6},{8,9},{9,8},{10,11... | collective-permute-start | bytes 3932168 | tf_op jit(solution)/shard_map/ppermute | solution.py:1604
  160.1 20.2 %collective-permute-start.21 = (bf16[512,1024]{1,0:T(8,128)(2,1)}, bf16[512,1024]{1,0:T(8,128)(2,1)S(1)}, u32[]{:S(2)}, u32[]{:S(2)}) collective-permute-start(bf16[512,1024]{1,0:T(8,128)(2,1)} %get-tuple-element.149), channel_id=1, source_target_pairs={{0,2},{2,0},{4,6},{6,4},{8,10},{10,8},{12,14},{14,12},{16,18},{18,... | collective-permute-start | bytes 3145736 | tf_op jit(solution)/shard_map/ppermute | solution.py:1609
  160.1 20.2 %collective-permute-start.22 = (bf16[512,1024]{1,0:T(8,128)(2,1)}, bf16[512,1024]{1,0:T(8,128)(2,1)}, u32[]{:S(2)}, u32[]{:S(2)}) collective-permute-start(bf16[512,1024]{1,0:T(8,128)(2,1)} %get-tuple-element.150), channel_id=1, source_target_pairs={{0,2},{2,0},{4,6},{6,4},{8,10},{10,8},{12,14},{14,12},{16,18},{18,... | collective-permute-start | bytes 3145736 | tf_op jit(solution)/shard_map/ppermute | solution.py:1609
  160.6 20.3 %collective-permute-start.23 = (bf16[512,1024]{1,0:T(8,128)(2,1)}, bf16[512,1024]{1,0:T(8,128)(2,1)}, u32[]{:S(2)}, u32[]{:S(2)}) collective-permute-start(bf16[512,1024]{1,0:T(8,128)(2,1)} %get-tuple-element.152), channel_id=1, source_target_pairs={{0,2},{2,0},{4,6},{6,4},{8,10},{10,8},{12,14},{14,12},{16,18},{18,... | collective-permute-start | bytes 3145736 | tf_op jit(solution)/shard_map/ppermute | solution.py:1609
  160.7 21.5 %collective-permute-start.24 = (bf16[512,1024]{1,0:T(8,128)(2,1)}, bf16[512,1024]{1,0:T(8,128)(2,1)}, u32[]{:S(2)}, u32[]{:S(2)}) collective-permute-start(bf16[512,1024]{1,0:T(8,128)(2,1)} %get-tuple-element.153), channel_id=1, source_target_pairs={{0,2},{2,0},{4,6},{6,4},{8,10},{10,8},{12,14},{14,12},{16,18},{18,... | collective-permute-start | bytes 3145736 | tf_op jit(solution)/shard_map/ppermute | solution.py:1609
  176.3 34.9 %collective-permute-start.17 = (bf16[640,1024]{1,0:T(8,128)(2,1)}, bf16[640,1024]{1,0:T(8,128)(2,1)S(1)}, u32[]{:S(2)}, u32[]{:S(2)}) collective-permute-start(bf16[640,1024]{1,0:T(8,128)(2,1)} %after_all.3), channel_id=1, source_target_pairs={{0,1},{1,0},{2,3},{3,2},{4,5},{5,4},{6,7},{7,6},{8,9},{9,8},{10,11... | collective-permute-start | bytes 3932168 | tf_op jit(solution)/shard_map/ppermute | solution.py:1604
  192.6 39.3 %collective-permute-start.30 = (bf16[256,2048]{1,0:T(8,128)(2,1)}, bf16[256,2048]{1,0:T(8,128)(2,1)S(1)}, u32[]{:S(2)}, u32[]{:S(2)}) collective-permute-start(bf16[256,2048]{1,0:T(8,128)(2,1)} %get-tuple-element.164), channel_id=1, source_target_pairs={{0,8},{2,10},{4,12},{6,14},{8,0},{10,2},{12,4},{14,6},{16,24},{18,... | collective-permute-start | bytes 3145736 | tf_op jit(solution)/shard_map/ppermute | solution.py:1609
  193.7 39.7 %collective-permute-start.31 = (bf16[256,2048]{1,0:T(8,128)(2,1)}, bf16[256,2048]{1,0:T(8,128)(2,1)S(1)}, u32[]{:S(2)}, u32[]{:S(2)}) collective-permute-start(bf16[256,2048]{1,0:T(8,128)(2,1)} %get-tuple-element.166), channel_id=1, source_target_pairs={{0,4},{2,6},{4,0},{6,2},{8,12},{10,14},{12,8},{14,10},{16,20},{18,... | collective-permute-start | bytes 3145736 | tf_op jit(solution)/shard_map/ppermute | solution.py:1609
  194.2 37.4 %collective-permute-start.32 = (bf16[512,640]{1,0:T(8,128)(2,1)}, bf16[512,640]{1,0:T(8,128)(2,1)}, u32[]{:S(2)}, u32[]{:S(2)}) collective-permute-start(bf16[512,640]{1,0:T(8,128)(2,1)} %get-tuple-element.167), channel_id=1, source_target_pairs={{0,2},{2,0},{4,6},{6,4},{8,10},{10,8},{12,14},{14,12},{16,18},{18,... | collective-permute-start | bytes 1966088 | tf_op jit(solution)/shard_map/ppermute | solution.py:1609
  209.2 31.4 %collective-permute-start.28 = (bf16[1536,256]{1,0:T(8,128)(2,1)}, bf16[1536,256]{1,0:T(8,128)(2,1)}, u32[]{:S(2)}, u32[]{:S(2)}) collective-permute-start(bf16[1536,256]{1,0:T(8,128)(2,1)} %get-tuple-element.161), channel_id=1, source_target_pairs={{0,24},{2,26},{4,28},{6,30},{8,0},{10,2},{12,4},{14,6},{16,8},{18,... | collective-permute-start | bytes 2359304 | tf_op jit(solution)/shard_map/ppermute | solution.py:1621
  211.2 43.5 %collective-permute-start.29 = (bf16[1536,256]{1,0:T(8,128)(2,1)}, bf16[1536,256]{1,0:T(8,128)(2,1)}, u32[]{:S(2)}, u32[]{:S(2)}) collective-permute-start(bf16[1536,256]{1,0:T(8,128)(2,1)} %get-tuple-element.162), channel_id=1, source_target_pairs={{0,8},{2,10},{4,12},{6,14},{8,16},{10,18},{12,20},{14,22},{16,24},... | collective-permute-start | bytes 2359304 | tf_op jit(solution)/shard_map/ppermute | solution.py:1621
  231.6 23.6 %collective-permute-start.25 = (bf16[640,128]{1,0:T(8,128)(2,1)}, bf16[640,128]{1,0:T(8,128)(2,1)}, u32[]{:S(2)}, u32[]{:S(2)}) collective-permute-start(bf16[640,128]{1,0:T(8,128)(2,1)} %get-tuple-element.157), channel_id=1, source_target_pairs={{0,2},{2,0},{4,6},{6,4},{8,10},{10,8},{12,14},{14,12},{16,18},{18,... | collective-permute-start | bytes 491528 | tf_op jit(solution)/shard_map/ppermute | solution.py:1609
  231.9 23.3 %collective-permute-start.26 = (bf16[640,128]{1,0:T(8,128)(2,1)}, bf16[640,128]{1,0:T(8,128)(2,1)}, u32[]{:S(2)}, u32[]{:S(2)}) collective-permute-start(bf16[640,128]{1,0:T(8,128)(2,1)} %get-tuple-element.158), channel_id=1, source_target_pairs={{0,4},{2,6},{4,0},{6,2},{8,12},{10,14},{12,8},{14,10},{16,20},{18,... | collective-permute-start | bytes 491528 | tf_op jit(solution)/shard_map/ppermute | solution.py:1609
  233.4 21.9 %collective-permute-start.27 = (bf16[640,128]{1,0:T(8,128)(2,1)}, bf16[640,128]{1,0:T(8,128)(2,1)}, u32[]{:S(2)}, u32[]{:S(2)}) collective-permute-start(bf16[640,128]{1,0:T(8,128)(2,1)} %get-tuple-element.159), channel_id=1, source_target_pairs={{0,6},{2,4},{4,2},{6,0},{8,14},{10,12},{12,10},{14,8},{16,22},{18,... | collective-permute-start | bytes 491528 | tf_op jit(solution)/shard_map/ppermute | solution.py:1609
  240.6 23.4 %collective-permute-start.37 = (bf16[128,2048]{1,0:T(8,128)(2,1)}, bf16[128,2048]{1,0:T(8,128)(2,1)}, u32[]{:S(2)}, u32[]{:S(2)}) collective-permute-start(bf16[128,2048]{1,0:T(8,128)(2,1)} %get-tuple-element.176), channel_id=1, source_target_pairs={{0,4},{2,6},{4,0},{6,2},{8,12},{10,14},{12,8},{14,10},{16,20},{18,... | collective-permute-start | bytes 1572872 | tf_op jit(solution)/shard_map/ppermute | solution.py:1609
  260.2 18.1 %collective-permute-start.36 = (bf16[128,2048]{1,0:T(8,128)(2,1)}, bf16[128,2048]{1,0:T(8,128)(2,1)S(1)}, u32[]{:S(2)}, u32[]{:S(2)}) collective-permute-start(bf16[128,2048]{1,0:T(8,128)(2,1)} %after_all.4), channel_id=1, source_target_pairs={{0,8},{2,10},{4,12},{6,14},{8,0},{10,2},{12,4},{14,6},{16,24},{18,... | collective-permute-start | bytes 1572872 | tf_op jit(solution)/shard_map/ppermute | solution.py:1609
  268.9 34.0 %collective-permute-start.42 = (bf16[64,2048]{1,0:T(8,128)(2,1)}, bf16[64,2048]{1,0:T(8,128)(2,1)S(1)}, u32[]{:S(2)}, u32[]{:S(2)}) collective-permute-start(bf16[64,2048]{1,0:T(8,128)(2,1)} %get-tuple-element.186), channel_id=1, source_target_pairs={{0,16},{2,18},{4,20},{6,22},{8,24},{10,26},{12,28},{14,30},{16,0},... | collective-permute-start | bytes 786440 | tf_op jit(solution)/shard_map/ppermute | solution.py:1609
  302.6 43.4 %collective-permute-start.41 = (bf16[640,1024]{1,0:T(8,128)(2,1)}, bf16[640,1024]{1,0:T(8,128)(2,1)S(1)}, u32[]{:S(2)}, u32[]{:S(2)}) collective-permute-start(bf16[640,1024]{1,0:T(8,128)(2,1)} %after_all.5), channel_id=1, source_target_pairs={{0,1},{1,0},{2,3},{3,2},{4,5},{5,4},{6,7},{7,6},{8,9},{9,8},{10,11... | collective-permute-start | bytes 3932168 | tf_op jit(solution)/shard_map/ppermute | solution.py:1604
  (83 other events, 520.8 us)

commit v5 on v4

--- a/solution.py
+++ b/solution.py
@@ -29,9 +29,8 @@
 SLOT_AT = (0, 2 * LISTS)
 LEVEL_AT = (LISTS, 3 * LISTS)
 COUNT_AT = (4 * LISTS, 4 * LISTS + TREE)
-UP_AT = 4 * LISTS + 2 * TREE
-DOWN_AT = UP_AT + INNER
-ORDER_AT = (DOWN_AT + INNER, DOWN_AT + INNER + TREE)
+UP_AT, DOWN_AT, OFFSET_AT, LISTED = 0, INNER, 2 * INNER, 32
+ORDER_AT = (4 * LISTS + 2 * TREE, 4 * LISTS + 3 * TREE)
 TABLE = 1024
 GROUP = 4
 
@@ -51,7 +50,7 @@
 
 
 LASTS = {
-    "project": 9, "tables": 9, "pack": 4, "attend_near": 14, "hidden_grad": 5, "attend_far": 15,
+    "project": 9, "lists": 2, "tables": 2, "pack": 1, "attend_near": 14, "hidden_grad": 5, "attend_far": 15,
     "feed": 18, "feed_grads": 20, "middle_back": 8, "output_grads": 9, "back_far": 14,
     "back_near": 15, "second_step": 5, "gather_back": 5, "third_step": 3, "join_stage": 7,
     "joined_first": 9, "joined_second": 60, "first_sums": 1, "second_sums": 1,
@@ -83,18 +82,14 @@
     return lax.broadcasted_iota(jnp.int32, shape, len(shape) - 2)
 
 
-def table_kernel(count, meta, parent, out, inner, place, starts):
+def lists_kernel(count, meta, parent, out, inner):
     member, group = meta[0], meta[1]
-    groups = count // TREE
-    below = lax.rem(group + groups - 1, groups)
-    above = lax.rem(group + 1, groups)
 
     def clear(i, _):
         inner[i] = 0
-        place[i] = EMPTY
         return _
 
-    lax.fori_loop(0, count, clear, 0)
+    lax.fori_loop(0, count, clear, 0, unroll=8)
 
     def mark(i, _):
         up = parent[i]
@@ -105,11 +100,12 @@
 
         return _
 
-    lax.fori_loop(0, count, mark, 0)
+    lax.fori_loop(0, count, mark, 0, unroll=4)
 
     def cover(i, mask):
         up = parent[i]
-        ahead = lax.rem(up - i + count, count)
+        ahead = up - i
+        ahead = jnp.where(ahead < 0, ahead + count, ahead)
         forward = ahead < TREE
         low = jnp.where(forward, i, up)
         length = jnp.where(forward, ahead, count - ahead)
@@ -121,23 +117,19 @@
         second = lax.shift_right_logical(bits, room)
         return mask | first | second
 
-    mask = lax.fori_loop(0, 2 * TREE - 1, cover, 0)
-
-    def find(c, found):
+    mask = lax.fori_loop(0, 2 * TREE - 1, cover, 0, unroll=3)
+    offset = 0
+    for c in range(TREE):
         free = (lax.shift_right_logical(mask, c) & 1) == 0
-        return jnp.where(free, c, found)
-
-    offset = lax.fori_loop(0, TREE, find, 0)
-
+        offset = jnp.where(free, c, offset)
+    out[OFFSET_AT] = offset
     for i in range(2 * INNER):
         out[UP_AT + i] = -1
 
     def own(p, ranks):
         up_rank, down_rank = ranks
         spot = ((p // SEG_DEV) ^ member) * SEG_DEV + lax.rem(p, SEG_DEV)
-        slot = group * TREE + p
-        place[slot] = spot
-        has = inner[slot] == 1
+        has = inner[group * TREE + p] == 1
         goes_up = has & (p >= offset) & (offset > 0) & (up_rank < INNER)
         goes_down = has & (p < offset) & (down_rank < INNER)
 
@@ -153,24 +145,40 @@
 
     lax.fori_loop(0, TREE, own, (0, 0))
 
-    def others(p, ranks):
+
+def make_lists(meta, parent):
+    count = parent.shape[0]
+    return pl.pallas_call(
+        partial(lists_kernel, count),
+        out_shape=[shaped((LISTED,), jnp.int32), shaped((count,), jnp.int32)],
+        in_specs=[SM, SM],
+        out_specs=[SM, SM],
+        compiler_params=params(8),
+        cost_estimate=lasting("lists"),
+        name="lists",
+    )(meta, parent)
+
+
+def table_kernel(count, meta, parent, lists, inner, out, place, starts):
+    member, group = meta[0], meta[1]
+    groups = count // TREE
+    below = lax.rem(group + groups - 1, groups)
+    above = lax.rem(group + 1, groups)
+    offset = lists[OFFSET_AT]
+
+    def known(p, ranks):
         low_rank, high_rank = ranks
+        spot = ((p // SEG_DEV) ^ member) * SEG_DEV + lax.rem(p, SEG_DEV)
+        place[group * TREE + p] = spot
         low_slot = below * TREE + p
         high_slot = above * TREE + p
         low = (inner[low_slot] == 1) & (p >= offset) & (offset > 0) & (low_rank < INNER)
         high = (inner[high_slot] == 1) & (p < offset) & (high_rank < INNER)
-
-        @pl.when(low)
-        def _low():
-            place[low_slot] = TREE + low_rank
-
-        @pl.when(high)
-        def _high():
-            place[high_slot] = TREE + INNER + high_rank
-
+        place[low_slot] = jnp.where(low, TREE + low_rank, EMPTY)
+        place[high_slot] = jnp.where(high, TREE + INNER + high_rank, EMPTY)
         return low_rank + low.astype(jnp.int32), high_rank + high.astype(jnp.int32)
 
-    lax.fori_loop(0, TREE, others, (0, 0))
+    lax.fori_loop(0, TREE, known, (0, 0))
 
     def chain(q, _):
         slot = group * TREE + ((q // SEG_DEV) ^ member) * SEG_DEV + lax.rem(q, SEG_DEV)
@@ -220,13 +228,11 @@
             return _
 
         lax.fori_loop(0, TREE, tally, 0)
-
-        def running(i, n):
-            number = starts[ANC - i]
-            starts[ANC - i] = n
-            return n + number
-
-        lax.fori_loop(0, ANC + 1, running, 0)
+        total = 0
+        for i in range(ANC, -1, -1):
+            number = starts[i]
+            starts[i] = total
+            total = total + number
 
         def put(q, _):
             number = out[COUNT_AT[side] + q]
@@ -238,16 +244,18 @@
         lax.fori_loop(0, TREE, put, 0)
 
 
-def make_tables(meta, parent):
+def make_tables(meta, parent, lists, inner, deps=()):
     count = parent.shape[0]
     return pl.pallas_call(
-        partial(table_kernel, count),
+        skipping(partial(table_kernel, count), 4, len(deps)),
         out_shape=shaped((TABLE,), jnp.int32),
-        in_specs=[SM, SM],
+        in_specs=[SM] * 4 + [ANY] * len(deps),
         out_specs=SM,
-        scratch_shapes=[pltpu.SMEM((size,), jnp.int32) for size in (count, count, 16)],
+        scratch_shapes=[pltpu.SMEM((size,), jnp.int32) for size in (count, 16)],
+        compiler_params=params(8),
+        cost_estimate=lasting("tables"),
         name="tables",
-    )(meta, parent)
+    )(meta, parent, lists, inner, *deps)
 
 
 def normal(block):
@@ -298,8 +306,8 @@
             @pl.when(d == j)
             def _store():
                 outs[j][...] = queries.astype(BF16)
-                outs[MEMBERS + j][:, :PAIR] = keys.astype(BF16)
-                outs[MEMBERS + j][:, PAIR:] = values.astype(BF16)
+                outs[MEMBERS + j][...] = keys.astype(BF16)
+                outs[2 * MEMBERS + j][...] = values.astype(BF16)
 
         return _
 
@@ -311,15 +319,14 @@
     outs = pl.pallas_call(
         project_kernel,
         out_shape=[shaped((rows, width), BF16)]
-        + [shaped((rows, PAIR), BF16)] * MEMBERS
-        + [shaped((rows, 2 * PAIR), BF16)] * MEMBERS,
+        + [shaped((rows, PAIR), BF16)] * (3 * MEMBERS),
         in_specs=[SM] + [VM] * 3,
-        out_specs=[VM] * (1 + 2 * MEMBERS),
+        out_specs=[VM] * (1 + 3 * MEMBERS),
         compiler_params=params(),
         cost_estimate=lasting("project"),
         name="project",
     )(meta, x, vectors, weight)
-    return outs[0], outs[1 : 1 + MEMBERS], outs[1 + MEMBERS :]
+    return outs[0], outs[1 : 1 + MEMBERS], outs[1 + MEMBERS : 1 + 2 * MEMBERS], outs[1 + 2 * MEMBERS :]
 
 
 def pack_kernel(table, kv0, kv1, kv2, kv3, up, down, sem):
@@ -344,18 +351,20 @@
             pltpu.make_async_copy(piece, piece, sem.at[side * INNER + i]).wait()
 
 
-def pack(table, pairs):
-    out = shaped((INNER * SEG, 2 * PAIR), BF16)
+def pack(table, pairs, deps=()):
+    out = shaped((INNER * SEG, PAIR), BF16)
+    specs = [SM] + [ANY] * MEMBERS
+    used = len(specs)
     return pl.pallas_call(
-        pack_kernel,
+        skipping(pack_kernel, used, len(deps)),
         out_shape=[out, out],
-        in_specs=[SM] + [ANY] * MEMBERS,
+        in_specs=specs + [ANY] * len(deps),
         out_specs=[ANY] * 2,
         scratch_shapes=[pltpu.SemaphoreType.DMA((2 * INNER,))],
         compiler_params=params(8),
         cost_estimate=lasting("pack"),
         name="pack",
-    )(table, *pairs)
+    )(table, *pairs, *deps)
 
 
 LEVELS = (1, 2, 3, 4, 5, 6, 8, 10)
@@ -408,13 +417,12 @@
         copy.wait()
 
 
-def loads(sources, target, sem, first):
+def loads(sources, target, sem, first, column=0):
     copies, at = [], 0
     for k, source in enumerate(sources):
-        rows = source.shape[0]
-        copies.append(
-            pltpu.make_async_copy(source, target.at[pl.ds(at, rows)], sem.at[first + k])
-        )
+        rows, across = source.shape
+        into = target.at[pl.ds(at, rows), pl.ds(column, across)]
+        copies.append(pltpu.make_async_copy(source, into, sem.at[first + k]))
         at += rows
     return copies
 
@@ -495,11 +503,12 @@
 
 
 def attend_near_kernel(
-    table, meta, slopes, q0, q1, q2, q3, kv0, kv1, kv2, kv3,
+    table, meta, slopes, q0, q1, q2, q3, k0, k1, k2, k3, v0, v1, v2, v3,
     kept, stats, pool, turned, queries, bias, sem,
 ):
-    copies = loads((kv0, kv1, kv2, kv3), pool, sem, 0)
-    copies += loads((q0, q1, q2, q3), queries, sem, MEMBERS)
+    copies = loads((k0, k1, k2, k3), pool, sem, 0)
+    copies += loads((v0, v1, v2, v3), pool, sem, MEMBERS, PAIR)
+    copies += loads((q0, q1, q2, q3), queries, sem, 2 * MEMBERS)
     start_all(copies)
     slope = slope_row(slopes, meta)
     fill_bias(bias, slope)
@@ -518,32 +527,35 @@
     by_groups(table, 0, body)
 
 
-def attend_near(table, meta, slopes, queries, pairs):
+def attend_near(table, meta, slopes, queries, keys, values, deps=()):
+    specs = [SM] * 3 + [ANY] * (3 * MEMBERS)
+    used = len(specs)
     return pl.pallas_call(
-        attend_near_kernel,
+        skipping(attend_near_kernel, used, len(deps)),
         out_shape=[shaped((TREE, PAIR, SEG), F32), shaped((TREE, 8, 2 * SEG), F32)],
-        in_specs=[SM] * 3 + [ANY] * (2 * MEMBERS),
+        in_specs=specs + [ANY] * len(deps),
         out_specs=[VM, VM],
         scratch_shapes=[
             pltpu.VMEM(((TREE + 1) * SEG, 2 * PAIR), BF16),
             pltpu.VMEM((TREE + 1, PAIR, SEG), BF16),
             pltpu.VMEM((TREE * SEG, PAIR), BF16),
             pltpu.VMEM((2, SEG, 2 * SEG), F32),
-            pltpu.SemaphoreType.DMA((2 * MEMBERS,)),
+            pltpu.SemaphoreType.DMA((3 * MEMBERS,)),
         ],
         compiler_params=params(),
         cost_estimate=lasting("attend_near"),
         name="attend_near",
-    )(table, meta, slopes, *queries, *pairs)
+    )(table, meta, slopes, *queries, *keys, *values, *deps)
 
 
 def attend_far_kernel(
-    table, meta, slopes, q0, q1, q2, q3, below, above, kept, stats,
+    table, meta, slopes, q0, q1, q2, q3, k_below, k_above, v_below, v_above, kept, stats,
     o0, o1, o2, o3, lse, pool, turned, queries, result, bias, sem,
 ):
     rows = SEG_DEV * SEG
-    copies = loads((below, above), pool, sem, 0)
-    copies += loads((q0, q1, q2, q3), queries, sem, 2)
+    copies = loads((k_below, k_above), pool, sem, 0)
+    copies += loads((v_below, v_above), pool, sem, 2, PAIR)
+    copies += loads((q0, q1, q2, q3), queries, sem, 4)
     start_all(copies)
     slope = slope_row(slopes, meta)
     fill_bias(bias, slope)
@@ -584,9 +596,9 @@
     wait_all(copies)
 
 
-def attend_far(table, meta, slopes, queries, below, above, kept, stats, deps=()):
+def attend_far(table, meta, slopes, queries, away, kept, stats, deps=()):
     rows = queries[0].shape[0]
-    specs = [SM] * 3 + [ANY] * (MEMBERS + 2) + [VM] * 2
+    specs = [SM] * 3 + [ANY] * (MEMBERS + 4) + [VM] * 2
     used = len(specs)
     outs = pl.pallas_call(
         skipping(attend_far_kernel, used, len(deps)),
@@ -599,12 +611,12 @@
             pltpu.VMEM((TREE * SEG, PAIR), BF16),
             pltpu.VMEM((TREE * SEG, PAIR), BF16),
             pltpu.VMEM((2, SEG, 2 * SEG), F32),
-            pltpu.SemaphoreType.DMA((MEMBERS + 2,)),
+            pltpu.SemaphoreType.DMA((MEMBERS + 4,)),
         ],
         compiler_params=params(),
         cost_estimate=lasting("attend_far"),
         name="attend_far",
-    )(table, meta, slopes, *queries, below, above, kept, stats, *deps)
+    )(table, meta, slopes, *queries, *away, kept, stats, *deps)
     return outs[:MEMBERS], outs[MEMBERS]
 
 
@@ -657,14 +669,15 @@
 
 
 def back_far_kernel(
-    table, meta, slopes, q0, q1, q2, q3, below, above, o0, o1, o2, o3, g0, g1, g2, g3, lse,
+    table, meta, slopes, q0, q1, q2, q3, k_below, k_above, v_below, v_above, o0, o1, o2, o3, g0, g1, g2, g3, lse,
     to_below, to_above, kept,
     pool, turned, queries, outs, grads, total, small, bias, sem,
 ):
-    copies = loads((below, above), pool, sem, 0)
-    copies += loads((q0, q1, q2, q3), queries, sem, 2)
-    copies += loads((o0, o1, o2, o3), outs, sem, 2 + MEMBERS)
-    copies += loads((g0, g1, g2, g3), grads, sem, 2 + 2 * MEMBERS)
+    copies = loads((k_below, k_above), pool, sem, 0)
+    copies += loads((v_below, v_above), pool, sem, 2, PAIR)
+    copies += loads((q0, q1, q2, q3), queries, sem, 4)
+    copies += loads((o0, o1, o2, o3), outs, sem, 4 + MEMBERS)
+    copies += loads((g0, g1, g2, g3), grads, sem, 4 + 2 * MEMBERS)
     start_all(copies)
     slope = slope_row(slopes, meta)
     fill_bias(bias, slope)
@@ -700,9 +713,9 @@
     wait_all(copies)
 
 
-def back_far(table, meta, slopes, queries, below, above, outs, grads, lse, deps=()):
+def back_far(table, meta, slopes, queries, away, outs, grads, lse, deps=()):
     side = shaped((INNER * SEG, 2 * PAIR), BF16)
-    specs = [SM] * 3 + [ANY] * (3 * MEMBERS + 2) + [VM]
+    specs = [SM] * 3 + [ANY] * (3 * MEMBERS + 4) + [VM]
     used = len(specs)
     return pl.pallas_call(
         skipping(back_far_kernel, used, len(deps)),
@@ -718,24 +731,25 @@
             pltpu.VMEM(((2 * INNER + 1) * SEG, 2 * PAIR), F32),
             pltpu.VMEM((2 * INNER * SEG, 2 * PAIR), BF16),
             pltpu.VMEM((2, SEG, 2 * SEG), F32),
-            pltpu.SemaphoreType.DMA((3 * MEMBERS + 2,)),
+            pltpu.SemaphoreType.DMA((3 * MEMBERS + 4,)),
         ],
         compiler_params=params(),
         cost_estimate=lasting("back_far"),
         name="back_far",
-    )(table, meta, slopes, *queries, below, above, *outs, *grads, lse, *deps)
+    )(table, meta, slopes, *queries, *away, *outs, *grads, lse, *deps)
 
 
 def back_near_kernel(
-    table, meta, slopes, q0, q1, q2, q3, kv0, kv1, kv2, kv3, o0, o1, o2, o3, g0, g1, g2, g3,
+    table, meta, slopes, q0, q1, q2, q3, k0, k1, k2, k3, v0, v1, v2, v3, o0, o1, o2, o3, g0, g1, g2, g3,
     lse, kept, dq0, dq1, dq2, dq3, own,
     pool, turned, queries, outs, grads, result, total, bias, sem,
 ):
     rows = SEG_DEV * SEG
-    copies = loads((kv0, kv1, kv2, kv3), pool, sem, 0)
-    copies += loads((q0, q1, q2, q3), queries, sem, MEMBERS)
-    copies += loads((o0, o1, o2, o3), outs, sem, 2 * MEMBERS)
-    copies += loads((g0, g1, g2, g3), grads, sem, 3 * MEMBERS)
+    copies = loads((k0, k1, k2, k3), pool, sem, 0)
+    copies += loads((v0, v1, v2, v3), pool, sem, MEMBERS, PAIR)
+    copies += loads((q0, q1, q2, q3), queries, sem, 2 * MEMBERS)
+    copies += loads((o0, o1, o2, o3), outs, sem, 3 * MEMBERS)
+    copies += loads((g0, g1, g2, g3), grads, sem, 4 * MEMBERS)
     start_all(copies)
     slope = slope_row(slopes, meta)
     fill_bias(bias, slope)
@@ -763,9 +777,9 @@
     wait_all(copies)
 
 
-def back_near(table, meta, slopes, queries, pairs, outs, grads, lse, kept, deps=()):
+def back_near(table, meta, slopes, queries, keys, values, outs, grads, lse, kept, deps=()):
     rows = queries[0].shape[0]
-    specs = [SM] * 3 + [ANY] * (4 * MEMBERS) + [VM] * 2
+    specs = [SM] * 3 + [ANY] * (5 * MEMBERS) + [VM] * 2
     used = len(specs)
     result = pl.pallas_call(
         skipping(back_near_kernel, used, len(deps)),
@@ -781,12 +795,12 @@
             pltpu.VMEM((TREE * SEG, PAIR), BF16),
             pltpu.VMEM(((TREE + 1) * SEG, 2 * PAIR), F32),
             pltpu.VMEM((2, SEG, 2 * SEG), F32),
-            pltpu.SemaphoreType.DMA((4 * MEMBERS,)),
+            pltpu.SemaphoreType.DMA((5 * MEMBERS,)),
         ],
         compiler_params=params(),
         cost_estimate=lasting("back_near"),
         name="back_near",
-    )(table, meta, slopes, *queries, *pairs, *outs, *grads, lse, kept, *deps)
+    )(table, meta, slopes, *queries, *keys, *values, *outs, *grads, lse, kept, *deps)
     return result[:MEMBERS], result[MEMBERS]
 
 
@@ -1698,20 +1712,25 @@
         attention_gain, attention_shift, feed_gain, feed_shift, output_bias, contract_bias,
         joined_bias, expand_bias,
     )
-    first_low, queries, pairs = project(meta, activations, vectors, joined_weight)
-    table = make_tables(meta, parent_slot)
-    pairs = within(pairs)
+    first_low, queries, keys, values = project(meta, activations, vectors, joined_weight)
+    lists, inner_marks = make_lists(meta, parent_slot)
+    keys = within(keys)
+    k_up, k_down = pack(lists, keys)
+    k_below, k_above = to_group(k_up, 1), to_group(k_down, -1)
+    values = within(values)
+    v_up, v_down = pack(lists, values, deps=(k_up,))
+    v_below, v_above = to_group(v_up, 1), to_group(v_down, -1)
     queries = within(queries)
-    up, down = pack(table, pairs)
-    below = to_group(up, 1)
-    above = to_group(down, -1)
-    hidden_grad = product("hidden_grad", cotangent, contract_weight, True, F32, deps=(up,))
+    table = make_tables(meta, parent_slot, lists, inner_marks, deps=(k_up,))
     other_output_weight = swap(output_weight)
-    kept, stats = attend_near(table, meta, slopes, queries, pairs)
+    kept, stats = attend_near(
+        table, meta, slopes, queries, keys, values, deps=(k_below, k_above)
+    )
+    away = (k_below, k_above, v_below, v_above)
     outs, lse = attend_far(
-        table, meta, slopes, queries, below, above, kept, stats,
-        deps=(hidden_grad, other_output_weight),
+        table, meta, slopes, queries, away, kept, stats, deps=(other_output_weight,)
     )
+    hidden_grad = product("hidden_grad", cotangent, contract_weight, True, F32, deps=(outs[0],))
     parts_other = [to_member_across(outs[d], d) for d in range(MEMBERS)]
     parts_own = within(outs)
     mixed, middle, second_low, hidden_low, pre_grad, second_part, bias_sums = feed(
@@ -1742,12 +1761,12 @@
         got_o, got_c, got_e = to_member(send_o, 1), to_member(send_c, 4), to_member(send_e, 2)
         fill = (keep_o,)
     to_below, to_above, kept_grad = back_far(
-        table, meta, slopes, queries, below, above, outs, grad_parts, lse, deps=fill
+        table, meta, slopes, queries, away, outs, grad_parts, lse, deps=fill
     )
     from_above = to_group(to_below, -1)
     from_below = to_group(to_above, 1)
     query_grads, own = back_near(
-        table, meta, slopes, queries, pairs, outs, grad_parts, lse, kept_grad, deps=(feed_other,)
+        table, meta, slopes, queries, keys, values, outs, grad_parts, lse, kept_grad, deps=(feed_other,)
     )
     query_grads = within(query_grads)
     layer_output = (
@@ -1761,7 +1780,7 @@
         got_c, got_o = to_member(send_c, 2), to_member(send_o, 2)
         fill = (keep_o,)
     own_pairs = gather_back(
-        table, own, from_above, from_below, deps=tuple(query_grads) + (layer_output,) + fill
+        lists, own, from_above, from_below, deps=tuple(query_grads) + (layer_output,) + fill
     )
     pair_grads = within(own_pairs)
     riders = ()

time: 361 us -> 345 us (0.956)
  waiting for transfers between devices: 60.1 us -> 45 us
  Pallas kernels: 219 us -> 207 us
  starting transfers between devices: 51.6 us -> 62.1 us
    pallas_call x1, Pallas kernels: 21.9 us -> 12.7 us  [attend_far(): pl.pallas_call(skipping(attend_far_kernel, used, len(deps)), out_shape=[s...]
    ppermute x4 -> x6, waiting for transfers between devices: 17.3 us -> 8.88 us  [to_group(): lax.ppermute(value, 'dp', [(i, (i + step) % count) for i in range(count)])]
    ppermute x4, waiting for transfers between devices: 8.9 us -> 0.67 us  [to_member_across(): return lax.ppermute(value, ('dp', 'tensor'), pairs)]
    ppermute x4 -> x6, starting transfers between devices: 5.96 us -> 13.9 us  [to_group(): lax.ppermute(value, 'dp', [(i, (i + step) % count) for i in range(count)])]
    pallas_call x1, Pallas kernels: 14.2 us -> 9.66 us  [back_far(): pl.pallas_call(skipping(back_far_kernel, used, len(deps)), out_shape=[sid...]
    ppermute x42 -> x45, starting transfers between devices: 34.8 us -> 37.7 us  [to_member(): return lax.ppermute(value, 'dp', [(i, i ^ d) for i in range(count)])]
    ppermute x42 -> x45, waiting for transfers between devices: 27.8 us -> 29.4 us  [to_member(): return lax.ppermute(value, 'dp', [(i, i ^ d) for i in range(count)])]
    pallas_call x3 -> x5, Pallas kernels: 30.9 us -> 32.4 us  [the longest x1 19 us: attend_near(): pl.pallas_call(skipping(attend_near_kernel, used, len(deps)), out_shape=[...]
  transfers between devices with their start and end apart: 55 -> 60, of which waited for: 17 -> 17; matrix products, arithmetic and copies ran while one was open for 3% -> 3% of each run, Pallas kernels for 46% -> 48%
where the time goes in v5:
time: 345 us; the launch traced here: 339 us
  Pallas kernels  207 us (60%)
  starting transfers between devices  62.1 us (18%)
  waiting for transfers between devices  45 us (13%)
  local copies, waits for them, and re-layouts  20.6 us (6%)
  other arithmetic  3.58 us (1%)
    ppermute x45, starting transfers between devices, to_member(): return lax.ppermute(value, 'dp', [(i, i ^ d) for i in range(count)])  37.7 us
    ppermute x45, waiting for transfers between devices, to_member(): return lax.ppermute(value, 'dp', [(i, i ^ d) for i in range(count)])  29.4 us
    pallas_call x1, Pallas kernels, feed_grads(): pl.pallas_call(feed_grads_kernel, grid=(2 * tiles,), out_shape=[kept, sen...  22.2 us
    pallas_call x1, Pallas kernels, back_near(): pl.pallas_call(skipping(back_near_kernel, used, len(deps)), out_shape=[sh...  19.9 us
    pallas_call x1, Pallas kernels, attend_near(): pl.pallas_call(skipping(attend_near_kernel, used, len(deps)), out_shape=[...  19 us
    pallas_call x1, Pallas kernels, feed(): pl.pallas_call(feed_kernel, out_shape=[shaped((rows, half), BF16), shaped...  18.7 us
    unnamed x134, local copies, waits for them, and re-layouts  17.6 us
    ppermute x6, starting transfers between devices, to_group(): lax.ppermute(value, 'dp', [(i, (i + step) % count) for i in range(count)])  13.9 us
  transfers between devices with their start and end apart: 60, of which 17 were waited for; matrix products, arithmetic and copies ran while one was open for 3% of the time, Pallas kernels for 48%

profile of v5, /device:TPU:0, one launch (start us, length us, event | category | flops | bytes accessed | tf_op | source)
XLA Modules:
  0.0 339.4 jit_solution(313496843864165438)
XLA Ops:
  2.7 9.3 %project.1 = (bf16[640,1024]{1,0:T(8,128)(2,1)}, bf16[640,128]{1,0:T(8,128)(2,1)}, bf16[640,128]{1,0:T(8,128)(2,1)}, bf16[640,128]{1,0:T(8,128)(2,1)}, bf16[640,...) custom-call(s32[5]{0:T(128)} %stack.23.meta.refs_0_.refs_1_, ...), custom_call_target="tpu_custom_call" | custom-call | flops 4499999744 | tf_op jit(solution)/shard_map/project/pallas_call | solution.py:319
  36.2 6.2 %tables.1.refs_0_ = s32[1024]{0:T(1024)S(1)} custom-call(s32[5]{0:T(128)S(1)} %copy-done, s32[80]{0:T(128)S(1)} %copy-done.7, s32[32]{0:T(128)S(1)} %get-tuple-element.125.refs_0_.refs_2_, s32[80]{0:T(128)S(1)} %get-tuple-element.126.refs_3_, bf16[1536,128]{1,0:T(8,128)(2,1)S(1)} %get-tuple-element.131.refs_4_.refs_5_), custom_call_target="tpu_custom_call" | custom-call | flops 1000000000 | tf_op jit(solution)/shard_map/tables/pallas_call | solution.py:249
  48.7 19.0 %attend_near.1 = (f32[20,128,128]{2,1,0:T(8,128)}, f32[20,8,256]{2,1,0:T(8,128)}) custom-call(s32[1024]{0:T(1024)} %copy-done.11, s32[5]{0:T(128)} %stack.23.meta.refs_0_.refs_1_, f32[16]{0:T(128)} %multiply_exponential_fusion.refs_2_, bf16[640,128]{1,0:T(8,128)(2,1)} %get-tuple-element.132.refs_3_, bf16[640,128]{1,0:T(8,128)(2,1)} %copy-done.43, ...), custom_call_target="tpu_custom_call" | custom-call | flops 7000000000 | tf_op jit(solution)/shard_map/attend_near/pallas_call | solution.py:533
  68.7 12.7 %attend_far.1 = (bf16[640,128]{1,0:T(8,128)(2,1)}, bf16[640,128]{1,0:T(8,128)(2,1)}, bf16[640,128]{1,0:T(8,128)(2,1)}, bf16[640,128]{1,0:T(8,128)(2,1)}, f32[20,1,256]{2,1,0:T(1,128)}) custom-call(s32[1024]{0:T(1024)} %copy-done.11, s32[5]{0:T(128)} %stack.23.meta.refs_0_.refs_1_, f32[16]{0:T(128)} %multiply_exponential_fusion.refs_2_, ...), custom_call_target="tpu_custom_call" | custom-call | flops 7500000256 | tf_op jit(solution)/shard_map/attend_far/pallas_call | solution.py:603
  90.3 9.2 %hidden_grad.1 = f32[640,2048]{1,0:T(8,128)} custom-call(bf16[640,1024]{1,0:T(8,128)(2,1)} %refs_4_.3, bf16[2048,1024]{1,0:T(8,128)(2,1)} %weight.4, bf16[640,128]{1,0:T(8,128)(2,1)} %get-tuple-element.145.refs_2_.a0.refs_11_.refs_15_), custom_call_target="tpu_custom_call" | custom-call | flops 2500000000 | tf_op jit(solution)/shard_map/hidden_grad/pallas_call | solution.py:977
  101.7 18.7 %feed.1 = (bf16[640,512]{1,0:T(8,128)(2,1)}, f32[640,1024]{1,0:T(8,128)}, bf16[640,1024]{1,0:T(8,128)(2,1)}, bf16[640,2048]{1,0:T(8,128)(2,1)}, bf16[640,2048]{1...) custom-call(s32[5]{0:T(128)} %stack.23.meta.refs_0_.refs_1_, bf16[640,1024]{1,0:T(8,128)(2,1)} %x.5, ...), custom_call_target="tpu_custom_call" | custom-call | flops 8999999488 | tf_op jit(solution)/shard_map/feed/pallas_call | solution.py:937
  122.0 22.2 %feed_grads.1 = (bf16[512,2048]{1,0:T(8,128)(2,1)}, bf16[512,1024]{1,0:T(8,128)(2,1)}, bf16[512,1024]{1,0:T(8,128)(2,1)}, bf16[512,2048]{1,0:T(8,128)(2,1)}, bf1...) custom-call(s32[5]{0:T(128)} %stack.23.meta.refs_0_.refs_1_, ...), custom_call_target="tpu_custom_call" | custom-call | flops 10000000000 | tf_op jit(solution)/shard_map/feed_grads/pallas_call | solution.py:1095
  152.1 8.1 %middle_back.1 = (bf16[640,1024]{1,0:T(8,128)(2,1)}, f32[8,1024]{1,0:T(8,128)}, bf16[640,128]{1,0:T(8,128)(2,1)}, bf16[640,128]{1,0:T(8,128)(2,1)}, bf16[640,128]{1,0:T(8,128)(2,1)}, /*index=5*/bf16[640,128]{1,0:T(8,128)(2,1)}) custom-call(s32[5]{0:T(128)} %stack.23.meta.refs_0_.refs_1_, f32[640,1024]{1,0:T(8,128)} %get-tuple-element.149.refs_1_, ...), custom_call_target="tpu_custom_call" | custom-call | flops 4000000000 | tf_op jit(solution)/shard_map/middle_back/pallas_call | solution.py:1387
  166.4 10.5 %output_grads.1 = (bf16[512,640]{1,0:T(8,128)(2,1)}, bf16[512,640]{1,0:T(8,128)(2,1)}, f32[256,2048]{1,0:T(8,128)}, bf16[256,2048]{1,0:T(8,128)(2,1)}, f32[256,2048]{1,0:T(8,128)}, /*index=5*/bf16[256,2048]{1,0:T(8,128)(2,1)}) custom-call(s32[5]{0:T(128)} %stack.23.meta.refs_0_.refs_1_, bf16[640,1024]{1,0:T(8,128)(2,1)} %get-tuple-element.155.refs_1_.branch.middle_grad, ...), custom_call_target="tpu_custom_call" | custom-call | flops 4499999744 | tf_op jit(solution)/shard_map/output_grads/pallas_call | solution.py:1240
  179.4 9.7 %back_far.1 = (bf16[1536,256]{1,0:T(8,128)(2,1)}, bf16[1536,256]{1,0:T(8,128)(2,1)}, f32[20,128,128]{2,1,0:T(8,128)}) custom-call(s32[1024]{0:T(1024)} %copy-done.11, s32[5]{0:T(128)} %stack.23.meta.refs_0_.refs_1_, f32[16]{0:T(128)} %multiply_exponential_fusion.refs_2_, bf16[640,128]{1,0:T(8,128)(2,1)} %get-tuple-element.132.refs_3_, ...), custom_call_target="tpu_custom_call" | custom-call | flops 7000000000 | tf_op jit(solution)/shard_map/back_far/pallas_call | solution.py:720
  189.0 6.1 %collective-permute-start.33 = (bf16[1536,256]{1,0:T(8,128)(2,1)}, bf16[1536,256]{1,0:T(8,128)(2,1)}, u32[]{:S(2)}, u32[]{:S(2)}) collective-permute-start(bf16[1536,256]{1,0:T(8,128)(2,1)} %get-tuple-element.177), channel_id=1, source_target_pairs={{0,24},{2,26},{4,28},{6,30},{8,0},{10,2},{12,4},{14,6},{16,8},{18,... | collective-permute-start | bytes 2359304 | tf_op jit(solution)/shard_map/ppermute | solution.py:1635
  196.2 19.9 %back_near.1 = (bf16[640,128]{1,0:T(8,128)(2,1)}, bf16[640,128]{1,0:T(8,128)(2,1)}, bf16[640,128]{1,0:T(8,128)(2,1)}, bf16[640,128]{1,0:T(8,128)(2,1)}, f32[2560,256]{1,0:T(8,128)}) custom-call(s32[1024]{0:T(1024)} %copy-done.11, s32[5]{0:T(128)} %stack.23.meta.refs_0_.refs_1_, f32[16]{0:T(128)} %multiply_exponential_fusion.refs_2_, ...), custom_call_target="tpu_custom_call" | custom-call | flops 7500000256 | tf_op jit(solution)/shard_map/back_near/pallas_call | solution.py:784
  218.8 6.2 %second_step.1 = (f32[128,2048]{1,0:T(8,128)}, bf16[128,2048]{1,0:T(8,128)(2,1)}, f32[128,2048]{1,0:T(8,128)}, bf16[128,2048]{1,0:T(8,128)(2,1)}, f32[256,640]{1,0:T(8,128)}, /*index=5*/bf16[256,640]{1,0:T(8,128)(2,1)}) custom-call(f32[256,2048]{1,0:T(8,128)} %get-tuple-element.179.refs_0_, bf16[256,2048]{1,0:T(8,128)(2,1)} %copy-done.16, ...), custom_call_target="tpu_custom_call" | custom-call | flops 2500000000 | tf_op jit(solution)/shard_map/second_step/pallas_call | solution.py:1168
  228.8 7.8 %collective-permute-done.34.refs_3_ = bf16[1536,256]{1,0:T(8,128)(2,1)} collective-permute-done((bf16[1536,256]{1,0:T(8,128)(2,1)}, bf16[1536,256]{1,0:T(8,128)(2,1)}, u32[]{:S(2)}, u32[]{:S(2)}) %collective-permute-start.34) | collective-permute-done | bytes 786464 | tf_op jit(solution)/shard_map/ppermute | solution.py:1635
  237.2 4.9 %gather_back.1 = (bf16[640,256]{1,0:T(8,128)(2,1)}, bf16[640,256]{1,0:T(8,128)(2,1)}, bf16[640,256]{1,0:T(8,128)(2,1)}, bf16[640,256]{1,0:T(8,128)(2,1)}) custom-call(s32[32]{0:T(128)} %copy-done.10, f32[2560,256]{1,0:T(8,128)} %get-tuple-element.176.refs_6_.refs_1_, bf16[1536,256]{1,0:T(8,128)(2,1)} %collective-permute-done.33.refs_2_, ...), custom_call_target="tpu_custom_call" | custom-call | flops 2500000000 | tf_op jit(solution)/shard_map/gather_back/pallas_call | solution.py:837
  247.0 4.0 %third_step.1 = (f32[64,2048]{1,0:T(8,128)}, bf16[64,2048]{1,0:T(8,128)(2,1)}, f32[128,640]{1,0:T(8,128)}, bf16[128,640]{1,0:T(8,128)(2,1)}) custom-call(f32[128,2048]{1,0:T(8,128)} %get-tuple-element.191.refs_0_, bf16[128,2048]{1,0:T(8,128)(2,1)} %collective-permute-done.42.refs_1_, f32[256,640]{1,0:T(8,128)} %get-tuple-element.184.refs_9_.refs_2_, ...), custom_call_target="tpu_custom_call" | custom-call | flops 1500000000 | tf_op jit(solution)/shard_map/third_step/pallas_call | solution.py:1168
  254.6 5.3 %collective-permute-done.40.k3 = bf16[640,256]{1,0:T(8,128)(2,1)S(1)} collective-permute-done((bf16[640,256]{1,0:T(8,128)(2,1)S(1)}, bf16[640,256]{1,0:T(8,128)(2,1)S(1)}, u32[]{:S(2)}, u32[]{:S(2)}) %collective-permute-start.40) | collective-permute-done | bytes 327712 | tf_op jit(solution)/shard_map/ppermute | solution.py:1623
  263.1 8.3 %join_stage.1 = (bf16[640,1536]{1,0:T(8,128)(2,1)}, bf16[640,1024]{1,0:T(8,128)(2,1)}, f32[8,1024]{1,0:T(8,128)}, f32[64,2048]{1,0:T(8,128)}, f32[64,640]{1,0:T(8,128)}, /*index=5*/bf16[64,2688]{1,0:T(8,128)(2,1)}) custom-call(s32[5]{0:T(128)} %stack.23.meta.refs_0_.refs_1_, bf16[1024,1536]{1,0:T(8,128)(2,1)} %weight.5, ...), custom_call_target="tpu_custom_call" | custom-call | flops 3500000000 | tf_op jit(solution)/shard_map/join_stage/pallas_call | solution.py:1452
  271.4 8.8 %joined_first.1 = (bf16[512,1024]{1,0:T(8,128)(2,1)}, bf16[512,1024]{1,0:T(8,128)(2,1)}, f32[8,1024]{1,0:T(8,128)}) custom-call(s32[5]{0:T(128)} %stack.23.meta.refs_0_.refs_1_, bf16[640,1024]{1,0:T(8,128)(2,1)} %x.5, bf16[640,1024]{1,0:T(8,128)(2,1)} %get-tuple-element.196.refs_2_.part, bf16[640,1024]{1,0:T(8,128)(2,1)} %get-tuple-element.197.refs_3_.normed, ...), custom_call_target="tpu_custom_call" | custom-call | flops 4499999744 | tf_op jit(solution)/shard_map/joined_first/pallas_call | solution.py:1494
  289.3 6.5 %joined_second.1 = (bf16[512,640]{1,0:T(8,128)(2,1)}, bf16[512,256]{1,0:T(8,128)(2,1)}, bf16[512,384]{1,0:T(8,128)(2,1)}, f32[64,2048]{1,0:T(8,128)}, f32[64,2048]{1,0:T(8,128)}, /*index=5*/f32[64,640]{1,0:T(8,128)}) custom-call(s32[5]{0:T(128)} %stack.23.meta.refs_0_.refs_1_, bf16[640,1024]{1,0:T(8,128)(2,1)} %get-tuple-element.197.refs_3_.normed, ...), custom_call_target="tpu_custom_call" | custom-call | flops 30000001024 | tf_op jit(solution)/shard_map/joined_second/pallas_call | solution.py:1556
  299.3 3.5 %first_sums.1 = (f32[256,1024]{1,0:T(8,128)}, bf16[256,1024]{1,0:T(8,128)(2,1)}, f32[128,640]{1,0:T(8,128)}, bf16[128,640]{1,0:T(8,128)(2,1)}, bf16[128,640]{1,0:T(8,128)(2,1)}, /*index=5*/bf16[128,640]{1,0:T(8,128)(2,1)}) custom-call(bf16[512,1024]{1,0:T(8,128)(2,1)} %get-tuple-element.207.a, bf16[512,1024]{1,0:T(8,128)(2,1)} %copy-done.18, ...), custom_call_target="tpu_custom_call" | custom-call | flops 500000000 | tf_op jit(solution)/shard_map/first_sums/pallas_call | solution.py:1272
  308.6 8.6 %collective-permute-done.53.refs_3_ = bf16[128,640]{1,0:T(8,128)(2,1)S(1)} collective-permute-done((bf16[128,640]{1,0:T(8,128)(2,1)}, bf16[128,640]{1,0:T(8,128)(2,1)S(1)}, u32[]{:S(2)}, u32[]{:S(2)}) %collective-permute-start.53) | collective-permute-done | bytes 163872 | tf_op jit(solution)/shard_map/ppermute | solution.py:1623
  320.8 4.7 %collective-permute-start.56 = (bf16[64,1024]{1,0:T(8,128)(2,1)}, bf16[64,1024]{1,0:T(8,128)(2,1)S(1)}, u32[]{:S(2)}, u32[]{:S(2)}) collective-permute-start(bf16[64,1024]{1,0:T(8,128)(2,1)} %get-tuple-element.219), channel_id=1, source_target_pairs={{0,16},{2,18},{4,20},{6,22},{8,24},{10,26},{12,28},{14,30},{16,0},... | collective-permute-start | bytes 393224 | tf_op jit(solution)/shard_map/ppermute | solution.py:1623
  328.7 5.8 %input_back.1 = bf16[640,1024]{1,0:T(8,128)(2,1)} custom-call(bf16[640,1024]{1,0:T(8,128)(2,1)} %x.5, bf16[640,1024]{1,0:T(8,128)(2,1)} %get-tuple-element.196.refs_2_.part, bf16[640,1024]{1,0:T(8,128)(2,1)} %copy-done.26, f32[9,1024]{1,0:T(8,128)} %stack_vectors.1.vectors.refs_5_.gains, bf16[640,1024]{1,0:T(8,128)(2,1)} %get-tuple-element.155.refs_1_.branch.middle_grad), custom_call_target="tpu_custom_call" | custom-call | flops 3000000000 | tf_op jit(solution)/shard_map/input_back/pallas_call | solution.py:1586
  (266 shorter events, 112.2 us)
Async XLA Ops:
  25.9 20.9 %collective-permute-start.6 = (bf16[1536,128]{1,0:T(8,128)(2,1)S(1)}, bf16[1536,128]{1,0:T(8,128)(2,1)S(1)}, u32[]{:S(2)}, u32[]{:S(2)}) collective-permute-start(bf16[1536,128]{1,0:T(8,128)(2,1)S(1)} %get-tuple-element.131.refs_4_.refs_5_), channel_id=1, source_target_pairs={{0,8},{2,10},{4,12},{6,14},{8,16},{10,18},{12,20},{14,22},{16,24},... | collective-permute-start | bytes 1179656 | tf_op jit(solution)/shard_map/ppermute | solution.py:1635
  27.6 20.4 %collective-permute-start.7 = (bf16[1536,128]{1,0:T(8,128)(2,1)S(1)}, bf16[1536,128]{1,0:T(8,128)(2,1)S(1)}, u32[]{:S(2)}, u32[]{:S(2)}) collective-permute-start(bf16[1536,128]{1,0:T(8,128)(2,1)S(1)} %get-tuple-element.136), channel_id=1, source_target_pairs={{0,24},{2,26},{4,28},{6,30},{8,0},{10,2},{12,4},{14,6},{16,8},{18,... | collective-permute-start | bytes 1179656 | tf_op jit(solution)/shard_map/ppermute | solution.py:1635
  29.8 37.8 %collective-permute-start.13 = (bf16[512,1024]{1,0:T(8,128)(2,1)S(1)}, bf16[512,1024]{1,0:T(8,128)(2,1)S(1)}, u32[]{:S(2)}, u32[]{:S(2)}) collective-permute-start(bf16[512,1024]{1,0:T(8,128)(2,1)S(1)} %copy-done.28), channel_id=1, source_target_pairs={{0,1},{1,0},{2,3},{3,2},{4,5},{5,4},{6,7},{7,6},{8,9},{9,8},{10,11... | collective-permute-start | bytes 3145736 | tf_op jit(solution)/shard_map/ppermute | solution.py:1618
  43.0 24.7 %collective-permute-start.11 = (bf16[1536,128]{1,0:T(8,128)(2,1)S(1)}, bf16[1536,128]{1,0:T(8,128)(2,1)}, u32[]{:S(2)}, u32[]{:S(2)}) collective-permute-start(bf16[1536,128]{1,0:T(8,128)(2,1)S(1)} %get-tuple-element.141), channel_id=1, source_target_pairs={{0,8},{2,10},{4,12},{6,14},{8,16},{10,18},{12,20},{14,22},{16,24},... | collective-permute-start | bytes 1179656 | tf_op jit(solution)/shard_map/ppermute | solution.py:1635
  43.6 24.1 %collective-permute-start.12 = (bf16[1536,128]{1,0:T(8,128)(2,1)S(1)}, bf16[1536,128]{1,0:T(8,128)(2,1)}, u32[]{:S(2)}, u32[]{:S(2)}) collective-permute-start(bf16[1536,128]{1,0:T(8,128)(2,1)S(1)} %get-tuple-element.142), channel_id=1, source_target_pairs={{0,24},{2,26},{4,28},{6,30},{8,0},{10,2},{12,4},{14,6},{16,8},{18,... | collective-permute-start | bytes 1179656 | tf_op jit(solution)/shard_map/ppermute | solution.py:1635
  83.0 17.2 %collective-permute-start.18 = (bf16[640,128]{1,0:T(8,128)(2,1)}, bf16[640,128]{1,0:T(8,128)(2,1)S(1)}, u32[]{:S(2)}, u32[]{:S(2)}) collective-permute-start(bf16[640,128]{1,0:T(8,128)(2,1)} %get-tuple-element.146.refs_12_.refs_16_), channel_id=1, source_target_pairs={{0,3},{1,2},{2,1},{3,0},{4,7},{5,6},{6,5},{7,4},{8,11},{9,10},{10,... | collective-permute-start | bytes 491528 | tf_op jit(solution)/shard_map/ppermute | solution.py:1629
  120.4 30.6 %collective-permute-start.21 = (bf16[640,1024]{1,0:T(8,128)(2,1)}, bf16[640,1024]{1,0:T(8,128)(2,1)S(1)}, u32[]{:S(2)}, u32[]{:S(2)}) collective-permute-start(bf16[640,1024]{1,0:T(8,128)(2,1)} %get-tuple-element.154.refs_2_), channel_id=1, source_target_pairs={{0,1},{1,0},{2,3},{3,2},{4,5},{5,4},{6,7},{7,6},{8,9},{9,8},{10,11... | collective-permute-start | bytes 3932168 | tf_op jit(solution)/shard_map/ppermute | solution.py:1618
  144.2 20.2 %collective-permute-start.26 = (bf16[512,1024]{1,0:T(8,128)(2,1)}, bf16[512,1024]{1,0:T(8,128)(2,1)S(1)}, u32[]{:S(2)}, u32[]{:S(2)}) collective-permute-start(bf16[512,1024]{1,0:T(8,128)(2,1)} %get-tuple-element.165), channel_id=1, source_target_pairs={{0,2},{2,0},{4,6},{6,4},{8,10},{10,8},{12,14},{14,12},{16,18},{18,... | collective-permute-start | bytes 3145736 | tf_op jit(solution)/shard_map/ppermute | solution.py:1623
  144.3 20.2 %collective-permute-start.27 = (bf16[512,1024]{1,0:T(8,128)(2,1)}, bf16[512,1024]{1,0:T(8,128)(2,1)}, u32[]{:S(2)}, u32[]{:S(2)}) collective-permute-start(bf16[512,1024]{1,0:T(8,128)(2,1)} %get-tuple-element.166), channel_id=1, source_target_pairs={{0,2},{2,0},{4,6},{6,4},{8,10},{10,8},{12,14},{14,12},{16,18},{18,... | collective-permute-start | bytes 3145736 | tf_op jit(solution)/shard_map/ppermute | solution.py:1623
  144.8 20.4 %collective-permute-start.28 = (bf16[512,1024]{1,0:T(8,128)(2,1)}, bf16[512,1024]{1,0:T(8,128)(2,1)}, u32[]{:S(2)}, u32[]{:S(2)}) collective-permute-start(bf16[512,1024]{1,0:T(8,128)(2,1)} %get-tuple-element.168), channel_id=1, source_target_pairs={{0,2},{2,0},{4,6},{6,4},{8,10},{10,8},{12,14},{14,12},{16,18},{18,... | collective-permute-start | bytes 3145736 | tf_op jit(solution)/shard_map/ppermute | solution.py:1623
  144.9 21.5 %collective-permute-start.29 = (bf16[512,1024]{1,0:T(8,128)(2,1)}, bf16[512,1024]{1,0:T(8,128)(2,1)}, u32[]{:S(2)}, u32[]{:S(2)}) collective-permute-start(bf16[512,1024]{1,0:T(8,128)(2,1)} %get-tuple-element.169), channel_id=1, source_target_pairs={{0,2},{2,0},{4,6},{6,4},{8,10},{10,8},{12,14},{14,12},{16,18},{18,... | collective-permute-start | bytes 3145736 | tf_op jit(solution)/shard_map/ppermute | solution.py:1623
  160.2 34.9 %collective-permute-start.22 = (bf16[640,1024]{1,0:T(8,128)(2,1)}, bf16[640,1024]{1,0:T(8,128)(2,1)S(1)}, u32[]{:S(2)}, u32[]{:S(2)}) collective-permute-start(bf16[640,1024]{1,0:T(8,128)(2,1)} %after_all.3), channel_id=1, source_target_pairs={{0,1},{1,0},{2,3},{3,2},{4,5},{5,4},{6,7},{7,6},{8,9},{9,8},{10,11... | collective-permute-start | bytes 3932168 | tf_op jit(solution)/shard_map/ppermute | solution.py:1618
  176.8 39.4 %collective-permute-start.35 = (bf16[256,2048]{1,0:T(8,128)(2,1)}, bf16[256,2048]{1,0:T(8,128)(2,1)S(1)}, u32[]{:S(2)}, u32[]{:S(2)}) collective-permute-start(bf16[256,2048]{1,0:T(8,128)(2,1)} %get-tuple-element.180), channel_id=1, source_target_pairs={{0,8},{2,10},{4,12},{6,14},{8,0},{10,2},{12,4},{14,6},{16,24},{18,... | collective-permute-start | bytes 3145736 | tf_op jit(solution)/shard_map/ppermute | solution.py:1623
  178.1 39.7 %collective-permute-start.36 = (bf16[256,2048]{1,0:T(8,128)(2,1)}, bf16[256,2048]{1,0:T(8,128)(2,1)S(1)}, u32[]{:S(2)}, u32[]{:S(2)}) collective-permute-start(bf16[256,2048]{1,0:T(8,128)(2,1)} %get-tuple-element.182), channel_id=1, source_target_pairs={{0,4},{2,6},{4,0},{6,2},{8,12},{10,14},{12,8},{14,10},{16,20},{18,... | collective-permute-start | bytes 3145736 | tf_op jit(solution)/shard_map/ppermute | solution.py:1623
  178.6 37.4 %collective-permute-start.37 = (bf16[512,640]{1,0:T(8,128)(2,1)}, bf16[512,640]{1,0:T(8,128)(2,1)}, u32[]{:S(2)}, u32[]{:S(2)}) collective-permute-start(bf16[512,640]{1,0:T(8,128)(2,1)} %get-tuple-element.183), channel_id=1, source_target_pairs={{0,2},{2,0},{4,6},{6,4},{8,10},{10,8},{12,14},{14,12},{16,18},{18,... | collective-permute-start | bytes 1966088 | tf_op jit(solution)/shard_map/ppermute | solution.py:1623
  189.0 36.0 %collective-permute-start.33 = (bf16[1536,256]{1,0:T(8,128)(2,1)}, bf16[1536,256]{1,0:T(8,128)(2,1)}, u32[]{:S(2)}, u32[]{:S(2)}) collective-permute-start(bf16[1536,256]{1,0:T(8,128)(2,1)} %get-tuple-element.177), channel_id=1, source_target_pairs={{0,24},{2,26},{4,28},{6,30},{8,0},{10,2},{12,4},{14,6},{16,8},{18,... | collective-permute-start | bytes 2359304 | tf_op jit(solution)/shard_map/ppermute | solution.py:1635
  195.1 41.5 %collective-permute-start.34 = (bf16[1536,256]{1,0:T(8,128)(2,1)}, bf16[1536,256]{1,0:T(8,128)(2,1)}, u32[]{:S(2)}, u32[]{:S(2)}) collective-permute-start(bf16[1536,256]{1,0:T(8,128)(2,1)} %get-tuple-element.178), channel_id=1, source_target_pairs={{0,8},{2,10},{4,12},{6,14},{8,16},{10,18},{12,20},{14,22},{16,24},... | collective-permute-start | bytes 2359304 | tf_op jit(solution)/shard_map/ppermute | solution.py:1635
  216.0 21.1 %collective-permute-start.30 = (bf16[640,128]{1,0:T(8,128)(2,1)}, bf16[640,128]{1,0:T(8,128)(2,1)}, u32[]{:S(2)}, u32[]{:S(2)}) collective-permute-start(bf16[640,128]{1,0:T(8,128)(2,1)} %get-tuple-element.173), channel_id=1, source_target_pairs={{0,2},{2,0},{4,6},{6,4},{8,10},{10,8},{12,14},{14,12},{16,18},{18,... | collective-permute-start | bytes 491528 | tf_op jit(solution)/shard_map/ppermute | solution.py:1623
  216.3 20.9 %collective-permute-start.31 = (bf16[640,128]{1,0:T(8,128)(2,1)}, bf16[640,128]{1,0:T(8,128)(2,1)}, u32[]{:S(2)}, u32[]{:S(2)}) collective-permute-start(bf16[640,128]{1,0:T(8,128)(2,1)} %get-tuple-element.174), channel_id=1, source_target_pairs={{0,4},{2,6},{4,0},{6,2},{8,12},{10,14},{12,8},{14,10},{16,20},{18,... | collective-permute-start | bytes 491528 | tf_op jit(solution)/shard_map/ppermute | solution.py:1623
  217.8 19.4 %collective-permute-start.32 = (bf16[640,128]{1,0:T(8,128)(2,1)}, bf16[640,128]{1,0:T(8,128)(2,1)}, u32[]{:S(2)}, u32[]{:S(2)}) collective-permute-start(bf16[640,128]{1,0:T(8,128)(2,1)} %get-tuple-element.175), channel_id=1, source_target_pairs={{0,6},{2,4},{4,2},{6,0},{8,14},{10,12},{12,10},{14,8},{16,22},{18,... | collective-permute-start | bytes 491528 | tf_op jit(solution)/shard_map/ppermute | solution.py:1623
  225.1 21.2 %collective-permute-start.42 = (bf16[128,2048]{1,0:T(8,128)(2,1)}, bf16[128,2048]{1,0:T(8,128)(2,1)}, u32[]{:S(2)}, u32[]{:S(2)}) collective-permute-start(bf16[128,2048]{1,0:T(8,128)(2,1)} %get-tuple-element.192), channel_id=1, source_target_pairs={{0,4},{2,6},{4,0},{6,2},{8,12},{10,14},{12,8},{14,10},{16,20},{18,... | collective-permute-start | bytes 1572872 | tf_op jit(solution)/shard_map/ppermute | solution.py:1623
  242.1 18.0 %collective-permute-start.41 = (bf16[128,2048]{1,0:T(8,128)(2,1)}, bf16[128,2048]{1,0:T(8,128)(2,1)S(1)}, u32[]{:S(2)}, u32[]{:S(2)}) collective-permute-start(bf16[128,2048]{1,0:T(8,128)(2,1)} %after_all.4), channel_id=1, source_target_pairs={{0,8},{2,10},{4,12},{6,14},{8,0},{10,2},{12,4},{14,6},{16,24},{18,... | collective-permute-start | bytes 1572872 | tf_op jit(solution)/shard_map/ppermute | solution.py:1623
  251.7 33.5 %collective-permute-start.47 = (bf16[64,2048]{1,0:T(8,128)(2,1)}, bf16[64,2048]{1,0:T(8,128)(2,1)S(1)}, u32[]{:S(2)}, u32[]{:S(2)}) collective-permute-start(bf16[64,2048]{1,0:T(8,128)(2,1)} %get-tuple-element.202), channel_id=1, source_target_pairs={{0,16},{2,18},{4,20},{6,22},{8,24},{10,26},{12,28},{14,30},{16,0},... | collective-permute-start | bytes 786440 | tf_op jit(solution)/shard_map/ppermute | solution.py:1623
  284.9 42.7 %collective-permute-start.46 = (bf16[640,1024]{1,0:T(8,128)(2,1)}, bf16[640,1024]{1,0:T(8,128)(2,1)S(1)}, u32[]{:S(2)}, u32[]{:S(2)}) collective-permute-start(bf16[640,1024]{1,0:T(8,128)(2,1)} %after_all.5), channel_id=1, source_target_pairs={{0,1},{1,0},{2,3},{3,2},{4,5},{5,4},{6,7},{7,6},{8,9},{9,8},{10,11... | collective-permute-start | bytes 3932168 | tf_op jit(solution)/shard_map/ppermute | solution.py:1618
  (102 other events, 734.0 us)

commit v6 on v5

--- a/solution.py
+++ b/solution.py
@@ -273,7 +273,7 @@
         body(pl.ds(pl.multiple_of(i * NORM_ROWS, NORM_ROWS), NORM_ROWS))
         return _
 
-    lax.fori_loop(0, rows // NORM_ROWS, step, 0)
+    lax.fori_loop(0, rows // NORM_ROWS, step, 0, unroll=True)
 
 
 def project_kernel(meta, x, vectors, weight, normed, *outs):
@@ -311,7 +311,7 @@
 
         return _
 
-    lax.fori_loop(0, MEMBERS, one, 0)
+    lax.fori_loop(0, MEMBERS, one, 0, unroll=True)
 
 
 def project(meta, x, vectors, weight):
@@ -887,7 +887,7 @@
         )
         return _
 
-    lax.fori_loop(0, width // TILE, column, 0)
+    lax.fori_loop(0, width // TILE, column, 0, unroll=2)
     stores.append(pltpu.make_async_copy(middle, middle_out, out_sem.at[1]))
     stores[1].start()
 
@@ -916,7 +916,7 @@
         sums[0:1, at] = jnp.sum(grad.astype(F32), axis=0, keepdims=True)
         return _
 
-    lax.fori_loop(0, inner // TILE, hidden_step, 0)
+    lax.fori_loop(0, inner // TILE, hidden_step, 0, unroll=2)
     stores.append(pltpu.make_async_copy(act, act_out, out_sem.at[3]))
     stores.append(pltpu.make_async_copy(pre_grad, pre_out, out_sem.at[4]))
     start_all(stores[3:])
@@ -926,7 +926,7 @@
         part[:, at] = dot(pre_grad[...], up[at, :], ((1,), (1,))).astype(BF16)
         return _
 
-    lax.fori_loop(0, width // TILE, back, 0)
+    lax.fori_loop(0, width // TILE, back, 0, unroll=2)
     wait_all(stores)
 
 
@@ -1178,7 +1178,7 @@
     return [tuple(got[2 * k : 2 * k + 2]) for k in range(len(pairs))]
 
 
-def output_grads_kernel(count, meta, branch, mixed, vectors, extra, *refs):
+def output_grads_kernel(count, meta, branch, mixed, vectors, sums, *refs):
     ins = refs[: 3 * count]
     keep, send = refs[3 * count : 3 * count + 2]
     outs = refs[3 * count + 2 : -2]
@@ -1193,8 +1193,17 @@
         turn_source(branch, turned, meta[4], X_FIRST, share)
         for i in range(width // SEG):
             at = slice(i * SEG, (i + 1) * SEG)
+            low = lanes((1, SEG)) < share
+            one = sums[0:1, 2 * i * SEG : (2 * i + 1) * SEG]
+            two = sums[0:1, (2 * i + 1) * SEG : (2 * i + 2) * SEG]
             rows8 = jnp.concatenate(
-                [vectors[0:4, at], extra[0:2, at], jnp.zeros((2, SEG), F32)], axis=0
+                [
+                    vectors[0:4, at],
+                    jnp.where(low, one, pltpu.roll(two, share, 1)),
+                    jnp.where(low, pltpu.roll(one, share, 1), two),
+                    jnp.zeros((2, SEG), F32),
+                ],
+                axis=0,
             )
             turn_ordered(in_two(rows8).T, small, i, meta[4], X_FIRST, share)
         keep[:, across:] = small[:half].astype(BF16)
@@ -1216,7 +1225,7 @@
             add_half(kept, high, outs[2 * k], outs[2 * k + 1])
 
 
-def output_grads(meta, branch, mixed, vectors, extra, pairs):
+def output_grads(meta, branch, mixed, vectors, sums, pairs):
     rows, width = branch.shape
     across = mixed.shape[1]
     half_steps = TAKE_STEPS // 2
@@ -1241,14 +1250,14 @@
         partial(output_grads_kernel, len(pairs)),
         grid=(TAKE_STEPS,),
         out_shape=[shaped((width // 2, across + SEG), BF16)] * 2 + shapes,
-        in_specs=[SM, whole(branch.shape), whole(mixed.shape), whole(vectors.shape), whole(extra.shape)]
+        in_specs=[SM, whole(branch.shape), whole(mixed.shape), whole(vectors.shape), whole(sums.shape)]
         + specs,
         out_specs=[own, own] + outs,
         scratch_shapes=[pltpu.VMEM((width, rows), BF16), pltpu.VMEM((width, SEG), F32)],
         compiler_params=params(),
         cost_estimate=lasting("output_grads"),
         name="output_grads",
-    )(meta, branch, mixed, vectors, extra, *args)
+    )(meta, branch, mixed, vectors, sums, *args)
     return (got[0], got[1]), [tuple(got[2 + 2 * k : 4 + 2 * k]) for k in range(len(pairs))]
 
 
@@ -1738,7 +1747,6 @@
         parts_own, parts_other, output_weight, other_output_weight, expand_weight, hidden_grad,
     )
     second_other = swap(second_part)
-    extra = bias_sums[0].reshape(count, 2, width // count).transpose(1, 0, 2).reshape(2, width)
     by_halves = count == DEVICES
     if by_halves:
         keep_c, c0, c1, keep_e, e0, e1, feed_part = feed_grads(
@@ -1756,7 +1764,7 @@
     fill = ()
     if by_halves:
         (keep_o, send_o), ((keep_c, send_c), (keep_e, send_e)) = output_grads(
-            meta, branch_low, mixed, feed_vectors, extra, [(keep_c, c0, c1), (keep_e, e0, e1)]
+            meta, branch_low, mixed, feed_vectors, bias_sums, [(keep_c, c0, c1), (keep_e, e0, e1)]
         )
         got_o, got_c, got_e = to_member(send_o, 1), to_member(send_c, 4), to_member(send_e, 2)
         fill = (keep_o,)
@@ -1819,6 +1827,7 @@
         )
     else:
         first_other = swap(first_part)
+        extra = bias_sums[0].reshape(count, 2, width // count).transpose(1, 0, 2).reshape(2, width)
         done = plain_sums(
             activations, first_part, first_low, joined_grad, joined_bias_sums, cotangent,
             hidden_low, second_low, pre_grad, branch_low, mixed, feed_vectors, extra,

time: 345 us -> 342 us (level)
  Pallas kernels: 207 us -> 201 us
  starting transfers between devices: 62.1 us -> 66.5 us
    ppermute x45, starting transfers between devices: 37.7 us -> 41.4 us  [to_member(): return lax.ppermute(value, 'dp', [(i, i ^ d) for i in range(count)])]
    unnamed x134 -> x138, local copies, waits for them, and re-layouts: 17.6 us -> 18.3 us
  transfers between devices with their start and end apart: 60 -> 60, of which waited for: 17 -> 16; matrix products, arithmetic and copies ran while one was open for 3% -> 2% of each run, Pallas kernels for 48% -> 47%
where the time goes in v6:
time: 342 us; the launch traced here: 336 us
  Pallas kernels  201 us (59%)
  starting transfers between devices  66.5 us (19%)
  waiting for transfers between devices  43.9 us (13%)
  local copies, waits for them, and re-layouts  19.6 us (6%)
  other arithmetic  3.58 us (1%)
    ppermute x45, starting transfers between devices, to_member(): return lax.ppermute(value, 'dp', [(i, i ^ d) for i in range(count)])  41.4 us
    ppermute x45, waiting for transfers between devices, to_member(): return lax.ppermute(value, 'dp', [(i, i ^ d) for i in range(count)])  27.1 us
    pallas_call x1, Pallas kernels, feed_grads(): pl.pallas_call(feed_grads_kernel, grid=(2 * tiles,), out_shape=[kept, sen...  22.3 us
    unnamed x138, local copies, waits for them, and re-layouts  18.3 us
    pallas_call x1, Pallas kernels, feed(): pl.pallas_call(feed_kernel, out_shape=[shaped((rows, half), BF16), shaped...  17.9 us
    pallas_call x1, Pallas kernels, back_near(): pl.pallas_call(skipping(back_near_kernel, used, len(deps)), out_shape=[sh...  16.8 us
    pallas_call x1, Pallas kernels, attend_near(): pl.pallas_call(skipping(attend_near_kernel, used, len(deps)), out_shape=[...  16.3 us
    pallas_call x1, Pallas kernels, attend_far(): pl.pallas_call(skipping(attend_far_kernel, used, len(deps)), out_shape=[s...  15.3 us
  transfers between devices with their start and end apart: 60, of which 16 were waited for; matrix products, arithmetic and copies ran while one was open for 2% of the time, Pallas kernels for 47%

profile of v6, /device:TPU:0, one launch (start us, length us, event | category | flops | bytes accessed | tf_op | source)
XLA Modules:
  0.0 336.3 jit_solution(4182352196186591802)
XLA Ops:
  2.7 6.6 %project.1 = (bf16[640,1024]{1,0:T(8,128)(2,1)}, bf16[640,128]{1,0:T(8,128)(2,1)}, bf16[640,128]{1,0:T(8,128)(2,1)}, bf16[640,128]{1,0:T(8,128)(2,1)}, bf16[640,...) custom-call(s32[5]{0:T(128)} %stack.23.meta.refs_0_.refs_1_, ...), custom_call_target="tpu_custom_call" | custom-call | flops 4499999744 | tf_op jit(solution)/shard_map/project/pallas_call | solution.py:319
  33.6 6.2 %tables.1.refs_0_ = s32[1024]{0:T(1024)S(1)} custom-call(s32[5]{0:T(128)S(1)} %copy-done, s32[80]{0:T(128)S(1)} %copy-done.7, s32[32]{0:T(128)S(1)} %get-tuple-element.125.refs_0_.refs_2_, s32[80]{0:T(128)S(1)} %get-tuple-element.126.refs_3_, bf16[1536,128]{1,0:T(8,128)(2,1)S(1)} %get-tuple-element.131.refs_4_.refs_5_), custom_call_target="tpu_custom_call" | custom-call | flops 1000000000 | tf_op jit(solution)/shard_map/tables/pallas_call | solution.py:249
  46.1 16.3 %attend_near.1 = (f32[20,128,128]{2,1,0:T(8,128)}, f32[20,8,256]{2,1,0:T(8,128)}) custom-call(s32[1024]{0:T(1024)} %copy-done.11, s32[5]{0:T(128)} %stack.23.meta.refs_0_.refs_1_, f32[16]{0:T(128)} %multiply_exponential_fusion.refs_2_, bf16[640,128]{1,0:T(8,128)(2,1)} %get-tuple-element.132.refs_3_, bf16[640,128]{1,0:T(8,128)(2,1)} %copy-done.45, ...), custom_call_target="tpu_custom_call" | custom-call | flops 7000000000 | tf_op jit(solution)/shard_map/attend_near/pallas_call | solution.py:533
  63.4 15.3 %attend_far.1 = (bf16[640,128]{1,0:T(8,128)(2,1)}, bf16[640,128]{1,0:T(8,128)(2,1)}, bf16[640,128]{1,0:T(8,128)(2,1)}, bf16[640,128]{1,0:T(8,128)(2,1)}, f32[20,1,256]{2,1,0:T(1,128)}) custom-call(s32[1024]{0:T(1024)} %copy-done.11, s32[5]{0:T(128)} %stack.23.meta.refs_0_.refs_1_, f32[16]{0:T(128)} %multiply_exponential_fusion.refs_2_, ...), custom_call_target="tpu_custom_call" | custom-call | flops 7500000256 | tf_op jit(solution)/shard_map/attend_far/pallas_call | solution.py:603
  87.7 9.2 %hidden_grad.1 = f32[640,2048]{1,0:T(8,128)} custom-call(bf16[640,1024]{1,0:T(8,128)(2,1)} %refs_4_.3, bf16[2048,1024]{1,0:T(8,128)(2,1)} %weight.4, bf16[640,128]{1,0:T(8,128)(2,1)} %get-tuple-element.145.refs_2_.a0.refs_11_.refs_15_), custom_call_target="tpu_custom_call" | custom-call | flops 2500000000 | tf_op jit(solution)/shard_map/hidden_grad/pallas_call | solution.py:977
  99.0 17.9 %feed.1 = (bf16[640,512]{1,0:T(8,128)(2,1)}, f32[640,1024]{1,0:T(8,128)}, bf16[640,1024]{1,0:T(8,128)(2,1)}, bf16[640,2048]{1,0:T(8,128)(2,1)}, bf16[640,2048]{1...) custom-call(s32[5]{0:T(128)} %stack.23.meta.refs_0_.refs_1_, bf16[640,1024]{1,0:T(8,128)(2,1)} %x.5, ...), custom_call_target="tpu_custom_call" | custom-call | flops 8999999488 | tf_op jit(solution)/shard_map/feed/pallas_call | solution.py:937
  118.5 22.3 %feed_grads.1 = (bf16[512,2048]{1,0:T(8,128)(2,1)}, bf16[512,1024]{1,0:T(8,128)(2,1)}, bf16[512,1024]{1,0:T(8,128)(2,1)}, bf16[512,2048]{1,0:T(8,128)(2,1)}, bf1...) custom-call(s32[5]{0:T(128)} %stack.23.meta.refs_0_.refs_1_, ...), custom_call_target="tpu_custom_call" | custom-call | flops 10000000000 | tf_op jit(solution)/shard_map/feed_grads/pallas_call | solution.py:1095
  148.9 7.6 %middle_back.1 = (bf16[640,1024]{1,0:T(8,128)(2,1)}, f32[8,1024]{1,0:T(8,128)}, bf16[640,128]{1,0:T(8,128)(2,1)}, bf16[640,128]{1,0:T(8,128)(2,1)}, bf16[640,128]{1,0:T(8,128)(2,1)}, /*index=5*/bf16[640,128]{1,0:T(8,128)(2,1)}) custom-call(s32[5]{0:T(128)} %stack.23.meta.refs_0_.refs_1_, f32[640,1024]{1,0:T(8,128)} %get-tuple-element.149.refs_1_, ...), custom_call_target="tpu_custom_call" | custom-call | flops 4000000000 | tf_op jit(solution)/shard_map/middle_back/pallas_call | solution.py:1396
  160.8 10.4 %output_grads.1 = (bf16[512,640]{1,0:T(8,128)(2,1)}, bf16[512,640]{1,0:T(8,128)(2,1)}, f32[256,2048]{1,0:T(8,128)}, bf16[256,2048]{1,0:T(8,128)(2,1)}, f32[256,2048]{1,0:T(8,128)}, /*index=5*/bf16[256,2048]{1,0:T(8,128)(2,1)}) custom-call(s32[5]{0:T(128)} %stack.23.meta.refs_0_.refs_1_, bf16[640,1024]{1,0:T(8,128)(2,1)} %get-tuple-element.155.refs_1_.branch.middle_grad, ...), custom_call_target="tpu_custom_call" | custom-call | flops 4499999744 | tf_op jit(solution)/shard_map/output_grads/pallas_call | solution.py:1249
  175.0 12.0 %back_far.1 = (bf16[1536,256]{1,0:T(8,128)(2,1)}, bf16[1536,256]{1,0:T(8,128)(2,1)}, f32[20,128,128]{2,1,0:T(8,128)}) custom-call(s32[1024]{0:T(1024)} %copy-done.11, s32[5]{0:T(128)} %stack.23.meta.refs_0_.refs_1_, f32[16]{0:T(128)} %multiply_exponential_fusion.refs_2_, bf16[640,128]{1,0:T(8,128)(2,1)} %get-tuple-element.132.refs_3_, ...), custom_call_target="tpu_custom_call" | custom-call | flops 7000000000 | tf_op jit(solution)/shard_map/back_far/pallas_call | solution.py:720
  187.0 6.5 %collective-permute-start.33 = (bf16[1536,256]{1,0:T(8,128)(2,1)}, bf16[1536,256]{1,0:T(8,128)(2,1)}, u32[]{:S(2)}, u32[]{:S(2)}) collective-permute-start(bf16[1536,256]{1,0:T(8,128)(2,1)} %get-tuple-element.177), channel_id=1, source_target_pairs={{0,24},{2,26},{4,28},{6,30},{8,0},{10,2},{12,4},{14,6},{16,8},{18,... | collective-permute-start | bytes 2359304 | tf_op jit(solution)/shard_map/ppermute | solution.py:1644
  194.6 16.8 %back_near.1 = (bf16[640,128]{1,0:T(8,128)(2,1)}, bf16[640,128]{1,0:T(8,128)(2,1)}, bf16[640,128]{1,0:T(8,128)(2,1)}, bf16[640,128]{1,0:T(8,128)(2,1)}, f32[2560,256]{1,0:T(8,128)}) custom-call(s32[1024]{0:T(1024)} %copy-done.11, s32[5]{0:T(128)} %stack.23.meta.refs_0_.refs_1_, f32[16]{0:T(128)} %multiply_exponential_fusion.refs_2_, ...), custom_call_target="tpu_custom_call" | custom-call | flops 7500000256 | tf_op jit(solution)/shard_map/back_near/pallas_call | solution.py:784
  213.8 6.2 %second_step.1 = (f32[128,2048]{1,0:T(8,128)}, bf16[128,2048]{1,0:T(8,128)(2,1)}, f32[128,2048]{1,0:T(8,128)}, bf16[128,2048]{1,0:T(8,128)(2,1)}, f32[256,640]{1,0:T(8,128)}, /*index=5*/bf16[256,640]{1,0:T(8,128)(2,1)}) custom-call(f32[256,2048]{1,0:T(8,128)} %get-tuple-element.179.refs_0_, bf16[256,2048]{1,0:T(8,128)(2,1)} %copy-done.16, ...), custom_call_target="tpu_custom_call" | custom-call | flops 2500000000 | tf_op jit(solution)/shard_map/second_step/pallas_call | solution.py:1168
  223.9 9.1 %collective-permute-done.34.refs_3_ = bf16[1536,256]{1,0:T(8,128)(2,1)} collective-permute-done((bf16[1536,256]{1,0:T(8,128)(2,1)}, bf16[1536,256]{1,0:T(8,128)(2,1)}, u32[]{:S(2)}, u32[]{:S(2)}) %collective-permute-start.34) | collective-permute-done | bytes 786464 | tf_op jit(solution)/shard_map/ppermute | solution.py:1644
  233.6 5.0 %gather_back.1 = (bf16[640,256]{1,0:T(8,128)(2,1)}, bf16[640,256]{1,0:T(8,128)(2,1)}, bf16[640,256]{1,0:T(8,128)(2,1)}, bf16[640,256]{1,0:T(8,128)(2,1)}) custom-call(s32[32]{0:T(128)} %copy-done.10, f32[2560,256]{1,0:T(8,128)} %get-tuple-element.176.refs_6_.refs_1_, bf16[1536,256]{1,0:T(8,128)(2,1)} %collective-permute-done.33.refs_2_, ...), custom_call_target="tpu_custom_call" | custom-call | flops 2500000000 | tf_op jit(solution)/shard_map/gather_back/pallas_call | solution.py:837
  243.5 4.1 %third_step.1 = (f32[64,2048]{1,0:T(8,128)}, bf16[64,2048]{1,0:T(8,128)(2,1)}, f32[128,640]{1,0:T(8,128)}, bf16[128,640]{1,0:T(8,128)(2,1)}) custom-call(f32[128,2048]{1,0:T(8,128)} %get-tuple-element.191.refs_0_, bf16[128,2048]{1,0:T(8,128)(2,1)} %collective-permute-done.42.refs_1_, f32[256,640]{1,0:T(8,128)} %get-tuple-element.184.refs_9_.refs_2_, ...), custom_call_target="tpu_custom_call" | custom-call | flops 1500000000 | tf_op jit(solution)/shard_map/third_step/pallas_call | solution.py:1168
  247.6 6.0 %collective-permute-start.47 = (bf16[64,2048]{1,0:T(8,128)(2,1)}, bf16[64,2048]{1,0:T(8,128)(2,1)S(1)}, u32[]{:S(2)}, u32[]{:S(2)}) collective-permute-start(bf16[64,2048]{1,0:T(8,128)(2,1)} %get-tuple-element.202), channel_id=1, source_target_pairs={{0,16},{2,18},{4,20},{6,22},{8,24},{10,26},{12,28},{14,30},{16,0},... | collective-permute-start | bytes 786440 | tf_op jit(solution)/shard_map/ppermute | solution.py:1632
  259.5 8.3 %join_stage.1 = (bf16[640,1536]{1,0:T(8,128)(2,1)}, bf16[640,1024]{1,0:T(8,128)(2,1)}, f32[8,1024]{1,0:T(8,128)}, f32[64,2048]{1,0:T(8,128)}, f32[64,640]{1,0:T(8,128)}, /*index=5*/bf16[64,2688]{1,0:T(8,128)(2,1)}) custom-call(s32[5]{0:T(128)} %stack.23.meta.refs_0_.refs_1_, bf16[1024,1536]{1,0:T(8,128)(2,1)} %weight.5, ...), custom_call_target="tpu_custom_call" | custom-call | flops 3500000000 | tf_op jit(solution)/shard_map/join_stage/pallas_call | solution.py:1461
  268.6 8.3 %joined_first.1 = (bf16[512,1024]{1,0:T(8,128)(2,1)}, bf16[512,1024]{1,0:T(8,128)(2,1)}, f32[8,1024]{1,0:T(8,128)}) custom-call(s32[5]{0:T(128)} %stack.23.meta.refs_0_.refs_1_, bf16[640,1024]{1,0:T(8,128)(2,1)} %x.5, bf16[640,1024]{1,0:T(8,128)(2,1)} %get-tuple-element.196.refs_2_.part, bf16[640,1024]{1,0:T(8,128)(2,1)} %get-tuple-element.197.refs_3_.normed, ...), custom_call_target="tpu_custom_call" | custom-call | flops 4499999744 | tf_op jit(solution)/shard_map/joined_first/pallas_call | solution.py:1503
  285.5 6.5 %joined_second.1 = (bf16[512,640]{1,0:T(8,128)(2,1)}, bf16[512,256]{1,0:T(8,128)(2,1)}, bf16[512,384]{1,0:T(8,128)(2,1)}, f32[64,2048]{1,0:T(8,128)}, f32[64,2048]{1,0:T(8,128)}, /*index=5*/f32[64,640]{1,0:T(8,128)}) custom-call(s32[5]{0:T(128)} %stack.23.meta.refs_0_.refs_1_, bf16[640,1024]{1,0:T(8,128)(2,1)} %get-tuple-element.197.refs_3_.normed, ...), custom_call_target="tpu_custom_call" | custom-call | flops 30000001024 | tf_op jit(solution)/shard_map/joined_second/pallas_call | solution.py:1565
  295.5 3.5 %first_sums.1 = (f32[256,1024]{1,0:T(8,128)}, bf16[256,1024]{1,0:T(8,128)(2,1)}, f32[128,640]{1,0:T(8,128)}, bf16[128,640]{1,0:T(8,128)(2,1)}, bf16[128,640]{1,0:T(8,128)(2,1)}, /*index=5*/bf16[128,640]{1,0:T(8,128)(2,1)}) custom-call(bf16[512,1024]{1,0:T(8,128)(2,1)} %get-tuple-element.207.a, bf16[512,1024]{1,0:T(8,128)(2,1)} %copy-done.18, ...), custom_call_target="tpu_custom_call" | custom-call | flops 500000000 | tf_op jit(solution)/shard_map/first_sums/pallas_call | solution.py:1281
  304.6 7.4 %collective-permute-done.53.refs_3_ = bf16[128,640]{1,0:T(8,128)(2,1)S(1)} collective-permute-done((bf16[128,640]{1,0:T(8,128)(2,1)}, bf16[128,640]{1,0:T(8,128)(2,1)S(1)}, u32[]{:S(2)}, u32[]{:S(2)}) %collective-permute-start.53) | collective-permute-done | bytes 163872 | tf_op jit(solution)/shard_map/ppermute | solution.py:1632
  318.0 3.4 %collective-permute-start.56 = (bf16[64,1024]{1,0:T(8,128)(2,1)}, bf16[64,1024]{1,0:T(8,128)(2,1)S(1)}, u32[]{:S(2)}, u32[]{:S(2)}) collective-permute-start(bf16[64,1024]{1,0:T(8,128)(2,1)} %get-tuple-element.219), channel_id=1, source_target_pairs={{0,16},{2,18},{4,20},{6,22},{8,24},{10,26},{12,28},{14,30},{16,0},... | collective-permute-start | bytes 393224 | tf_op jit(solution)/shard_map/ppermute | solution.py:1632
  326.0 5.5 %input_back.1 = bf16[640,1024]{1,0:T(8,128)(2,1)} custom-call(bf16[640,1024]{1,0:T(8,128)(2,1)} %x.5, bf16[640,1024]{1,0:T(8,128)(2,1)} %get-tuple-element.196.refs_2_.part, bf16[640,1024]{1,0:T(8,128)(2,1)} %copy-done.27, f32[9,1024]{1,0:T(8,128)} %stack_vectors.1.vectors.refs_5_.gains, bf16[640,1024]{1,0:T(8,128)(2,1)} %get-tuple-element.155.refs_1_.branch.middle_grad), custom_call_target="tpu_custom_call" | custom-call | flops 3000000000 | tf_op jit(solution)/shard_map/input_back/pallas_call | solution.py:1595
  (266 shorter events, 114.6 us)
Async XLA Ops:
  23.3 20.9 %collective-permute-start.6 = (bf16[1536,128]{1,0:T(8,128)(2,1)S(1)}, bf16[1536,128]{1,0:T(8,128)(2,1)S(1)}, u32[]{:S(2)}, u32[]{:S(2)}) collective-permute-start(bf16[1536,128]{1,0:T(8,128)(2,1)S(1)} %get-tuple-element.131.refs_4_.refs_5_), channel_id=1, source_target_pairs={{0,8},{2,10},{4,12},{6,14},{8,16},{10,18},{12,20},{14,22},{16,24},... | collective-permute-start | bytes 1179656 | tf_op jit(solution)/shard_map/ppermute | solution.py:1644
  25.0 20.3 %collective-permute-start.7 = (bf16[1536,128]{1,0:T(8,128)(2,1)S(1)}, bf16[1536,128]{1,0:T(8,128)(2,1)S(1)}, u32[]{:S(2)}, u32[]{:S(2)}) collective-permute-start(bf16[1536,128]{1,0:T(8,128)(2,1)S(1)} %get-tuple-element.136), channel_id=1, source_target_pairs={{0,24},{2,26},{4,28},{6,30},{8,0},{10,2},{12,4},{14,6},{16,8},{18,... | collective-permute-start | bytes 1179656 | tf_op jit(solution)/shard_map/ppermute | solution.py:1644
  27.2 35.1 %collective-permute-start.13 = (bf16[512,1024]{1,0:T(8,128)(2,1)S(1)}, bf16[512,1024]{1,0:T(8,128)(2,1)S(1)}, u32[]{:S(2)}, u32[]{:S(2)}) collective-permute-start(bf16[512,1024]{1,0:T(8,128)(2,1)S(1)} %copy-done.29), channel_id=1, source_target_pairs={{0,1},{1,0},{2,3},{3,2},{4,5},{5,4},{6,7},{7,6},{8,9},{9,8},{10,11... | collective-permute-start | bytes 3145736 | tf_op jit(solution)/shard_map/ppermute | solution.py:1627
  40.4 22.0 %collective-permute-start.11 = (bf16[1536,128]{1,0:T(8,128)(2,1)S(1)}, bf16[1536,128]{1,0:T(8,128)(2,1)}, u32[]{:S(2)}, u32[]{:S(2)}) collective-permute-start(bf16[1536,128]{1,0:T(8,128)(2,1)S(1)} %get-tuple-element.141), channel_id=1, source_target_pairs={{0,8},{2,10},{4,12},{6,14},{8,16},{10,18},{12,20},{14,22},{16,24},... | collective-permute-start | bytes 1179656 | tf_op jit(solution)/shard_map/ppermute | solution.py:1644
  41.0 21.4 %collective-permute-start.12 = (bf16[1536,128]{1,0:T(8,128)(2,1)S(1)}, bf16[1536,128]{1,0:T(8,128)(2,1)}, u32[]{:S(2)}, u32[]{:S(2)}) collective-permute-start(bf16[1536,128]{1,0:T(8,128)(2,1)S(1)} %get-tuple-element.142), channel_id=1, source_target_pairs={{0,24},{2,26},{4,28},{6,30},{8,0},{10,2},{12,4},{14,6},{16,8},{18,... | collective-permute-start | bytes 1179656 | tf_op jit(solution)/shard_map/ppermute | solution.py:1644
  80.3 17.2 %collective-permute-start.18 = (bf16[640,128]{1,0:T(8,128)(2,1)}, bf16[640,128]{1,0:T(8,128)(2,1)S(1)}, u32[]{:S(2)}, u32[]{:S(2)}) collective-permute-start(bf16[640,128]{1,0:T(8,128)(2,1)} %get-tuple-element.146.refs_12_.refs_16_), channel_id=1, source_target_pairs={{0,3},{1,2},{2,1},{3,0},{4,7},{5,6},{6,5},{7,4},{8,11},{9,10},{10,... | collective-permute-start | bytes 491528 | tf_op jit(solution)/shard_map/ppermute | solution.py:1638
  116.9 30.9 %collective-permute-start.21 = (bf16[640,1024]{1,0:T(8,128)(2,1)}, bf16[640,1024]{1,0:T(8,128)(2,1)S(1)}, u32[]{:S(2)}, u32[]{:S(2)}) collective-permute-start(bf16[640,1024]{1,0:T(8,128)(2,1)} %get-tuple-element.154.refs_2_), channel_id=1, source_target_pairs={{0,1},{1,0},{2,3},{3,2},{4,5},{5,4},{6,7},{7,6},{8,9},{9,8},{10,11... | collective-permute-start | bytes 3932168 | tf_op jit(solution)/shard_map/ppermute | solution.py:1627
  140.8 18.0 %collective-permute-start.26 = (bf16[512,1024]{1,0:T(8,128)(2,1)}, bf16[512,1024]{1,0:T(8,128)(2,1)S(1)}, u32[]{:S(2)}, u32[]{:S(2)}) collective-permute-start(bf16[512,1024]{1,0:T(8,128)(2,1)} %get-tuple-element.165), channel_id=1, source_target_pairs={{0,2},{2,0},{4,6},{6,4},{8,10},{10,8},{12,14},{14,12},{16,18},{18,... | collective-permute-start | bytes 3145736 | tf_op jit(solution)/shard_map/ppermute | solution.py:1632
  140.9 18.0 %collective-permute-start.27 = (bf16[512,1024]{1,0:T(8,128)(2,1)}, bf16[512,1024]{1,0:T(8,128)(2,1)S(1)}, u32[]{:S(2)}, u32[]{:S(2)}) collective-permute-start(bf16[512,1024]{1,0:T(8,128)(2,1)} %get-tuple-element.166), channel_id=1, source_target_pairs={{0,2},{2,0},{4,6},{6,4},{8,10},{10,8},{12,14},{14,12},{16,18},{18,... | collective-permute-start | bytes 3145736 | tf_op jit(solution)/shard_map/ppermute | solution.py:1632
  141.4 18.3 %collective-permute-start.28 = (bf16[512,1024]{1,0:T(8,128)(2,1)}, bf16[512,1024]{1,0:T(8,128)(2,1)}, u32[]{:S(2)}, u32[]{:S(2)}) collective-permute-start(bf16[512,1024]{1,0:T(8,128)(2,1)} %get-tuple-element.168), channel_id=1, source_target_pairs={{0,2},{2,0},{4,6},{6,4},{8,10},{10,8},{12,14},{14,12},{16,18},{18,... | collective-permute-start | bytes 3145736 | tf_op jit(solution)/shard_map/ppermute | solution.py:1632
  141.5 19.4 %collective-permute-start.29 = (bf16[512,1024]{1,0:T(8,128)(2,1)}, bf16[512,1024]{1,0:T(8,128)(2,1)}, u32[]{:S(2)}, u32[]{:S(2)}) collective-permute-start(bf16[512,1024]{1,0:T(8,128)(2,1)} %get-tuple-element.169), channel_id=1, source_target_pairs={{0,2},{2,0},{4,6},{6,4},{8,10},{10,8},{12,14},{14,12},{16,18},{18,... | collective-permute-start | bytes 3145736 | tf_op jit(solution)/shard_map/ppermute | solution.py:1632
  156.5 37.0 %collective-permute-start.22 = (bf16[640,1024]{1,0:T(8,128)(2,1)}, bf16[640,1024]{1,0:T(8,128)(2,1)S(1)}, u32[]{:S(2)}, u32[]{:S(2)}) collective-permute-start(bf16[640,1024]{1,0:T(8,128)(2,1)} %after_all.3), channel_id=1, source_target_pairs={{0,1},{1,0},{2,3},{3,2},{4,5},{5,4},{6,7},{7,6},{8,9},{9,8},{10,11... | collective-permute-start | bytes 3932168 | tf_op jit(solution)/shard_map/ppermute | solution.py:1627
  171.2 40.2 %collective-permute-start.35 = (bf16[256,2048]{1,0:T(8,128)(2,1)}, bf16[256,2048]{1,0:T(8,128)(2,1)S(1)}, u32[]{:S(2)}, u32[]{:S(2)}) collective-permute-start(bf16[256,2048]{1,0:T(8,128)(2,1)} %get-tuple-element.180), channel_id=1, source_target_pairs={{0,8},{2,10},{4,12},{6,14},{8,0},{10,2},{12,4},{14,6},{16,24},{18,... | collective-permute-start | bytes 3145736 | tf_op jit(solution)/shard_map/ppermute | solution.py:1632
  173.6 39.1 %collective-permute-start.36 = (bf16[256,2048]{1,0:T(8,128)(2,1)}, bf16[256,2048]{1,0:T(8,128)(2,1)S(1)}, u32[]{:S(2)}, u32[]{:S(2)}) collective-permute-start(bf16[256,2048]{1,0:T(8,128)(2,1)} %get-tuple-element.182), channel_id=1, source_target_pairs={{0,4},{2,6},{4,0},{6,2},{8,12},{10,14},{12,8},{14,10},{16,20},{18,... | collective-permute-start | bytes 3145736 | tf_op jit(solution)/shard_map/ppermute | solution.py:1632
  175.0 36.4 %collective-permute-start.37 = (bf16[512,640]{1,0:T(8,128)(2,1)}, bf16[512,640]{1,0:T(8,128)(2,1)S(1)}, u32[]{:S(2)}, u32[]{:S(2)}) collective-permute-start(bf16[512,640]{1,0:T(8,128)(2,1)} %get-tuple-element.183), channel_id=1, source_target_pairs={{0,2},{2,0},{4,6},{6,4},{8,10},{10,8},{12,14},{14,12},{16,18},{18,... | collective-permute-start | bytes 1966088 | tf_op jit(solution)/shard_map/ppermute | solution.py:1632
  187.0 33.0 %collective-permute-start.33 = (bf16[1536,256]{1,0:T(8,128)(2,1)}, bf16[1536,256]{1,0:T(8,128)(2,1)}, u32[]{:S(2)}, u32[]{:S(2)}) collective-permute-start(bf16[1536,256]{1,0:T(8,128)(2,1)} %get-tuple-element.177), channel_id=1, source_target_pairs={{0,24},{2,26},{4,28},{6,30},{8,0},{10,2},{12,4},{14,6},{16,8},{18,... | collective-permute-start | bytes 2359304 | tf_op jit(solution)/shard_map/ppermute | solution.py:1644
  193.5 39.6 %collective-permute-start.34 = (bf16[1536,256]{1,0:T(8,128)(2,1)}, bf16[1536,256]{1,0:T(8,128)(2,1)}, u32[]{:S(2)}, u32[]{:S(2)}) collective-permute-start(bf16[1536,256]{1,0:T(8,128)(2,1)} %get-tuple-element.178), channel_id=1, source_target_pairs={{0,8},{2,10},{4,12},{6,14},{8,16},{10,18},{12,20},{14,22},{16,24},... | collective-permute-start | bytes 2359304 | tf_op jit(solution)/shard_map/ppermute | solution.py:1644
  211.3 22.2 %collective-permute-start.30 = (bf16[640,128]{1,0:T(8,128)(2,1)}, bf16[640,128]{1,0:T(8,128)(2,1)}, u32[]{:S(2)}, u32[]{:S(2)}) collective-permute-start(bf16[640,128]{1,0:T(8,128)(2,1)} %get-tuple-element.173), channel_id=1, source_target_pairs={{0,2},{2,0},{4,6},{6,4},{8,10},{10,8},{12,14},{14,12},{16,18},{18,... | collective-permute-start | bytes 491528 | tf_op jit(solution)/shard_map/ppermute | solution.py:1632
  211.4 22.1 %collective-permute-start.31 = (bf16[640,128]{1,0:T(8,128)(2,1)}, bf16[640,128]{1,0:T(8,128)(2,1)}, u32[]{:S(2)}, u32[]{:S(2)}) collective-permute-start(bf16[640,128]{1,0:T(8,128)(2,1)} %get-tuple-element.174), channel_id=1, source_target_pairs={{0,4},{2,6},{4,0},{6,2},{8,12},{10,14},{12,8},{14,10},{16,20},{18,... | collective-permute-start | bytes 491528 | tf_op jit(solution)/shard_map/ppermute | solution.py:1632
  212.8 20.8 %collective-permute-start.32 = (bf16[640,128]{1,0:T(8,128)(2,1)}, bf16[640,128]{1,0:T(8,128)(2,1)}, u32[]{:S(2)}, u32[]{:S(2)}) collective-permute-start(bf16[640,128]{1,0:T(8,128)(2,1)} %get-tuple-element.175), channel_id=1, source_target_pairs={{0,6},{2,4},{4,2},{6,0},{8,14},{10,12},{12,10},{14,8},{16,22},{18,... | collective-permute-start | bytes 491528 | tf_op jit(solution)/shard_map/ppermute | solution.py:1632
  220.0 22.8 %collective-permute-start.42 = (bf16[128,2048]{1,0:T(8,128)(2,1)}, bf16[128,2048]{1,0:T(8,128)(2,1)}, u32[]{:S(2)}, u32[]{:S(2)}) collective-permute-start(bf16[128,2048]{1,0:T(8,128)(2,1)} %get-tuple-element.192), channel_id=1, source_target_pairs={{0,4},{2,6},{4,0},{6,2},{8,12},{10,14},{12,8},{14,10},{16,20},{18,... | collective-permute-start | bytes 1572872 | tf_op jit(solution)/shard_map/ppermute | solution.py:1632
  238.6 17.8 %collective-permute-start.41 = (bf16[128,2048]{1,0:T(8,128)(2,1)}, bf16[128,2048]{1,0:T(8,128)(2,1)S(1)}, u32[]{:S(2)}, u32[]{:S(2)}) collective-permute-start(bf16[128,2048]{1,0:T(8,128)(2,1)} %after_all.4), channel_id=1, source_target_pairs={{0,8},{2,10},{4,12},{6,14},{8,0},{10,2},{12,4},{14,6},{16,24},{18,... | collective-permute-start | bytes 1572872 | tf_op jit(solution)/shard_map/ppermute | solution.py:1632
  247.6 34.5 %collective-permute-start.47 = (bf16[64,2048]{1,0:T(8,128)(2,1)}, bf16[64,2048]{1,0:T(8,128)(2,1)S(1)}, u32[]{:S(2)}, u32[]{:S(2)}) collective-permute-start(bf16[64,2048]{1,0:T(8,128)(2,1)} %get-tuple-element.202), channel_id=1, source_target_pairs={{0,16},{2,18},{4,20},{6,22},{8,24},{10,26},{12,28},{14,30},{16,0},... | collective-permute-start | bytes 786440 | tf_op jit(solution)/shard_map/ppermute | solution.py:1632
  281.6 43.3 %collective-permute-start.46 = (bf16[640,1024]{1,0:T(8,128)(2,1)}, bf16[640,1024]{1,0:T(8,128)(2,1)S(1)}, u32[]{:S(2)}, u32[]{:S(2)}) collective-permute-start(bf16[640,1024]{1,0:T(8,128)(2,1)} %after_all.5), channel_id=1, source_target_pairs={{0,1},{1,0},{2,3},{3,2},{4,5},{5,4},{6,7},{7,6},{8,9},{9,8},{10,11... | collective-permute-start | bytes 3932168 | tf_op jit(solution)/shard_map/ppermute | solution.py:1627
  (104 other events, 738.0 us)

commit v7 on v6

--- a/solution.py
+++ b/solution.py
@@ -45,7 +45,7 @@
     return jax.ShapeDtypeStruct(shape, kind)
 
 
-def params(mib=60):
+def params(mib=30):
     return pltpu.CompilerParams(vmem_limit_bytes=mib * 2**20)
 
 

time: 342 us -> 324 us (0.947)
  Pallas kernels: 201 us -> 157 us
  waiting for transfers between devices: 43.9 us -> 70.7 us
  local copies, waits for them, and re-layouts: 19.6 us -> 29.7 us
  starting transfers between devices: 66.5 us -> 57.5 us
    ppermute x6, waiting for transfers between devices: 10.2 us -> 24.4 us  [to_group(): lax.ppermute(value, 'dp', [(i, (i + step) % count) for i in range(count)])]
    ppermute x45, waiting for transfers between devices: 27.1 us -> 38.9 us  [to_member(): return lax.ppermute(value, 'dp', [(i, i ^ d) for i in range(count)])]
    unnamed x138 -> x206, local copies, waits for them, and re-layouts: 18.3 us -> 29.6 us
    ppermute x45, starting transfers between devices: 41.4 us -> 35.4 us  [to_member(): return lax.ppermute(value, 'dp', [(i, i ^ d) for i in range(count)])]
    pallas_call x2, Pallas kernels: 10.3 us -> 5.46 us  [takes(): pl.pallas_call(partial(takes_kernel, flags, len(deps)), grid=(TAKE_STEPS,...]
    pallas_call x1, Pallas kernels: 9.18 us -> 4.68 us  [product(): pl.pallas_call(skipping(partial(product_kernel, ((1,), (1,) if turned els...]
    pallas_call x1, Pallas kernels: 8.26 us -> 4.41 us  [join_stage(): pl.pallas_call(partial(join_kernel, len(riders)), out_shape=outs, in_spec...]
    pallas_call x1, Pallas kernels: 4.97 us -> 1.42 us  [gather_back(): pl.pallas_call(skipping(gather_back_kernel, used, len(deps)), out_shape=[...]
  transfers between devices with their start and end apart: 60 -> 60, of which waited for: 16 -> 20; matrix products, arithmetic and copies ran while one was open for 2% -> 1% of each run, Pallas kernels for 47% -> 38%
where the time goes in v7:
time: 324 us; the launch traced here: 317 us
  Pallas kernels  157 us (48%)
  waiting for transfers between devices  70.7 us (22%)
  starting transfers between devices  57.5 us (18%)
  local copies, waits for them, and re-layouts  29.7 us (9%)
    ppermute x45, waiting for transfers between devices, to_member(): return lax.ppermute(value, 'dp', [(i, i ^ d) for i in range(count)])  38.9 us
    ppermute x45, starting transfers between devices, to_member(): return lax.ppermute(value, 'dp', [(i, i ^ d) for i in range(count)])  35.4 us
    unnamed x206, local copies, waits for them, and re-layouts  29.6 us
    ppermute x6, waiting for transfers between devices, to_group(): lax.ppermute(value, 'dp', [(i, (i + step) % count) for i in range(count)])  24.4 us
    pallas_call x1, Pallas kernels, feed_grads(): pl.pallas_call(feed_grads_kernel, grid=(2 * tiles,), out_shape=[kept, sen...  21.9 us
    pallas_call x1, Pallas kernels, back_near(): pl.pallas_call(skipping(back_near_kernel, used, len(deps)), out_shape=[sh...  17.1 us
    pallas_call x1, Pallas kernels, feed(): pl.pallas_call(feed_kernel, out_shape=[shaped((rows, half), BF16), shaped...  15.2 us
    pallas_call x1, Pallas kernels, attend_near(): pl.pallas_call(skipping(attend_near_kernel, used, len(deps)), out_shape=[...  14.6 us
  transfers between devices with their start and end apart: 60, of which 20 were waited for; matrix products, arithmetic and copies ran while one was open for 1% of the time, Pallas kernels for 38%

profile of v7, /device:TPU:0, one launch (start us, length us, event | category | flops | bytes accessed | tf_op | source)
XLA Modules:
  0.0 317.3 jit_solution(8728240383888118678)
XLA Ops:
  6.3 4.1 %project.1 = (bf16[640,1024]{1,0:T(8,128)(2,1)S(1)}, bf16[640,128]{1,0:T(8,128)(2,1)S(1)}, bf16[640,128]{1,0:T(8,128)(2,1)S(1)}, bf16[640,128]{1,0:T(8,128)(2,1)...) custom-call(s32[5]{0:T(128)S(1)} %stack.23.meta.refs_0_.refs_1_, ...), custom_call_target="tpu_custom_call" | custom-call | flops 4499999744 | tf_op jit(solution)/shard_map/project/pallas_call | solution.py:319
  33.8 6.2 %tables.1.refs_0_ = s32[1024]{0:T(1024)S(1)} custom-call(s32[5]{0:T(128)S(1)} %stack.23.meta.refs_0_.refs_1_, s32[80]{0:T(128)S(1)} %copy-done.72, s32[32]{0:T(128)S(1)} %get-tuple-element.125.refs_0_.refs_2_, s32[80]{0:T(128)S(1)} %get-tuple-element.126.refs_3_, bf16[1536,128]{1,0:T(8,128)(2,1)S(1)} %get-tuple-element.131.refs_4_.refs_5_), custom_call_target="tpu_custom_call" | custom-call | flops 1000000000 | tf_op jit(solution)/shard_map/tables/pallas_call | solution.py:249
  46.2 14.6 %attend_near.1 = (f32[20,128,128]{2,1,0:T(8,128)S(1)}, f32[20,8,256]{2,1,0:T(8,128)S(1)}) custom-call(s32[1024]{0:T(1024)S(1)} %tables.1.refs_0_, s32[5]{0:T(128)S(1)} %stack.23.meta.refs_0_.refs_1_, f32[16]{0:T(128)S(1)} %multiply_exponential_fusion.refs_2_, bf16[640,128]{1,0:T(8,128)(2,1)S(1)} %get-tuple-element.132.refs_3_, ...), custom_call_target="tpu_custom_call" | custom-call | flops 7000000000 | tf_op jit(solution)/shard_map/attend_near/pallas_call | solution.py:533
  62.6 14.5 %attend_far.1 = (bf16[640,128]{1,0:T(8,128)(2,1)S(1)}, bf16[640,128]{1,0:T(8,128)(2,1)S(1)}, bf16[640,128]{1,0:T(8,128)(2,1)S(1)}, bf16[640,128]{1,0:T(8,128)(2,1)S(1)}, f32[20,1,256]{2,1,0:T(1,128)S(1)}) custom-call(s32[1024]{0:T(1024)S(1)} %tables.1.refs_0_, s32[5]{0:T(128)S(1)} %stack.23.meta.refs_0_.refs_1_, f32[16]{0:T(128)S(1)} %multiply_exponential_fusion.refs_2_, ...), custom_call_target="tpu_custom_call" | custom-call | flops 7500000256 | tf_op jit(solution)/shard_map/attend_far/pallas_call | solution.py:603
  85.8 4.7 %hidden_grad.1 = f32[640,2048]{1,0:T(8,128)S(1)} custom-call(bf16[640,1024]{1,0:T(8,128)(2,1)S(1)} %copy-done.7, bf16[2048,1024]{1,0:T(8,128)(2,1)S(1)} %copy-done.1, bf16[640,128]{1,0:T(8,128)(2,1)S(1)} %get-tuple-element.145.refs_2_.a0.refs_11_.refs_15_), custom_call_target="tpu_custom_call" | custom-call | flops 2500000000 | tf_op jit(solution)/shard_map/hidden_grad/pallas_call | solution.py:977
  95.9 15.2 %feed.1 = (bf16[640,512]{1,0:T(8,128)(2,1)S(1)}, f32[640,1024]{1,0:T(8,128)S(1)}, bf16[640,1024]{1,0:T(8,128)(2,1)S(1)}, bf16[640,2048]{1,0:T(8,128)(2,1)S(1)}, ...) custom-call(s32[5]{0:T(128)S(1)} %stack.23.meta.refs_0_.refs_1_, ...), custom_call_target="tpu_custom_call" | custom-call | flops 8999999488 | tf_op jit(solution)/shard_map/feed/pallas_call | solution.py:937
  115.0 21.9 %feed_grads.1 = (bf16[512,2048]{1,0:T(8,128)(2,1)S(1)}, bf16[512,1024]{1,0:T(8,128)(2,1)}, bf16[512,1024]{1,0:T(8,128)(2,1)}, bf16[512,2048]{1,0:T(8,128)(2,1)S(...) custom-call(s32[5]{0:T(128)S(1)} %stack.23.meta.refs_0_.refs_1_, ...), custom_call_target="tpu_custom_call" | custom-call | flops 10000000000 | tf_op jit(solution)/shard_map/feed_grads/pallas_call | solution.py:1095
  142.7 4.3 %middle_back.1 = (bf16[640,1024]{1,0:T(8,128)(2,1)S(1)}, f32[8,1024]{1,0:T(8,128)S(1)}, bf16[640,128]{1,0:T(8,128)(2,1)S(1)}, bf16[640,128]{1,0:T(8,128)(2,1)S(1...) custom-call(s32[5]{0:T(128)S(1)} %stack.23.meta.refs_0_.refs_1_, ...), custom_call_target="tpu_custom_call" | custom-call | flops 4000000000 | tf_op jit(solution)/shard_map/middle_back/pallas_call | solution.py:1396
  158.5 7.1 %output_grads.1 = (bf16[512,640]{1,0:T(8,128)(2,1)S(1)}, bf16[512,640]{1,0:T(8,128)(2,1)S(1)}, f32[256,2048]{1,0:T(8,128)S(1)}, bf16[256,2048]{1,0:T(8,128)(2,1)...) custom-call(s32[5]{0:T(128)S(1)} %stack.23.meta.refs_0_.refs_1_, bf16[640,1024]{1,0:T(8,128)(2,1)S(1)} %copy-done.5, ...), custom_call_target="tpu_custom_call" | custom-call | flops 4499999744 | tf_op jit(solution)/shard_map/output_grads/pallas_call | solution.py:1249
  167.6 11.6 %back_far.1 = (bf16[1536,256]{1,0:T(8,128)(2,1)S(1)}, bf16[1536,256]{1,0:T(8,128)(2,1)S(1)}, f32[20,128,128]{2,1,0:T(8,128)S(1)}) custom-call(s32[1024]{0:T(1024)S(1)} %tables.1.refs_0_, s32[5]{0:T(128)S(1)} %stack.23.meta.refs_0_.refs_1_, f32[16]{0:T(128)S(1)} %multiply_exponential_fusion.refs_2_, bf16[640,128]{1,0:T(8,128)(2,1)S(1)} %copy-done.99, ...), custom_call_target="tpu_custom_call" | custom-call | flops 7000000000 | tf_op jit(solution)/shard_map/back_far/pallas_call | solution.py:720
  179.2 3.3 %collective-permute-start.33 = (bf16[1536,256]{1,0:T(8,128)(2,1)S(1)}, bf16[1536,256]{1,0:T(8,128)(2,1)S(1)}, u32[]{:S(2)}, u32[]{:S(2)}) collective-permute-start(bf16[1536,256]{1,0:T(8,128)(2,1)S(1)} %get-tuple-element.177), channel_id=1, source_target_pairs={{0,24},{2,26},{4,28},{6,30},{8,0},{10,2},{12,4},{14,6},{16,8},{18,... | collective-permute-start | bytes 2359304 | tf_op jit(solution)/shard_map/ppermute | solution.py:1644
  182.9 17.1 %back_near.1 = (bf16[640,128]{1,0:T(8,128)(2,1)S(1)}, bf16[640,128]{1,0:T(8,128)(2,1)S(1)}, bf16[640,128]{1,0:T(8,128)(2,1)S(1)}, bf16[640,128]{1,0:T(8,128)(2,1)S(1)}, f32[2560,256]{1,0:T(8,128)S(1)}) custom-call(s32[1024]{0:T(1024)S(1)} %tables.1.refs_0_, s32[5]{0:T(128)S(1)} %stack.23.meta.refs_0_.refs_1_, f32[16]{0:T(128)S(1)} %multiply_exponential_fusion.refs_2_, ...), custom_call_target="tpu_custom_call" | custom-call | flops 7500000256 | tf_op jit(solution)/shard_map/back_near/pallas_call | solution.py:784
  203.8 4.2 %collective-permute-done.33.refs_2_ = bf16[1536,256]{1,0:T(8,128)(2,1)S(1)} collective-permute-done((bf16[1536,256]{1,0:T(8,128)(2,1)S(1)}, bf16[1536,256]{1,0:T(8,128)(2,1)S(1)}, u32[]{:S(2)}, u32[]{:S(2)}) %collective-permute-start.33) | collective-permute-done | bytes 786464 | tf_op jit(solution)/shard_map/ppermute | solution.py:1644
  209.2 16.3 %collective-permute-done.34.refs_3_ = bf16[1536,256]{1,0:T(8,128)(2,1)S(1)} collective-permute-done((bf16[1536,256]{1,0:T(8,128)(2,1)S(1)}, bf16[1536,256]{1,0:T(8,128)(2,1)S(1)}, u32[]{:S(2)}, u32[]{:S(2)}) %collective-permute-start.34) | collective-permute-done | bytes 786464 | tf_op jit(solution)/shard_map/ppermute | solution.py:1644
  231.3 5.1 %collective-permute-done.43.refs_3_ = bf16[256,640]{1,0:T(8,128)(2,1)} collective-permute-done((bf16[256,640]{1,0:T(8,128)(2,1)}, bf16[256,640]{1,0:T(8,128)(2,1)}, u32[]{:S(2)}, u32[]{:S(2)}) %collective-permute-start.43) | collective-permute-done | bytes 327712 | tf_op jit(solution)/shard_map/ppermute | solution.py:1632
  237.6 3.5 %third_step.1 = (f32[64,2048]{1,0:T(8,128)S(1)}, bf16[64,2048]{1,0:T(8,128)(2,1)}, f32[128,640]{1,0:T(8,128)S(1)}, bf16[128,640]{1,0:T(8,128)(2,1)S(1)}) custom-call(f32[128,2048]{1,0:T(8,128)S(1)} %copy-done.29, bf16[128,2048]{1,0:T(8,128)(2,1)} %collective-permute-done.42.refs_1_, f32[256,640]{1,0:T(8,128)S(1)} %copy-done.31, ...), custom_call_target="tpu_custom_call" | custom-call | flops 1500000000 | tf_op jit(solution)/shard_map/third_step/pallas_call | solution.py:1168
  243.4 4.0 %collective-permute-done.40.k3 = bf16[640,256]{1,0:T(8,128)(2,1)S(1)} collective-permute-done((bf16[640,256]{1,0:T(8,128)(2,1)}, bf16[640,256]{1,0:T(8,128)(2,1)S(1)}, u32[]{:S(2)}, u32[]{:S(2)}) %collective-permute-start.40) | collective-permute-done | bytes 327712 | tf_op jit(solution)/shard_map/ppermute | solution.py:1632
  250.0 4.4 %join_stage.1 = (bf16[640,1536]{1,0:T(8,128)(2,1)S(1)}, bf16[640,1024]{1,0:T(8,128)(2,1)S(1)}, f32[8,1024]{1,0:T(8,128)S(1)}, f32[64,2048]{1,0:T(8,128)S(1)}, f3...) custom-call(s32[5]{0:T(128)S(1)} %stack.23.meta.refs_0_.refs_1_, bf16[1024,1536]{1,0:T(8,128)(2,1)S(1)} %copy-done.19, ...), custom_call_target="tpu_custom_call" | custom-call | flops 3500000000 | tf_op jit(solution)/shard_map/join_stage/pallas_call | solution.py:1461
  254.5 5.1 %joined_first.1 = (bf16[512,1024]{1,0:T(8,128)(2,1)S(1)}, bf16[512,1024]{1,0:T(8,128)(2,1)}, f32[8,1024]{1,0:T(8,128)S(1)}) custom-call(s32[5]{0:T(128)S(1)} %stack.23.meta.refs_0_.refs_1_, bf16[640,1024]{1,0:T(8,128)(2,1)S(1)} %copy-done.22, bf16[640,1024]{1,0:T(8,128)(2,1)S(1)} %get-tuple-element.196.refs_2_.part, bf16[640,1024]{1,0:T(8,128)(2,1)S(1)} %copy-done.92, ...), custom_call_target="tpu_custom_call" | custom-call | flops 4499999744 | tf_op jit(solution)/shard_map/joined_first/pallas_call | solution.py:1503
  264.8 7.2 %collective-permute-done.48.got_eo = bf16[64,2688]{1,0:T(8,128)(2,1)} collective-permute-done((bf16[64,2688]{1,0:T(8,128)(2,1)S(1)}, bf16[64,2688]{1,0:T(8,128)(2,1)}, u32[]{:S(2)}, u32[]{:S(2)}) %collective-permute-start.48) | collective-permute-done | bytes 344096 | tf_op jit(solution)/shard_map/ppermute | solution.py:1632
  277.8 4.7 %joined_second.1 = (bf16[512,640]{1,0:T(8,128)(2,1)S(1)}, bf16[512,256]{1,0:T(8,128)(2,1)S(1)}, bf16[512,384]{1,0:T(8,128)(2,1)S(1)}, f32[64,2048]{1,0:T(8,128)}...) custom-call(s32[5]{0:T(128)S(1)} %stack.23.meta.refs_0_.refs_1_, bf16[640,1024]{1,0:T(8,128)(2,1)S(1)} %copy-done.93, ...), custom_call_target="tpu_custom_call" | custom-call | flops 30000001024 | tf_op jit(solution)/shard_map/joined_second/pallas_call | solution.py:1565
  291.2 6.5 %collective-permute-done.53.refs_3_ = bf16[128,640]{1,0:T(8,128)(2,1)S(1)} collective-permute-done((bf16[128,640]{1,0:T(8,128)(2,1)S(1)}, bf16[128,640]{1,0:T(8,128)(2,1)S(1)}, u32[]{:S(2)}, u32[]{:S(2)}) %collective-permute-start.53) | collective-permute-done | bytes 163872 | tf_op jit(solution)/shard_map/ppermute | solution.py:1632
  300.7 4.1 %collective-permute-start.56 = (bf16[64,1024]{1,0:T(8,128)(2,1)S(1)}, bf16[64,1024]{1,0:T(8,128)(2,1)S(1)}, u32[]{:S(2)}, u32[]{:S(2)}) collective-permute-start(bf16[64,1024]{1,0:T(8,128)(2,1)S(1)} %get-tuple-element.219), channel_id=1, source_target_pairs={{0,16},{2,18},{4,20},{6,22},{8,24},{10,26},{12,28},{14,30},{16,0},... | collective-permute-start | bytes 393224 | tf_op jit(solution)/shard_map/ppermute | solution.py:1632
  311.9 4.2 %collective-permute-done.58.g3 = bf16[64,1024]{1,0:T(8,128)(2,1)S(1)} collective-permute-done((bf16[64,1024]{1,0:T(8,128)(2,1)S(1)}, bf16[64,1024]{1,0:T(8,128)(2,1)S(1)}, u32[]{:S(2)}, u32[]{:S(2)}) %collective-permute-start.58) | collective-permute-done | bytes 131104 | tf_op jit(solution)/shard_map/ppermute | solution.py:1632
  (334 shorter events, 121.4 us)
Async XLA Ops:
  24.1 19.7 %collective-permute-start.6 = (bf16[1536,128]{1,0:T(8,128)(2,1)S(1)}, bf16[1536,128]{1,0:T(8,128)(2,1)S(1)}, u32[]{:S(2)}, u32[]{:S(2)}) collective-permute-start(bf16[1536,128]{1,0:T(8,128)(2,1)S(1)} %get-tuple-element.131.refs_4_.refs_5_), channel_id=1, source_target_pairs={{0,8},{2,10},{4,12},{6,14},{8,16},{10,18},{12,20},{14,22},{16,24},... | collective-permute-start | bytes 1179656 | tf_op jit(solution)/shard_map/ppermute | solution.py:1644
  25.8 20.3 %collective-permute-start.7 = (bf16[1536,128]{1,0:T(8,128)(2,1)S(1)}, bf16[1536,128]{1,0:T(8,128)(2,1)S(1)}, u32[]{:S(2)}, u32[]{:S(2)}) collective-permute-start(bf16[1536,128]{1,0:T(8,128)(2,1)S(1)} %get-tuple-element.136), channel_id=1, source_target_pairs={{0,24},{2,26},{4,28},{6,30},{8,0},{10,2},{12,4},{14,6},{16,8},{18,... | collective-permute-start | bytes 1179656 | tf_op jit(solution)/shard_map/ppermute | solution.py:1644
  28.0 34.5 %collective-permute-start.13 = (bf16[512,1024]{1,0:T(8,128)(2,1)S(1)}, bf16[512,1024]{1,0:T(8,128)(2,1)S(1)}, u32[]{:S(2)}, u32[]{:S(2)}) collective-permute-start(bf16[512,1024]{1,0:T(8,128)(2,1)S(1)} %copy-done.24), channel_id=1, source_target_pairs={{0,1},{1,0},{2,3},{3,2},{4,5},{5,4},{6,7},{7,6},{8,9},{9,8},{10,11... | collective-permute-start | bytes 3145736 | tf_op jit(solution)/shard_map/ppermute | solution.py:1627
  40.0 20.8 %collective-permute-start.11 = (bf16[1536,128]{1,0:T(8,128)(2,1)S(1)}, bf16[1536,128]{1,0:T(8,128)(2,1)S(1)}, u32[]{:S(2)}, u32[]{:S(2)}) collective-permute-start(bf16[1536,128]{1,0:T(8,128)(2,1)S(1)} %get-tuple-element.141), channel_id=1, source_target_pairs={{0,8},{2,10},{4,12},{6,14},{8,16},{10,18},{12,20},{14,22},{16,24},... | collective-permute-start | bytes 1179656 | tf_op jit(solution)/shard_map/ppermute | solution.py:1644
  40.7 21.8 %collective-permute-start.12 = (bf16[1536,128]{1,0:T(8,128)(2,1)S(1)}, bf16[1536,128]{1,0:T(8,128)(2,1)S(1)}, u32[]{:S(2)}, u32[]{:S(2)}) collective-permute-start(bf16[1536,128]{1,0:T(8,128)(2,1)S(1)} %get-tuple-element.142), channel_id=1, source_target_pairs={{0,24},{2,26},{4,28},{6,30},{8,0},{10,2},{12,4},{14,6},{16,8},{18,... | collective-permute-start | bytes 1179656 | tf_op jit(solution)/shard_map/ppermute | solution.py:1644
  78.8 17.0 %collective-permute-start.18 = (bf16[640,128]{1,0:T(8,128)(2,1)S(1)}, bf16[640,128]{1,0:T(8,128)(2,1)S(1)}, u32[]{:S(2)}, u32[]{:S(2)}) collective-permute-start(bf16[640,128]{1,0:T(8,128)(2,1)S(1)} %get-tuple-element.146.refs_12_.refs_16_), channel_id=1, source_target_pairs={{0,3},{1,2},{2,1},{3,0},{4,7},{5,6},{6,5},{7,4},{8,11},{9,10},{10,... | collective-permute-start | bytes 491528 | tf_op jit(solution)/shard_map/ppermute | solution.py:1638
  80.1 15.8 %collective-permute-start.19 = (bf16[640,128]{1,0:T(8,128)(2,1)S(1)}, bf16[640,128]{1,0:T(8,128)(2,1)S(1)}, u32[]{:S(2)}, u32[]{:S(2)}) collective-permute-start(bf16[640,128]{1,0:T(8,128)(2,1)S(1)} %get-tuple-element.147.refs_13_.refs_17_), channel_id=1, source_target_pairs={{0,5},{1,4},{2,7},{3,6},{4,1},{5,0},{6,3},{7,2},{8,13},{9,12},{10,... | collective-permute-start | bytes 491528 | tf_op jit(solution)/shard_map/ppermute | solution.py:1638
  112.2 30.5 %collective-permute-start.21 = (bf16[640,1024]{1,0:T(8,128)(2,1)S(1)}, bf16[640,1024]{1,0:T(8,128)(2,1)S(1)}, u32[]{:S(2)}, u32[]{:S(2)}) collective-permute-start(bf16[640,1024]{1,0:T(8,128)(2,1)S(1)} %get-tuple-element.154.refs_2_), channel_id=1, source_target_pairs={{0,1},{1,0},{2,3},{3,2},{4,5},{5,4},{6,7},{7,6},{8,9},{9,8},{10,11... | collective-permute-start | bytes 3932168 | tf_op jit(solution)/shard_map/ppermute | solution.py:1627
  138.8 15.4 %collective-permute-start.29 = (bf16[512,1024]{1,0:T(8,128)(2,1)}, bf16[512,1024]{1,0:T(8,128)(2,1)}, u32[]{:S(2)}, u32[]{:S(2)}) collective-permute-start(bf16[512,1024]{1,0:T(8,128)(2,1)} %get-tuple-element.169), channel_id=1, source_target_pairs={{0,2},{2,0},{4,6},{6,4},{8,10},{10,8},{12,14},{14,12},{16,18},{18,... | collective-permute-start | bytes 3145736 | tf_op jit(solution)/shard_map/ppermute | solution.py:1632
  150.7 31.8 %collective-permute-start.22 = (bf16[640,1024]{1,0:T(8,128)(2,1)}, bf16[640,1024]{1,0:T(8,128)(2,1)S(1)}, u32[]{:S(2)}, u32[]{:S(2)}) collective-permute-start(bf16[640,1024]{1,0:T(8,128)(2,1)} %after_all.3), channel_id=1, source_target_pairs={{0,1},{1,0},{2,3},{3,2},{4,5},{5,4},{6,7},{7,6},{8,9},{9,8},{10,11... | collective-permute-start | bytes 3932168 | tf_op jit(solution)/shard_map/ppermute | solution.py:1627
  165.7 34.6 %collective-permute-start.35 = (bf16[256,2048]{1,0:T(8,128)(2,1)S(1)}, bf16[256,2048]{1,0:T(8,128)(2,1)S(1)}, u32[]{:S(2)}, u32[]{:S(2)}) collective-permute-start(bf16[256,2048]{1,0:T(8,128)(2,1)S(1)} %get-tuple-element.180), channel_id=1, source_target_pairs={{0,8},{2,10},{4,12},{6,14},{8,0},{10,2},{12,4},{14,6},{16,24},{18,... | collective-permute-start | bytes 3145736 | tf_op jit(solution)/shard_map/ppermute | solution.py:1632
  166.9 34.9 %collective-permute-start.36 = (bf16[256,2048]{1,0:T(8,128)(2,1)S(1)}, bf16[256,2048]{1,0:T(8,128)(2,1)S(1)}, u32[]{:S(2)}, u32[]{:S(2)}) collective-permute-start(bf16[256,2048]{1,0:T(8,128)(2,1)S(1)} %get-tuple-element.182), channel_id=1, source_target_pairs={{0,4},{2,6},{4,0},{6,2},{8,12},{10,14},{12,8},{14,10},{16,20},{18,... | collective-permute-start | bytes 3145736 | tf_op jit(solution)/shard_map/ppermute | solution.py:1632
  167.4 32.6 %collective-permute-start.37 = (bf16[512,640]{1,0:T(8,128)(2,1)S(1)}, bf16[512,640]{1,0:T(8,128)(2,1)S(1)}, u32[]{:S(2)}, u32[]{:S(2)}) collective-permute-start(bf16[512,640]{1,0:T(8,128)(2,1)S(1)} %get-tuple-element.183), channel_id=1, source_target_pairs={{0,2},{2,0},{4,6},{6,4},{8,10},{10,8},{12,14},{14,12},{16,18},{18,... | collective-permute-start | bytes 1966088 | tf_op jit(solution)/shard_map/ppermute | solution.py:1632
  179.2 28.9 %collective-permute-start.33 = (bf16[1536,256]{1,0:T(8,128)(2,1)S(1)}, bf16[1536,256]{1,0:T(8,128)(2,1)S(1)}, u32[]{:S(2)}, u32[]{:S(2)}) collective-permute-start(bf16[1536,256]{1,0:T(8,128)(2,1)S(1)} %get-tuple-element.177), channel_id=1, source_target_pairs={{0,24},{2,26},{4,28},{6,30},{8,0},{10,2},{12,4},{14,6},{16,8},{18,... | collective-permute-start | bytes 2359304 | tf_op jit(solution)/shard_map/ppermute | solution.py:1644
  182.5 43.0 %collective-permute-start.34 = (bf16[1536,256]{1,0:T(8,128)(2,1)S(1)}, bf16[1536,256]{1,0:T(8,128)(2,1)S(1)}, u32[]{:S(2)}, u32[]{:S(2)}) collective-permute-start(bf16[1536,256]{1,0:T(8,128)(2,1)S(1)} %get-tuple-element.178), channel_id=1, source_target_pairs={{0,8},{2,10},{4,12},{6,14},{8,16},{10,18},{12,20},{14,22},{16,24},... | collective-permute-start | bytes 2359304 | tf_op jit(solution)/shard_map/ppermute | solution.py:1644
  200.0 26.0 %collective-permute-start.30 = (bf16[640,128]{1,0:T(8,128)(2,1)S(1)}, bf16[640,128]{1,0:T(8,128)(2,1)S(1)}, u32[]{:S(2)}, u32[]{:S(2)}) collective-permute-start(bf16[640,128]{1,0:T(8,128)(2,1)S(1)} %get-tuple-element.173), channel_id=1, source_target_pairs={{0,2},{2,0},{4,6},{6,4},{8,10},{10,8},{12,14},{14,12},{16,18},{18,... | collective-permute-start | bytes 491528 | tf_op jit(solution)/shard_map/ppermute | solution.py:1632
  200.3 25.8 %collective-permute-start.31 = (bf16[640,128]{1,0:T(8,128)(2,1)S(1)}, bf16[640,128]{1,0:T(8,128)(2,1)S(1)}, u32[]{:S(2)}, u32[]{:S(2)}) collective-permute-start(bf16[640,128]{1,0:T(8,128)(2,1)S(1)} %get-tuple-element.174), channel_id=1, source_target_pairs={{0,4},{2,6},{4,0},{6,2},{8,12},{10,14},{12,8},{14,10},{16,20},{18,... | collective-permute-start | bytes 491528 | tf_op jit(solution)/shard_map/ppermute | solution.py:1632
  201.8 24.2 %collective-permute-start.32 = (bf16[640,128]{1,0:T(8,128)(2,1)S(1)}, bf16[640,128]{1,0:T(8,128)(2,1)S(1)}, u32[]{:S(2)}, u32[]{:S(2)}) collective-permute-start(bf16[640,128]{1,0:T(8,128)(2,1)S(1)} %get-tuple-element.175), channel_id=1, source_target_pairs={{0,6},{2,4},{4,2},{6,0},{8,14},{10,12},{12,10},{14,8},{16,22},{18,... | collective-permute-start | bytes 491528 | tf_op jit(solution)/shard_map/ppermute | solution.py:1632
  208.0 28.5 %collective-permute-start.42 = (bf16[128,2048]{1,0:T(8,128)(2,1)S(1)}, bf16[128,2048]{1,0:T(8,128)(2,1)}, u32[]{:S(2)}, u32[]{:S(2)}) collective-permute-start(bf16[128,2048]{1,0:T(8,128)(2,1)S(1)} %get-tuple-element.192), channel_id=1, source_target_pairs={{0,4},{2,6},{4,0},{6,2},{8,12},{10,14},{12,8},{14,10},{16,20},{18,... | collective-permute-start | bytes 1572872 | tf_op jit(solution)/shard_map/ppermute | solution.py:1632
  229.3 18.2 %collective-permute-start.41 = (bf16[128,2048]{1,0:T(8,128)(2,1)}, bf16[128,2048]{1,0:T(8,128)(2,1)S(1)}, u32[]{:S(2)}, u32[]{:S(2)}) collective-permute-start(bf16[128,2048]{1,0:T(8,128)(2,1)} %after_all.4), channel_id=1, source_target_pairs={{0,8},{2,10},{4,12},{6,14},{8,0},{10,2},{12,4},{14,6},{16,24},{18,... | collective-permute-start | bytes 1572872 | tf_op jit(solution)/shard_map/ppermute | solution.py:1632
  241.2 23.7 %collective-permute-start.47 = (bf16[64,2048]{1,0:T(8,128)(2,1)}, bf16[64,2048]{1,0:T(8,128)(2,1)}, u32[]{:S(2)}, u32[]{:S(2)}) collective-permute-start(bf16[64,2048]{1,0:T(8,128)(2,1)} %get-tuple-element.202), channel_id=1, source_target_pairs={{0,16},{2,18},{4,20},{6,22},{8,24},{10,26},{12,28},{14,30},{16,0},... | collective-permute-start | bytes 786440 | tf_op jit(solution)/shard_map/ppermute | solution.py:1632
  254.4 17.6 %collective-permute-start.48 = (bf16[64,2688]{1,0:T(8,128)(2,1)S(1)}, bf16[64,2688]{1,0:T(8,128)(2,1)}, u32[]{:S(2)}, u32[]{:S(2)}) collective-permute-start(bf16[64,2688]{1,0:T(8,128)(2,1)S(1)} %get-tuple-element.205), channel_id=1, source_target_pairs={{0,16},{2,18},{4,20},{6,22},{8,24},{10,26},{12,28},{14,30},{16,0},... | collective-permute-start | bytes 1032200 | tf_op jit(solution)/shard_map/ppermute | solution.py:1632
  261.4 23.2 %collective-permute-start.49 = (bf16[512,1024]{1,0:T(8,128)(2,1)}, bf16[512,1024]{1,0:T(8,128)(2,1)}, u32[]{:S(2)}, u32[]{:S(2)}) collective-permute-start(bf16[512,1024]{1,0:T(8,128)(2,1)} %get-tuple-element.208), channel_id=1, source_target_pairs={{0,2},{2,0},{4,6},{6,4},{8,10},{10,8},{12,14},{14,12},{16,18},{18,... | collective-permute-start | bytes 3145736 | tf_op jit(solution)/shard_map/ppermute | solution.py:1632
  264.3 43.5 %collective-permute-start.46 = (bf16[640,1024]{1,0:T(8,128)(2,1)}, bf16[640,1024]{1,0:T(8,128)(2,1)S(1)}, u32[]{:S(2)}, u32[]{:S(2)}) collective-permute-start(bf16[640,1024]{1,0:T(8,128)(2,1)} %after_all.5), channel_id=1, source_target_pairs={{0,1},{1,0},{2,3},{3,2},{4,5},{5,4},{6,7},{7,6},{8,9},{9,8},{10,11... | collective-permute-start | bytes 3932168 | tf_op jit(solution)/shard_map/ppermute | solution.py:1627
  (138 other events, 1439.4 us)
